TPU v7x, 32 devices: a whole 2x2x4 slice. The times are simulated.
32 devices in a mesh: dp: 32 (over z, y, x, core).
Axes of the slice: x: 2, y: 2, z: 4, core: 2. Of those that a mesh axis runs over, the one named last changes fastest.
Arguments:
- hidden_in: bfloat16 [32768, 768], P('dp'), may hold values from -6 to 6
- lengths: int32 [64], P('dp'), may hold values from 128 to 512, as said below
- cotangent: bfloat16 [32768, 768], P('dp'), may hold values from -6 to 6
- proj_qkv: float32 [768, 2304], P('dp'), may hold values from -0.21875 to 0.21875
- proj_attn: float32 [768, 768], P('dp'), may hold values from -1.75 to 1.75
- proj_up: float32 [768, 3072], P('dp'), may hold values from -0.21875 to 0.21875
- proj_down: float32 [3072, 768], P('dp'), may hold values from -0.21875 to 0.21875
- vectors: float32 [9216], P('dp'), may hold values from -1 to 2
- first_qkv: float32 [768, 2304], P('dp'), may hold values from -6 to 6
- first_attn: float32 [768, 768], P('dp'), may hold values from -40 to 40
- first_up: float32 [768, 3072], P('dp'), may hold values from -40 to 40
- first_down: float32 [3072, 768], P('dp'), may hold values from -40 to 40
- first_vectors: float32 [9216], P('dp'), may hold values from -40 to 40
- second_qkv: float32 [768, 2304], P('dp'), may hold values from 0.128 to 2.048
- second_attn: float32 [768, 768], P('dp'), may hold values from 0.16384 to 2.62144
- second_up: float32 [768, 3072], P('dp'), may hold values from 2.048 to 32.768
- second_down: float32 [3072, 768], P('dp'), may hold values from 2.048 to 32.768
- second_vectors: float32 [9216], P('dp'), may hold values from 2.048 to 32.768
Outputs:
- layer_output: bfloat16 [32768, 768], P('dp')
- input_grad: bfloat16 [32768, 768], P('dp')
- next_first_qkv: float32 [768, 2304], P('dp')
- next_second_qkv: float32 [768, 2304], P('dp')
- next_qkv: float32 [768, 2304], P('dp')
- next_first_attn: float32 [768, 768], P('dp')
- next_second_attn: float32 [768, 768], P('dp')
- next_attn: float32 [768, 768], P('dp')
- next_first_up: float32 [768, 3072], P('dp')
- next_second_up: float32 [768, 3072], P('dp')
- next_up: float32 [768, 3072], P('dp')
- next_first_down: float32 [3072, 768], P('dp')
- next_second_down: float32 [3072, 768], P('dp')
- next_down: float32 [3072, 768], P('dp')
- next_first_vectors: float32 [9216], P('dp')
- next_second_vectors: float32 [9216], P('dp')
- next_vectors: float32 [9216], P('dp')
Inputs may be any that keep to these rules, and one draw needn't show every extreme that they name: Slot s of a device's 2 * 1 sequences belongs to micro-batch s // 1 of that device. Some sequence has length 512 in every draw; a device's lengths are at least half of a per-device ceiling between 256 and 512.
All inputs are finite; a program needn't handle non-finite values.
Results may differ from a plain program's by a relative error of at most 0.019.
The roundings to bfloat16 on the way count: a program that leaves them out, or rounds other values in their place, can miss the bound.
Values may be sent and summed in bfloat16 or wider, within the bound.
No kernel may reach another device: no remote copies, remote signals or barrier semaphores. Data moves between devices by JAX's collectives and lax.ppermute only.
A program may use at most 192 MiB of HBM per device.

v0:
```python
import math

import jax
import jax.numpy as jnp
from jax import lax
from jax.sharding import PartitionSpec as P

HEAD = 64
BATCH = 1
STEP = 10


EPSILON_NORM = 1e-05
BETA_ONE = 0.9
BETA_TWO = 0.999
LEARN_RATE = 0.1
LEARN_RATE_VECTOR = 0.4
WEIGHT_DECAY = 0.01
EPSILON_ADAM = 1e-08


def gelu_exact(upper):
    return 0.5 * upper * (1.0 + jax.scipy.special.erf(upper * (1.0 / math.sqrt(2.0))))


def matmul(left_arr, right_arr):
    return jnp.dot(left_arr, right_arr, preferred_element_type=jnp.float32)


def matmul_tn(left_arr, right_arr):
    return lax.dot_general(
        left_arr, right_arr, (((0,), (0,)), ((), ())), preferred_element_type=jnp.float32
    )


def matmul_nt(left_arr, right_arr):
    return lax.dot_general(
        left_arr, right_arr, (((1,), (1,)), ((), ())), preferred_element_type=jnp.float32
    )


def split_vector(vector, width, inner):
    base = 3 * width + inner
    return (
        vector[:width],
        vector[width : 2 * width],
        vector[2 * width : 3 * width],
        vector[3 * width : base],
        vector[base : base + width],
        vector[base + width : base + 2 * width],
        vector[base + 2 * width : base + 3 * width],
        vector[base + 3 * width : base + 4 * width],
        vector[base + 4 * width : base + 5 * width],
    )


def norm_forward(resid, gain, shift):
    centred = resid - jnp.mean(resid, axis=-1, keepdims=True)
    inverse = lax.rsqrt(jnp.mean(centred * centred, axis=-1, keepdims=True) + EPSILON_NORM)
    scaled = centred * inverse
    return (scaled * gain + shift, scaled, inverse)


def norm_backward(grad, scaled, inverse, gain):
    grad_scaled = grad * gain
    return inverse * (
        grad_scaled
        - jnp.mean(grad_scaled, axis=-1, keepdims=True)
        - scaled * jnp.mean(grad_scaled * scaled, axis=-1, keepdims=True)
    )


def split_heads(packed, batch, width):
    seq_len = packed.shape[0] // batch
    shaped = packed.reshape(batch, seq_len, 3, width // HEAD, HEAD)
    return (shaped[:, :, 0], shaped[:, :, 1], shaped[:, :, 2])


def masked_scores(query, keyset, seq_lengths):
    scores = jnp.einsum("bqhd,bkhd->bhqk", query, keyset, preferred_element_type=jnp.float32) * (
        1.0 / math.sqrt(HEAD)
    )
    alive = jnp.arange(query.shape[1])[None, :] < seq_lengths[:, None]
    return jnp.where(alive[:, None, None, :], scores, -1e30)


def attend_forward(packed, seq_lengths, width):
    query, keyset, valset = split_heads(packed, seq_lengths.shape[0], width)
    scores = masked_scores(query, keyset, seq_lengths)
    highest = jnp.max(scores, axis=-1, keepdims=True)
    expo = jnp.exp(scores - highest)
    summed = jnp.sum(expo, axis=-1, keepdims=True)
    probs_low = (expo / summed).astype(jnp.bfloat16)
    mixed = jnp.einsum("bhqk,bkhd->bqhd", probs_low, valset, preferred_element_type=jnp.float32)
    return (mixed.reshape(packed.shape[0], width).astype(jnp.bfloat16), highest + jnp.log(summed))


def attend_backward(packed, seq_lengths, log_total, grad_mixed, width):
    batch = seq_lengths.shape[0]
    query, keyset, valset = split_heads(packed, batch, width)
    probs = jnp.exp(masked_scores(query, keyset, seq_lengths) - log_total)
    grad_heads = grad_mixed.reshape(batch, -1, width // HEAD, HEAD)
    grad_val = jnp.einsum(
        "bhqk,bqhd->bkhd",
        probs.astype(jnp.bfloat16),
        grad_heads,
        preferred_element_type=jnp.float32,
    )
    grad_probs = jnp.einsum(
        "bqhd,bkhd->bhqk", grad_heads, valset, preferred_element_type=jnp.float32
    )
    grad_scores = (
        probs * (grad_probs - jnp.sum(probs * grad_probs, axis=-1, keepdims=True))
    ).astype(jnp.bfloat16)
    factor = 1.0 / math.sqrt(HEAD)
    grad_query = (
        jnp.einsum("bhqk,bkhd->bqhd", grad_scores, keyset, preferred_element_type=jnp.float32)
        * factor
    )
    grad_key = (
        jnp.einsum("bhqk,bqhd->bkhd", grad_scores, query, preferred_element_type=jnp.float32)
        * factor
    )
    stacked = jnp.stack([grad_query, grad_key, grad_val], axis=2)
    return stacked.reshape(packed.shape[0], 3 * width).astype(jnp.bfloat16)


def forward(x_rows, seq_lengths, weights):
    w_qkv, w_attn, w_up, w_down, vector = weights
    width = x_rows.shape[1]
    inner = w_up.shape[1]
    q_bias, v_bias, attn_bias, up_bias, down_bias, gain_one, shift_one, gain_two, shift_two = (
        split_vector(vector.astype(jnp.float32), width, inner)
    )
    packed = (
        matmul(x_rows, w_qkv) + jnp.concatenate([q_bias, jnp.zeros_like(q_bias), v_bias])
    ).astype(jnp.bfloat16)
    mixed, log_total = attend_forward(packed, seq_lengths, width)
    resid_one = x_rows.astype(jnp.float32) + matmul(mixed, w_attn) + attn_bias
    first, scaled_one, inverse_one = norm_forward(resid_one, gain_one, shift_one)
    first_low = first.astype(jnp.bfloat16)
    upper = matmul(first_low, w_up) + up_bias
    active = gelu_exact(upper).astype(jnp.bfloat16)
    resid_two = first + matmul(active, w_down) + down_bias
    output, scaled_two, inverse_two = norm_forward(resid_two, gain_two, shift_two)
    saved = (
        packed,
        log_total,
        mixed,
        scaled_one,
        inverse_one,
        first_low,
        upper,
        active,
        scaled_two,
        inverse_two,
    )
    return (output.astype(jnp.bfloat16), saved)


def backward(cot_rows, seq_lengths, x_rows, weights, saved):
    w_qkv, w_attn, w_up, w_down, vector = weights
    width = x_rows.shape[1]
    inner = w_up.shape[1]
    pieces = split_vector(vector.astype(jnp.float32), width, inner)
    gain_one = pieces[5]
    gain_two = pieces[7]
    (
        packed,
        log_total,
        mixed,
        scaled_one,
        inverse_one,
        first_low,
        upper,
        active,
        scaled_two,
        inverse_two,
    ) = saved
    seq_len = x_rows.shape[0] // seq_lengths.shape[0]
    alive = (jnp.arange(seq_len)[None, :] < seq_lengths[:, None]).reshape(-1, 1)
    grad_out = jnp.where(alive, cot_rows.astype(jnp.float32), 0.0)
    grad_resid_two = norm_backward(grad_out, scaled_two, inverse_two, gain_two)
    grad_branch = grad_resid_two.astype(jnp.bfloat16)
    grad_active = matmul_nt(grad_branch, w_down)
    slope_fn = jax.vjp(gelu_exact, upper)[1]
    grad_upper = slope_fn(grad_active)[0].astype(jnp.bfloat16)
    grad_first = grad_resid_two + matmul_nt(grad_upper, w_up)
    grad_resid_one = norm_backward(grad_first, scaled_one, inverse_one, gain_one)
    grad_attn = grad_resid_one.astype(jnp.bfloat16)
    grad_mixed = matmul_nt(grad_attn, w_attn).astype(jnp.bfloat16)
    grad_packed = attend_backward(packed, seq_lengths, log_total, grad_mixed, width)
    grad_rows = (grad_resid_one + matmul_nt(grad_packed, w_qkv)).astype(jnp.bfloat16)
    packed_sums = jnp.sum(grad_packed.astype(jnp.float32), axis=0)
    grad_vector = jnp.concatenate(
        [
            packed_sums[:width],
            packed_sums[2 * width :],
            jnp.sum(grad_attn.astype(jnp.float32), axis=0),
            jnp.sum(grad_upper.astype(jnp.float32), axis=0),
            jnp.sum(grad_branch.astype(jnp.float32), axis=0),
            jnp.sum(grad_first * scaled_one, axis=0),
            jnp.sum(grad_first, axis=0),
            jnp.sum(grad_out * scaled_two, axis=0),
            jnp.sum(grad_out, axis=0),
        ]
    )
    gradients = (
        matmul_tn(x_rows, grad_packed),
        matmul_tn(mixed, grad_attn),
        matmul_tn(first_low, grad_upper),
        matmul_tn(active, grad_branch),
        grad_vector,
    )
    return (gradients, grad_rows)


def adamw(weight, grad, first, second, decay, rate):
    new_first = BETA_ONE * first + (1.0 - BETA_ONE) * grad
    new_second = BETA_TWO * second + (1.0 - BETA_TWO) * grad * grad
    corrected = new_first / (1.0 - BETA_ONE**STEP)
    scale_sq = new_second / (1.0 - BETA_TWO**STEP)
    new_weight = weight - rate * (corrected / (jnp.sqrt(scale_sq) + EPSILON_ADAM) + decay * weight)
    return (new_first, new_second, new_weight)


def on_device(
    hidden_in,
    lengths,
    cotangent,
    proj_qkv,
    proj_attn,
    proj_up,
    proj_down,
    vectors,
    first_qkv,
    first_attn,
    first_up,
    first_down,
    first_vectors,
    second_qkv,
    second_attn,
    second_up,
    second_down,
    second_vectors,
):
    copy_qkv = proj_qkv.astype(jnp.bfloat16)
    copy_attn = proj_attn.astype(jnp.bfloat16)
    copy_up = proj_up.astype(jnp.bfloat16)
    copy_down = proj_down.astype(jnp.bfloat16)
    copy_vector = vectors.astype(jnp.bfloat16)
    masters = (proj_qkv, proj_attn, proj_up, proj_down, vectors)
    seq_count = lengths.shape[0]
    seq_len = hidden_in.shape[0] // seq_count
    micro_count = seq_count // BATCH
    row_count = BATCH * seq_len
    devices = lax.axis_size("dp")
    totals = tuple(
        (
            jnp.zeros((master.shape[0] * devices,) + master.shape[1:], jnp.float32)
            for master in masters
        )
    )
    outputs = []
    grad_parts = []
    for micro_index in range(micro_count):
        x_rows = hidden_in[micro_index * row_count : (micro_index + 1) * row_count]
        cot_rows = cotangent[micro_index * row_count : (micro_index + 1) * row_count]
        seq_lengths = lengths[micro_index * BATCH : (micro_index + 1) * BATCH]
        gathered = (
            lax.all_gather(copy_qkv, "dp", axis=0, tiled=True),
            lax.all_gather(copy_attn, "dp", axis=0, tiled=True),
            lax.all_gather(copy_up, "dp", axis=0, tiled=True),
            lax.all_gather(copy_down, "dp", axis=0, tiled=True),
            lax.all_gather(copy_vector, "dp", axis=0, tiled=True),
        )
        output, saved = forward(x_rows, seq_lengths, gathered)
        gathered = (
            lax.all_gather(copy_qkv, "dp", axis=0, tiled=True),
            lax.all_gather(copy_attn, "dp", axis=0, tiled=True),
            lax.all_gather(copy_up, "dp", axis=0, tiled=True),
            lax.all_gather(copy_down, "dp", axis=0, tiled=True),
            lax.all_gather(copy_vector, "dp", axis=0, tiled=True),
        )
        gradients, grad_rows = backward(cot_rows, seq_lengths, x_rows, gathered, saved)
        totals = tuple((running + update for running, update in zip(totals, gradients)))
        outputs.append(output)
        grad_parts.append(grad_rows)
    totals = (
        lax.psum_scatter(totals[0], "dp", scatter_dimension=0, tiled=True),
        lax.psum_scatter(totals[1], "dp", scatter_dimension=0, tiled=True),
        lax.psum_scatter(totals[2], "dp", scatter_dimension=0, tiled=True),
        lax.psum_scatter(totals[3], "dp", scatter_dimension=0, tiled=True),
        lax.psum_scatter(totals[4], "dp", scatter_dimension=0, tiled=True),
    )
    m_qkv, v_qkv, w_qkv = adamw(
        proj_qkv, totals[0], first_qkv, second_qkv, WEIGHT_DECAY, LEARN_RATE
    )
    m_attn, v_attn, w_attn = adamw(
        proj_attn, totals[1], first_attn, second_attn, WEIGHT_DECAY, LEARN_RATE
    )
    m_up, v_up, w_up = adamw(proj_up, totals[2], first_up, second_up, WEIGHT_DECAY, LEARN_RATE)
    m_down, v_down, w_down = adamw(
        proj_down, totals[3], first_down, second_down, WEIGHT_DECAY, LEARN_RATE
    )
    m_vec, v_vec, w_vec = adamw(
        vectors, totals[4], first_vectors, second_vectors, 0.0, LEARN_RATE_VECTOR
    )
    return (
        jnp.concatenate(outputs, axis=0),
        jnp.concatenate(grad_parts, axis=0),
        m_qkv,
        v_qkv,
        w_qkv,
        m_attn,
        v_attn,
        w_attn,
        m_up,
        v_up,
        w_up,
        m_down,
        v_down,
        w_down,
        m_vec,
        v_vec,
        w_vec,
    )


def solution(mesh):
    placed = (
        P("dp", None),
        P("dp"),
        P("dp", None),
        P("dp", None),
        P("dp", None),
        P("dp", None),
        P("dp", None),
        P("dp"),
        P("dp", None),
        P("dp", None),
        P("dp", None),
        P("dp", None),
        P("dp"),
        P("dp", None),
        P("dp", None),
        P("dp", None),
        P("dp", None),
        P("dp"),
    )
    return jax.shard_map(
        on_device,
        mesh=mesh,
        in_specs=placed,
        out_specs=(
            P("dp", None),
            P("dp", None),
            P("dp", None),
            P("dp", None),
            P("dp", None),
            P("dp", None),
            P("dp", None),
            P("dp", None),
            P("dp", None),
            P("dp", None),
            P("dp", None),
            P("dp", None),
            P("dp", None),
            P("dp", None),
            P("dp"),
            P("dp"),
            P("dp"),
        ),
        check_vma=False,
    )
```

profile of v0, /device:TPU:0, one launch (start us, length us, event | category | flops | bytes accessed | tf_op | source)
XLA Modules:
  0.0 847.7 jit_solution(16409839408796806634)
XLA Ops:
  14.8 42.5 %all-reduce = bf16[9216]{0:T(1024)(128)(2,1)S(1)} all-reduce(bf16[9216]{0:T(1024)(128)(2,1)S(1)} %dynamic-update-slice), channel_id=1, replica_groups=mesh['dp'=32] {'dp'}, use_global_device_ids=true, to_apply=%add | all-reduce | flops 9216 | bytes 36864
  59.9 14.7 %all-gather.5.cloned.1.call-done = bf16[768,2304]{1,0:T(8,128)(2,1)} async-done(((bf16[24,2304]{1,0:T(8,128)(2,1)}), bf16[768,2304]{1,0:T(8,128)(2,1)}) %all-gather.5.cloned.1.call-update) | async-done | bytes 3538960 | tf_op jit(solution)/shard_map/all_gather | solution.py:271
  74.6 5.7 fusion.12
  80.2 2.8 copy.98
  83.1 3.0 fusion.74
  88.0 2.9 copy-done.1
  90.9 5.4 fusion.13
  96.3 3.0 copy.100
  99.3 8.0 fusion.27
  107.3 23.6 %all-gather.7.cloned.1.call-done = bf16[768,768]{1,0:T(8,128)(2,1)} async-done(((bf16[24,768]{1,0:T(8,128)(2,1)}), bf16[768,768]{1,0:T(8,128)(2,1)}) %all-gather.7.cloned.1.call-update) | async-done | bytes 1179664 | tf_op jit(solution)/shard_map/all_gather | solution.py:272
  130.9 2.4 fusion.75
  134.5 3.0 fusion.76
  139.4 2.6 copy-done
  142.0 2.4 fusion.26
  146.9 50.0 %all-gather.9.cloned.1.call-done = bf16[768,3072]{1,0:T(8,128)(2,1)} async-done(((bf16[24,3072]{1,0:T(8,128)(2,1)}), bf16[768,3072]{1,0:T(8,128)(2,1)}) %all-gather.9.cloned.1.call-update) | async-done | bytes 4718608 | tf_op jit(solution)/shard_map/all_gather | solution.py:273
  196.9 5.3 fusion.59
  202.2 2.7 copy-done.62
  205.0 7.7 multiply_convert_fusion.3
  212.7 50.0 %all-gather.11.cloned.1.call-done = bf16[3072,768]{1,0:T(8,128)(2,1)} async-done(((bf16[96,768]{1,0:T(8,128)(2,1)}), bf16[3072,768]{1,0:T(8,128)(2,1)}) %all-gather.11.cloned.1.call-update) | async-done | bytes 4718608 | tf_op jit(solution)/shard_map/all_gather | solution.py:274
  262.7 6.6 fusion.79
  269.7 2.8 fusion.78
  275.8 2.6 convert_reduce_fusion.4
  278.4 8.4 convert_reduce_fusion.1
  286.9 3.1 multiply_reduce_fusion.5
  290.0 6.8 convert_reduce_fusion
  296.8 4.6 convert_reduce_fusion.7
  301.4 2.3 fusion.49
  306.8 7.5 fusion.20
  314.3 9.3 %multiply_reduce_fusion.1 = (f32[12,512]{1,0:T(8,128)S(1)}, f32[12,512,512]{1,2,0:T(8,128)}) fusion(f32[12,512,512]{1,2,0:T(8,128)} %copy-done.1, f32[12,512]{1,0:T(8,128)S(1)} %log_add_fusion.1, bf16[512,12,64]{0,2,1:T(8,128)(2,1)S(1)} %bitcast.152, bf16[1,512,3,12,64]{1,4,3,2,0:T(8,128)(2,1)} %bitcast.142), kind=kOutput, calls=%fused_computation.4 | convolution fusion | flops 412084224 | bytes 26787840 | tf_op jit(solution)/shard_map/bqhd,bkhd->bhqk/dot_general | solution.py:109
  328.6 4.9 convolution_add_fusion.4
  333.6 10.7 %multiply_convert_fusion.1 = bf16[12,512,512]{1,2,0:T(8,128)(2,1)S(1)} fusion(f32[12,512,512]{1,2,0:T(8,128)} %get-tuple-element.157, f32[12,512,512]{1,2,0:T(8,128)} %copy-done.1, f32[12,512]{1,0:T(8,128)S(1)} %get-tuple-element.156, f32[12,512]{1,0:T(8,128)S(1)} %log_add_fusion.1), kind=kLoop, calls=%fused_computation.3 | loop fusion | flops 12582912 | bytes 31506432 | tf_op jit(solution)/shard_map/convert_element_type | solution.py:114
  344.3 4.5 multiply_bitcast_fusion.2
  348.8 6.0 multiply_reduce_fusion
  354.8 7.3 multiply_convert_fusion
  368.4 2.0 fusion.23
  374.0 4.9 add_bitcast_fusion
  378.9 8.0 copy.121
  388.4 5.0 fusion.61
  393.4 6.1 convolution_add_fusion.1
  400.9 4.8 fusion.52
  405.7 5.3 convolution_add_fusion
  411.6 40.1 %all-reduce.1 = f32[9216]{0:T(1024)S(1)} all-reduce(f32[9216]{0:T(1024)S(1)} %add.326), channel_id=6, replica_groups=mesh['dp'=32] {'dp'}, use_global_device_ids=true, to_apply=%region_42.43.clone | all-reduce | flops 9216 | bytes 73728
  451.8 4.8 add_convert_fusion.3
  456.9 2.0 add_convert_fusion.2
  463.3 92.9 %reduce-scatter.13.cloned.1.call-done = f32[24,2304]{1,0:T(8,128)} async-done(((f32[768,2304]{1,0:T(8,128)}), f32[24,2304]{1,0:T(8,128)}) %reduce-scatter.13.cloned.1.call-update) | async-done | bytes 221200 | tf_op jit(solution)/shard_map/reduce_scatter | solution.py:290
  558.1 138.8 %reduce-scatter.9.cloned.1.call-done = f32[24,3072]{1,0:T(8,128)} async-done(((f32[768,3072]{1,0:T(8,128)}), f32[24,3072]{1,0:T(8,128)}) %reduce-scatter.9.cloned.1.call-update) | async-done | bytes 294928 | tf_op jit(solution)/shard_map/reduce_scatter | solution.py:292
  698.9 139.5 %reduce-scatter.11.cloned.1.call-done = f32[96,768]{1,0:T(8,128)} async-done(((f32[3072,768]{1,0:T(8,128)}), f32[96,768]{1,0:T(8,128)}) %reduce-scatter.11.cloned.1.call-update) | async-done | bytes 294928 | tf_op jit(solution)/shard_map/reduce_scatter | solution.py:293
  838.5 2.0 multiply_subtract_fusion
  (236 shorter events, 50.5 us)
Async XLA Ops:
  7.2 67.4 %all-gather.5.cloned.1.call-start = ((), (), s32[]{:S(2)}) async-start(), calls=%async_computation.4 | async-start | bytes 3649536 | tf_op jit(solution)/shard_map/all_gather | solution.py:271
  8.9 122.1 %all-gather.7.cloned.1.call-start = ((), (), s32[]{:S(2)}) async-start(), calls=%async_computation.5 | async-start | bytes 1216512 | tf_op jit(solution)/shard_map/all_gather | solution.py:272
  10.4 186.5 %all-gather.9.cloned.1.call-start = ((), (), s32[]{:S(2)}) async-start(), calls=%async_computation.6 | async-start | bytes 4866048 | tf_op jit(solution)/shard_map/all_gather | solution.py:273
  12.2 250.6 %all-gather.11.cloned.1.call-start = ((), (), s32[]{:S(2)}) async-start(), calls=%async_computation.7 | async-start | bytes 4866048 | tf_op jit(solution)/shard_map/all_gather | solution.py:274
  13.9 447.8 %reduce-scatter.7.cloned.1.call-start = ((), (), s32[]{:S(2)}) async-start(), calls=%async_computation.8 | async-start | bytes 2433024 | tf_op jit(solution)/shard_map/reduce_scatter | solution.py:291
  86.1 4.7 copy-start.1
  86.1 4.7 copy-start.31
  99.3 249.5 %copy-start.2 = (bf16[512,2304]{0,1:T(8,128)(2,1)}, bf16[512,2304]{0,1:T(8,128)(2,1)S(1)}, u32[]{:S(2)}) copy-start(bf16[512,2304]{0,1:T(8,128)(2,1)S(1)} %copy.100) | copy-start | bytes 7077892
  137.5 4.5 copy-start
  196.9 8.0 copy-start.35
  196.9 8.0 copy-start.56
  262.7 6.9 copy-start.7
  262.7 7.0 copy-start.16
  262.7 7.0 copy-start.57
  275.8 11.0 %slice-start.3 = ((s8[4718592]{0:T(1024)(128)(4,1)}), s8[4194304]{0:T(1024)(128)(4,1)S(1)}, s32[]{:S(2)}) async-start(s8[4718592]{0:T(1024)(128)(4,1)} %bitcast.157), calls=%async_computation.15 | async-start | bytes 8388608
  278.4 8.5 copy-start.20
  278.4 18.4 %copy-start.18 = (f32[512,768]{1,0:T(8,128)}, f32[512,768]{1,0:T(8,128)S(1)}, u32[]{:S(2)}) copy-start(f32[512,768]{1,0:T(8,128)S(1)} %get-tuple-element.91) | copy-start | bytes 4718596
  278.4 8.5 copy-start.36
  278.4 8.5 %slice-start.4 = ((s8[4718592]{0:T(1024)(128)(4,1)}), s8[524288]{0:T(1024)(128)(4,1)S(1)}, s32[]{:S(2)}) async-start(s8[4718592]{0:T(1024)(128)(4,1)} %bitcast.157), calls=%async_computation.16 | async-start | bytes 1048576
  296.8 4.6 copy-start.25
  314.3 9.4 %copy-start.8 = (f32[512,768]{1,0:T(8,128)S(1)}, f32[512,768]{1,0:T(8,128)}, u32[]{:S(2)}) copy-start(f32[512,768]{1,0:T(8,128)} %copy-done.6) | copy-start | bytes 4718596
  314.3 9.4 %copy-start.39 = (f32[512,768]{1,0:T(8,128)S(1)}, f32[512,768]{1,0:T(8,128)}, u32[]{:S(2)}) copy-start(f32[512,768]{1,0:T(8,128)} %get-tuple-element.153) | copy-start | bytes 4718596
  328.5 20.3 %copy-start.14 = (bf16[512,768]{0,1:T(8,128)(2,1)}, bf16[512,768]{0,1:T(8,128)(2,1)S(1)}, u32[]{:S(2)}) copy-start(bf16[512,768]{0,1:T(8,128)(2,1)S(1)} %copy.106) | copy-start | bytes 2359300
  333.5 222.7 %reduce-scatter.13.cloned.1.call-start = ((), (), s32[]{:S(2)}) async-start(), calls=%async_computation.11 | async-start | bytes 7299072 | tf_op jit(solution)/shard_map/reduce_scatter | solution.py:290
  333.5 15.3 %slice-start = ((s8[12582912]{0:T(1024)(128)(4,1)}), s8[4194304]{0:T(1024)(128)(4,1)S(1)}, s32[]{:S(2)}) async-start(s8[12582912]{0:T(1024)(128)(4,1)} %bitcast.133), calls=%async_computation.12 | async-start | bytes 8388608
  333.6 15.2 %slice-start.1 = ((s8[12582912]{0:T(1024)(128)(4,1)}), s8[4194304]{0:T(1024)(128)(4,1)S(1)}, s32[]{:S(2)}) async-start(s8[12582912]{0:T(1024)(128)(4,1)} %bitcast.133), calls=%async_computation.13 | async-start | bytes 8388608
  333.6 15.2 %slice-start.2 = ((s8[12582912]{0:T(1024)(128)(4,1)}), s8[4194304]{0:T(1024)(128)(4,1)S(1)}, s32[]{:S(2)}) async-start(s8[12582912]{0:T(1024)(128)(4,1)} %bitcast.133), calls=%async_computation.14 | async-start | bytes 8388608
  354.8 7.3 copy-start.5
  365.2 5.6 copy-start.12
  387.0 6.4 copy-start.9
  387.0 309.9 %reduce-scatter.9.cloned.1.call-start = ((), (), s32[]{:S(2)}) async-start(), calls=%async_computation.9 | async-start | bytes 9732096 | tf_op jit(solution)/shard_map/reduce_scatter | solution.py:292
  388.4 5.0 copy-start.26
  399.5 6.2 copy-start.19
  399.5 438.9 %reduce-scatter.11.cloned.1.call-start = ((), (), s32[]{:S(2)}) async-start(), calls=%async_computation.10 | async-start | bytes 9732096 | tf_op jit(solution)/shard_map/reduce_scatter | solution.py:293
  400.9 4.8 copy-start.17
  411.0 40.7 %copy-start.13 = (bf16[1,512,3,12,64]{1,4,3,2,0:T(8,128)(2,1)S(1)}, bf16[1,512,3,12,64]{1,4,3,2,0:T(8,128)(2,1)}, u32[]{:S(2)}) copy-start(bf16[1,512,3,12,64]{1,4,3,2,0:T(8,128)(2,1)} %copy-done.12) | copy-start | bytes 7077892
  451.7 4.9 copy-start.11
  451.7 4.9 copy-start.24
  451.7 5.1 copy-start.58
  459.0 97.2 %copy-start.42 = (f32[24,2304]{1,0:T(8,128)S(1)}, f32[24,2304]{1,0:T(8,128)}, u32[]{:S(2)}) copy-start(f32[24,2304]{1,0:T(8,128)} %param.21) | copy-start | bytes 663556
  459.0 97.2 %copy-start.49 = (f32[24,2304]{1,0:T(8,128)S(1)}, f32[24,2304]{1,0:T(8,128)}, u32[]{:S(2)}) copy-start(f32[24,2304]{1,0:T(8,128)} %param.31) | copy-start | bytes 663556
  459.1 97.2 %copy-start.50 = (f32[24,2304]{1,0:T(8,128)S(1)}, f32[24,2304]{1,0:T(8,128)}, u32[]{:S(2)}) copy-start(f32[24,2304]{1,0:T(8,128)} %param.26) | copy-start | bytes 663556
  459.1 237.8 %copy-start.40 = (f32[24,3072]{1,0:T(8,128)S(1)}, f32[24,3072]{1,0:T(8,128)}, u32[]{:S(2)}) copy-start(f32[24,3072]{1,0:T(8,128)} %param.23) | copy-start | bytes 884740
  459.1 237.8 %copy-start.45 = (f32[24,3072]{1,0:T(8,128)S(1)}, f32[24,3072]{1,0:T(8,128)}, u32[]{:S(2)}) copy-start(f32[24,3072]{1,0:T(8,128)} %param.33) | copy-start | bytes 884740
  459.1 237.8 %copy-start.46 = (f32[24,3072]{1,0:T(8,128)S(1)}, f32[24,3072]{1,0:T(8,128)}, u32[]{:S(2)}) copy-start(f32[24,3072]{1,0:T(8,128)} %param.28) | copy-start | bytes 884740
  461.0 377.5 %copy-start.41 = (f32[96,768]{1,0:T(8,128)S(1)}, f32[96,768]{1,0:T(8,128)}, u32[]{:S(2)}) copy-start(f32[96,768]{1,0:T(8,128)} %param.24) | copy-start | bytes 884740
  461.0 377.5 %copy-start.47 = (f32[96,768]{1,0:T(8,128)S(1)}, f32[96,768]{1,0:T(8,128)}, u32[]{:S(2)}) copy-start(f32[96,768]{1,0:T(8,128)} %param.34) | copy-start | bytes 884740
  461.0 377.5 %copy-start.48 = (f32[96,768]{1,0:T(8,128)S(1)}, f32[96,768]{1,0:T(8,128)}, u32[]{:S(2)}) copy-start(f32[96,768]{1,0:T(8,128)} %param.29) | copy-start | bytes 884740
  (29 other events, 57.0 us)
Sparse Core Ops, SparseCore 0:
  11.5 63.0 all-gather.4
  78.1 52.8 all-gather.6
  134.4 62.4 all-gather.8
  200.3 62.4 all-gather.10
  333.6 97.8 reduce-scatter.6
  438.0 118.1 reduce-scatter.12
  562.1 134.7 reduce-scatter.8
  703.8 134.6 reduce-scatter.10
where the time goes:
time: 856 us; the launch traced here: 848 us
  waiting for transfers between devices  510 us (60%)
  matrix products  155 us (18%)
  blocking collectives  82.5 us (10%)
  other arithmetic  47.2 us (6%)
  local copies, waits for them, and re-layouts  36.9 us (4%)
  between operations  15.7 us (2%)
    reduce_scatter x1, waiting for transfers between devices, on_device(): lax.psum_scatter(totals[3], 'dp', scatter_dimension=0, tiled=True)  140 us
    reduce_scatter x1, waiting for transfers between devices, on_device(): lax.psum_scatter(totals[2], 'dp', scatter_dimension=0, tiled=True)  139 us
    reduce_scatter x1, waiting for transfers between devices, on_device(): lax.psum_scatter(totals[0], 'dp', scatter_dimension=0, tiled=True)  92.9 us
    unnamed x2, blocking collectives  82.5 us
    all_gather x1, waiting for transfers between devices, on_device(): lax.all_gather(copy_down, 'dp', axis=0, tiled=True)  50 us
    all_gather x1, waiting for transfers between devices, on_device(): lax.all_gather(copy_up, 'dp', axis=0, tiled=True)  50 us
    dot_general x8, matrix products, matmul(): return jnp.dot(left_arr, right_arr, preferred_element_type=jnp.float32)  36.8 us
    dot_general x8, matrix products, matmul_tn(): lax.dot_general(left_arr, right_arr, (((0,), (0,)), ((), ())), preferred_...  35.2 us
  transfers between devices with their start and end apart: 8, of which 7 were waited for; matrix products, arithmetic and copies ran while one was open for 18% of the time, Pallas kernels for 0%

commit v1 on v0

v1 whole, which is shorter than its diff:
```python
import functools
import math

import jax
import jax.numpy as jnp
from jax import lax
from jax.experimental import pallas as pl
from jax.experimental.pallas import tpu as pltpu
from jax.sharding import PartitionSpec as P

HEAD = 64
STEP = 10

EPSILON_NORM = 1e-05
BETA_ONE = 0.9
BETA_TWO = 0.999
LEARN_RATE = 0.1
LEARN_RATE_VECTOR = 0.4
WEIGHT_DECAY = 0.01
EPSILON_ADAM = 1e-08

LANES = 128
ROWS = 256
GROUPS = 2
VMEM_BYTES = 56 * 1024 * 1024
BF = jnp.bfloat16
F32 = jnp.float32

NN = (((1,), (0,)), ((), ()))
NT = (((1,), (1,)), ((), ()))
TN = (((0,), (0,)), ((), ()))


def dot(left, right, dims=NN):
    return lax.dot_general(left, right, dims, preferred_element_type=F32)


def params(grid_rank):
    return pltpu.CompilerParams(
        dimension_semantics=("arbitrary",) * grid_rank, vmem_limit_bytes=VMEM_BYTES
    )


def cost(flops, moved, exps=0):
    return pl.CostEstimate(flops=int(flops), bytes_accessed=int(moved), transcendentals=int(exps))


def qkv_kernel(x_ref, w_ref, vec_ref, out_ref):
    width = x_ref.shape[1]
    x = x_ref[...]
    for part in range(3):
        cols = pl.ds(part * width, width)
        value = dot(x, w_ref[:, cols])
        if part == 0:
            value = value + vec_ref[0:1, :]
        if part == 2:
            value = value + vec_ref[1:2, :]
        out_ref[:, cols] = value.astype(BF)


def project_qkv(x, gathered, vec):
    rows, width = x.shape
    return pl.pallas_call(
        qkv_kernel,
        grid=(rows // ROWS,),
        in_specs=[
            pl.BlockSpec((ROWS, width), lambda i: (i, 0)),
            pl.BlockSpec((width, 3 * width), lambda i: (0, 0), pipeline_mode=pl.Buffered(1)),
            pl.BlockSpec(vec.shape, lambda i: (0, 0)),
        ],
        out_specs=pl.BlockSpec((ROWS, 3 * width), lambda i: (i, 0)),
        out_shape=jax.ShapeDtypeStruct((rows, 3 * width), BF),
        compiler_params=params(1),
        cost_estimate=cost(6 * rows * width * width, 2 * (4 * rows * width + 3 * width * width)),
        name="project_qkv",
    )(x, gathered, vec)


def attend_kernel(len_ref, q_ref, k_ref, v_ref, out_ref, lse_ref):
    length = len_ref[pl.program_id(0)]
    seq = q_ref.shape[0]
    query = q_ref[...] * jnp.asarray(1.0 / math.sqrt(HEAD), BF)
    keyset = k_ref[...]
    val_t = v_ref[...].T
    lane = lax.broadcasted_iota(jnp.int32, (seq, LANES), 1)
    alive = lax.broadcasted_iota(jnp.int32, (seq, seq), 0) < length
    mixed = []
    for head in range(2):
        mine = (lane < HEAD) if head == 0 else (lane >= HEAD)
        scores = dot(keyset, jnp.where(mine, query, jnp.zeros_like(query)), NT)
        scores = jnp.where(alive, scores, -1e30)
        highest = jnp.max(scores, axis=0, keepdims=True)
        expo = jnp.exp(scores - highest)
        summed = jnp.sum(expo, axis=0, keepdims=True)
        probs = (expo * (1.0 / summed)).astype(BF)
        mixed.append(dot(val_t[head * HEAD : (head + 1) * HEAD], probs))
        lse_ref[0, head : head + 1, :] = highest + jnp.log(summed)
    out_ref[...] = jnp.concatenate(mixed, axis=0).T.astype(BF)


def attend_forward(packed, lengths, width):
    rows = packed.shape[0]
    batch = lengths.shape[0]
    seq = rows // batch
    pairs = width // LANES
    grid_spec = pltpu.PrefetchScalarGridSpec(
        num_scalar_prefetch=1,
        grid=(batch, pairs),
        in_specs=[
            pl.BlockSpec((seq, LANES), lambda b, h, ln: (b, h)),
            pl.BlockSpec((seq, LANES), lambda b, h, ln: (b, pairs + h)),
            pl.BlockSpec((seq, LANES), lambda b, h, ln: (b, 2 * pairs + h)),
        ],
        out_specs=[
            pl.BlockSpec((seq, LANES), lambda b, h, ln: (b, h)),
            pl.BlockSpec((1, 2, seq), lambda b, h, ln: (b * pairs + h, 0, 0)),
        ],
    )
    return pl.pallas_call(
        attend_kernel,
        grid_spec=grid_spec,
        out_shape=[
            jax.ShapeDtypeStruct((rows, width), BF),
            jax.ShapeDtypeStruct((batch * pairs, 2, seq), F32),
        ],
        compiler_params=params(2),
        cost_estimate=cost(16 * rows * seq * width, 8 * rows * width, rows * seq * width // HEAD),
        name="attend_forward",
    )(lengths, packed, packed, packed)


def attend_back_kernel(len_ref, q_ref, k_ref, v_ref, g_ref, lse_ref, out_ref):
    length = len_ref[pl.program_id(0)]
    seq = q_ref.shape[0]
    factor = 1.0 / math.sqrt(HEAD)
    query = q_ref[...] * jnp.asarray(factor, BF)
    keyset = k_ref[...]
    valset = v_ref[...]
    grad = g_ref[...]
    key_t = keyset.T
    lane = lax.broadcasted_iota(jnp.int32, (seq, LANES), 1)
    alive = lax.broadcasted_iota(jnp.int32, (seq, seq), 0) < length
    grad_q = []
    grad_k = 0.0
    grad_v = 0.0
    for head in range(2):
        mine = (lane < HEAD) if head == 0 else (lane >= HEAD)
        query_h = jnp.where(mine, query, jnp.zeros_like(query))
        grad_h = jnp.where(mine, grad, jnp.zeros_like(grad))
        scores = jnp.where(alive, dot(keyset, query_h, NT), -1e30)
        probs = jnp.exp(scores - lse_ref[0, head : head + 1, :])
        grad_probs = dot(valset, grad_h, NT)
        total = jnp.sum(probs * grad_probs, axis=0, keepdims=True)
        grad_scores = (probs * (grad_probs - total)).astype(BF)
        grad_v = grad_v + dot(probs.astype(BF), grad_h)
        grad_k = grad_k + dot(grad_scores, query_h)
        grad_q.append(dot(key_t[head * HEAD : (head + 1) * HEAD], grad_scores))
    out_ref[0] = (jnp.concatenate(grad_q, axis=0).T * factor).astype(BF)
    out_ref[1] = grad_k.astype(BF)
    out_ref[2] = grad_v.astype(BF)


def attend_backward(packed, lengths, lse, grad_mixed, group):
    rows, width = grad_mixed.shape
    batch = lengths.shape[0]
    seq = rows // batch
    pairs = width // LANES
    here = pairs // GROUPS
    base = group * here
    grid_spec = pltpu.PrefetchScalarGridSpec(
        num_scalar_prefetch=1,
        grid=(batch, here),
        in_specs=[
            pl.BlockSpec((seq, LANES), lambda b, h, ln: (b, base + h)),
            pl.BlockSpec((seq, LANES), lambda b, h, ln: (b, pairs + base + h)),
            pl.BlockSpec((seq, LANES), lambda b, h, ln: (b, 2 * pairs + base + h)),
            pl.BlockSpec((seq, LANES), lambda b, h, ln: (b, base + h)),
            pl.BlockSpec((1, 2, seq), lambda b, h, ln: (b * pairs + base + h, 0, 0)),
        ],
        out_specs=pl.BlockSpec((3, seq, LANES), lambda b, h, ln: (0, b, h)),
    )
    return pl.pallas_call(
        attend_back_kernel,
        grid_spec=grid_spec,
        out_shape=jax.ShapeDtypeStruct((3, rows, here * LANES), BF),
        compiler_params=params(2),
        cost_estimate=cost(
            40 * rows * seq * here * LANES,
            14 * rows * here * LANES,
            rows * seq * here * 2,
        ),
        name="attend_backward",
    )(lengths, packed, packed, packed, grad_mixed, lse)


def norm_forward(resid, gain, shift):
    centred = resid - jnp.mean(resid, axis=-1, keepdims=True)
    inverse = lax.rsqrt(jnp.mean(centred * centred, axis=-1, keepdims=True) + EPSILON_NORM)
    scaled = centred * inverse
    return (scaled * gain + shift, scaled, inverse)


def norm_backward(grad, scaled, inverse, gain):
    grad_scaled = grad * gain
    return inverse * (
        grad_scaled
        - jnp.mean(grad_scaled, axis=-1, keepdims=True)
        - scaled * jnp.mean(grad_scaled * scaled, axis=-1, keepdims=True)
    )


def column_sum(value):
    return jnp.sum(value, axis=0, keepdims=True)


def middle_kernel(
    len_ref,
    x_ref,
    mixed_ref,
    cot_ref,
    w_attn,
    w_up,
    w_down,
    vec_ref,
    out_ref,
    first_ref,
    active_ref,
    upper_ref,
    branch_ref,
    attn_ref,
    gmix_ref,
    resid_ref,
    sum_ref,
    slope_ref,
    *,
    seq,
):
    step = pl.program_id(0)
    rows, width = x_ref.shape
    chunks = w_up.shape[1] // width
    start = (step * rows) % seq
    length = len_ref[(step * rows) // seq]

    def vec(index):
        return vec_ref[index : index + 1, :]

    gain_one, shift_one, gain_two, shift_two = vec(8), vec(9), vec(10), vec(11)

    @pl.when(step == 0)
    def _():
        sum_ref[...] = jnp.zeros_like(sum_ref)

    resid_one = x_ref[...].astype(F32) + dot(mixed_ref[...], w_attn[...]) + vec(2)
    first, scaled_one, inverse_one = norm_forward(resid_one, gain_one, shift_one)
    first_low = first.astype(BF)
    first_ref[...] = first_low
    total = first + vec(7)
    for j in range(chunks):
        cols = pl.ds(j * width, width)
        upper = dot(first_low, w_up[:, cols]) + vec(3 + j)
        half = 0.5 + 0.5 * lax.erf(upper * (1.0 / math.sqrt(2.0)))
        active = (upper * half).astype(BF)
        active_ref[:, cols] = active
        slope_ref[:, cols] = half + upper * jnp.exp(-0.5 * upper * upper) * (
            1.0 / math.sqrt(2.0 * math.pi)
        )
        total = total + dot(active, w_down[cols, :])
    output, scaled_two, inverse_two = norm_forward(total, gain_two, shift_two)
    out_ref[...] = output.astype(BF)

    @pl.when(start < length)
    def _():
        alive = lax.broadcasted_iota(jnp.int32, (rows, 1), 0) + start < length
        grad_out = jnp.where(alive, cot_ref[...].astype(F32), 0.0)
        grad_two = norm_backward(grad_out, scaled_two, inverse_two, gain_two)
        branch = grad_two.astype(BF)
        branch_ref[...] = branch
        grad_first = grad_two
        for j in range(chunks):
            cols = pl.ds(j * width, width)
            grad_upper = (dot(branch, w_down[cols, :], NT) * slope_ref[:, cols]).astype(BF)
            upper_ref[:, cols] = grad_upper
            sum_ref[3 + j : 4 + j, :] += column_sum(grad_upper.astype(F32))
            grad_first = grad_first + dot(grad_upper, w_up[:, cols], NT)
        grad_one = norm_backward(grad_first, scaled_one, inverse_one, gain_one)
        resid_ref[...] = grad_one
        grad_attn = grad_one.astype(BF)
        attn_ref[...] = grad_attn
        gmix_ref[...] = dot(grad_attn, w_attn[...], NT).astype(BF)
        sum_ref[2:3, :] += column_sum(grad_attn.astype(F32))
        sum_ref[7:8, :] += column_sum(branch.astype(F32))
        sum_ref[8:9, :] += column_sum(grad_first * scaled_one)
        sum_ref[9:10, :] += column_sum(grad_first)
        sum_ref[10:11, :] += column_sum(grad_out * scaled_two)
        sum_ref[11:12, :] += column_sum(grad_out)

    @pl.when(start >= length)
    def _():
        upper_ref[...] = jnp.zeros_like(upper_ref)
        branch_ref[...] = jnp.zeros_like(branch_ref)
        attn_ref[...] = jnp.zeros_like(attn_ref)
        gmix_ref[...] = jnp.zeros_like(gmix_ref)
        resid_ref[...] = jnp.zeros_like(resid_ref)


def middle(x, mixed, cotangent, lengths, gathered, w_down, vec):
    rows, width = x.shape
    inner = w_down.shape[0]
    seq = rows // lengths.shape[0]
    once = pl.Buffered(1)
    thin = pl.BlockSpec((ROWS, width), lambda i, ln: (i, 0))
    wide = pl.BlockSpec((ROWS, inner), lambda i, ln: (i, 0))
    grid_spec = pltpu.PrefetchScalarGridSpec(
        num_scalar_prefetch=1,
        grid=(rows // ROWS,),
        in_specs=[
            thin,
            thin,
            thin,
            pl.BlockSpec((width, width), lambda i, ln: (0, 3), pipeline_mode=once),
            pl.BlockSpec((width, inner), lambda i, ln: (0, 1), pipeline_mode=once),
            pl.BlockSpec((inner, width), lambda i, ln: (0, 0), pipeline_mode=once),
            pl.BlockSpec(vec.shape, lambda i, ln: (0, 0)),
        ],
        out_specs=[
            thin,
            thin,
            wide,
            wide,
            thin,
            thin,
            thin,
            thin,
            pl.BlockSpec(vec.shape, lambda i, ln: (0, 0)),
        ],
        scratch_shapes=[pltpu.VMEM((ROWS, inner), F32)],
    )
    low = jax.ShapeDtypeStruct((rows, width), BF)
    low_wide = jax.ShapeDtypeStruct((rows, inner), BF)
    return pl.pallas_call(
        functools.partial(middle_kernel, seq=seq),
        grid_spec=grid_spec,
        out_shape=[
            low,
            low,
            low_wide,
            low_wide,
            low,
            low,
            low,
            jax.ShapeDtypeStruct((rows, width), F32),
            jax.ShapeDtypeStruct(vec.shape, F32),
        ],
        compiler_params=params(1),
        cost_estimate=cost(
            8 * rows * width * inner + 4 * rows * width * width,
            rows * (4 * inner + 20 * width) + 4 * width * inner,
            2 * rows * inner,
        ),
        name="middle",
    )(lengths, x, mixed, cotangent, gathered, gathered, w_down, vec)


def weight_kernel(src_ref, left_ref, right_ref, *refs, sums):
    keep_ref, send_ref, acc_ref = refs[0], refs[1], refs[-1]
    half, piece, _ = keep_ref.shape
    right = right_ref[0] if len(right_ref.shape) == 3 else right_ref[...]
    acc_ref[...] = dot(left_ref[...], right, TN)
    if sums:
        refs[2][0] = jnp.broadcast_to(column_sum(right.astype(F32)), refs[2].shape[1:])
    for slot in range(half):
        for ref, offset in ((keep_ref, 0), (send_ref, half)):
            begin = pl.multiple_of(src_ref[offset + slot] * piece, 8)
            ref[slot] = acc_ref[pl.ds(begin, piece), :].astype(BF)


def plain_weight_kernel(left_ref, right_ref, out_ref, *refs):
    right = right_ref[0] if len(right_ref.shape) == 3 else right_ref[...]
    out_ref[...] = dot(left_ref[...], right, TN).astype(BF)
    if refs:
        refs[0][0] = jnp.broadcast_to(column_sum(right.astype(F32)), refs[0].shape[1:])


def weight_gradient(left, right, source, sums=False):
    rows, tall = left.shape
    devices = source.shape[0]
    piece = tall // devices
    if right.ndim == 3:
        steps, _, tile = right.shape
        right_block = pl.BlockSpec((1, rows, tile), lambda j, *s: (j, 0, 0))
    else:
        tile = min(right.shape[1], 768)
        steps = right.shape[1] // tile
        right_block = pl.BlockSpec((rows, tile), lambda j, *s: (0, j))
    left_block = pl.BlockSpec((rows, tall), lambda j, *s: (0, 0))
    extra_specs = [pl.BlockSpec((1, 8, tile), lambda j, *s: (j, 0, 0))] if sums else []
    extra_shapes = [jax.ShapeDtypeStruct((steps, 8, tile), F32)] if sums else []
    estimate = cost(2 * rows * tall * tile * steps, 2 * tall * tile * steps + 2 * rows * (tall + tile * steps))
    if piece % 8:
        whole, *rest = pl.pallas_call(
            plain_weight_kernel,
            grid=(steps,),
            in_specs=[left_block, right_block],
            out_specs=[pl.BlockSpec((tall, tile), lambda j: (0, j))] + extra_specs,
            out_shape=[jax.ShapeDtypeStruct((tall, steps * tile), BF)] + extra_shapes,
            compiler_params=params(1),
            cost_estimate=estimate,
            name="weight_gradient",
        )(left, right)
        ordered = jnp.take(whole.reshape(devices, piece, steps * tile), source, axis=0)
        return (ordered[: devices // 2], ordered[devices // 2 :], *rest)
    block = pl.BlockSpec((devices // 2, piece, tile), lambda j, s: (0, 0, j))
    shape = jax.ShapeDtypeStruct((devices // 2, piece, steps * tile), BF)
    grid_spec = pltpu.PrefetchScalarGridSpec(
        num_scalar_prefetch=1,
        grid=(steps,),
        in_specs=[left_block, right_block],
        out_specs=[block, block] + extra_specs,
        scratch_shapes=[pltpu.VMEM((tall, tile), F32)],
    )
    return pl.pallas_call(
        functools.partial(weight_kernel, sums=sums),
        grid_spec=grid_spec,
        out_shape=[shape, shape] + extra_shapes,
        compiler_params=params(1),
        cost_estimate=estimate,
        name="weight_gradient",
    )(source, left, right)


def tall_kernel(slot_ref, left_ref, right_ref, keep_ref, send_ref, acc_ref):
    step = pl.program_id(0)
    half, piece, _ = keep_ref.shape
    here = left_ref.shape[1] // piece
    acc_ref[...] = dot(left_ref[...], right_ref[...], TN)
    for index in range(here):
        slot = slot_ref[step * here + index]
        part = acc_ref[index * piece : (index + 1) * piece, :].astype(BF)

        @pl.when(slot < half)
        def _():
            keep_ref[jnp.minimum(slot, half - 1)] = part

        @pl.when(slot >= half)
        def _():
            send_ref[jnp.maximum(slot - half, 0)] = part


def plain_tall_kernel(left_ref, right_ref, out_ref):
    out_ref[...] = dot(left_ref[...], right_ref[...], TN).astype(BF)


def tall_gradient(left, right, source, slot_of):
    rows, tall = left.shape
    width = right.shape[1]
    devices = source.shape[0]
    piece = tall // devices
    steps = tall // width
    left_block = pl.BlockSpec((rows, width), lambda j, *s: (0, j))
    right_block = pl.BlockSpec((rows, width), lambda j, *s: (0, 0))
    estimate = cost(2 * rows * tall * width, 2 * tall * width + 2 * rows * (tall + width))
    if piece % 16:
        whole = pl.pallas_call(
            plain_tall_kernel,
            grid=(steps,),
            in_specs=[left_block, right_block],
            out_specs=pl.BlockSpec((width, width), lambda j: (j, 0)),
            out_shape=jax.ShapeDtypeStruct((tall, width), BF),
            compiler_params=params(1),
            cost_estimate=estimate,
            name="tall_gradient",
        )(left, right)
        ordered = jnp.take(whole.reshape(devices, piece, width), source, axis=0)
        return (ordered[: devices // 2], ordered[devices // 2 :])
    block = pl.BlockSpec((devices // 2, piece, width), lambda j, s: (0, 0, 0))
    shape = jax.ShapeDtypeStruct((devices // 2, piece, width), BF)
    grid_spec = pltpu.PrefetchScalarGridSpec(
        num_scalar_prefetch=1,
        grid=(steps,),
        in_specs=[left_block, right_block],
        out_specs=[block, block],
        scratch_shapes=[pltpu.VMEM((width, width), F32)],
    )
    return pl.pallas_call(
        tall_kernel,
        grid_spec=grid_spec,
        out_shape=[shape, shape],
        compiler_params=params(1),
        cost_estimate=estimate,
        name="tall_gradient",
    )(slot_of, left, right)


def input_kernel(resid_ref, w_ref, *refs):
    out_ref = refs[-1]
    width = resid_ref.shape[1]
    total = resid_ref[...]
    for group, grad_ref in enumerate(refs[:-1]):
        here = grad_ref.shape[2]
        for part in range(3):
            total = total + dot(grad_ref[part], w_ref[:, pl.ds(part * width + group * here, here)], NT)
    out_ref[...] = total.astype(BF)


def input_gradient(resid, gathered, grads):
    rows, width = resid.shape
    return pl.pallas_call(
        input_kernel,
        grid=(rows // ROWS,),
        in_specs=[
            pl.BlockSpec((ROWS, width), lambda i: (i, 0)),
            pl.BlockSpec((width, 3 * width), lambda i: (0, 0), pipeline_mode=pl.Buffered(1)),
        ]
        + [pl.BlockSpec((3, ROWS, grad.shape[2]), lambda i: (0, i, 0)) for grad in grads],
        out_specs=pl.BlockSpec((ROWS, width), lambda i: (i, 0)),
        out_shape=jax.ShapeDtypeStruct((rows, width), BF),
        compiler_params=params(1),
        cost_estimate=cost(6 * rows * width * width, 12 * rows * width + 6 * width * width),
        name="input_gradient",
    )(resid, gathered, *grads)


def stages(devices):
    bits = devices.bit_length() - 1
    found = [(0, 1)]
    at = 1
    while at < bits:
        count = min(2, bits - at)
        found.append((at, count))
        at += count
    return found


def relative_order(devices):
    order = [0]
    for at, count in stages(devices):
        order = [base | (value << at) for base in order for value in range(1 << count)]
    return order


def swap(value, mask, devices):
    return lax.ppermute(value, "dp", [(index, index ^ mask) for index in range(devices)])


def sum_of(terms, begin, size):
    total = terms[0][begin : begin + size].astype(F32)
    for term in terms[1:]:
        total = total + term[begin : begin + size].astype(F32)
    return total


def reduce_to_owner(keep, send, devices):
    terms = [keep, swap(send, 1, devices)]
    for at, count in stages(devices)[1:]:
        size = terms[0].shape[0] >> count
        parts = [
            sum_of(terms, value * size, size).astype(keep.dtype) for value in range(1 << count)
        ]
        terms = [parts[0]] + [
            swap(parts[value], value << at, devices) for value in range(1, 1 << count)
        ]
    return sum_of(terms, 0, 1)[0]


def adamw(weight, grad, first, second, decay, rate):
    new_first = BETA_ONE * first + (1.0 - BETA_ONE) * grad
    new_second = BETA_TWO * second + (1.0 - BETA_TWO) * grad * grad
    corrected = new_first / (1.0 - BETA_ONE**STEP)
    scale_sq = new_second / (1.0 - BETA_TWO**STEP)
    new_weight = weight - rate * (corrected / (jnp.sqrt(scale_sq) + EPSILON_ADAM) + decay * weight)
    return (new_first, new_second, new_weight)


def on_device(
    hidden_in,
    lengths,
    cotangent,
    proj_qkv,
    proj_attn,
    proj_up,
    proj_down,
    vectors,
    first_qkv,
    first_attn,
    first_up,
    first_down,
    first_vectors,
    second_qkv,
    second_attn,
    second_up,
    second_down,
    second_vectors,
):
    devices = lax.axis_size("dp")
    me = lax.axis_index("dp")
    width = hidden_in.shape[1]
    piece = proj_qkv.shape[0]
    inner = proj_up.shape[1]
    ratio = inner // width
    relative = jnp.asarray(relative_order(devices), jnp.int32)
    source = relative ^ me
    slots = [0] * devices
    for slot, value in enumerate(relative_order(devices)):
        slots[value] = slot
    slot_of = jnp.take(jnp.asarray(slots, jnp.int32), jnp.arange(devices, dtype=jnp.int32) ^ me)

    entries = vectors.shape[0] // piece
    shard = jnp.concatenate(
        [
            proj_qkv.astype(BF),
            proj_attn.astype(BF),
            proj_up.astype(BF),
            proj_down.astype(BF).reshape(ratio, piece, width).transpose(1, 0, 2).reshape(piece, inner),
            jnp.pad(vectors.astype(BF).reshape(piece, entries), ((0, 0), (0, LANES - entries))),
        ],
        axis=1,
    )
    gathered = lax.all_gather(shard, "dp", axis=0, tiled=True)
    base = 4 * width + inner
    w_down = (
        gathered[:, base : base + inner]
        .reshape(devices, piece, ratio, width)
        .transpose(0, 2, 1, 3)
        .reshape(inner, width)
    )
    vec = gathered[:, base + inner : base + inner + entries].astype(F32).reshape(-1, width)

    packed = project_qkv(hidden_in, gathered, vec)
    mixed, lse = attend_forward(packed, lengths, width)
    output, first_low, active, grad_upper, grad_branch, grad_attn, grad_mixed, grad_one, sums = middle(
        hidden_in, mixed, cotangent, lengths, gathered, w_down, vec
    )
    total_down = reduce_to_owner(*tall_gradient(active, grad_branch, source, slot_of), devices)
    total_up = reduce_to_owner(*weight_gradient(first_low, grad_upper, source), devices)
    total_attn = reduce_to_owner(*weight_gradient(mixed, grad_attn, source), devices)
    totals = []
    parts = []
    part_sums = []
    for group in range(GROUPS):
        part = attend_backward(packed, lengths, lse, grad_mixed, group)
        keep, send, part_sum = weight_gradient(hidden_in, part, source, sums=True)
        totals.append(reduce_to_owner(keep, send, devices).reshape(piece, 3, -1))
        parts.append(part)
        part_sums.append(part_sum)
    total_qkv = jnp.concatenate(totals, axis=2).reshape(piece, 3 * width)
    part_sums = jnp.concatenate(part_sums, axis=2)
    vector_sums = jnp.concatenate([part_sums[0, :1], part_sums[2, :1], sums[2:]], axis=0)
    ordered = jnp.take(vector_sums.reshape(devices, 1, -1), source, axis=0)
    total_vectors = reduce_to_owner(ordered[: devices // 2], ordered[devices // 2 :], devices)[0]
    input_grad = input_gradient(grad_one, gathered, parts)

    m_qkv, v_qkv, w_qkv = adamw(proj_qkv, total_qkv, first_qkv, second_qkv, WEIGHT_DECAY, LEARN_RATE)
    m_attn, v_attn, w_attn = adamw(
        proj_attn, total_attn, first_attn, second_attn, WEIGHT_DECAY, LEARN_RATE
    )
    m_up, v_up, w_up = adamw(proj_up, total_up, first_up, second_up, WEIGHT_DECAY, LEARN_RATE)
    m_down, v_down, w_down = adamw(
        proj_down, total_down, first_down, second_down, WEIGHT_DECAY, LEARN_RATE
    )
    m_vec, v_vec, w_vec = adamw(
        vectors, total_vectors, first_vectors, second_vectors, 0.0, LEARN_RATE_VECTOR
    )
    return (
        output,
        input_grad,
        m_qkv,
        v_qkv,
        w_qkv,
        m_attn,
        v_attn,
        w_attn,
        m_up,
        v_up,
        w_up,
        m_down,
        v_down,
        w_down,
        m_vec,
        v_vec,
        w_vec,
    )


def solution(mesh):
    rows, flat = P("dp", None), P("dp")
    return jax.shard_map(
        on_device,
        mesh=mesh,
        in_specs=(rows, flat, rows) + (rows, rows, rows, rows, flat) * 3,
        out_specs=(rows, rows) + (rows,) * 12 + (flat,) * 3,
        check_vma=False,
    )
```

time: 856 us -> 425 us (0.50)
  waiting for transfers between devices: 510 us -> 175 us
  matrix products: 155 us -> 0 us
  Pallas kernels: 0 us -> 140 us
  blocking collectives: 82.5 us -> 0 us
  starting transfers between devices: 0.33 us -> 53.6 us
  other arithmetic: 47.2 us -> 17.1 us
  local copies, waits for them, and re-layouts: 36.9 us -> 23.4 us
    reduce_scatter x4 -> x0, waiting for transfers between devices: 371 us -> none  [the longest x1 140 us: on_device(): lax.psum_scatter(totals[3], 'dp', scatter_dimension=0, tiled=True)]
    dot_general x36 -> x0, matrix products: 155 us -> none  [the longest x8 36.8 us: matmul(): return jnp.dot(left_arr, right_arr, preferred_element_type=jnp.float32)]
    pallas_call x0 -> x11, Pallas kernels: none -> 140 us  [the longest x1 32.3 us: middle(): pl.pallas_call(functools.partial(middle_kernel, seq=seq), grid_spec=grid_...]
    unnamed x2 -> x0, blocking collectives: 82.5 us -> none
    ppermute x0 -> x42, waiting for transfers between devices: none -> 69.2 us  [swap(): lax.ppermute(value, 'dp', [(index, index ^ mask) for index in range(devic...]
    ppermute x0 -> x42, starting transfers between devices: none -> 53.6 us  [swap(): lax.ppermute(value, 'dp', [(index, index ^ mask) for index in range(devic...]
    all_gather x4 -> x1, waiting for transfers between devices: 138 us -> 106 us  [on_device(): gathered = lax.all_gather(shard, 'dp', axis=0, tiled=True)]
    unnamed x157 -> x62, local copies, waits for them, and re-layouts: 26.6 us -> 0.98 us
  transfers between devices with their start and end apart: 8 -> 43, of which waited for: 7 -> 19; matrix products, arithmetic and copies ran while one was open for 18% -> 3% of each run, Pallas kernels for 0% -> 10%
where the time goes in v1:
time: 425 us; the launch traced here: 424 us
  waiting for transfers between devices  175 us (41%)
  Pallas kernels  140 us (33%)
  starting transfers between devices  53.6 us (13%)
  local copies, waits for them, and re-layouts  23.4 us (6%)
  other arithmetic  17.1 us (4%)
  between operations  14.6 us (3%)
    all_gather x1, waiting for transfers between devices, on_device(): gathered = lax.all_gather(shard, 'dp', axis=0, tiled=True)  106 us
    ppermute x42, waiting for transfers between devices, swap(): lax.ppermute(value, 'dp', [(index, index ^ mask) for index in range(devic...  69.2 us
    ppermute x42, starting transfers between devices, swap(): lax.ppermute(value, 'dp', [(index, index ^ mask) for index in range(devic...  53.6 us
    pallas_call x1, Pallas kernels, middle(): pl.pallas_call(functools.partial(middle_kernel, seq=seq), grid_spec=grid_...  32.3 us
    pallas_call x2, Pallas kernels, attend_backward(): pl.pallas_call(attend_back_kernel, grid_spec=grid_spec, out_shape=jax.Sha...  31.1 us
    pallas_call x4, Pallas kernels, weight_gradient(): pl.pallas_call(functools.partial(weight_kernel, sums=sums), grid_spec=gri...  28.5 us
    pallas_call x1, Pallas kernels, attend_forward(): pl.pallas_call(attend_kernel, grid_spec=grid_spec, out_shape=[jax.ShapeDt...  19.6 us
    pallas_call x1, Pallas kernels, tall_gradient(): pl.pallas_call(tall_kernel, grid_spec=grid_spec, out_shape=[shape, shape]...  11.5 us
  transfers between devices with their start and end apart: 43, of which 19 were waited for; matrix products, arithmetic and copies ran while one was open for 3% of the time, Pallas kernels for 10%

profile of v1, /device:TPU:0, one launch (start us, length us, event | category | flops | bytes accessed | tf_op | source)
XLA Modules:
  0.0 423.6 jit_solution(11975519136063841832)
XLA Ops:
  13.2 105.6 %all-gather.2.cloned.1.call-done.w_ref.w_attn.w_up = bf16[768,9344]{1,0:T(8,128)(2,1)} async-done(((bf16[24,9344]{1,0:T(8,128)(2,1)}), bf16[768,9344]{1,0:T(8,128)(2,1)}) %all-gather.2.cloned.1.call-update) | async-done | bytes 14352400 | tf_op jit(solution)/shard_map/all_gather | solution.py:618
  120.6 4.8 %slice.610 = bf16[768,3072]{1,0:T(8,128)(2,1)} slice(bf16[768,9344]{1,0:T(8,128)(2,1)} %all-gather.2.cloned.1.call-done.w_ref.w_attn.w_up), slice={[0:768], [6144:9216]} | slice | bytes 9437184 | tf_op jit(solution)/shard_map/slice | solution.py:621
  125.4 9.8 %reshape.116 = bf16[32,24,4,768]{3,2,1,0:T(4,128)(2,1)} reshape(bf16[768,3072]{1,0:T(8,128)(2,1)} %slice.610) | data formatting | bytes 9437184 | tf_op jit(solution)/shard_map/reshape | solution.py:622
  135.2 5.3 %copy.40 = bf16[32,4,24,768]{3,2,1,0:T(8,128)(2,1)} copy(bf16[32,4,24,768]{3,1,2,0:T(4,128)(2,1)} %bitcast.37) | data formatting | bytes 9437184 | tf_op jit(solution)/shard_map/transpose | solution.py:623
  140.5 7.8 %project_qkv.1.q_ref.k_ref.v_ref = bf16[1024,2304]{1,0:T(8,128)(2,1)} custom-call(bf16[1024,768]{1,0:T(8,128)(2,1)} %left_ref.3, bf16[768,9344]{1,0:T(8,128)(2,1)} %all-gather.2.cloned.1.call-done.w_ref.w_attn.w_up, f32[12,768]{1,0:T(8,128)} %reshape.121.vec_ref), custom_call_target="tpu_custom_call" | custom-call | flops 3623878656 | bytes 9830400 | tf_op jit(solution)/shard_map/project_qkv/pallas_call | solution.py:63
  148.3 19.6 %attend_forward.1 = (bf16[1024,768]{1,0:T(8,128)(2,1)}, f32[12,2,512]{2,1,0:T(2,128)}) custom-call(s32[2]{0:T(128)} %len_ref.7, bf16[1024,2304]{1,0:T(8,128)(2,1)} %project_qkv.1.q_ref.k_ref.v_ref, bf16[1024,2304]{1,0:T(8,128)(2,1)} %project_qkv.1.q_ref.k_ref.v_ref, bf16[1024,2304]{1,0:T(8,128)(2,1)} %project_qkv.1.q_ref.k_ref.v_ref), custom_call_target="tpu_custom_call" | custom-call | flops 6442450944 | bytes 6291456 | tf_op jit(solution)/shard_map/attend_forward/pallas_call | solution.py:119
  167.9 32.3 %middle.1 = (bf16[1024,768]{1,0:T(8,128)(2,1)}, bf16[1024,768]{1,0:T(8,128)(2,1)}, bf16[1024,3072]{1,0:T(8,128)(2,1)}, bf16[1024,3072]{1,0:T(8,128)(2,1)}, bf16[...) custom-call(s32[2]{0:T(128)} %len_ref.7, ...), custom_call_target="tpu_custom_call" | custom-call | flops 21743271936 | bytes 37748736 | tf_op jit(solution)/shard_map/middle/pallas_call | solution.py:340
  200.2 15.6 %attend_backward.2.refs_0_.right_ref = bf16[3,1024,384]{2,1,0:T(8,128)(2,1)} custom-call(s32[2]{0:T(128)} %len_ref.7, bf16[1024,2304]{1,0:T(8,128)(2,1)} %project_qkv.1.q_ref.k_ref.v_ref, bf16[1024,2304]{1,0:T(8,128)(2,1)} %project_qkv.1.q_ref.k_ref.v_ref, bf16[1024,2304]{1,0:T(8,128)(2,1)} %project_qkv.1.q_ref.k_ref.v_ref, ...), custom_call_target="tpu_custom_call" | custom-call | flops 8053063680 | bytes 5505024 | tf_op jit(solution)/shard_map/attend_backward/pallas_call | solution.py:182
  215.8 15.4 %attend_backward.3.refs_1_.right_ref = bf16[3,1024,384]{2,1,0:T(8,128)(2,1)} custom-call(s32[2]{0:T(128)} %len_ref.7, bf16[1024,2304]{1,0:T(8,128)(2,1)} %project_qkv.1.q_ref.k_ref.v_ref, bf16[1024,2304]{1,0:T(8,128)(2,1)} %project_qkv.1.q_ref.k_ref.v_ref, bf16[1024,2304]{1,0:T(8,128)(2,1)} %project_qkv.1.q_ref.k_ref.v_ref, ...), custom_call_target="tpu_custom_call" | custom-call | flops 8053063680 | bytes 5505024 | tf_op jit(solution)/shard_map/attend_backward/pallas_call | solution.py:182
  231.2 6.6 %weight_gradient.5 = (bf16[16,24,1152]{2,1,0:T(8,128)(2,1)}, bf16[16,24,1152]{2,1,0:T(8,128)(2,1)}, f32[3,8,384]{2,1,0:T(8,128)}) custom-call(s32[32]{0:T(128)} %get-tuple-element.125.src_ref, bf16[1024,768]{1,0:T(8,128)(2,1)} %left_ref.3, bf16[3,1024,384]{2,1,0:T(8,128)(2,1)} %attend_backward.3.refs_1_.right_ref), custom_call_target="tpu_custom_call" | custom-call | flops 1811939328 | bytes 5701632 | tf_op jit(solution)/shard_map/weight_gradient/pallas_call | solution.py:421
  238.1 6.6 %weight_gradient.4 = (bf16[16,24,1152]{2,1,0:T(8,128)(2,1)}, bf16[16,24,1152]{2,1,0:T(8,128)(2,1)}, f32[3,8,384]{2,1,0:T(8,128)}) custom-call(s32[32]{0:T(128)} %get-tuple-element.125.src_ref, bf16[1024,768]{1,0:T(8,128)(2,1)} %left_ref.3, bf16[3,1024,384]{2,1,0:T(8,128)(2,1)} %attend_backward.2.refs_0_.right_ref), custom_call_target="tpu_custom_call" | custom-call | flops 1811939328 | bytes 5701632 | tf_op jit(solution)/shard_map/weight_gradient/pallas_call | solution.py:421
  244.8 5.2 %weight_gradient.6 = (bf16[16,24,768]{2,1,0:T(8,128)(2,1)}, bf16[16,24,768]{2,1,0:T(8,128)(2,1)}) custom-call(s32[32]{0:T(128)} %get-tuple-element.125.src_ref, bf16[1024,768]{1,0:T(8,128)(2,1)} %get-tuple-element.40.mixed_ref.left_ref, bf16[1024,768]{1,0:T(8,128)(2,1)} %get-tuple-element.49.right_ref), custom_call_target="tpu_custom_call" | custom-call | flops 1207959552 | bytes 4325376 | tf_op jit(solution)/shard_map/weight_gradient/pallas_call | solution.py:421
  251.4 10.1 %weight_gradient.7 = (bf16[16,24,3072]{2,1,0:T(8,128)(2,1)}, bf16[16,24,3072]{2,1,0:T(8,128)(2,1)}) custom-call(s32[32]{0:T(128)} %get-tuple-element.125.src_ref, bf16[1024,768]{1,0:T(8,128)(2,1)} %get-tuple-element.52.left_ref, bf16[1024,3072]{1,0:T(8,128)(2,1)} %get-tuple-element.53.right_ref), custom_call_target="tpu_custom_call" | custom-call | flops 4831838208 | bytes 12582912 | tf_op jit(solution)/shard_map/weight_gradient/pallas_call | solution.py:421
  261.4 5.0 %collective-permute-start.38 = (f32[4,1,288]{2,0,1:T(4,128)S(1)}, f32[4,1,288]{2,0,1:T(4,128)S(1)}, u32[]{:S(2)}, u32[]{:S(2)}) collective-permute-start(f32[4,1,288]{2,0,1:T(4,128)S(1)} %get-tuple-element.116), channel_id=1, source_target_pairs={{0,6},{1,7},{2,4},{3,5},{4,2},{5,3},{6,0},{7,1},{8,14},{9,15},{10,... | collective-permute-start | bytes 13832 | tf_op jit(solution)/shard_map/ppermute | solution.py:542
  266.4 1.4 collective-permute-start.37
  267.9 11.5 %tall_gradient.1 = (bf16[16,96,768]{2,1,0:T(8,128)(2,1)}, bf16[16,96,768]{2,1,0:T(8,128)(2,1)}) custom-call(s32[32]{0:T(128)} %get-tuple-element.124.slot_ref, bf16[1024,3072]{1,0:T(8,128)(2,1)} %get-tuple-element.56.left_ref, bf16[1024,768]{1,0:T(8,128)(2,1)} %get-tuple-element.57.right_ref), custom_call_target="tpu_custom_call" | custom-call | flops 4831838208 | bytes 12582912 | tf_op jit(solution)/shard_map/tall_gradient/pallas_call | solution.py:484
  279.4 5.4 %collective-permute-start.41 = (f32[1,1,288]{2,0,1:T(1,128)S(1)}, f32[1,1,288]{2,0,1:T(1,128)S(1)}, u32[]{:S(2)}, u32[]{:S(2)}) collective-permute-start(f32[1,1,288]{2,0,1:T(1,128)S(1)} %get-tuple-element.122), channel_id=1, source_target_pairs={{0,24},{1,25},{2,26},{3,27},{4,28},{5,29},{6,30},{7,31},{8,16},{9,... | collective-permute-start | bytes 3464 | tf_op jit(solution)/shard_map/ppermute | solution.py:542
  285.7 1.5 collective-permute-start.17
  287.2 1.5 collective-permute-start.16
  289.3 1.4 collective-permute-start.15
  290.8 9.3 %input_gradient.1 = bf16[1024,768]{1,0:T(8,128)(2,1)} custom-call(f32[1024,768]{1,0:T(8,128)} %get-tuple-element.42.resid_ref, bf16[768,9344]{1,0:T(8,128)(2,1)} %all-gather.2.cloned.1.call-done.w_ref.w_attn.w_up, bf16[3,1024,384]{2,1,0:T(8,128)(2,1)} %attend_backward.2.refs_0_.right_ref, bf16[3,1024,384]{2,1,0:T(8,128)(2,1)} %attend_backward.3.refs_1_.right_ref), custom_call_target="tpu_custom_call" | custom-call | flops 3623878656 | bytes 12976128 | tf_op jit(solution)/shard_map/input_gradient/pallas_call | solution.py:507
  300.3 2.3 collective-permute-start.20
  302.6 2.2 collective-permute-start.18
  308.6 1.6 collective-permute-start.10
  312.4 5.5 %collective-permute-done.10 = bf16[4,24,1152]{2,1,0:T(8,128)(2,1)S(1)} collective-permute-done((bf16[4,24,1152]{2,1,0:T(8,128)(2,1)S(1)}, bf16[4,24,1152]{2,1,0:T(8,128)(2,1)S(1)}, u32[]{:S(2)}, u32[]{:S(2)}) %collective-permute-start.10) | collective-permute-done | bytes 221216 | tf_op jit(solution)/shard_map/ppermute | solution.py:542
  317.9 1.5 collective-permute-start.3
  319.4 3.1 collective-permute-done.9
  322.5 1.3 collective-permute-start.2
  324.7 2.6 collective-permute-done.3
  327.4 2.2 collective-permute-start.13
  329.6 2.1 collective-permute-done.2
  332.3 2.2 collective-permute-start.11
  334.6 1.7 collective-permute-start.6
  337.7 2.4 collective-permute-start.4
  341.2 1.8 collective-permute-done.5
  344.6 2.7 add_convert_fusion.7
  347.3 1.5 collective-permute-start.24
  351.8 2.3 add_convert_fusion.3
  354.1 1.5 collective-permute-start.31
  356.6 7.9 %collective-permute-done.24 = bf16[4,24,3072]{2,1,0:T(8,128)(2,1)S(1)} collective-permute-done((bf16[4,24,3072]{2,1,0:T(8,128)(2,1)S(1)}, bf16[4,24,3072]{2,1,0:T(8,128)(2,1)S(1)}, u32[]{:S(2)}, u32[]{:S(2)}) %collective-permute-start.24) | collective-permute-done | bytes 589856 | tf_op jit(solution)/shard_map/ppermute | solution.py:542
  365.6 11.7 %collective-permute-done.23 = bf16[4,24,3072]{2,1,0:T(8,128)(2,1)S(1)} collective-permute-done((bf16[4,24,3072]{2,1,0:T(8,128)(2,1)S(1)}, bf16[4,24,3072]{2,1,0:T(8,128)(2,1)S(1)}, u32[]{:S(2)}, u32[]{:S(2)}) %collective-permute-start.23) | collective-permute-done | bytes 589856 | tf_op jit(solution)/shard_map/ppermute | solution.py:542
  377.5 1.7 collective-permute-start.27
  380.1 9.8 %collective-permute-done.31 = bf16[4,96,768]{2,1,0:T(8,128)(2,1)S(1)} collective-permute-done((bf16[4,96,768]{2,1,0:T(8,128)(2,1)S(1)}, bf16[4,96,768]{2,1,0:T(8,128)(2,1)S(1)}, u32[]{:S(2)}, u32[]{:S(2)}) %collective-permute-start.31) | collective-permute-done | bytes 589856 | tf_op jit(solution)/shard_map/ppermute | solution.py:542
  390.8 9.9 %collective-permute-done.30 = bf16[4,96,768]{2,1,0:T(8,128)(2,1)S(1)} collective-permute-done((bf16[4,96,768]{2,1,0:T(8,128)(2,1)S(1)}, bf16[4,96,768]{2,1,0:T(8,128)(2,1)S(1)}, u32[]{:S(2)}, u32[]{:S(2)}) %collective-permute-start.30) | collective-permute-done | bytes 589856 | tf_op jit(solution)/shard_map/ppermute | solution.py:542
  401.0 1.3 collective-permute-start.34
  402.9 2.6 collective-permute-start.32
  406.7 3.1 collective-permute-done.34
  409.7 5.8 %collective-permute-done.33 = bf16[1,96,768]{2,1,0:T(8,128)(2,1)S(1)} collective-permute-done((bf16[1,96,768]{2,1,0:T(8,128)(2,1)S(1)}, bf16[1,96,768]{2,1,0:T(8,128)(2,1)S(1)}, u32[]{:S(2)}, u32[]{:S(2)}) %collective-permute-start.33) | collective-permute-done | bytes 147488 | tf_op jit(solution)/shard_map/ppermute | solution.py:542
  (162 shorter events, 32.9 us)
Async XLA Ops:
  7.2 111.6 %all-gather.2.cloned.1.call-start = ((), (), s32[]{:S(2)}) async-start(), calls=%async_computation | async-start | bytes 14800896 | tf_op jit(solution)/shard_map/all_gather | solution.py:618
  237.9 70.6 %collective-permute-start.7 = (bf16[16,24,1152]{2,1,0:T(8,128)(2,1)}, bf16[16,24,1152]{2,1,0:T(8,128)(2,1)S(1)}, u32[]{:S(2)}, u32[]{:S(2)}) collective-permute-start(bf16[16,24,1152]{2,1,0:T(8,128)(2,1)} %get-tuple-element.48), channel_id=1, source_target_pairs={{0,1},{1,0},{2,3},{3,2},{4,5},{5,4},{6,7},{7,6},{8,9},{9,8},{10,11... | collective-permute-start | bytes 2654216 | tf_op jit(solution)/shard_map/ppermute | solution.py:542
  249.9 35.6 %collective-permute-start.14 = (bf16[16,24,768]{2,1,0:T(8,128)(2,1)}, bf16[16,24,768]{2,1,0:T(8,128)(2,1)S(1)}, u32[]{:S(2)}, u32[]{:S(2)}) collective-permute-start(bf16[16,24,768]{2,1,0:T(8,128)(2,1)} %get-tuple-element.51), channel_id=1, source_target_pairs={{0,1},{1,0},{2,3},{3,2},{4,5},{5,4},{6,7},{7,6},{8,9},{9,8},{10,11... | collective-permute-start | bytes 1769480 | tf_op jit(solution)/shard_map/ppermute | solution.py:542
  251.1 10.4 %collective-permute-start.35 = (f32[16,1,288]{2,0,1:T(8,128)S(1)}, f32[16,1,288]{2,0,1:T(8,128)S(1)}, u32[]{:S(2)}, u32[]{:S(2)}) collective-permute-start(f32[16,1,288]{2,0,1:T(8,128)S(1)} %slice.714), channel_id=1, source_target_pairs={{0,1},{1,0},{2,3},{3,2},{4,5},{5,4},{6,7},{7,6},{8,9},{9,8},{10,11... | collective-permute-start | bytes 55304 | tf_op jit(solution)/shard_map/ppermute | solution.py:542
  261.4 17.9 %collective-permute-start.38 = (f32[4,1,288]{2,0,1:T(4,128)S(1)}, f32[4,1,288]{2,0,1:T(4,128)S(1)}, u32[]{:S(2)}, u32[]{:S(2)}) collective-permute-start(f32[4,1,288]{2,0,1:T(4,128)S(1)} %get-tuple-element.116), channel_id=1, source_target_pairs={{0,6},{1,7},{2,4},{3,5},{4,2},{5,3},{6,0},{7,1},{8,14},{9,15},{10,... | collective-permute-start | bytes 13832 | tf_op jit(solution)/shard_map/ppermute | solution.py:542
  266.4 12.9 %collective-permute-start.37 = (f32[4,1,288]{2,0,1:T(4,128)S(1)}, f32[4,1,288]{2,0,1:T(4,128)S(1)}, u32[]{:S(2)}, u32[]{:S(2)}) collective-permute-start(f32[4,1,288]{2,0,1:T(4,128)S(1)} %get-tuple-element.117), channel_id=1, source_target_pairs={{0,4},{1,5},{2,6},{3,7},{4,0},{5,1},{6,2},{7,3},{8,12},{9,13},{10,... | collective-permute-start | bytes 13832 | tf_op jit(solution)/shard_map/ppermute | solution.py:542
  267.8 11.5 %collective-permute-start.36 = (f32[4,1,288]{2,0,1:T(4,128)S(1)}, f32[4,1,288]{2,0,1:T(4,128)S(1)}, u32[]{:S(2)}, u32[]{:S(2)}) collective-permute-start(f32[4,1,288]{2,0,1:T(4,128)S(1)} %get-tuple-element.118), channel_id=1, source_target_pairs={{0,2},{1,3},{2,0},{3,1},{4,6},{5,7},{6,4},{7,5},{8,10},{9,11},{10,... | collective-permute-start | bytes 13832 | tf_op jit(solution)/shard_map/ppermute | solution.py:542
  267.9 17.6 %copy-start.9 = (bf16[16,24,768]{2,1,0:T(8,128)(2,1)S(1)}, bf16[16,24,768]{2,1,0:T(8,128)(2,1)}, u32[]{:S(2)}) copy-start(bf16[16,24,768]{2,1,0:T(8,128)(2,1)} %get-tuple-element.50) | copy-start | bytes 1769476
  279.4 7.8 %collective-permute-start.41 = (f32[1,1,288]{2,0,1:T(1,128)S(1)}, f32[1,1,288]{2,0,1:T(1,128)S(1)}, u32[]{:S(2)}, u32[]{:S(2)}) collective-permute-start(f32[1,1,288]{2,0,1:T(1,128)S(1)} %get-tuple-element.122), channel_id=1, source_target_pairs={{0,24},{1,25},{2,26},{3,27},{4,28},{5,29},{6,30},{7,31},{8,16},{9,... | collective-permute-start | bytes 3464 | tf_op jit(solution)/shard_map/ppermute | solution.py:542
  284.8 4.5 %collective-permute-start.40 = (f32[1,1,288]{2,0,1:T(1,128)S(1)}, f32[1,1,288]{2,0,1:T(1,128)S(1)}, u32[]{:S(2)}, u32[]{:S(2)}) collective-permute-start(f32[1,1,288]{2,0,1:T(1,128)S(1)} %get-tuple-element.123), channel_id=1, source_target_pairs={{0,16},{1,17},{2,18},{3,19},{4,20},{5,21},{6,22},{7,23},{8,24},{9,... | collective-permute-start | bytes 3464 | tf_op jit(solution)/shard_map/ppermute | solution.py:542
  285.5 14.6 %collective-permute-start.39 = (f32[1,1,288]{2,0,1:T(1,128)S(1)}, f32[1,1,288]{2,0,1:T(1,128)S(1)}, u32[]{:S(2)}, u32[]{:S(2)}) collective-permute-start(f32[1,1,288]{2,0,1:T(1,128)S(1)} %get-tuple-element.121), channel_id=1, source_target_pairs={{0,8},{1,9},{2,10},{3,11},{4,12},{5,13},{6,14},{7,15},{8,0},{9,1},... | collective-permute-start | bytes 3464 | tf_op jit(solution)/shard_map/ppermute | solution.py:542
  285.7 14.6 %collective-permute-start.17 = (bf16[4,24,768]{2,1,0:T(8,128)(2,1)S(1)}, bf16[4,24,768]{2,1,0:T(8,128)(2,1)S(1)}, u32[]{:S(2)}, u32[]{:S(2)}) collective-permute-start(bf16[4,24,768]{2,1,0:T(8,128)(2,1)S(1)} %get-tuple-element.103), channel_id=1, source_target_pairs={{0,6},{1,7},{2,4},{3,5},{4,2},{5,3},{6,0},{7,1},{8,14},{9,15},{10,... | collective-permute-start | bytes 442376 | tf_op jit(solution)/shard_map/ppermute | solution.py:542
  287.2 13.1 %collective-permute-start.16 = (bf16[4,24,768]{2,1,0:T(8,128)(2,1)S(1)}, bf16[4,24,768]{2,1,0:T(8,128)(2,1)S(1)}, u32[]{:S(2)}, u32[]{:S(2)}) collective-permute-start(bf16[4,24,768]{2,1,0:T(8,128)(2,1)S(1)} %get-tuple-element.104), channel_id=1, source_target_pairs={{0,4},{1,5},{2,6},{3,7},{4,0},{5,1},{6,2},{7,3},{8,12},{9,13},{10,... | collective-permute-start | bytes 442376 | tf_op jit(solution)/shard_map/ppermute | solution.py:542
  289.3 10.9 %collective-permute-start.15 = (bf16[4,24,768]{2,1,0:T(8,128)(2,1)S(1)}, bf16[4,24,768]{2,1,0:T(8,128)(2,1)S(1)}, u32[]{:S(2)}, u32[]{:S(2)}) collective-permute-start(bf16[4,24,768]{2,1,0:T(8,128)(2,1)S(1)} %get-tuple-element.105), channel_id=1, source_target_pairs={{0,2},{1,3},{2,0},{3,1},{4,6},{5,7},{6,4},{7,5},{8,10},{9,11},{10,... | collective-permute-start | bytes 442376 | tf_op jit(solution)/shard_map/ppermute | solution.py:542
  290.7 16.9 %copy-start.10 = (f32[24,768]{1,0:T(8,128)S(1)}, f32[24,768]{1,0:T(8,128)}, u32[]{:S(2)}) copy-start(f32[24,768]{1,0:T(8,128)} %param.24) | copy-start | bytes 221188
  290.8 16.9 %copy-start.19 = (f32[24,768]{1,0:T(8,128)S(1)}, f32[24,768]{1,0:T(8,128)}, u32[]{:S(2)}) copy-start(f32[24,768]{1,0:T(8,128)} %param.34) | copy-start | bytes 221188
  300.1 11.3 %collective-permute-start = (bf16[16,24,1152]{2,1,0:T(8,128)(2,1)S(1)}, bf16[16,24,1152]{2,1,0:T(8,128)(2,1)S(1)}, u32[]{:S(2)}, u32[]{:S(2)}) collective-permute-start(bf16[16,24,1152]{2,1,0:T(8,128)(2,1)S(1)} %copy-done.28), channel_id=1, source_target_pairs={{0,1},{1,0},{2,3},{3,2},{4,5},{5,4},{6,7},{7,6},{8,9},{9,8},{10,11... | collective-permute-start | bytes 2654216 | tf_op jit(solution)/shard_map/ppermute | solution.py:542
  300.3 6.1 %collective-permute-start.20 = (bf16[1,24,768]{2,1,0:T(8,128)(2,1)S(1)}, bf16[1,24,768]{2,1,0:T(8,128)(2,1)S(1)}, u32[]{:S(2)}, u32[]{:S(2)}) collective-permute-start(bf16[1,24,768]{2,1,0:T(8,128)(2,1)S(1)} %get-tuple-element.113), channel_id=1, source_target_pairs={{0,24},{1,25},{2,26},{3,27},{4,28},{5,29},{6,30},{7,31},{8,16},{9,... | collective-permute-start | bytes 110600 | tf_op jit(solution)/shard_map/ppermute | solution.py:542
  302.6 5.1 %collective-permute-start.19 = (bf16[1,24,768]{2,1,0:T(8,128)(2,1)S(1)}, bf16[1,24,768]{2,1,0:T(8,128)(2,1)S(1)}, u32[]{:S(2)}, u32[]{:S(2)}) collective-permute-start(bf16[1,24,768]{2,1,0:T(8,128)(2,1)S(1)} %get-tuple-element.114), channel_id=1, source_target_pairs={{0,16},{1,17},{2,18},{3,19},{4,20},{5,21},{6,22},{7,23},{8,24},{9,... | collective-permute-start | bytes 110600 | tf_op jit(solution)/shard_map/ppermute | solution.py:542
  302.6 5.1 %collective-permute-start.18 = (bf16[1,24,768]{2,1,0:T(8,128)(2,1)S(1)}, bf16[1,24,768]{2,1,0:T(8,128)(2,1)S(1)}, u32[]{:S(2)}, u32[]{:S(2)}) collective-permute-start(bf16[1,24,768]{2,1,0:T(8,128)(2,1)S(1)} %get-tuple-element.112), channel_id=1, source_target_pairs={{0,8},{1,9},{2,10},{3,11},{4,12},{5,13},{6,14},{7,15},{8,0},{9,1},... | collective-permute-start | bytes 110600 | tf_op jit(solution)/shard_map/ppermute | solution.py:542
  306.5 38.1 %collective-permute-start.21 = (bf16[16,24,3072]{2,1,0:T(8,128)(2,1)}, bf16[16,24,3072]{2,1,0:T(8,128)(2,1)}, u32[]{:S(2)}, u32[]{:S(2)}) collective-permute-start(bf16[16,24,3072]{2,1,0:T(8,128)(2,1)} %get-tuple-element.55), channel_id=1, source_target_pairs={{0,1},{1,0},{2,3},{3,2},{4,5},{5,4},{6,7},{7,6},{8,9},{9,8},{10,11... | collective-permute-start | bytes 7077896 | tf_op jit(solution)/shard_map/ppermute | solution.py:542
  307.6 44.2 %collective-permute-start.28 = (bf16[16,96,768]{2,1,0:T(8,128)(2,1)}, bf16[16,96,768]{2,1,0:T(8,128)(2,1)}, u32[]{:S(2)}, u32[]{:S(2)}) collective-permute-start(bf16[16,96,768]{2,1,0:T(8,128)(2,1)} %get-tuple-element.59), channel_id=1, source_target_pairs={{0,1},{1,0},{2,3},{3,2},{4,5},{5,4},{6,7},{7,6},{8,9},{9,8},{10,11... | collective-permute-start | bytes 7077896 | tf_op jit(solution)/shard_map/ppermute | solution.py:542
  308.6 9.2 %collective-permute-start.10 = (bf16[4,24,1152]{2,1,0:T(8,128)(2,1)S(1)}, bf16[4,24,1152]{2,1,0:T(8,128)(2,1)S(1)}, u32[]{:S(2)}, u32[]{:S(2)}) collective-permute-start(bf16[4,24,1152]{2,1,0:T(8,128)(2,1)S(1)} %get-tuple-element.99), channel_id=1, source_target_pairs={{0,6},{1,7},{2,4},{3,5},{4,2},{5,3},{6,0},{7,1},{8,14},{9,15},{10,... | collective-permute-start | bytes 663560 | tf_op jit(solution)/shard_map/ppermute | solution.py:542
  310.2 12.3 %collective-permute-start.9 = (bf16[4,24,1152]{2,1,0:T(8,128)(2,1)S(1)}, bf16[4,24,1152]{2,1,0:T(8,128)(2,1)S(1)}, u32[]{:S(2)}, u32[]{:S(2)}) collective-permute-start(bf16[4,24,1152]{2,1,0:T(8,128)(2,1)S(1)} %get-tuple-element.100), channel_id=1, source_target_pairs={{0,4},{1,5},{2,6},{3,7},{4,0},{5,1},{6,2},{7,3},{8,12},{9,13},{10,... | collective-permute-start | bytes 663560 | tf_op jit(solution)/shard_map/ppermute | solution.py:542
  311.4 12.4 %collective-permute-start.8 = (bf16[4,24,1152]{2,1,0:T(8,128)(2,1)S(1)}, bf16[4,24,1152]{2,1,0:T(8,128)(2,1)S(1)}, u32[]{:S(2)}, u32[]{:S(2)}) collective-permute-start(bf16[4,24,1152]{2,1,0:T(8,128)(2,1)S(1)} %get-tuple-element.101), channel_id=1, source_target_pairs={{0,2},{1,3},{2,0},{3,1},{4,6},{5,7},{6,4},{7,5},{8,10},{9,11},{10,... | collective-permute-start | bytes 663560 | tf_op jit(solution)/shard_map/ppermute | solution.py:542
  317.9 9.5 %collective-permute-start.3 = (bf16[4,24,1152]{2,1,0:T(8,128)(2,1)S(1)}, bf16[4,24,1152]{2,1,0:T(8,128)(2,1)S(1)}, u32[]{:S(2)}, u32[]{:S(2)}) collective-permute-start(bf16[4,24,1152]{2,1,0:T(8,128)(2,1)S(1)} %get-tuple-element.95), channel_id=1, source_target_pairs={{0,6},{1,7},{2,4},{3,5},{4,2},{5,3},{6,0},{7,1},{8,14},{9,15},{10,... | collective-permute-start | bytes 663560 | tf_op jit(solution)/shard_map/ppermute | solution.py:542
  322.5 9.2 %collective-permute-start.2 = (bf16[4,24,1152]{2,1,0:T(8,128)(2,1)S(1)}, bf16[4,24,1152]{2,1,0:T(8,128)(2,1)S(1)}, u32[]{:S(2)}, u32[]{:S(2)}) collective-permute-start(bf16[4,24,1152]{2,1,0:T(8,128)(2,1)S(1)} %get-tuple-element.96), channel_id=1, source_target_pairs={{0,4},{1,5},{2,6},{3,7},{4,0},{5,1},{6,2},{7,3},{8,12},{9,13},{10,... | collective-permute-start | bytes 663560 | tf_op jit(solution)/shard_map/ppermute | solution.py:542
  323.8 8.5 %collective-permute-start.1 = (bf16[4,24,1152]{2,1,0:T(8,128)(2,1)S(1)}, bf16[4,24,1152]{2,1,0:T(8,128)(2,1)S(1)}, u32[]{:S(2)}, u32[]{:S(2)}) collective-permute-start(bf16[4,24,1152]{2,1,0:T(8,128)(2,1)S(1)} %get-tuple-element.97), channel_id=1, source_target_pairs={{0,2},{1,3},{2,0},{3,1},{4,6},{5,7},{6,4},{7,5},{8,10},{9,11},{10,... | collective-permute-start | bytes 663560 | tf_op jit(solution)/shard_map/ppermute | solution.py:542
  327.4 7.2 %collective-permute-start.13 = (bf16[1,24,1152]{2,1,0:T(8,128)(2,1)S(1)}, bf16[1,24,1152]{2,1,0:T(8,128)(2,1)S(1)}, u32[]{:S(2)}, u32[]{:S(2)}) collective-permute-start(bf16[1,24,1152]{2,1,0:T(8,128)(2,1)S(1)} %get-tuple-element.110), channel_id=1, source_target_pairs={{0,24},{1,25},{2,26},{3,27},{4,28},{5,29},{6,30},{7,31},{8,16},{9,... | collective-permute-start | bytes 165896 | tf_op jit(solution)/shard_map/ppermute | solution.py:542
  331.7 5.7 %collective-permute-start.12 = (bf16[1,24,1152]{2,1,0:T(8,128)(2,1)S(1)}, bf16[1,24,1152]{2,1,0:T(8,128)(2,1)S(1)}, u32[]{:S(2)}, u32[]{:S(2)}) collective-permute-start(bf16[1,24,1152]{2,1,0:T(8,128)(2,1)S(1)} %get-tuple-element.111), channel_id=1, source_target_pairs={{0,16},{1,17},{2,18},{3,19},{4,20},{5,21},{6,22},{7,23},{8,24},{9,... | collective-permute-start | bytes 165896 | tf_op jit(solution)/shard_map/ppermute | solution.py:542
  332.3 5.4 %collective-permute-start.11 = (bf16[1,24,1152]{2,1,0:T(8,128)(2,1)S(1)}, bf16[1,24,1152]{2,1,0:T(8,128)(2,1)S(1)}, u32[]{:S(2)}, u32[]{:S(2)}) collective-permute-start(bf16[1,24,1152]{2,1,0:T(8,128)(2,1)S(1)} %get-tuple-element.109), channel_id=1, source_target_pairs={{0,8},{1,9},{2,10},{3,11},{4,12},{5,13},{6,14},{7,15},{8,0},{9,1},... | collective-permute-start | bytes 165896 | tf_op jit(solution)/shard_map/ppermute | solution.py:542
  334.6 6.6 %collective-permute-start.6 = (bf16[1,24,1152]{2,1,0:T(8,128)(2,1)S(1)}, bf16[1,24,1152]{2,1,0:T(8,128)(2,1)}, u32[]{:S(2)}, u32[]{:S(2)}) collective-permute-start(bf16[1,24,1152]{2,1,0:T(8,128)(2,1)S(1)} %get-tuple-element.107), channel_id=1, source_target_pairs={{0,24},{1,25},{2,26},{3,27},{4,28},{5,29},{6,30},{7,31},{8,16},{9,... | collective-permute-start | bytes 165896 | tf_op jit(solution)/shard_map/ppermute | solution.py:542
  337.4 5.6 %collective-permute-start.5 = (bf16[1,24,1152]{2,1,0:T(8,128)(2,1)S(1)}, bf16[1,24,1152]{2,1,0:T(8,128)(2,1)}, u32[]{:S(2)}, u32[]{:S(2)}) collective-permute-start(bf16[1,24,1152]{2,1,0:T(8,128)(2,1)S(1)} %get-tuple-element.108), channel_id=1, source_target_pairs={{0,16},{1,17},{2,18},{3,19},{4,20},{5,21},{6,22},{7,23},{8,24},{9,... | collective-permute-start | bytes 165896 | tf_op jit(solution)/shard_map/ppermute | solution.py:542
  337.7 5.7 %collective-permute-start.4 = (bf16[1,24,1152]{2,1,0:T(8,128)(2,1)S(1)}, bf16[1,24,1152]{2,1,0:T(8,128)(2,1)}, u32[]{:S(2)}, u32[]{:S(2)}) collective-permute-start(bf16[1,24,1152]{2,1,0:T(8,128)(2,1)S(1)} %get-tuple-element.106), channel_id=1, source_target_pairs={{0,8},{1,9},{2,10},{3,11},{4,12},{5,13},{6,14},{7,15},{8,0},{9,1},... | collective-permute-start | bytes 165896 | tf_op jit(solution)/shard_map/ppermute | solution.py:542
  347.3 17.3 %collective-permute-start.24 = (bf16[4,24,3072]{2,1,0:T(8,128)(2,1)S(1)}, bf16[4,24,3072]{2,1,0:T(8,128)(2,1)S(1)}, u32[]{:S(2)}, u32[]{:S(2)}) collective-permute-start(bf16[4,24,3072]{2,1,0:T(8,128)(2,1)S(1)} %get-tuple-element.85), channel_id=1, source_target_pairs={{0,6},{1,7},{2,4},{3,5},{4,2},{5,3},{6,0},{7,1},{8,14},{9,15},{10,... | collective-permute-start | bytes 1769480 | tf_op jit(solution)/shard_map/ppermute | solution.py:542
  348.8 28.4 %collective-permute-start.23 = (bf16[4,24,3072]{2,1,0:T(8,128)(2,1)S(1)}, bf16[4,24,3072]{2,1,0:T(8,128)(2,1)S(1)}, u32[]{:S(2)}, u32[]{:S(2)}) collective-permute-start(bf16[4,24,3072]{2,1,0:T(8,128)(2,1)S(1)} %get-tuple-element.86), channel_id=1, source_target_pairs={{0,4},{1,5},{2,6},{3,7},{4,0},{5,1},{6,2},{7,3},{8,12},{9,13},{10,... | collective-permute-start | bytes 1769480 | tf_op jit(solution)/shard_map/ppermute | solution.py:542
  349.9 27.4 %collective-permute-start.22 = (bf16[4,24,3072]{2,1,0:T(8,128)(2,1)S(1)}, bf16[4,24,3072]{2,1,0:T(8,128)(2,1)S(1)}, u32[]{:S(2)}, u32[]{:S(2)}) collective-permute-start(bf16[4,24,3072]{2,1,0:T(8,128)(2,1)S(1)} %get-tuple-element.87), channel_id=1, source_target_pairs={{0,2},{1,3},{2,0},{3,1},{4,6},{5,7},{6,4},{7,5},{8,10},{9,11},{10,... | collective-permute-start | bytes 1769480 | tf_op jit(solution)/shard_map/ppermute | solution.py:542
  354.1 35.8 %collective-permute-start.31 = (bf16[4,96,768]{2,1,0:T(8,128)(2,1)S(1)}, bf16[4,96,768]{2,1,0:T(8,128)(2,1)S(1)}, u32[]{:S(2)}, u32[]{:S(2)}) collective-permute-start(bf16[4,96,768]{2,1,0:T(8,128)(2,1)S(1)} %get-tuple-element.81), channel_id=1, source_target_pairs={{0,6},{1,7},{2,4},{3,5},{4,2},{5,3},{6,0},{7,1},{8,14},{9,15},{10,... | collective-permute-start | bytes 1769480 | tf_op jit(solution)/shard_map/ppermute | solution.py:542
  355.6 45.1 %collective-permute-start.30 = (bf16[4,96,768]{2,1,0:T(8,128)(2,1)S(1)}, bf16[4,96,768]{2,1,0:T(8,128)(2,1)S(1)}, u32[]{:S(2)}, u32[]{:S(2)}) collective-permute-start(bf16[4,96,768]{2,1,0:T(8,128)(2,1)S(1)} %get-tuple-element.82), channel_id=1, source_target_pairs={{0,4},{1,5},{2,6},{3,7},{4,0},{5,1},{6,2},{7,3},{8,12},{9,13},{10,... | collective-permute-start | bytes 1769480 | tf_op jit(solution)/shard_map/ppermute | solution.py:542
  364.6 36.2 %collective-permute-start.29 = (bf16[4,96,768]{2,1,0:T(8,128)(2,1)S(1)}, bf16[4,96,768]{2,1,0:T(8,128)(2,1)S(1)}, u32[]{:S(2)}, u32[]{:S(2)}) collective-permute-start(bf16[4,96,768]{2,1,0:T(8,128)(2,1)S(1)} %get-tuple-element.83), channel_id=1, source_target_pairs={{0,2},{1,3},{2,0},{3,1},{4,6},{5,7},{6,4},{7,5},{8,10},{9,11},{10,... | collective-permute-start | bytes 1769480 | tf_op jit(solution)/shard_map/ppermute | solution.py:542
  377.5 28.0 %copy-start.11 = (f32[24,3072]{1,0:T(8,128)S(1)}, f32[24,3072]{1,0:T(8,128)}, u32[]{:S(2)}) copy-start(f32[24,3072]{1,0:T(8,128)} %param.35) | copy-start | bytes 884740
  377.5 28.0 %copy-start.12 = (f32[24,3072]{1,0:T(8,128)S(1)}, f32[24,3072]{1,0:T(8,128)}, u32[]{:S(2)}) copy-start(f32[24,3072]{1,0:T(8,128)} %param.30) | copy-start | bytes 884740
  377.5 25.4 %collective-permute-start.27 = (bf16[1,24,3072]{2,1,0:T(8,128)(2,1)S(1)}, bf16[1,24,3072]{2,1,0:T(8,128)(2,1)S(1)}, u32[]{:S(2)}, u32[]{:S(2)}) collective-permute-start(bf16[1,24,3072]{2,1,0:T(8,128)(2,1)S(1)} %get-tuple-element.92), channel_id=1, source_target_pairs={{0,24},{1,25},{2,26},{3,27},{4,28},{5,29},{6,30},{7,31},{8,16},{9,... | collective-permute-start | bytes 442376 | tf_op jit(solution)/shard_map/ppermute | solution.py:542
  379.2 26.2 %collective-permute-start.26 = (bf16[1,24,3072]{2,1,0:T(8,128)(2,1)S(1)}, bf16[1,24,3072]{2,1,0:T(8,128)(2,1)S(1)}, u32[]{:S(2)}, u32[]{:S(2)}) collective-permute-start(bf16[1,24,3072]{2,1,0:T(8,128)(2,1)S(1)} %get-tuple-element.93), channel_id=1, source_target_pairs={{0,16},{1,17},{2,18},{3,19},{4,20},{5,21},{6,22},{7,23},{8,24},{9,... | collective-permute-start | bytes 442376 | tf_op jit(solution)/shard_map/ppermute | solution.py:542
  389.9 15.6 %collective-permute-start.25 = (bf16[1,24,3072]{2,1,0:T(8,128)(2,1)S(1)}, bf16[1,24,3072]{2,1,0:T(8,128)(2,1)S(1)}, u32[]{:S(2)}, u32[]{:S(2)}) collective-permute-start(bf16[1,24,3072]{2,1,0:T(8,128)(2,1)S(1)} %get-tuple-element.91), channel_id=1, source_target_pairs={{0,8},{1,9},{2,10},{3,11},{4,12},{5,13},{6,14},{7,15},{8,0},{9,1},... | collective-permute-start | bytes 442376 | tf_op jit(solution)/shard_map/ppermute | solution.py:542
  401.0 8.7 %collective-permute-start.34 = (bf16[1,96,768]{2,1,0:T(8,128)(2,1)S(1)}, bf16[1,96,768]{2,1,0:T(8,128)(2,1)S(1)}, u32[]{:S(2)}, u32[]{:S(2)}) collective-permute-start(bf16[1,96,768]{2,1,0:T(8,128)(2,1)S(1)} %get-tuple-element.89), channel_id=1, source_target_pairs={{0,24},{1,25},{2,26},{3,27},{4,28},{5,29},{6,30},{7,31},{8,16},{9,... | collective-permute-start | bytes 442376 | tf_op jit(solution)/shard_map/ppermute | solution.py:542
  402.3 13.2 %collective-permute-start.33 = (bf16[1,96,768]{2,1,0:T(8,128)(2,1)S(1)}, bf16[1,96,768]{2,1,0:T(8,128)(2,1)S(1)}, u32[]{:S(2)}, u32[]{:S(2)}) collective-permute-start(bf16[1,96,768]{2,1,0:T(8,128)(2,1)S(1)} %get-tuple-element.90), channel_id=1, source_target_pairs={{0,16},{1,17},{2,18},{3,19},{4,20},{5,21},{6,22},{7,23},{8,24},{9,... | collective-permute-start | bytes 442376 | tf_op jit(solution)/shard_map/ppermute | solution.py:542
  402.9 12.6 %collective-permute-start.32 = (bf16[1,96,768]{2,1,0:T(8,128)(2,1)S(1)}, bf16[1,96,768]{2,1,0:T(8,128)(2,1)S(1)}, u32[]{:S(2)}, u32[]{:S(2)}) collective-permute-start(bf16[1,96,768]{2,1,0:T(8,128)(2,1)S(1)} %get-tuple-element.88), channel_id=1, source_target_pairs={{0,8},{1,9},{2,10},{3,11},{4,12},{5,13},{6,14},{7,15},{8,0},{9,1},... | collective-permute-start | bytes 442376 | tf_op jit(solution)/shard_map/ppermute | solution.py:542
  (24 other events, 208.4 us)
Sparse Core Ops, SparseCore 0:
  12.0 106.7 all-gather.1

commit v2 on v1

--- a/solution.py
+++ b/solution.py
@@ -76,8 +76,9 @@
     )(x, gathered, vec)
 
 
-def attend_kernel(len_ref, q_ref, k_ref, v_ref, out_ref, lse_ref):
-    length = len_ref[pl.program_id(0)]
+def attend_kernel(len_ref, q_ref, k_ref, v_ref, *refs, which):
+    out_ref, lse_ref = refs[-2:]
+    length = len_ref[which]
     seq = q_ref.shape[0]
     query = q_ref[...] * jnp.asarray(1.0 / math.sqrt(HEAD), BF)
     keyset = k_ref[...]
@@ -98,39 +99,42 @@
     out_ref[...] = jnp.concatenate(mixed, axis=0).T.astype(BF)
 
 
-def attend_forward(packed, lengths, width):
+def attend_forward(packed, lengths, width, which, filled):
     rows = packed.shape[0]
     batch = lengths.shape[0]
     seq = rows // batch
     pairs = width // LANES
     grid_spec = pltpu.PrefetchScalarGridSpec(
         num_scalar_prefetch=1,
-        grid=(batch, pairs),
+        grid=(pairs,),
         in_specs=[
-            pl.BlockSpec((seq, LANES), lambda b, h, ln: (b, h)),
-            pl.BlockSpec((seq, LANES), lambda b, h, ln: (b, pairs + h)),
-            pl.BlockSpec((seq, LANES), lambda b, h, ln: (b, 2 * pairs + h)),
+            pl.BlockSpec((seq, LANES), lambda h, ln: (which, h)),
+            pl.BlockSpec((seq, LANES), lambda h, ln: (which, pairs + h)),
+            pl.BlockSpec((seq, LANES), lambda h, ln: (which, 2 * pairs + h)),
+        ]
+        + [pl.BlockSpec(memory_space=pl.ANY)] * len(filled),
+        out_specs=[
+            pl.BlockSpec((seq, LANES), lambda h, ln: (which, h)),
+            pl.BlockSpec((1, 2, seq), lambda h, ln: (which * pairs + h, 0, 0)),
         ],
-        out_specs=[
-            pl.BlockSpec((seq, LANES), lambda b, h, ln: (b, h)),
-            pl.BlockSpec((1, 2, seq), lambda b, h, ln: (b * pairs + h, 0, 0)),
-        ],
     )
     return pl.pallas_call(
-        attend_kernel,
+        functools.partial(attend_kernel, which=which),
         grid_spec=grid_spec,
         out_shape=[
             jax.ShapeDtypeStruct((rows, width), BF),
             jax.ShapeDtypeStruct((batch * pairs, 2, seq), F32),
         ],
-        compiler_params=params(2),
-        cost_estimate=cost(16 * rows * seq * width, 8 * rows * width, rows * seq * width // HEAD),
+        input_output_aliases={4 + index: index for index in range(len(filled))},
+        compiler_params=params(1),
+        cost_estimate=cost(16 * seq * seq * width, 8 * seq * width, seq * seq * width // HEAD),
         name="attend_forward",
-    )(lengths, packed, packed, packed)
-
-
-def attend_back_kernel(len_ref, q_ref, k_ref, v_ref, g_ref, lse_ref, out_ref):
-    length = len_ref[pl.program_id(0)]
+    )(lengths, packed, packed, packed, *filled)
+
+
+def attend_back_kernel(len_ref, q_ref, k_ref, v_ref, g_ref, lse_ref, *refs, which):
+    out_ref = refs[-1]
+    length = len_ref[which]
     seq = q_ref.shape[0]
     factor = 1.0 / math.sqrt(HEAD)
     query = q_ref[...] * jnp.asarray(factor, BF)
@@ -160,7 +164,7 @@
     out_ref[2] = grad_v.astype(BF)
 
 
-def attend_backward(packed, lengths, lse, grad_mixed, group):
+def attend_backward(packed, lengths, lse, grad_mixed, group, which, filled):
     rows, width = grad_mixed.shape
     batch = lengths.shape[0]
     seq = rows // batch
@@ -169,28 +173,28 @@
     base = group * here
     grid_spec = pltpu.PrefetchScalarGridSpec(
         num_scalar_prefetch=1,
-        grid=(batch, here),
+        grid=(here,),
         in_specs=[
-            pl.BlockSpec((seq, LANES), lambda b, h, ln: (b, base + h)),
-            pl.BlockSpec((seq, LANES), lambda b, h, ln: (b, pairs + base + h)),
-            pl.BlockSpec((seq, LANES), lambda b, h, ln: (b, 2 * pairs + base + h)),
-            pl.BlockSpec((seq, LANES), lambda b, h, ln: (b, base + h)),
-            pl.BlockSpec((1, 2, seq), lambda b, h, ln: (b * pairs + base + h, 0, 0)),
-        ],
-        out_specs=pl.BlockSpec((3, seq, LANES), lambda b, h, ln: (0, b, h)),
+            pl.BlockSpec((seq, LANES), lambda h, ln: (which, base + h)),
+            pl.BlockSpec((seq, LANES), lambda h, ln: (which, pairs + base + h)),
+            pl.BlockSpec((seq, LANES), lambda h, ln: (which, 2 * pairs + base + h)),
+            pl.BlockSpec((seq, LANES), lambda h, ln: (which, base + h)),
+            pl.BlockSpec((1, 2, seq), lambda h, ln: (which * pairs + base + h, 0, 0)),
+        ]
+        + [pl.BlockSpec(memory_space=pl.ANY)] * len(filled),
+        out_specs=pl.BlockSpec((3, seq, LANES), lambda h, ln: (0, which, h)),
     )
     return pl.pallas_call(
-        attend_back_kernel,
+        functools.partial(attend_back_kernel, which=which),
         grid_spec=grid_spec,
         out_shape=jax.ShapeDtypeStruct((3, rows, here * LANES), BF),
-        compiler_params=params(2),
+        input_output_aliases={6 + index: index for index in range(len(filled))},
+        compiler_params=params(1),
         cost_estimate=cost(
-            40 * rows * seq * here * LANES,
-            14 * rows * here * LANES,
-            rows * seq * here * 2,
+            40 * seq * seq * here * LANES, 14 * seq * here * LANES, seq * seq * here * 2
         ),
         name="attend_backward",
-    )(lengths, packed, packed, packed, grad_mixed, lse)
+    )(lengths, packed, packed, packed, grad_mixed, lse, *filled)
 
 
 def norm_forward(resid, gain, shift):
@@ -317,8 +321,8 @@
             thin,
             thin,
             thin,
-            pl.BlockSpec((width, width), lambda i, ln: (0, 3), pipeline_mode=once),
-            pl.BlockSpec((width, inner), lambda i, ln: (0, 1), pipeline_mode=once),
+            pl.BlockSpec((width, width), lambda i, ln: (0, inner // width), pipeline_mode=once),
+            pl.BlockSpec((width, inner), lambda i, ln: (0, 0), pipeline_mode=once),
             pl.BlockSpec((inner, width), lambda i, ln: (0, 0), pipeline_mode=once),
             pl.BlockSpec(vec.shape, lambda i, ln: (0, 0)),
         ],
@@ -428,6 +432,61 @@
     )(source, left, right)
 
 
+def joint_kernel(src_ref, left_ref, last_left_ref, right_ref, last_right_ref, keep_ref, send_ref, acc_ref):
+    half, piece, _ = keep_ref.shape
+    last = pl.num_programs(0) - 1
+
+    @pl.when(pl.program_id(0) < last)
+    def _():
+        acc_ref[...] = dot(left_ref[...], right_ref[...], TN)
+
+    @pl.when(pl.program_id(0) == last)
+    def _():
+        acc_ref[...] = dot(last_left_ref[...], last_right_ref[...], TN)
+
+    for slot in range(half):
+        for ref, offset in ((keep_ref, 0), (send_ref, half)):
+            begin = pl.multiple_of(src_ref[offset + slot] * piece, 8)
+            ref[slot] = acc_ref[pl.ds(begin, piece), :].astype(BF)
+
+
+def joint_gradient(left, right, last_left, last_right, source):
+    rows, tall = left.shape
+    devices = source.shape[0]
+    piece = tall // devices
+    tile = last_right.shape[1]
+    wide = right.shape[1] // tile
+    if piece % 8:
+        one = weight_gradient(left, right, source)
+        two = weight_gradient(last_left, last_right, source)
+        return [jnp.concatenate(both, axis=2) for both in zip(one, two)]
+    full = pl.BlockSpec((rows, tall), lambda j, s: (0, 0))
+    block = pl.BlockSpec((devices // 2, piece, tile), lambda j, s: (0, 0, j))
+    shape = jax.ShapeDtypeStruct((devices // 2, piece, (wide + 1) * tile), BF)
+    grid_spec = pltpu.PrefetchScalarGridSpec(
+        num_scalar_prefetch=1,
+        grid=(wide + 1,),
+        in_specs=[
+            full,
+            full,
+            pl.BlockSpec((rows, tile), lambda j, s: (0, jnp.minimum(j, wide - 1))),
+            pl.BlockSpec((rows, tile), lambda j, s: (0, 0)),
+        ],
+        out_specs=[block, block],
+        scratch_shapes=[pltpu.VMEM((tall, tile), F32)],
+    )
+    return pl.pallas_call(
+        joint_kernel,
+        grid_spec=grid_spec,
+        out_shape=[shape, shape],
+        compiler_params=params(1),
+        cost_estimate=cost(
+            2 * rows * tall * tile * (wide + 1), 2 * (tall + rows) * tile * (wide + 1) + 4 * rows * tall
+        ),
+        name="joint_gradient",
+    )(source, left, last_left, right, last_right)
+
+
 def tall_kernel(slot_ref, left_ref, right_ref, keep_ref, send_ref, acc_ref):
     step = pl.program_id(0)
     half, piece, _ = keep_ref.shape
@@ -520,46 +579,140 @@
     )(resid, gathered, *grads)
 
 
-def stages(devices):
-    bits = devices.bit_length() - 1
-    found = [(0, 1)]
-    at = 1
-    while at < bits:
-        count = min(2, bits - at)
-        found.append((at, count))
-        at += count
-    return found
-
-
-def relative_order(devices):
-    order = [0]
-    for at, count in stages(devices):
-        order = [base | (value << at) for base in order for value in range(1 << count)]
-    return order
-
-
 def swap(value, mask, devices):
     return lax.ppermute(value, "dp", [(index, index ^ mask) for index in range(devices)])
 
 
-def sum_of(terms, begin, size):
-    total = terms[0][begin : begin + size].astype(F32)
-    for term in terms[1:]:
-        total = total + term[begin : begin + size].astype(F32)
-    return total
-
-
-def reduce_to_owner(keep, send, devices):
-    terms = [keep, swap(send, 1, devices)]
-    for at, count in stages(devices)[1:]:
-        size = terms[0].shape[0] >> count
-        parts = [
-            sum_of(terms, value * size, size).astype(keep.dtype) for value in range(1 << count)
+def hold(value, *others):
+    return lax.optimization_barrier((value, others))[0]
+
+
+def masks_of(bits):
+    found = [0]
+    for bit in bits:
+        found = found + [mask | (1 << bit) for mask in found]
+    return found
+
+
+def relative_order(order):
+    relative = [0]
+    for bits in order:
+        relative = [base | mask for base in relative for mask in masks_of(bits)]
+    return relative
+
+
+def stage_orders(devices):
+    bits = devices.bit_length() - 1
+    rest = [(bit,) for bit in range(3, bits)]
+    low = [(bit,) for bit in range(min(3, bits))]
+    by_x = low + rest
+    by_y = low[:1] + low[1:][::-1] + rest
+    both = low[:1] + ([tuple(range(1, min(3, bits)))] if bits > 1 else []) + rest
+    return by_x, by_y, both
+
+
+class Reduce:
+    def __init__(self, keep, send, order, devices):
+        self.order, self.devices, self.at = order, devices, 0
+        self.parts = [keep, send]
+        self.terms = None
+
+    def send(self):
+        masks = masks_of(self.order[self.at])
+        self.terms = [self.parts[0]] + [
+            swap(part, mask, self.devices) for part, mask in zip(self.parts[1:], masks[1:])
         ]
-        terms = [parts[0]] + [
-            swap(parts[value], value << at, devices) for value in range(1, 1 << count)
-        ]
-    return sum_of(terms, 0, 1)[0]
+        self.at += 1
+        return self
+
+    def total(self, begin, size):
+        result = self.terms[0][begin : begin + size].astype(F32)
+        for term in self.terms[1:]:
+            result = result + term[begin : begin + size].astype(F32)
+        return result
+
+    def join(self):
+        ways = len(masks_of(self.order[self.at]))
+        size = self.terms[0].shape[0] // ways
+        self.parts = [self.total(way * size, size).astype(BF) for way in range(ways)]
+        return self
+
+    def finish(self):
+        if self.terms is None:
+            self.send()
+        while self.at < len(self.order):
+            self.join().send()
+        return self.total(0, 1)[0]
+
+
+class Gather:
+    def __init__(self, shard, order, devices):
+        self.order, self.devices, self.at = order, devices, 0
+        self.held = shard[None]
+        self.taken = None
+
+    def send(self):
+        masks = masks_of(self.order[self.at])
+        self.taken = [swap(self.held, mask, self.devices) for mask in masks[1:]]
+        self.at += 1
+        return self
+
+    def join(self):
+        self.held = jnp.concatenate([self.held] + self.taken, axis=0)
+        return self
+
+
+def lay_pairs_kernel(index_ref, odd_ref, held_ref, taken_ref, out_ref):
+    half, piece, _ = held_ref.shape
+    odd = odd_ref[0] == 1
+    for slot in range(half):
+        mine = held_ref[slot].astype(F32)
+        other = taken_ref[slot].astype(F32)
+        both = jnp.concatenate(
+            [jnp.where(odd, other, mine), jnp.where(odd, mine, other)], axis=0
+        ).astype(BF)
+        begin = pl.multiple_of((index_ref[slot] // 2) * (2 * piece), 16)
+        out_ref[pl.ds(begin, 2 * piece), :] = both
+
+
+def lay_kernel(index_ref, odd_ref, held_ref, taken_ref, out_ref):
+    half, piece, _ = held_ref.shape
+    for slot in range(half):
+        for ref, flip in ((held_ref, 0), (taken_ref, 1)):
+            begin = pl.multiple_of((index_ref[slot] ^ flip) * piece, 16)
+            out_ref[pl.ds(begin, piece), :] = ref[slot]
+
+
+def lay_out(gather, me):
+    held, taken = gather.held, gather.taken[0]
+    half, piece, columns = held.shape
+    devices = 2 * half
+    relative = [0]
+    for bits in gather.order[:-1]:
+        relative = [base | mask for mask in masks_of(bits) for base in relative]
+    index = jnp.asarray(relative, jnp.int32) ^ me
+    if piece % 8:
+        where = [0] * devices
+        for slot, value in enumerate(relative):
+            where[value], where[value ^ 1] = slot, half + slot
+        natural = jnp.take(jnp.asarray(where, jnp.int32), jnp.arange(devices, dtype=jnp.int32) ^ me)
+        both = jnp.concatenate([held, taken], axis=0)
+        return jnp.take(both, natural, axis=0).reshape(devices * piece, columns)
+    whole = pl.BlockSpec(held.shape, lambda i, *s: (0, 0, 0))
+    grid_spec = pltpu.PrefetchScalarGridSpec(
+        num_scalar_prefetch=2,
+        grid=(1,),
+        in_specs=[whole, whole],
+        out_specs=pl.BlockSpec((devices * piece, columns), lambda i, *s: (0, 0)),
+    )
+    return pl.pallas_call(
+        lay_pairs_kernel if piece % 16 else lay_kernel,
+        grid_spec=grid_spec,
+        out_shape=jax.ShapeDtypeStruct((devices * piece, columns), BF),
+        compiler_params=params(1),
+        cost_estimate=cost(devices * piece * columns, 4 * devices * piece * columns),
+        name="lay_out",
+    )(index, (me & 1).reshape(1), held, taken)
 
 
 def adamw(weight, grad, first, second, decay, rate):
@@ -596,58 +749,115 @@
     width = hidden_in.shape[1]
     piece = proj_qkv.shape[0]
     inner = proj_up.shape[1]
-    ratio = inner // width
-    relative = jnp.asarray(relative_order(devices), jnp.int32)
-    source = relative ^ me
+    batch = lengths.shape[0]
+    by_x, by_y, both = stage_orders(devices)
+    outward = both[::-1]
+
+    def source_of(order):
+        return jnp.asarray(relative_order(order), jnp.int32) ^ me
+
     slots = [0] * devices
-    for slot, value in enumerate(relative_order(devices)):
+    for slot, value in enumerate(relative_order(by_x)):
         slots[value] = slot
     slot_of = jnp.take(jnp.asarray(slots, jnp.int32), jnp.arange(devices, dtype=jnp.int32) ^ me)
 
     entries = vectors.shape[0] // piece
+    wide = lax.all_gather(
+        jnp.concatenate([proj_up.astype(BF), proj_attn.astype(BF)], axis=1), "dp", axis=0, tiled=True
+    )
     shard = jnp.concatenate(
         [
             proj_qkv.astype(BF),
-            proj_attn.astype(BF),
-            proj_up.astype(BF),
-            proj_down.astype(BF).reshape(ratio, piece, width).transpose(1, 0, 2).reshape(piece, inner),
             jnp.pad(vectors.astype(BF).reshape(piece, entries), ((0, 0), (0, LANES - entries))),
         ],
         axis=1,
     )
-    gathered = lax.all_gather(shard, "dp", axis=0, tiled=True)
-    base = 4 * width + inner
-    w_down = (
-        gathered[:, base : base + inner]
-        .reshape(devices, piece, ratio, width)
-        .transpose(0, 2, 1, 3)
-        .reshape(inner, width)
-    )
-    vec = gathered[:, base + inner : base + inner + entries].astype(F32).reshape(-1, width)
+    qkv = Gather(shard, outward, devices)
+    down = Gather(proj_down.astype(BF), outward, devices)
+    for _ in range(len(outward) - 2):
+        qkv.send().join()
+    down.held = hold(down.held, qkv.held)
+    qkv.send()
+    for _ in range(len(outward) - 2):
+        down.send().join()
+    qkv.join()
+    down.held = hold(down.held, qkv.held)
+    qkv.held = hold(qkv.held, down.held)
+    down.send()
+    qkv.send()
+    gathered = lay_out(qkv, me)
+    vec = gathered[:, 3 * width : 3 * width + entries].astype(F32).reshape(-1, width)
 
     packed = project_qkv(hidden_in, gathered, vec)
-    mixed, lse = attend_forward(packed, lengths, width)
+    filled = ()
+    for which in range(batch):
+        filled = attend_forward(packed, lengths, width, which, filled)
+        if which == 0:
+            down.taken = [hold(value, filled) for value in down.taken]
+            down.join()
+            packed = hold(packed, down.held)
+            down.send()
+    mixed, lse = filled
+    w_down = lay_out(down, me)
     output, first_low, active, grad_upper, grad_branch, grad_attn, grad_mixed, grad_one, sums = middle(
-        hidden_in, mixed, cotangent, lengths, gathered, w_down, vec
-    )
-    total_down = reduce_to_owner(*tall_gradient(active, grad_branch, source, slot_of), devices)
-    total_up = reduce_to_owner(*weight_gradient(first_low, grad_upper, source), devices)
-    total_attn = reduce_to_owner(*weight_gradient(mixed, grad_attn, source), devices)
-    totals = []
-    parts = []
-    part_sums = []
+        hidden_in, mixed, cotangent, lengths, wide, w_down, vec
+    )
+
+    total = Reduce(*tall_gradient(active, grad_branch, source_of(by_x), slot_of), by_x, devices)
+    total.send()
+    grad_upper = hold(grad_upper, total.parts)
+    joint = Reduce(
+        *joint_gradient(first_low, grad_upper, mixed, grad_attn, source_of(by_y)), by_y, devices
+    )
+    total.join()
+    grad_mixed = hold(grad_mixed, total.parts, joint.parts)
+    total.send()
+    joint.send()
+    parts, part_sums, queue = [], [], []
     for group in range(GROUPS):
-        part = attend_backward(packed, lengths, lse, grad_mixed, group)
-        keep, send, part_sum = weight_gradient(hidden_in, part, source, sums=True)
-        totals.append(reduce_to_owner(keep, send, devices).reshape(piece, 3, -1))
-        parts.append(part)
+        part = ()
+        for which in range(batch):
+            part = (attend_backward(packed, lengths, lse, grad_mixed, group, which, part),)
+            if group == 0 and which == 0:
+                joint.join()
+                grad_mixed = hold(grad_mixed, joint.parts)
+                joint.send()
+            if group == 1 and which == 0:
+                queue[0].join()
+                grad_mixed = hold(grad_mixed, queue[0].parts)
+                queue[0].send()
+        if group == GROUPS - 1:
+            joint.join()
+            part = (hold(part[0], joint.parts),)
+            joint.send()
+        keep, send, part_sum = weight_gradient(hidden_in, part[0], source_of(both), sums=True)
+        parts.append(part[0])
         part_sums.append(part_sum)
-    total_qkv = jnp.concatenate(totals, axis=2).reshape(piece, 3 * width)
+        if group == 0:
+            queue.append(Reduce(keep, send, both, devices))
+            total.join()
+            grad_mixed = hold(grad_mixed, total.parts, keep)
+            total.send()
+            queue[0].send()
     part_sums = jnp.concatenate(part_sums, axis=2)
     vector_sums = jnp.concatenate([part_sums[0, :1], part_sums[2, :1], sums[2:]], axis=0)
-    ordered = jnp.take(vector_sums.reshape(devices, 1, -1), source, axis=0)
-    total_vectors = reduce_to_owner(ordered[: devices // 2], ordered[devices // 2 :], devices)[0]
+    ordered = jnp.take(vector_sums.reshape(devices, piece, entries), source_of(both), axis=0)
+    ordered = jnp.pad(ordered.astype(BF), ((0, 0), (0, 0), (0, LANES - entries)))
+    keep = jnp.concatenate([keep, ordered[: devices // 2]], axis=2)
+    send = jnp.concatenate([send, ordered[devices // 2 :]], axis=2)
+    queue.append(Reduce(keep, send, both, devices).send())
+    grad_one = hold(grad_one, queue[1].parts)
     input_grad = input_gradient(grad_one, gathered, parts)
+
+    total_qkv = [chain.finish() for chain in queue]
+    total_vectors = total_qkv[1][:, 3 * width // GROUPS : 3 * width // GROUPS + entries].reshape(-1)
+    here = width // GROUPS
+    total_qkv = jnp.concatenate(
+        [part[:, at * here : (at + 1) * here] for at in range(3) for part in total_qkv], axis=1
+    )
+    total_wide = joint.finish()
+    total_up, total_attn = total_wide[:, :inner], total_wide[:, inner:]
+    total_down = total.finish()
 
     m_qkv, v_qkv, w_qkv = adamw(proj_qkv, total_qkv, first_qkv, second_qkv, WEIGHT_DECAY, LEARN_RATE)
     m_attn, v_attn, w_attn = adamw(

time: 425 us -> 360 us (0.85)
  waiting for transfers between devices: 175 us -> 110 us
  Pallas kernels: 140 us -> 160 us
  starting transfers between devices: 53.6 us -> 41 us
  local copies, waits for them, and re-layouts: 23.4 us -> 12.5 us
  other arithmetic: 17.1 us -> 21.7 us
    all_gather x1, waiting for transfers between devices: 106 us -> 0.01 us  [on_device(): lax.all_gather(jnp.concatenate([proj_up.astype(BF), proj_attn.astype(BF)]...]
    ppermute x42 -> x34, waiting for transfers between devices: 69.2 us -> 110 us  [swap(): lax.ppermute(value, 'dp', [(index, index ^ mask) for index in range(devic...]
    pallas_call x3 -> x9, Pallas kernels: 50.7 us -> 81.9 us  [the longest x4 36.2 us: attend_backward(): pl.pallas_call(functools.partial(attend_back_kernel, which=which), grid_s...]
    pallas_call x4 -> x2, Pallas kernels: 28.5 us -> 13.5 us  [weight_gradient(): pl.pallas_call(functools.partial(weight_kernel, sums=sums), grid_spec=gri...]
    ppermute x42 -> x34, starting transfers between devices: 53.6 us -> 41 us  [swap(): lax.ppermute(value, 'dp', [(index, index ^ mask) for index in range(devic...]
    reshape x4 -> x3, local copies, waits for them, and re-layouts: 10.8 us -> 1.39 us  [the longest x1 0.86 us: on_device(): gathered[:, 3 * width:3 * width + entries].astype(F32).reshape(-1, width)]
    unnamed x62 -> x73, local copies, waits for them, and re-layouts: 0.98 us -> 6.83 us
    transpose x1 -> x0, local copies, waits for them, and re-layouts: 5.35 us -> none  [on_device(): w_down = gathered[:, base:base + inner].reshape(devices, piece, ratio, wi...]
  transfers between devices with their start and end apart: 43 -> 35, of which waited for: 19 -> 15; matrix products, arithmetic and copies ran while one was open for 3% -> 8% of each run, Pallas kernels for 10% -> 31%
where the time goes in v2:
time: 360 us; the launch traced here: 359 us
  Pallas kernels  160 us (44%)
  waiting for transfers between devices  110 us (31%)
  starting transfers between devices  41 us (11%)
  other arithmetic  21.7 us (6%)
  between operations  14.6 us (4%)
  local copies, waits for them, and re-layouts  12.5 us (3%)
    ppermute x34, waiting for transfers between devices, swap(): lax.ppermute(value, 'dp', [(index, index ^ mask) for index in range(devic...  110 us
    ppermute x34, starting transfers between devices, swap(): lax.ppermute(value, 'dp', [(index, index ^ mask) for index in range(devic...  41 us
    pallas_call x4, Pallas kernels, attend_backward(): pl.pallas_call(functools.partial(attend_back_kernel, which=which), grid_s...  36.2 us
    pallas_call x1, Pallas kernels, middle(): pl.pallas_call(functools.partial(middle_kernel, seq=seq), grid_spec=grid_...  35.7 us
    pallas_call x2, Pallas kernels, attend_forward(): pl.pallas_call(functools.partial(attend_kernel, which=which), grid_spec=g...  21.7 us
    pallas_call x2, Pallas kernels, weight_gradient(): pl.pallas_call(functools.partial(weight_kernel, sums=sums), grid_spec=gri...  13.5 us
    pallas_call x1, Pallas kernels, joint_gradient(): pl.pallas_call(joint_kernel, grid_spec=grid_spec, out_shape=[shape, shape...  13 us
    pallas_call x1, Pallas kernels, tall_gradient(): pl.pallas_call(tall_kernel, grid_spec=grid_spec, out_shape=[shape, shape]...  11.5 us
  transfers between devices with their start and end apart: 35, of which 15 were waited for; matrix products, arithmetic and copies ran while one was open for 8% of the time, Pallas kernels for 31%

profile of v2, /device:TPU:0, one launch (start us, length us, event | category | flops | bytes accessed | tf_op | source)
XLA Modules:
  0.0 359.3 jit_solution(4664039187494647370)
XLA Ops:
  11.6 4.1 %collective-permute-start = (bf16[1,24,2432]{2,1,0:T(8,128)(2,1)S(1)}, bf16[1,24,2432]{2,1,0:T(8,128)(2,1)S(1)}, u32[]{:S(2)}, u32[]{:S(2)}) collective-permute-start(bf16[1,24,2432]{2,1,0:T(8,128)(2,1)S(1)} %fusion.10), channel_id=1, source_target_pairs={{0,16},{1,17},{2,18},{3,19},{4,20},{5,21},{6,22},{7,23},{8,24},{9,... | collective-permute-start | bytes 350216 | tf_op jit(solution)/shard_map/ppermute | solution.py:583
  16.4 5.0 %collective-permute-done = bf16[1,24,2432]{2,1,0:T(8,128)(2,1)S(1)} collective-permute-done((bf16[1,24,2432]{2,1,0:T(8,128)(2,1)S(1)}, bf16[1,24,2432]{2,1,0:T(8,128)(2,1)S(1)}, u32[]{:S(2)}, u32[]{:S(2)}) %collective-permute-start) | collective-permute-done | bytes 116768 | tf_op jit(solution)/shard_map/ppermute | solution.py:583
  22.3 7.7 %collective-permute-done.1 = bf16[2,24,2432]{2,1,0:T(8,128)(2,1)S(1)} collective-permute-done((bf16[2,24,2432]{2,1,0:T(8,128)(2,1)S(1)}, bf16[2,24,2432]{2,1,0:T(8,128)(2,1)S(1)}, u32[]{:S(2)}, u32[]{:S(2)}) %collective-permute-start.1) | collective-permute-done | bytes 233504 | tf_op jit(solution)/shard_map/ppermute | solution.py:583
  30.1 4.4 %collective-permute-start.5 = (bf16[1,96,768]{2,1,0:T(8,128)(2,1)S(1)}, bf16[1,96,768]{2,1,0:T(8,128)(2,1)S(1)}, u32[]{:S(2)}, u32[]{:S(2)}) collective-permute-start(bf16[1,96,768]{2,1,0:T(8,128)(2,1)S(1)} %convert_bitcast_fusion), channel_id=1, source_target_pairs={{0,16},{1,17},{2,18},{3,19},{4,20},{5,21},{6,22},{7,23},{8,24},{9,... | collective-permute-start | bytes 442376 | tf_op jit(solution)/shard_map/ppermute | solution.py:583
  35.2 1.5 collective-permute-start.2
  36.7 1.6 collective-permute-start.3
  38.7 2.7 collective-permute-done.5
  42.3 11.7 %collective-permute-done.6 = bf16[2,96,768]{2,1,0:T(8,128)(2,1)S(1)} collective-permute-done((bf16[2,96,768]{2,1,0:T(8,128)(2,1)S(1)}, bf16[2,96,768]{2,1,0:T(8,128)(2,1)S(1)}, u32[]{:S(2)}, u32[]{:S(2)}) %collective-permute-start.6) | collective-permute-done | bytes 294944 | tf_op jit(solution)/shard_map/ppermute | solution.py:583
  55.7 7.1 %collective-permute-done.4 = bf16[4,24,2432]{2,1,0:T(8,128)(2,1)S(1)} collective-permute-done((bf16[4,24,2432]{2,1,0:T(8,128)(2,1)S(1)}, bf16[4,24,2432]{2,1,0:T(8,128)(2,1)S(1)}, u32[]{:S(2)}, u32[]{:S(2)}) %collective-permute-start.4) | collective-permute-done | bytes 466976 | tf_op jit(solution)/shard_map/ppermute | solution.py:583
  64.2 1.3 collective-permute-start.10
  65.5 1.9 collective-permute-start.9
  67.7 1.9 collective-permute-done.7.taken_ref
  69.6 5.4 %lay_out.2.w_ref = bf16[768,2432]{1,0:T(8,128)(2,1)} custom-call(s32[16]{0:T(128)} %broadcast_xor_fusion.1.index_ref, s32[1]{0:T(128)} %bitcast.odd_ref, bf16[16,24,2432]{2,1,0:T(8,128)(2,1)} %constant_dynamic-update-slice_fusion.held_ref, bf16[16,24,2432]{2,1,0:T(8,128)(2,1)} %collective-permute-done.7.taken_ref), custom_call_target="tpu_custom_call" | custom-call | flops 1867776 | bytes 7471104 | tf_op jit(solution)/shard_map/lay_out/pallas_call | solution.py:708
  76.9 7.8 %project_qkv.1.q_ref.k_ref.v_ref = bf16[1024,2304]{1,0:T(8,128)(2,1)} custom-call(bf16[1024,768]{1,0:T(8,128)(2,1)} %left_ref.3, bf16[768,2432]{1,0:T(8,128)(2,1)} %lay_out.2.w_ref, f32[12,768]{1,0:T(8,128)} %reshape.85.vec_ref), custom_call_target="tpu_custom_call" | custom-call | flops 3623878656 | bytes 9830400 | tf_op jit(solution)/shard_map/project_qkv/pallas_call | solution.py:63
  84.6 10.8 %attend_forward.2 = (bf16[1024,768]{1,0:T(8,128)(2,1)}, f32[12,2,512]{2,1,0:T(2,128)}) custom-call(s32[2]{0:T(128)} %len_ref.13, bf16[1024,2304]{1,0:T(8,128)(2,1)} %project_qkv.1.q_ref.k_ref.v_ref, bf16[1024,2304]{1,0:T(8,128)(2,1)} %project_qkv.1.q_ref.k_ref.v_ref, bf16[1024,2304]{1,0:T(8,128)(2,1)} %project_qkv.1.q_ref.k_ref.v_ref), custom_call_target="tpu_custom_call" | custom-call | flops 3221225472 | bytes 3145728 | tf_op jit(solution)/shard_map/attend_forward/pallas_call | solution.py:121
  95.5 7.2 %collective-permute-done.9 = bf16[4,96,768]{2,1,0:T(8,128)(2,1)} collective-permute-done((bf16[4,96,768]{2,1,0:T(8,128)(2,1)S(1)}, bf16[4,96,768]{2,1,0:T(8,128)(2,1)}, u32[]{:S(2)}, u32[]{:S(2)}) %collective-permute-start.9) | collective-permute-done | bytes 589856 | tf_op jit(solution)/shard_map/ppermute | solution.py:583
  107.4 10.9 %attend_forward.3 = (bf16[1024,768]{1,0:T(8,128)(2,1)}, f32[12,2,512]{2,1,0:T(2,128)}) custom-call(s32[2]{0:T(128)} %len_ref.13, bf16[1024,2304]{1,0:T(8,128)(2,1)} %project_qkv.1.q_ref.k_ref.v_ref, bf16[1024,2304]{1,0:T(8,128)(2,1)} %project_qkv.1.q_ref.k_ref.v_ref, ...), custom_call_target="tpu_custom_call", output_to_operand_aliasing={{0}: (4, {}), {1}: (5, {})} | custom-call | flops 3221225472 | bytes 3145728 | tf_op jit(solution)/shard_map/attend_forward/pallas_call | solution.py:121
  118.3 5.5 %lay_out.3.w_down = bf16[3072,768]{1,0:T(8,128)(2,1)} custom-call(s32[16]{0:T(128)} %broadcast_xor_fusion.1.index_ref, s32[1]{0:T(128)} %bitcast.odd_ref, bf16[16,96,768]{2,1,0:T(8,128)(2,1)} %copy-done.1, bf16[16,96,768]{2,1,0:T(8,128)(2,1)} %collective-permute-done.11.taken_ref), custom_call_target="tpu_custom_call" | custom-call | flops 2359296 | bytes 9437184 | tf_op jit(solution)/shard_map/lay_out/pallas_call | solution.py:708
  123.8 35.7 %middle.1 = (bf16[1024,768]{1,0:T(8,128)(2,1)}, bf16[1024,768]{1,0:T(8,128)(2,1)}, bf16[1024,3072]{1,0:T(8,128)(2,1)}, bf16[1024,3072]{1,0:T(8,128)(2,1)}, bf16[...) custom-call(s32[2]{0:T(128)} %len_ref.13, ...), custom_call_target="tpu_custom_call" | custom-call | flops 21743271936 | bytes 37748736 | tf_op jit(solution)/shard_map/middle/pallas_call | solution.py:344
  159.4 11.5 %tall_gradient.1 = (bf16[16,96,768]{2,1,0:T(8,128)(2,1)}, bf16[16,96,768]{2,1,0:T(8,128)(2,1)}) custom-call(s32[32]{0:T(128)} %get-tuple-element.136.slot_ref, bf16[1024,3072]{1,0:T(8,128)(2,1)} %get-tuple-element.67.left_ref, bf16[1024,768]{1,0:T(8,128)(2,1)} %get-tuple-element.68.right_ref), custom_call_target="tpu_custom_call" | custom-call | flops 4831838208 | bytes 12582912 | tf_op jit(solution)/shard_map/tall_gradient/pallas_call | solution.py:543
  171.0 13.0 %joint_gradient.1 = (bf16[16,24,3840]{2,1,0:T(8,128)(2,1)}, bf16[16,24,3840]{2,1,0:T(8,128)(2,1)}) custom-call(s32[32]{0:T(128)} %get-tuple-element.137.src_ref, bf16[1024,768]{1,0:T(8,128)(2,1)} %get-tuple-element.71.left_ref, bf16[1024,768]{1,0:T(8,128)(2,1)} %get-tuple-element.63.mixed_ref.last_left_ref, bf16[1024,3072]{1,0:T(8,128)(2,1)} %get-tuple-element.73.right_ref, ...), custom_call_target="tpu_custom_call" | custom-call | flops 6039797760 | bytes 16908288 | tf_op jit(solution)/shard_map/joint_gradient/pallas_call | solution.py:478
  184.5 1.7 add_convert_fusion.2
  186.2 4.9 %collective-permute-start.14 = (bf16[8,96,768]{2,1,0:T(8,128)(2,1)}, bf16[8,96,768]{2,1,0:T(8,128)(2,1)S(1)}, u32[]{:S(2)}, u32[]{:S(2)}) collective-permute-start(bf16[8,96,768]{2,1,0:T(8,128)(2,1)} %get-tuple-element.110), channel_id=1, source_target_pairs={{0,2},{1,3},{2,0},{3,1},{4,6},{5,7},{6,4},{7,5},{8,10},{9,11},{10,... | collective-permute-start | bytes 3538952 | tf_op jit(solution)/shard_map/ppermute | solution.py:583
  191.1 9.1 %attend_backward.4.refs_0_ = bf16[3,1024,384]{2,1,0:T(8,128)(2,1)} custom-call(s32[2]{0:T(128)} %len_ref.13, bf16[1024,2304]{1,0:T(8,128)(2,1)} %project_qkv.1.q_ref.k_ref.v_ref, bf16[1024,2304]{1,0:T(8,128)(2,1)} %project_qkv.1.q_ref.k_ref.v_ref, bf16[1024,2304]{1,0:T(8,128)(2,1)} %project_qkv.1.q_ref.k_ref.v_ref, ...), custom_call_target="tpu_custom_call" | custom-call | flops 4026531840 | bytes 2752512 | tf_op jit(solution)/shard_map/attend_backward/pallas_call | solution.py:187
  200.2 2.5 add_convert_fusion
  202.7 9.0 %attend_backward.5.right_ref.refs_0_ = bf16[3,1024,384]{2,1,0:T(8,128)(2,1)} custom-call(s32[2]{0:T(128)} %len_ref.13, bf16[1024,2304]{1,0:T(8,128)(2,1)} %project_qkv.1.q_ref.k_ref.v_ref, bf16[1024,2304]{1,0:T(8,128)(2,1)} %project_qkv.1.q_ref.k_ref.v_ref, bf16[1024,2304]{1,0:T(8,128)(2,1)} %project_qkv.1.q_ref.k_ref.v_ref, ...), custom_call_target="tpu_custom_call", output_to_operand_aliasing={{}: (6, {})} | custom-call | flops 4026531840 | bytes 2752512 | tf_op jit(solution)/shard_map/attend_backward/pallas_call | solution.py:187
  211.7 6.8 %weight_gradient.2 = (bf16[16,24,1152]{2,1,0:T(8,128)(2,1)}, bf16[16,24,1152]{2,1,0:T(8,128)(2,1)}, f32[3,8,384]{2,1,0:T(8,128)}) custom-call(s32[32]{0:T(128)} %get-tuple-element.137.src_ref, bf16[1024,768]{1,0:T(8,128)(2,1)} %left_ref.3, bf16[3,1024,384]{2,1,0:T(8,128)(2,1)} %attend_backward.5.right_ref.refs_0_), custom_call_target="tpu_custom_call" | custom-call | flops 1811939328 | bytes 5701632 | tf_op jit(solution)/shard_map/weight_gradient/pallas_call | solution.py:425
  221.7 1.5 collective-permute-start.31
  224.3 2.7 collective-permute-start.19
  227.0 9.2 %attend_backward.6.refs_0_ = bf16[3,1024,384]{2,1,0:T(8,128)(2,1)} custom-call(s32[2]{0:T(128)} %len_ref.13, bf16[1024,2304]{1,0:T(8,128)(2,1)} %project_qkv.1.q_ref.k_ref.v_ref, bf16[1024,2304]{1,0:T(8,128)(2,1)} %project_qkv.1.q_ref.k_ref.v_ref, bf16[1024,2304]{1,0:T(8,128)(2,1)} %project_qkv.1.q_ref.k_ref.v_ref, ...), custom_call_target="tpu_custom_call" | custom-call | flops 4026531840 | bytes 2752512 | tf_op jit(solution)/shard_map/attend_backward/pallas_call | solution.py:187
  236.1 39.8 %collective-permute-done.18 = bf16[4,24,1152]{2,1,0:T(8,128)(2,1)S(1)} collective-permute-done((bf16[4,24,1152]{2,1,0:T(8,128)(2,1)S(1)}, bf16[4,24,1152]{2,1,0:T(8,128)(2,1)S(1)}, u32[]{:S(2)}, u32[]{:S(2)}) %collective-permute-start.18) | collective-permute-done | bytes 221216 | tf_op jit(solution)/shard_map/ppermute | solution.py:583
  276.0 1.6 collective-permute-start.20
  277.6 8.9 %attend_backward.7.right_ref.refs_1_ = bf16[3,1024,384]{2,1,0:T(8,128)(2,1)} custom-call(s32[2]{0:T(128)} %len_ref.13, bf16[1024,2304]{1,0:T(8,128)(2,1)} %project_qkv.1.q_ref.k_ref.v_ref, bf16[1024,2304]{1,0:T(8,128)(2,1)} %project_qkv.1.q_ref.k_ref.v_ref, bf16[1024,2304]{1,0:T(8,128)(2,1)} %project_qkv.1.q_ref.k_ref.v_ref, ...), custom_call_target="tpu_custom_call", output_to_operand_aliasing={{}: (6, {})} | custom-call | flops 4026531840 | bytes 2752512 | tf_op jit(solution)/shard_map/attend_backward/pallas_call | solution.py:187
  286.6 2.3 collective-permute-start.21
  289.1 3.2 collective-permute-done.21
  293.0 4.5 %collective-permute-done.32 = bf16[2,96,768]{2,1,0:T(8,128)(2,1)S(1)} collective-permute-done((bf16[2,96,768]{2,1,0:T(8,128)(2,1)S(1)}, bf16[2,96,768]{2,1,0:T(8,128)(2,1)S(1)}, u32[]{:S(2)}, u32[]{:S(2)}) %collective-permute-start.32) | collective-permute-done | bytes 294944 | tf_op jit(solution)/shard_map/ppermute | solution.py:583
  299.0 1.2 add_convert_fusion.4
  300.6 6.8 %weight_gradient.3 = (bf16[16,24,1152]{2,1,0:T(8,128)(2,1)}, bf16[16,24,1152]{2,1,0:T(8,128)(2,1)}, f32[3,8,384]{2,1,0:T(8,128)}) custom-call(s32[32]{0:T(128)} %get-tuple-element.137.src_ref, bf16[1024,768]{1,0:T(8,128)(2,1)} %left_ref.3, bf16[3,1024,384]{2,1,0:T(8,128)(2,1)} %attend_backward.7.right_ref.refs_1_), custom_call_target="tpu_custom_call" | custom-call | flops 1811939328 | bytes 5701632 | tf_op jit(solution)/shard_map/weight_gradient/pallas_call | solution.py:425
  309.7 9.3 %input_gradient.1 = bf16[1024,768]{1,0:T(8,128)(2,1)} custom-call(f32[1024,768]{1,0:T(8,128)} %get-tuple-element.90.resid_ref, bf16[768,2432]{1,0:T(8,128)(2,1)} %lay_out.2.w_ref, bf16[3,1024,384]{2,1,0:T(8,128)(2,1)} %attend_backward.5.right_ref.refs_0_, bf16[3,1024,384]{2,1,0:T(8,128)(2,1)} %attend_backward.7.right_ref.refs_1_), custom_call_target="tpu_custom_call" | custom-call | flops 3623878656 | bytes 12976128 | tf_op jit(solution)/shard_map/input_gradient/pallas_call | solution.py:566
  319.1 2.1 multiply_subtract_fusion
  321.3 1.1 collective-permute-start.29
  322.7 1.8 collective-permute-start.23
  325.0 1.2 collective-permute-start.25
  326.3 6.0 %collective-permute-done.29 = bf16[2,24,3840]{2,1,0:T(8,128)(2,1)S(1)} collective-permute-done((bf16[2,24,3840]{2,1,0:T(8,128)(2,1)S(1)}, bf16[2,24,3840]{2,1,0:T(8,128)(2,1)S(1)}, u32[]{:S(2)}, u32[]{:S(2)}) %collective-permute-start.29) | collective-permute-done | bytes 368672 | tf_op jit(solution)/shard_map/ppermute | solution.py:583
  332.4 2.1 collective-permute-start.30
  334.5 3.1 collective-permute-done.24
  338.7 4.9 %collective-permute-done.30 = bf16[1,24,3840]{2,1,0:T(8,128)(2,1)S(1)} collective-permute-done((bf16[1,24,3840]{2,1,0:T(8,128)(2,1)S(1)}, bf16[1,24,3840]{2,1,0:T(8,128)(2,1)S(1)}, u32[]{:S(2)}, u32[]{:S(2)}) %collective-permute-start.30) | collective-permute-done | bytes 184352 | tf_op jit(solution)/shard_map/ppermute | solution.py:583
  346.4 4.2 %collective-permute-done.27 = bf16[1,24,1280]{2,1,0:T(8,128)(2,1)S(1)} collective-permute-done((bf16[1,24,1280]{2,1,0:T(8,128)(2,1)S(1)}, bf16[1,24,1280]{2,1,0:T(8,128)(2,1)S(1)}, u32[]{:S(2)}, u32[]{:S(2)}) %collective-permute-start.27) | collective-permute-done | bytes 61472 | tf_op jit(solution)/shard_map/ppermute | solution.py:583
  (169 shorter events, 34.3 us)
Async XLA Ops:
  7.2 15.1 %copy-start.4 = (f32[96,768]{1,0:T(8,128)S(1)}, f32[96,768]{1,0:T(8,128)}, u32[]{:S(2)}) copy-start(f32[96,768]{1,0:T(8,128)} %param.31) | copy-start | bytes 884740
  7.2 116.6 %all-gather.2.cloned.1.call-start = ((), (), s32[]{:S(2)}) async-start(), calls=%async_computation | async-start | bytes 6082560 | tf_op jit(solution)/shard_map/all_gather | solution.py:765
  11.6 9.8 %collective-permute-start = (bf16[1,24,2432]{2,1,0:T(8,128)(2,1)S(1)}, bf16[1,24,2432]{2,1,0:T(8,128)(2,1)S(1)}, u32[]{:S(2)}, u32[]{:S(2)}) collective-permute-start(bf16[1,24,2432]{2,1,0:T(8,128)(2,1)S(1)} %fusion.10), channel_id=1, source_target_pairs={{0,16},{1,17},{2,18},{3,19},{4,20},{5,21},{6,22},{7,23},{8,24},{9,... | collective-permute-start | bytes 350216 | tf_op jit(solution)/shard_map/ppermute | solution.py:583
  21.5 8.6 %collective-permute-start.1 = (bf16[2,24,2432]{2,1,0:T(8,128)(2,1)S(1)}, bf16[2,24,2432]{2,1,0:T(8,128)(2,1)S(1)}, u32[]{:S(2)}, u32[]{:S(2)}) collective-permute-start(bf16[2,24,2432]{2,1,0:T(8,128)(2,1)S(1)} %pad_maximum_fusion.5), channel_id=1, source_target_pairs={{0,8},{1,9},{2,10},{3,11},{4,12},{5,13},{6,14},{7,15},{8,0},{9,1},... | collective-permute-start | bytes 700424 | tf_op jit(solution)/shard_map/ppermute | solution.py:583
  30.1 11.3 %collective-permute-start.5 = (bf16[1,96,768]{2,1,0:T(8,128)(2,1)S(1)}, bf16[1,96,768]{2,1,0:T(8,128)(2,1)S(1)}, u32[]{:S(2)}, u32[]{:S(2)}) collective-permute-start(bf16[1,96,768]{2,1,0:T(8,128)(2,1)S(1)} %convert_bitcast_fusion), channel_id=1, source_target_pairs={{0,16},{1,17},{2,18},{3,19},{4,20},{5,21},{6,22},{7,23},{8,24},{9,... | collective-permute-start | bytes 442376 | tf_op jit(solution)/shard_map/ppermute | solution.py:583
  35.2 18.9 %collective-permute-start.2 = (bf16[4,24,2432]{2,1,0:T(8,128)(2,1)S(1)}, bf16[4,24,2432]{2,1,0:T(8,128)(2,1)S(1)}, u32[]{:S(2)}, u32[]{:S(2)}) collective-permute-start(bf16[4,24,2432]{2,1,0:T(8,128)(2,1)S(1)} %pad_maximum_fusion.3), channel_id=1, source_target_pairs={{0,2},{1,3},{2,0},{3,1},{4,6},{5,7},{6,4},{7,5},{8,10},{9,11},{10,... | collective-permute-start | bytes 1400840 | tf_op jit(solution)/shard_map/ppermute | solution.py:583
  36.7 18.3 %collective-permute-start.3 = (bf16[4,24,2432]{2,1,0:T(8,128)(2,1)S(1)}, bf16[4,24,2432]{2,1,0:T(8,128)(2,1)S(1)}, u32[]{:S(2)}, u32[]{:S(2)}) collective-permute-start(bf16[4,24,2432]{2,1,0:T(8,128)(2,1)S(1)} %pad_maximum_fusion.3), channel_id=1, source_target_pairs={{0,4},{1,5},{2,6},{3,7},{4,0},{5,1},{6,2},{7,3},{8,12},{9,13},{10,... | collective-permute-start | bytes 1400840 | tf_op jit(solution)/shard_map/ppermute | solution.py:583
  38.3 24.6 %collective-permute-start.4 = (bf16[4,24,2432]{2,1,0:T(8,128)(2,1)S(1)}, bf16[4,24,2432]{2,1,0:T(8,128)(2,1)S(1)}, u32[]{:S(2)}, u32[]{:S(2)}) collective-permute-start(bf16[4,24,2432]{2,1,0:T(8,128)(2,1)S(1)} %pad_maximum_fusion.3), channel_id=1, source_target_pairs={{0,6},{1,7},{2,4},{3,5},{4,2},{5,3},{6,0},{7,1},{8,14},{9,15},{10,... | collective-permute-start | bytes 1400840 | tf_op jit(solution)/shard_map/ppermute | solution.py:583
  41.4 12.6 %collective-permute-start.6 = (bf16[2,96,768]{2,1,0:T(8,128)(2,1)S(1)}, bf16[2,96,768]{2,1,0:T(8,128)(2,1)S(1)}, u32[]{:S(2)}, u32[]{:S(2)}) collective-permute-start(bf16[2,96,768]{2,1,0:T(8,128)(2,1)S(1)} %pad_maximum_fusion.4), channel_id=1, source_target_pairs={{0,8},{1,9},{2,10},{3,11},{4,12},{5,13},{6,14},{7,15},{8,0},{9,1},... | collective-permute-start | bytes 884744 | tf_op jit(solution)/shard_map/ppermute | solution.py:583
  42.3 21.4 %copy-start.29 = (s32[16]{0:T(128)S(1)}, s32[16]{0:T(128)}, u32[]{:S(2)}) copy-start(s32[16]{0:T(128)} %constant.46.clone) | copy-start | bytes 196
  63.7 5.9 %collective-permute-start.7 = (bf16[16,24,2432]{2,1,0:T(8,128)(2,1)}, bf16[16,24,2432]{2,1,0:T(8,128)(2,1)}, u32[]{:S(2)}, u32[]{:S(2)}) collective-permute-start(bf16[16,24,2432]{2,1,0:T(8,128)(2,1)} %constant_dynamic-update-slice_fusion.held_ref), channel_id=1, source_target_pairs={{0,1},{1,0},{2,3},{3,2},{4,5},{5,4},{6,7},{7,6},{8,9},{9,8},{10,11... | collective-permute-start | bytes 5603336 | tf_op jit(solution)/shard_map/ppermute | solution.py:583
  64.2 31.3 %collective-permute-start.10 = (bf16[4,96,768]{2,1,0:T(8,128)(2,1)S(1)}, bf16[4,96,768]{2,1,0:T(8,128)(2,1)}, u32[]{:S(2)}, u32[]{:S(2)}) collective-permute-start(bf16[4,96,768]{2,1,0:T(8,128)(2,1)S(1)} %pad_maximum_fusion.2), channel_id=1, source_target_pairs={{0,6},{1,7},{2,4},{3,5},{4,2},{5,3},{6,0},{7,1},{8,14},{9,15},{10,... | collective-permute-start | bytes 1769480 | tf_op jit(solution)/shard_map/ppermute | solution.py:583
  65.5 37.2 %collective-permute-start.9 = (bf16[4,96,768]{2,1,0:T(8,128)(2,1)S(1)}, bf16[4,96,768]{2,1,0:T(8,128)(2,1)}, u32[]{:S(2)}, u32[]{:S(2)}) collective-permute-start(bf16[4,96,768]{2,1,0:T(8,128)(2,1)S(1)} %pad_maximum_fusion.2), channel_id=1, source_target_pairs={{0,4},{1,5},{2,6},{3,7},{4,0},{5,1},{6,2},{7,3},{8,12},{9,13},{10,... | collective-permute-start | bytes 1769480 | tf_op jit(solution)/shard_map/ppermute | solution.py:583
  67.4 35.3 %collective-permute-start.8 = (bf16[4,96,768]{2,1,0:T(8,128)(2,1)S(1)}, bf16[4,96,768]{2,1,0:T(8,128)(2,1)}, u32[]{:S(2)}, u32[]{:S(2)}) collective-permute-start(bf16[4,96,768]{2,1,0:T(8,128)(2,1)S(1)} %pad_maximum_fusion.2), channel_id=1, source_target_pairs={{0,2},{1,3},{2,0},{3,1},{4,6},{5,7},{6,4},{7,5},{8,10},{9,11},{10,... | collective-permute-start | bytes 1769480 | tf_op jit(solution)/shard_map/ppermute | solution.py:583
  95.5 10.7 %copy-start = (s32[32]{0:T(128)S(1)}, s32[32]{0:T(128)}, u32[]{:S(2)}) copy-start(s32[32]{0:T(128)} %constant.45.clone) | copy-start | bytes 388
  95.5 11.4 %copy-start.28 = (s32[32]{0:T(128)S(1)}, s32[32]{0:T(128)}, u32[]{:S(2)}) copy-start(s32[32]{0:T(128)} %constant.47.clone) | copy-start | bytes 388
  106.0 12.3 %copy-start.1 = (bf16[16,96,768]{2,1,0:T(8,128)(2,1)}, bf16[16,96,768]{2,1,0:T(8,128)(2,1)S(1)}, u32[]{:S(2)}) copy-start(bf16[16,96,768]{2,1,0:T(8,128)(2,1)S(1)} %constant_dynamic-update-slice_fusion.6.held_ref) | copy-start | bytes 7077892
  106.0 12.3 %collective-permute-start.11 = (bf16[16,96,768]{2,1,0:T(8,128)(2,1)S(1)}, bf16[16,96,768]{2,1,0:T(8,128)(2,1)}, u32[]{:S(2)}, u32[]{:S(2)}) collective-permute-start(bf16[16,96,768]{2,1,0:T(8,128)(2,1)S(1)} %constant_dynamic-update-slice_fusion.6.held_ref), channel_id=1, source_target_pairs={{0,1},{1,0},{2,3},{3,2},{4,5},{5,4},{6,7},{7,6},{8,9},{9,8},{10,11... | collective-permute-start | bytes 7077896 | tf_op jit(solution)/shard_map/ppermute | solution.py:583
  171.0 13.5 %collective-permute-start.12 = (bf16[16,96,768]{2,1,0:T(8,128)(2,1)}, bf16[16,96,768]{2,1,0:T(8,128)(2,1)S(1)}, u32[]{:S(2)}, u32[]{:S(2)}) collective-permute-start(bf16[16,96,768]{2,1,0:T(8,128)(2,1)} %get-tuple-element.70), channel_id=1, source_target_pairs={{0,1},{1,0},{2,3},{3,2},{4,5},{5,4},{6,7},{7,6},{8,9},{9,8},{10,11... | collective-permute-start | bytes 7077896 | tf_op jit(solution)/shard_map/ppermute | solution.py:583
  171.0 13.5 %copy-start.3 = (bf16[16,96,768]{2,1,0:T(8,128)(2,1)S(1)}, bf16[16,96,768]{2,1,0:T(8,128)(2,1)}, u32[]{:S(2)}) copy-start(bf16[16,96,768]{2,1,0:T(8,128)(2,1)} %get-tuple-element.69) | copy-start | bytes 7077892
  184.0 16.2 %collective-permute-start.13 = (bf16[16,24,3840]{2,1,0:T(8,128)(2,1)}, bf16[16,24,3840]{2,1,0:T(8,128)(2,1)}, u32[]{:S(2)}, u32[]{:S(2)}) collective-permute-start(bf16[16,24,3840]{2,1,0:T(8,128)(2,1)} %get-tuple-element.76), channel_id=1, source_target_pairs={{0,1},{1,0},{2,3},{3,2},{4,5},{5,4},{6,7},{7,6},{8,9},{9,8},{10,11... | collective-permute-start | bytes 8847368 | tf_op jit(solution)/shard_map/ppermute | solution.py:583
  186.2 34.4 %collective-permute-start.14 = (bf16[8,96,768]{2,1,0:T(8,128)(2,1)}, bf16[8,96,768]{2,1,0:T(8,128)(2,1)S(1)}, u32[]{:S(2)}, u32[]{:S(2)}) collective-permute-start(bf16[8,96,768]{2,1,0:T(8,128)(2,1)} %get-tuple-element.110), channel_id=1, source_target_pairs={{0,2},{1,3},{2,0},{3,1},{4,6},{5,7},{6,4},{7,5},{8,10},{9,11},{10,... | collective-permute-start | bytes 3538952 | tf_op jit(solution)/shard_map/ppermute | solution.py:583
  218.5 4.7 %collective-permute-start.15 = (bf16[16,24,1152]{2,1,0:T(8,128)(2,1)}, bf16[16,24,1152]{2,1,0:T(8,128)(2,1)S(1)}, u32[]{:S(2)}, u32[]{:S(2)}) collective-permute-start(bf16[16,24,1152]{2,1,0:T(8,128)(2,1)} %get-tuple-element.82), channel_id=1, source_target_pairs={{0,1},{1,0},{2,3},{3,2},{4,5},{5,4},{6,7},{7,6},{8,9},{9,8},{10,11... | collective-permute-start | bytes 2654216 | tf_op jit(solution)/shard_map/ppermute | solution.py:583
  219.2 79.8 %collective-permute-start.16 = (bf16[8,24,3840]{2,1,0:T(8,128)(2,1)S(1)}, bf16[8,24,3840]{2,1,0:T(8,128)(2,1)S(1)}, u32[]{:S(2)}, u32[]{:S(2)}) collective-permute-start(bf16[8,24,3840]{2,1,0:T(8,128)(2,1)S(1)} %get-tuple-element.108), channel_id=1, source_target_pairs={{0,4},{1,5},{2,6},{3,7},{4,0},{5,1},{6,2},{7,3},{8,12},{9,13},{10,... | collective-permute-start | bytes 4423688 | tf_op jit(solution)/shard_map/ppermute | solution.py:583
  221.7 67.2 %collective-permute-start.31 = (bf16[4,96,768]{2,1,0:T(8,128)(2,1)}, bf16[4,96,768]{2,1,0:T(8,128)(2,1)S(1)}, u32[]{:S(2)}, u32[]{:S(2)}) collective-permute-start(bf16[4,96,768]{2,1,0:T(8,128)(2,1)} %get-tuple-element.114), channel_id=1, source_target_pairs={{0,4},{1,5},{2,6},{3,7},{4,0},{5,1},{6,2},{7,3},{8,12},{9,13},{10,... | collective-permute-start | bytes 1769480 | tf_op jit(solution)/shard_map/ppermute | solution.py:583
  223.4 12.7 %collective-permute-start.17 = (bf16[4,24,1152]{2,1,0:T(8,128)(2,1)S(1)}, bf16[4,24,1152]{2,1,0:T(8,128)(2,1)S(1)}, u32[]{:S(2)}, u32[]{:S(2)}) collective-permute-start(bf16[4,24,1152]{2,1,0:T(8,128)(2,1)S(1)} %get-tuple-element.122), channel_id=1, source_target_pairs={{0,2},{1,3},{2,0},{3,1},{4,6},{5,7},{6,4},{7,5},{8,10},{9,11},{10,... | collective-permute-start | bytes 663560 | tf_op jit(solution)/shard_map/ppermute | solution.py:583
  223.8 52.2 %collective-permute-start.18 = (bf16[4,24,1152]{2,1,0:T(8,128)(2,1)S(1)}, bf16[4,24,1152]{2,1,0:T(8,128)(2,1)S(1)}, u32[]{:S(2)}, u32[]{:S(2)}) collective-permute-start(bf16[4,24,1152]{2,1,0:T(8,128)(2,1)S(1)} %get-tuple-element.121), channel_id=1, source_target_pairs={{0,4},{1,5},{2,6},{3,7},{4,0},{5,1},{6,2},{7,3},{8,12},{9,13},{10,... | collective-permute-start | bytes 663560 | tf_op jit(solution)/shard_map/ppermute | solution.py:583
  224.3 51.6 %collective-permute-start.19 = (bf16[4,24,1152]{2,1,0:T(8,128)(2,1)S(1)}, bf16[4,24,1152]{2,1,0:T(8,128)(2,1)S(1)}, u32[]{:S(2)}, u32[]{:S(2)}) collective-permute-start(bf16[4,24,1152]{2,1,0:T(8,128)(2,1)S(1)} %get-tuple-element.120), channel_id=1, source_target_pairs={{0,6},{1,7},{2,4},{3,5},{4,2},{5,3},{6,0},{7,1},{8,14},{9,15},{10,... | collective-permute-start | bytes 663560 | tf_op jit(solution)/shard_map/ppermute | solution.py:583
  276.0 10.5 %collective-permute-start.20 = (bf16[2,24,1152]{2,1,0:T(8,128)(2,1)S(1)}, bf16[2,24,1152]{2,1,0:T(8,128)(2,1)S(1)}, u32[]{:S(2)}, u32[]{:S(2)}) collective-permute-start(bf16[2,24,1152]{2,1,0:T(8,128)(2,1)S(1)} %get-tuple-element.131), channel_id=1, source_target_pairs={{0,8},{1,9},{2,10},{3,11},{4,12},{5,13},{6,14},{7,15},{8,0},{9,1},... | collective-permute-start | bytes 331784 | tf_op jit(solution)/shard_map/ppermute | solution.py:583
  286.6 5.8 %collective-permute-start.21 = (bf16[1,24,1152]{2,1,0:T(8,128)(2,1)S(1)}, bf16[1,24,1152]{2,1,0:T(8,128)(2,1)S(1)}, u32[]{:S(2)}, u32[]{:S(2)}) collective-permute-start(bf16[1,24,1152]{2,1,0:T(8,128)(2,1)S(1)} %add_convert_fusion.30), channel_id=1, source_target_pairs={{0,16},{1,17},{2,18},{3,19},{4,20},{5,21},{6,22},{7,23},{8,24},{9,... | collective-permute-start | bytes 165896 | tf_op jit(solution)/shard_map/ppermute | solution.py:583
  289.0 8.5 %collective-permute-start.32 = (bf16[2,96,768]{2,1,0:T(8,128)(2,1)S(1)}, bf16[2,96,768]{2,1,0:T(8,128)(2,1)S(1)}, u32[]{:S(2)}, u32[]{:S(2)}) collective-permute-start(bf16[2,96,768]{2,1,0:T(8,128)(2,1)S(1)} %get-tuple-element.127), channel_id=1, source_target_pairs={{0,8},{1,9},{2,10},{3,11},{4,12},{5,13},{6,14},{7,15},{8,0},{9,1},... | collective-permute-start | bytes 884744 | tf_op jit(solution)/shard_map/ppermute | solution.py:583
  298.3 20.7 %collective-permute-start.33 = (bf16[1,96,768]{2,1,0:T(8,128)(2,1)}, bf16[1,96,768]{2,1,0:T(8,128)(2,1)}, u32[]{:S(2)}, u32[]{:S(2)}) collective-permute-start(bf16[1,96,768]{2,1,0:T(8,128)(2,1)} %add_convert_fusion.22), channel_id=1, source_target_pairs={{0,16},{1,17},{2,18},{3,19},{4,20},{5,21},{6,22},{7,23},{8,24},{9,... | collective-permute-start | bytes 442376 | tf_op jit(solution)/shard_map/ppermute | solution.py:583
  300.3 20.9 %collective-permute-start.28 = (bf16[4,24,3840]{2,1,0:T(8,128)(2,1)}, bf16[4,24,3840]{2,1,0:T(8,128)(2,1)S(1)}, u32[]{:S(2)}, u32[]{:S(2)}) collective-permute-start(bf16[4,24,3840]{2,1,0:T(8,128)(2,1)} %get-tuple-element.112), channel_id=1, source_target_pairs={{0,2},{1,3},{2,0},{3,1},{4,6},{5,7},{6,4},{7,5},{8,10},{9,11},{10,... | collective-permute-start | bytes 2211848 | tf_op jit(solution)/shard_map/ppermute | solution.py:583
  309.5 12.9 %collective-permute-start.22 = (bf16[16,24,1280]{2,1,0:T(8,128)(2,1)S(1)}, bf16[16,24,1280]{2,1,0:T(8,128)(2,1)S(1)}, u32[]{:S(2)}, u32[]{:S(2)}) collective-permute-start(bf16[16,24,1280]{2,1,0:T(8,128)(2,1)S(1)} %pad_maximum_fusion.1), channel_id=1, source_target_pairs={{0,1},{1,0},{2,3},{3,2},{4,5},{5,4},{6,7},{7,6},{8,9},{9,8},{10,11... | collective-permute-start | bytes 2949128 | tf_op jit(solution)/shard_map/ppermute | solution.py:583
  309.6 9.4 %copy-start.5 = (f32[96,768]{1,0:T(8,128)S(1)}, f32[96,768]{1,0:T(8,128)}, u32[]{:S(2)}) copy-start(f32[96,768]{1,0:T(8,128)} %param.31) | copy-start | bytes 884740
  309.6 9.4 %copy-start.12 = (f32[96,768]{1,0:T(8,128)S(1)}, f32[96,768]{1,0:T(8,128)}, u32[]{:S(2)}) copy-start(f32[96,768]{1,0:T(8,128)} %param.41) | copy-start | bytes 884740
  309.7 9.4 %copy-start.13 = (f32[96,768]{1,0:T(8,128)S(1)}, f32[96,768]{1,0:T(8,128)}, u32[]{:S(2)}) copy-start(f32[96,768]{1,0:T(8,128)} %param.36) | copy-start | bytes 884740
  321.3 11.0 %collective-permute-start.29 = (bf16[2,24,3840]{2,1,0:T(8,128)(2,1)S(1)}, bf16[2,24,3840]{2,1,0:T(8,128)(2,1)S(1)}, u32[]{:S(2)}, u32[]{:S(2)}) collective-permute-start(bf16[2,24,3840]{2,1,0:T(8,128)(2,1)S(1)} %get-tuple-element.125), channel_id=1, source_target_pairs={{0,8},{1,9},{2,10},{3,11},{4,12},{5,13},{6,14},{7,15},{8,0},{9,1},... | collective-permute-start | bytes 1105928 | tf_op jit(solution)/shard_map/ppermute | solution.py:583
  322.7 21.0 %copy-start.6 = (f32[24,3072]{1,0:T(8,128)S(1)}, f32[24,3072]{1,0:T(8,128)}, u32[]{:S(2)}) copy-start(f32[24,3072]{1,0:T(8,128)} %param.30) | copy-start | bytes 884740
  322.7 21.0 %copy-start.17 = (f32[24,3072]{1,0:T(8,128)S(1)}, f32[24,3072]{1,0:T(8,128)}, u32[]{:S(2)}) copy-start(f32[24,3072]{1,0:T(8,128)} %param.40) | copy-start | bytes 884740
  322.7 21.0 %copy-start.18 = (f32[24,3072]{1,0:T(8,128)S(1)}, f32[24,3072]{1,0:T(8,128)}, u32[]{:S(2)}) copy-start(f32[24,3072]{1,0:T(8,128)} %param.35) | copy-start | bytes 884740
  322.7 11.8 %collective-permute-start.23 = (bf16[4,24,1280]{2,1,0:T(8,128)(2,1)S(1)}, bf16[4,24,1280]{2,1,0:T(8,128)(2,1)S(1)}, u32[]{:S(2)}, u32[]{:S(2)}) collective-permute-start(bf16[4,24,1280]{2,1,0:T(8,128)(2,1)S(1)} %get-tuple-element.117), channel_id=1, source_target_pairs={{0,2},{1,3},{2,0},{3,1},{4,6},{5,7},{6,4},{7,5},{8,10},{9,11},{10,... | collective-permute-start | bytes 737288 | tf_op jit(solution)/shard_map/ppermute | solution.py:583
  324.5 13.0 %collective-permute-start.24 = (bf16[4,24,1280]{2,1,0:T(8,128)(2,1)S(1)}, bf16[4,24,1280]{2,1,0:T(8,128)(2,1)S(1)}, u32[]{:S(2)}, u32[]{:S(2)}) collective-permute-start(bf16[4,24,1280]{2,1,0:T(8,128)(2,1)S(1)} %get-tuple-element.118), channel_id=1, source_target_pairs={{0,4},{1,5},{2,6},{3,7},{4,0},{5,1},{6,2},{7,3},{8,12},{9,13},{10,... | collective-permute-start | bytes 737288 | tf_op jit(solution)/shard_map/ppermute | solution.py:583
  325.0 12.5 %collective-permute-start.25 = (bf16[4,24,1280]{2,1,0:T(8,128)(2,1)S(1)}, bf16[4,24,1280]{2,1,0:T(8,128)(2,1)S(1)}, u32[]{:S(2)}, u32[]{:S(2)}) collective-permute-start(bf16[4,24,1280]{2,1,0:T(8,128)(2,1)S(1)} %get-tuple-element.119), channel_id=1, source_target_pairs={{0,6},{1,7},{2,4},{3,5},{4,2},{5,3},{6,0},{7,1},{8,14},{9,15},{10,... | collective-permute-start | bytes 737288 | tf_op jit(solution)/shard_map/ppermute | solution.py:583
  332.4 11.2 %collective-permute-start.30 = (bf16[1,24,3840]{2,1,0:T(8,128)(2,1)S(1)}, bf16[1,24,3840]{2,1,0:T(8,128)(2,1)S(1)}, u32[]{:S(2)}, u32[]{:S(2)}) collective-permute-start(bf16[1,24,3840]{2,1,0:T(8,128)(2,1)S(1)} %add_convert_fusion.20), channel_id=1, source_target_pairs={{0,16},{1,17},{2,18},{3,19},{4,20},{5,21},{6,22},{7,23},{8,24},{9,... | collective-permute-start | bytes 552968 | tf_op jit(solution)/shard_map/ppermute | solution.py:583
  337.7 12.9 %copy-start.11 = (f32[24,2304]{1,0:T(8,128)S(1)}, f32[24,2304]{1,0:T(8,128)}, u32[]{:S(2)}) copy-start(f32[24,2304]{1,0:T(8,128)} %slice_dynamic-update-slice_fusion.5) | copy-start | bytes 663556
  337.8 7.7 %collective-permute-start.26 = (bf16[2,24,1280]{2,1,0:T(8,128)(2,1)S(1)}, bf16[2,24,1280]{2,1,0:T(8,128)(2,1)S(1)}, u32[]{:S(2)}, u32[]{:S(2)}) collective-permute-start(bf16[2,24,1280]{2,1,0:T(8,128)(2,1)S(1)} %get-tuple-element.129), channel_id=1, source_target_pairs={{0,8},{1,9},{2,10},{3,11},{4,12},{5,13},{6,14},{7,15},{8,0},{9,1},... | collective-permute-start | bytes 368648 | tf_op jit(solution)/shard_map/ppermute | solution.py:583
  345.4 5.2 %collective-permute-start.27 = (bf16[1,24,1280]{2,1,0:T(8,128)(2,1)S(1)}, bf16[1,24,1280]{2,1,0:T(8,128)(2,1)S(1)}, u32[]{:S(2)}, u32[]{:S(2)}) collective-permute-start(bf16[1,24,1280]{2,1,0:T(8,128)(2,1)S(1)} %add_convert_fusion.28), channel_id=1, source_target_pairs={{0,16},{1,17},{2,18},{3,19},{4,20},{5,21},{6,22},{7,23},{8,24},{9,... | collective-permute-start | bytes 184328 | tf_op jit(solution)/shard_map/ppermute | solution.py:583
  (17 other events, 114.0 us)
Sparse Core Ops, SparseCore 0:
  11.5 100.3 all-gather.1

commit v3 on v2

--- a/solution.py
+++ b/solution.py
@@ -41,8 +41,10 @@
     )
 
 
-def cost(flops, moved, exps=0):
-    return pl.CostEstimate(flops=int(flops), bytes_accessed=int(moved), transcendentals=int(exps))
+def cost(flops, moved, exps=0, longer=1):
+    return pl.CostEstimate(
+        flops=longer * int(flops), bytes_accessed=int(moved), transcendentals=int(exps)
+    )
 
 
 def qkv_kernel(x_ref, w_ref, vec_ref, out_ref):
@@ -191,7 +193,7 @@
         input_output_aliases={6 + index: index for index in range(len(filled))},
         compiler_params=params(1),
         cost_estimate=cost(
-            40 * seq * seq * here * LANES, 14 * seq * here * LANES, seq * seq * here * 2
+            40 * seq * seq * here * LANES, 14 * seq * here * LANES, seq * seq * here * 2, 8
         ),
         name="attend_backward",
     )(lengths, packed, packed, packed, grad_mixed, lse, *filled)
@@ -399,7 +401,11 @@
     left_block = pl.BlockSpec((rows, tall), lambda j, *s: (0, 0))
     extra_specs = [pl.BlockSpec((1, 8, tile), lambda j, *s: (j, 0, 0))] if sums else []
     extra_shapes = [jax.ShapeDtypeStruct((steps, 8, tile), F32)] if sums else []
-    estimate = cost(2 * rows * tall * tile * steps, 2 * tall * tile * steps + 2 * rows * (tall + tile * steps))
+    estimate = cost(
+        2 * rows * tall * tile * steps,
+        2 * tall * tile * steps + 2 * rows * (tall + tile * steps),
+        longer=64,
+    )
     if piece % 8:
         whole, *rest = pl.pallas_call(
             plain_weight_kernel,
@@ -481,7 +487,9 @@
         out_shape=[shape, shape],
         compiler_params=params(1),
         cost_estimate=cost(
-            2 * rows * tall * tile * (wide + 1), 2 * (tall + rows) * tile * (wide + 1) + 4 * rows * tall
+            2 * rows * tall * tile * (wide + 1),
+            2 * (tall + rows) * tile * (wide + 1) + 4 * rows * tall,
+            longer=8,
         ),
         name="joint_gradient",
     )(source, left, last_left, right, last_right)
@@ -550,33 +558,41 @@
     )(slot_of, left, right)
 
 
-def input_kernel(resid_ref, w_ref, *refs):
+def input_kernel(resid_ref, w_ref, *refs, groups):
     out_ref = refs[-1]
     width = resid_ref.shape[1]
     total = resid_ref[...]
-    for group, grad_ref in enumerate(refs[:-1]):
+    for group, grad_ref in enumerate(refs[:groups]):
         here = grad_ref.shape[2]
         for part in range(3):
             total = total + dot(grad_ref[part], w_ref[:, pl.ds(part * width + group * here, here)], NT)
     out_ref[...] = total.astype(BF)
 
 
-def input_gradient(resid, gathered, grads):
+def input_gradient(resid, gathered, grads, which, batch, filled):
     rows, width = resid.shape
+    steps = rows // batch // ROWS
+    base = which * steps
     return pl.pallas_call(
-        input_kernel,
-        grid=(rows // ROWS,),
+        functools.partial(input_kernel, groups=len(grads)),
+        grid=(steps,),
         in_specs=[
-            pl.BlockSpec((ROWS, width), lambda i: (i, 0)),
+            pl.BlockSpec((ROWS, width), lambda i: (base + i, 0)),
             pl.BlockSpec((width, 3 * width), lambda i: (0, 0), pipeline_mode=pl.Buffered(1)),
         ]
-        + [pl.BlockSpec((3, ROWS, grad.shape[2]), lambda i: (0, i, 0)) for grad in grads],
-        out_specs=pl.BlockSpec((ROWS, width), lambda i: (i, 0)),
+        + [pl.BlockSpec((3, ROWS, grad.shape[2]), lambda i: (0, base + i, 0)) for grad in grads]
+        + [pl.BlockSpec(memory_space=pl.ANY)] * len(filled),
+        out_specs=pl.BlockSpec((ROWS, width), lambda i: (base + i, 0)),
         out_shape=jax.ShapeDtypeStruct((rows, width), BF),
+        input_output_aliases={2 + len(grads): 0} if filled else {},
         compiler_params=params(1),
-        cost_estimate=cost(6 * rows * width * width, 12 * rows * width + 6 * width * width),
+        cost_estimate=cost(
+            6 * rows * width * width // batch,
+            (12 * rows * width + 6 * width * width) // batch,
+            longer=64,
+        ),
         name="input_gradient",
-    )(resid, gathered, *grads)
+    )(resid, gathered, *grads, *filled)
 
 
 def swap(value, mask, devices):
@@ -635,6 +651,10 @@
         ways = len(masks_of(self.order[self.at]))
         size = self.terms[0].shape[0] // ways
         self.parts = [self.total(way * size, size).astype(BF) for way in range(ways)]
+        return self
+
+    def after(self, *values):
+        self.terms = list(lax.optimization_barrier((tuple(self.terms), values))[0])
         return self
 
     def finish(self):
@@ -809,36 +829,37 @@
     joint = Reduce(
         *joint_gradient(first_low, grad_upper, mixed, grad_attn, source_of(by_y)), by_y, devices
     )
-    total.join()
+    total.after(joint.parts).join()
     grad_mixed = hold(grad_mixed, total.parts, joint.parts)
     total.send()
     joint.send()
     parts, part_sums, queue = [], [], []
     for group in range(GROUPS):
+        final = group == GROUPS - 1
         part = ()
         for which in range(batch):
             part = (attend_backward(packed, lengths, lse, grad_mixed, group, which, part),)
-            if group == 0 and which == 0:
-                joint.join()
-                grad_mixed = hold(grad_mixed, joint.parts)
-                joint.send()
-            if group == 1 and which == 0:
-                queue[0].join()
-                grad_mixed = hold(grad_mixed, queue[0].parts)
-                queue[0].send()
-        if group == GROUPS - 1:
-            joint.join()
-            part = (hold(part[0], joint.parts),)
-            joint.send()
-        keep, send, part_sum = weight_gradient(hidden_in, part[0], source_of(both), sums=True)
+            if which == 0 and group < 2:
+                chain = joint if group == 0 else queue[0]
+                chain.after(part).join()
+                grad_mixed = hold(grad_mixed, chain.parts)
+                chain.send()
+        left = hidden_in
+        if final:
+            for chain in (joint, total, *queue):
+                chain.after(part).join()
+            left = hold(hidden_in, *(chain.parts for chain in (joint, total, *queue)))
+            for chain in (joint, total, *queue):
+                chain.send()
+        order = both if final else by_x
+        keep, send, part_sum = weight_gradient(left, part[0], source_of(order), sums=True)
         parts.append(part[0])
         part_sums.append(part_sum)
         if group == 0:
-            queue.append(Reduce(keep, send, both, devices))
-            total.join()
+            queue.append(Reduce(keep, send, order, devices).send())
+            total.after(keep).join()
             grad_mixed = hold(grad_mixed, total.parts, keep)
             total.send()
-            queue[0].send()
     part_sums = jnp.concatenate(part_sums, axis=2)
     vector_sums = jnp.concatenate([part_sums[0, :1], part_sums[2, :1], sums[2:]], axis=0)
     ordered = jnp.take(vector_sums.reshape(devices, piece, entries), source_of(both), axis=0)
@@ -846,8 +867,19 @@
     keep = jnp.concatenate([keep, ordered[: devices // 2]], axis=2)
     send = jnp.concatenate([send, ordered[devices // 2 :]], axis=2)
     queue.append(Reduce(keep, send, both, devices).send())
-    grad_one = hold(grad_one, queue[1].parts)
-    input_grad = input_gradient(grad_one, gathered, parts)
+    grad_one = hold(grad_one, send)
+    filled = ()
+    for which in range(batch):
+        if which == batch - 1:
+            for chain in (queue[1], joint, total, queue[0]):
+                chain.after(filled).join()
+            grad_one = hold(grad_one, *(chain.parts for chain in (joint, total, *queue)))
+            for chain in (queue[1], joint, total, queue[0]):
+                chain.send()
+        filled = (input_gradient(grad_one, gathered, parts, which, batch, filled),)
+    input_grad = filled[0]
+    for chain in (joint, total, *queue):
+        chain.after(filled)
 
     total_qkv = [chain.finish() for chain in queue]
     total_vectors = total_qkv[1][:, 3 * width // GROUPS : 3 * width // GROUPS + entries].reshape(-1)

time: 360 us -> 327 us (0.908)
  waiting for transfers between devices: 110 us -> 66.9 us
  starting transfers between devices: 41 us -> 32.9 us
  Pallas kernels: 160 us -> 167 us
  other arithmetic: 21.7 us -> 28.1 us
    ppermute x34 -> x33, waiting for transfers between devices: 110 us -> 66.9 us  [swap(): lax.ppermute(value, 'dp', [(index, index ^ mask) for index in range(devic...]
    ppermute x34 -> x33, starting transfers between devices: 41 us -> 32.9 us  [swap(): lax.ppermute(value, 'dp', [(index, index ^ mask) for index in range(devic...]
    convert_element_type x14 -> x15, other arithmetic: 8.38 us -> 14.6 us  [join(): self.total(way * size, size).astype(BF)]
    pallas_call x1 -> x2, Pallas kernels: 9.33 us -> 12.5 us  [input_gradient(): pl.pallas_call(functools.partial(input_kernel, groups=len(grads)), grid=(...]
  transfers between devices with their start and end apart: 35 -> 34, of which waited for: 15 -> 12; matrix products, arithmetic and copies ran while one was open for 8% -> 11% of each run, Pallas kernels for 31% -> 36%
where the time goes in v3:
time: 327 us; the launch traced here: 323 us
  Pallas kernels  167 us (51%)
  waiting for transfers between devices  66.9 us (20%)
  starting transfers between devices  32.9 us (10%)
  other arithmetic  28.1 us (9%)
  between operations  15 us (5%)
  local copies, waits for them, and re-layouts  13.2 us (4%)
    ppermute x33, waiting for transfers between devices, swap(): lax.ppermute(value, 'dp', [(index, index ^ mask) for index in range(devic...  66.9 us
    pallas_call x1, Pallas kernels, middle(): pl.pallas_call(functools.partial(middle_kernel, seq=seq), grid_spec=grid_...  39.1 us
    pallas_call x4, Pallas kernels, attend_backward(): pl.pallas_call(functools.partial(attend_back_kernel, which=which), grid_s...  36.3 us
    ppermute x33, starting transfers between devices, swap(): lax.ppermute(value, 'dp', [(index, index ^ mask) for index in range(devic...  32.9 us
    pallas_call x2, Pallas kernels, attend_forward(): pl.pallas_call(functools.partial(attend_kernel, which=which), grid_spec=g...  21.7 us
    convert_element_type x15, other arithmetic, join(): self.total(way * size, size).astype(BF)  14.6 us
    pallas_call x2, Pallas kernels, weight_gradient(): pl.pallas_call(functools.partial(weight_kernel, sums=sums), grid_spec=gri...  13.5 us
    pallas_call x1, Pallas kernels, joint_gradient(): pl.pallas_call(joint_kernel, grid_spec=grid_spec, out_shape=[shape, shape...  13 us
  transfers between devices with their start and end apart: 34, of which 12 were waited for; matrix products, arithmetic and copies ran while one was open for 11% of the time, Pallas kernels for 36%

profile of v3, /device:TPU:0, one launch (start us, length us, event | category | flops | bytes accessed | tf_op | source)
XLA Modules:
  0.0 322.7 jit_solution(18147202150699771659)
XLA Ops:
  11.6 4.1 %collective-permute-start = (bf16[1,24,2432]{2,1,0:T(8,128)(2,1)S(1)}, bf16[1,24,2432]{2,1,0:T(8,128)(2,1)S(1)}, u32[]{:S(2)}, u32[]{:S(2)}) collective-permute-start(bf16[1,24,2432]{2,1,0:T(8,128)(2,1)S(1)} %fusion.6), channel_id=1, source_target_pairs={{0,16},{1,17},{2,18},{3,19},{4,20},{5,21},{6,22},{7,23},{8,24},{9,... | collective-permute-start | bytes 350216 | tf_op jit(solution)/shard_map/ppermute | solution.py:599
  16.4 5.0 %collective-permute-done = bf16[1,24,2432]{2,1,0:T(8,128)(2,1)S(1)} collective-permute-done((bf16[1,24,2432]{2,1,0:T(8,128)(2,1)S(1)}, bf16[1,24,2432]{2,1,0:T(8,128)(2,1)S(1)}, u32[]{:S(2)}, u32[]{:S(2)}) %collective-permute-start) | collective-permute-done | bytes 116768 | tf_op jit(solution)/shard_map/ppermute | solution.py:599
  22.3 7.7 %collective-permute-done.1 = bf16[2,24,2432]{2,1,0:T(8,128)(2,1)S(1)} collective-permute-done((bf16[2,24,2432]{2,1,0:T(8,128)(2,1)S(1)}, bf16[2,24,2432]{2,1,0:T(8,128)(2,1)S(1)}, u32[]{:S(2)}, u32[]{:S(2)}) %collective-permute-start.1) | collective-permute-done | bytes 233504 | tf_op jit(solution)/shard_map/ppermute | solution.py:599
  30.1 4.4 %collective-permute-start.5 = (bf16[1,96,768]{2,1,0:T(8,128)(2,1)S(1)}, bf16[1,96,768]{2,1,0:T(8,128)(2,1)S(1)}, u32[]{:S(2)}, u32[]{:S(2)}) collective-permute-start(bf16[1,96,768]{2,1,0:T(8,128)(2,1)S(1)} %convert_bitcast_fusion), channel_id=1, source_target_pairs={{0,16},{1,17},{2,18},{3,19},{4,20},{5,21},{6,22},{7,23},{8,24},{9,... | collective-permute-start | bytes 442376 | tf_op jit(solution)/shard_map/ppermute | solution.py:599
  35.2 1.5 collective-permute-start.2
  36.6 1.6 collective-permute-start.3
  38.6 2.7 collective-permute-done.5
  42.3 11.7 %collective-permute-done.6 = bf16[2,96,768]{2,1,0:T(8,128)(2,1)S(1)} collective-permute-done((bf16[2,96,768]{2,1,0:T(8,128)(2,1)S(1)}, bf16[2,96,768]{2,1,0:T(8,128)(2,1)S(1)}, u32[]{:S(2)}, u32[]{:S(2)}) %collective-permute-start.6) | collective-permute-done | bytes 294944 | tf_op jit(solution)/shard_map/ppermute | solution.py:599
  55.7 7.1 %collective-permute-done.4 = bf16[4,24,2432]{2,1,0:T(8,128)(2,1)S(1)} collective-permute-done((bf16[4,24,2432]{2,1,0:T(8,128)(2,1)S(1)}, bf16[4,24,2432]{2,1,0:T(8,128)(2,1)S(1)}, u32[]{:S(2)}, u32[]{:S(2)}) %collective-permute-start.4) | collective-permute-done | bytes 466976 | tf_op jit(solution)/shard_map/ppermute | solution.py:599
  64.2 1.3 collective-permute-start.10
  65.5 1.9 collective-permute-start.9
  67.7 1.9 collective-permute-done.7.taken_ref
  69.6 5.4 %lay_out.2.w_ref = bf16[768,2432]{1,0:T(8,128)(2,1)} custom-call(s32[16]{0:T(128)} %broadcast_xor_fusion.2.index_ref, s32[1]{0:T(128)} %bitcast.odd_ref, bf16[16,24,2432]{2,1,0:T(8,128)(2,1)} %constant_dynamic-update-slice_fusion.held_ref, bf16[16,24,2432]{2,1,0:T(8,128)(2,1)} %collective-permute-done.7.taken_ref), custom_call_target="tpu_custom_call" | custom-call | flops 1867776 | bytes 7471104 | tf_op jit(solution)/shard_map/lay_out/pallas_call | solution.py:728
  76.9 7.9 %project_qkv.1.q_ref.k_ref.v_ref = bf16[1024,2304]{1,0:T(8,128)(2,1)} custom-call(bf16[1024,768]{1,0:T(8,128)(2,1)} %left_ref.2, bf16[768,2432]{1,0:T(8,128)(2,1)} %lay_out.2.w_ref, f32[12,768]{1,0:T(8,128)} %reshape.85.vec_ref), custom_call_target="tpu_custom_call" | custom-call | flops 3623878656 | bytes 9830400 | tf_op jit(solution)/shard_map/project_qkv/pallas_call | solution.py:65
  84.8 10.8 %attend_forward.2 = (bf16[1024,768]{1,0:T(8,128)(2,1)}, f32[12,2,512]{2,1,0:T(2,128)}) custom-call(s32[2]{0:T(128)} %len_ref.13, bf16[1024,2304]{1,0:T(8,128)(2,1)} %project_qkv.1.q_ref.k_ref.v_ref, bf16[1024,2304]{1,0:T(8,128)(2,1)} %project_qkv.1.q_ref.k_ref.v_ref, bf16[1024,2304]{1,0:T(8,128)(2,1)} %project_qkv.1.q_ref.k_ref.v_ref), custom_call_target="tpu_custom_call" | custom-call | flops 3221225472 | bytes 3145728 | tf_op jit(solution)/shard_map/attend_forward/pallas_call | solution.py:123
  95.7 7.0 %collective-permute-done.9 = bf16[4,96,768]{2,1,0:T(8,128)(2,1)} collective-permute-done((bf16[4,96,768]{2,1,0:T(8,128)(2,1)S(1)}, bf16[4,96,768]{2,1,0:T(8,128)(2,1)}, u32[]{:S(2)}, u32[]{:S(2)}) %collective-permute-start.9) | collective-permute-done | bytes 589856 | tf_op jit(solution)/shard_map/ppermute | solution.py:599
  109.0 10.9 %attend_forward.3 = (bf16[1024,768]{1,0:T(8,128)(2,1)}, f32[12,2,512]{2,1,0:T(2,128)}) custom-call(s32[2]{0:T(128)} %len_ref.13, bf16[1024,2304]{1,0:T(8,128)(2,1)} %project_qkv.1.q_ref.k_ref.v_ref, bf16[1024,2304]{1,0:T(8,128)(2,1)} %project_qkv.1.q_ref.k_ref.v_ref, ...), custom_call_target="tpu_custom_call", output_to_operand_aliasing={{0}: (4, {}), {1}: (5, {})} | custom-call | flops 3221225472 | bytes 3145728 | tf_op jit(solution)/shard_map/attend_forward/pallas_call | solution.py:123
  119.9 5.5 %lay_out.3.w_down = bf16[3072,768]{1,0:T(8,128)(2,1)} custom-call(s32[16]{0:T(128)} %broadcast_xor_fusion.2.index_ref, s32[1]{0:T(128)} %bitcast.odd_ref, bf16[16,96,768]{2,1,0:T(8,128)(2,1)} %copy-done.3, bf16[16,96,768]{2,1,0:T(8,128)(2,1)} %collective-permute-done.11.taken_ref), custom_call_target="tpu_custom_call" | custom-call | flops 2359296 | bytes 9437184 | tf_op jit(solution)/shard_map/lay_out/pallas_call | solution.py:728
  125.4 39.1 %middle.1 = (bf16[1024,768]{1,0:T(8,128)(2,1)}, bf16[1024,768]{1,0:T(8,128)(2,1)}, bf16[1024,3072]{1,0:T(8,128)(2,1)}, bf16[1024,3072]{1,0:T(8,128)(2,1)}, bf16[...) custom-call(s32[2]{0:T(128)} %len_ref.13, ...), custom_call_target="tpu_custom_call" | custom-call | flops 21743271936 | bytes 37748736 | tf_op jit(solution)/shard_map/middle/pallas_call | solution.py:346
  164.5 11.5 %tall_gradient.1 = (bf16[16,96,768]{2,1,0:T(8,128)(2,1)}, bf16[16,96,768]{2,1,0:T(8,128)(2,1)}) custom-call(s32[32]{0:T(128)} %get-tuple-element.204.slot_ref, bf16[1024,3072]{1,0:T(8,128)(2,1)} %get-tuple-element.101.left_ref, bf16[1024,768]{1,0:T(8,128)(2,1)} %get-tuple-element.102.right_ref), custom_call_target="tpu_custom_call" | custom-call | flops 4831838208 | bytes 12582912 | tf_op jit(solution)/shard_map/tall_gradient/pallas_call | solution.py:551
  176.5 13.0 %joint_gradient.1 = (bf16[16,24,3840]{2,1,0:T(8,128)(2,1)}, bf16[16,24,3840]{2,1,0:T(8,128)(2,1)}) custom-call(s32[32]{0:T(128)} %get-tuple-element.205.src_ref, bf16[1024,768]{1,0:T(8,128)(2,1)} %get-tuple-element.99.left_ref, bf16[1024,768]{1,0:T(8,128)(2,1)} %get-tuple-element.96.mixed_ref.last_left_ref, bf16[1024,3072]{1,0:T(8,128)(2,1)} %get-tuple-element.105.right_ref, ...), custom_call_target="tpu_custom_call" | custom-call | flops 48318382080 | bytes 16908288 | tf_op jit(solution)/shard_map/joint_gradient/pallas_call | solution.py:484
  190.2 2.1 add_convert_fusion.2
  192.3 1.4 collective-permute-start.15
  193.7 9.1 %attend_backward.4.refs_0_ = bf16[3,1024,384]{2,1,0:T(8,128)(2,1)} custom-call(s32[2]{0:T(128)} %len_ref.13, bf16[1024,2304]{1,0:T(8,128)(2,1)} %project_qkv.1.q_ref.k_ref.v_ref, bf16[1024,2304]{1,0:T(8,128)(2,1)} %project_qkv.1.q_ref.k_ref.v_ref, bf16[1024,2304]{1,0:T(8,128)(2,1)} %project_qkv.1.q_ref.k_ref.v_ref, ...), custom_call_target="tpu_custom_call" | custom-call | flops 32212254720 | bytes 2752512 | tf_op jit(solution)/shard_map/attend_backward/pallas_call | solution.py:189
  202.9 2.3 add_convert_fusion
  205.7 8.9 %attend_backward.5.right_ref.refs_0_ = bf16[3,1024,384]{2,1,0:T(8,128)(2,1)} custom-call(s32[2]{0:T(128)} %len_ref.13, bf16[1024,2304]{1,0:T(8,128)(2,1)} %project_qkv.1.q_ref.k_ref.v_ref, bf16[1024,2304]{1,0:T(8,128)(2,1)} %project_qkv.1.q_ref.k_ref.v_ref, bf16[1024,2304]{1,0:T(8,128)(2,1)} %project_qkv.1.q_ref.k_ref.v_ref, ...), custom_call_target="tpu_custom_call", output_to_operand_aliasing={{}: (6, {})} | custom-call | flops 32212254720 | bytes 2752512 | tf_op jit(solution)/shard_map/attend_backward/pallas_call | solution.py:189
  214.6 6.8 %weight_gradient.2 = (bf16[16,24,1152]{2,1,0:T(8,128)(2,1)}, bf16[16,24,1152]{2,1,0:T(8,128)(2,1)}, f32[3,8,384]{2,1,0:T(8,128)}) custom-call(s32[32]{0:T(128)} %broadcast_xor_fusion.src_ref, bf16[1024,768]{1,0:T(8,128)(2,1)} %left_ref.2, bf16[3,1024,384]{2,1,0:T(8,128)(2,1)} %attend_backward.5.right_ref.refs_0_), custom_call_target="tpu_custom_call" | custom-call | flops 115964116992 | bytes 5701632 | tf_op jit(solution)/shard_map/weight_gradient/pallas_call | solution.py:431
  221.4 1.4 constant_dynamic-update-slice_fusion.11
  222.8 1.5 add_convert_fusion.6
  224.3 1.5 collective-permute-start.17
  225.9 9.3 %attend_backward.6.refs_0_ = bf16[3,1024,384]{2,1,0:T(8,128)(2,1)} custom-call(s32[2]{0:T(128)} %len_ref.13, bf16[1024,2304]{1,0:T(8,128)(2,1)} %project_qkv.1.q_ref.k_ref.v_ref, bf16[1024,2304]{1,0:T(8,128)(2,1)} %project_qkv.1.q_ref.k_ref.v_ref, bf16[1024,2304]{1,0:T(8,128)(2,1)} %project_qkv.1.q_ref.k_ref.v_ref, ...), custom_call_target="tpu_custom_call" | custom-call | flops 32212254720 | bytes 2752512 | tf_op jit(solution)/shard_map/attend_backward/pallas_call | solution.py:189
  236.1 8.9 %attend_backward.7.right_ref.refs_1_ = bf16[3,1024,384]{2,1,0:T(8,128)(2,1)} custom-call(s32[2]{0:T(128)} %len_ref.13, bf16[1024,2304]{1,0:T(8,128)(2,1)} %project_qkv.1.q_ref.k_ref.v_ref, bf16[1024,2304]{1,0:T(8,128)(2,1)} %project_qkv.1.q_ref.k_ref.v_ref, bf16[1024,2304]{1,0:T(8,128)(2,1)} %project_qkv.1.q_ref.k_ref.v_ref, ...), custom_call_target="tpu_custom_call", output_to_operand_aliasing={{}: (6, {})} | custom-call | flops 32212254720 | bytes 2752512 | tf_op jit(solution)/shard_map/attend_backward/pallas_call | solution.py:189
  245.0 7.4 %collective-permute-done.17 = bf16[4,96,768]{2,1,0:T(8,128)(2,1)S(1)} collective-permute-done((bf16[4,96,768]{2,1,0:T(8,128)(2,1)S(1)}, bf16[4,96,768]{2,1,0:T(8,128)(2,1)S(1)}, u32[]{:S(2)}, u32[]{:S(2)}) %collective-permute-start.17) | collective-permute-done | bytes 589856 | tf_op jit(solution)/shard_map/ppermute | solution.py:599
  253.3 1.5 collective-permute-start.20
  256.0 2.8 add_convert_fusion.4
  259.1 6.7 %weight_gradient.3 = (bf16[16,24,1152]{2,1,0:T(8,128)(2,1)}, bf16[16,24,1152]{2,1,0:T(8,128)(2,1)}, f32[3,8,384]{2,1,0:T(8,128)}) custom-call(s32[32]{0:T(128)} %get-tuple-element.205.src_ref, bf16[1024,768]{1,0:T(8,128)(2,1)} %left_ref.2, bf16[3,1024,384]{2,1,0:T(8,128)(2,1)} %attend_backward.7.right_ref.refs_1_), custom_call_target="tpu_custom_call" | custom-call | flops 115964116992 | bytes 5701632 | tf_op jit(solution)/shard_map/weight_gradient/pallas_call | solution.py:431
  268.3 6.3 %input_gradient.2.refs_2_ = bf16[1024,768]{1,0:T(8,128)(2,1)} custom-call(f32[1024,768]{1,0:T(8,128)} %get-tuple-element.146.resid_ref, bf16[768,2432]{1,0:T(8,128)(2,1)} %lay_out.2.w_ref, bf16[3,1024,384]{2,1,0:T(8,128)(2,1)} %attend_backward.5.right_ref.refs_0_, bf16[3,1024,384]{2,1,0:T(8,128)(2,1)} %attend_backward.7.right_ref.refs_1_), custom_call_target="tpu_custom_call" | custom-call | flops 115964116992 | bytes 6488064 | tf_op jit(solution)/shard_map/input_gradient/pallas_call | solution.py:576
  274.6 1.1 add_convert_fusion.22
  275.7 2.4 collective-permute-start.32
  279.8 1.3 add_convert_fusion.10
  281.0 1.6 collective-permute-start.30
  282.9 1.3 collective-permute-start.25
  284.1 1.7 collective-permute-start.26
  285.9 6.2 %input_gradient.3 = bf16[1024,768]{1,0:T(8,128)(2,1)} custom-call(f32[1024,768]{1,0:T(8,128)} %get-tuple-element.146.resid_ref, bf16[768,2432]{1,0:T(8,128)(2,1)} %lay_out.2.w_ref, bf16[3,1024,384]{2,1,0:T(8,128)(2,1)} %attend_backward.5.right_ref.refs_0_, bf16[3,1024,384]{2,1,0:T(8,128)(2,1)} %attend_backward.7.right_ref.refs_1_, ...), custom_call_target="tpu_custom_call", output_to_operand_aliasing={{}: (4, {})} | custom-call | flops 115964116992 | bytes 6488064 | tf_op jit(solution)/shard_map/input_gradient/pallas_call | solution.py:576
  294.5 3.8 %collective-permute-done.24 = bf16[1,24,1152]{2,1,0:T(8,128)(2,1)S(1)} collective-permute-done((bf16[1,24,1152]{2,1,0:T(8,128)(2,1)S(1)}, bf16[1,24,1152]{2,1,0:T(8,128)(2,1)S(1)}, u32[]{:S(2)}, u32[]{:S(2)}) %collective-permute-start.24) | collective-permute-done | bytes 55328 | tf_op jit(solution)/shard_map/ppermute | solution.py:599
  298.6 1.3 collective-permute-done.27
  300.5 6.7 %collective-permute-done.31 = bf16[1,24,3840]{2,1,0:T(8,128)(2,1)S(1)} collective-permute-done((bf16[1,24,3840]{2,1,0:T(8,128)(2,1)S(1)}, bf16[1,24,3840]{2,1,0:T(8,128)(2,1)S(1)}, u32[]{:S(2)}, u32[]{:S(2)}) %collective-permute-start.31) | collective-permute-done | bytes 184352 | tf_op jit(solution)/shard_map/ppermute | solution.py:599
  309.3 4.4 %collective-permute-done.29 = bf16[1,24,1280]{2,1,0:T(8,128)(2,1)S(1)} collective-permute-done((bf16[1,24,1280]{2,1,0:T(8,128)(2,1)S(1)}, bf16[1,24,1280]{2,1,0:T(8,128)(2,1)S(1)}, u32[]{:S(2)}, u32[]{:S(2)}) %collective-permute-start.29) | collective-permute-done | bytes 61472 | tf_op jit(solution)/shard_map/ppermute | solution.py:599
  (179 shorter events, 35.5 us)
Async XLA Ops:
  7.2 15.1 %copy-start.8 = (f32[96,768]{1,0:T(8,128)S(1)}, f32[96,768]{1,0:T(8,128)}, u32[]{:S(2)}) copy-start(f32[96,768]{1,0:T(8,128)} %param.31) | copy-start | bytes 884740
  7.2 118.2 %all-gather.2.cloned.1.call-start = ((), (), s32[]{:S(2)}) async-start(), calls=%async_computation | async-start | bytes 6082560 | tf_op jit(solution)/shard_map/all_gather | solution.py:785
  11.6 9.8 %collective-permute-start = (bf16[1,24,2432]{2,1,0:T(8,128)(2,1)S(1)}, bf16[1,24,2432]{2,1,0:T(8,128)(2,1)S(1)}, u32[]{:S(2)}, u32[]{:S(2)}) collective-permute-start(bf16[1,24,2432]{2,1,0:T(8,128)(2,1)S(1)} %fusion.6), channel_id=1, source_target_pairs={{0,16},{1,17},{2,18},{3,19},{4,20},{5,21},{6,22},{7,23},{8,24},{9,... | collective-permute-start | bytes 350216 | tf_op jit(solution)/shard_map/ppermute | solution.py:599
  21.5 8.6 %collective-permute-start.1 = (bf16[2,24,2432]{2,1,0:T(8,128)(2,1)S(1)}, bf16[2,24,2432]{2,1,0:T(8,128)(2,1)S(1)}, u32[]{:S(2)}, u32[]{:S(2)}) collective-permute-start(bf16[2,24,2432]{2,1,0:T(8,128)(2,1)S(1)} %pad_maximum_fusion.5), channel_id=1, source_target_pairs={{0,8},{1,9},{2,10},{3,11},{4,12},{5,13},{6,14},{7,15},{8,0},{9,1},... | collective-permute-start | bytes 700424 | tf_op jit(solution)/shard_map/ppermute | solution.py:599
  30.1 11.3 %collective-permute-start.5 = (bf16[1,96,768]{2,1,0:T(8,128)(2,1)S(1)}, bf16[1,96,768]{2,1,0:T(8,128)(2,1)S(1)}, u32[]{:S(2)}, u32[]{:S(2)}) collective-permute-start(bf16[1,96,768]{2,1,0:T(8,128)(2,1)S(1)} %convert_bitcast_fusion), channel_id=1, source_target_pairs={{0,16},{1,17},{2,18},{3,19},{4,20},{5,21},{6,22},{7,23},{8,24},{9,... | collective-permute-start | bytes 442376 | tf_op jit(solution)/shard_map/ppermute | solution.py:599
  35.2 18.9 %collective-permute-start.2 = (bf16[4,24,2432]{2,1,0:T(8,128)(2,1)S(1)}, bf16[4,24,2432]{2,1,0:T(8,128)(2,1)S(1)}, u32[]{:S(2)}, u32[]{:S(2)}) collective-permute-start(bf16[4,24,2432]{2,1,0:T(8,128)(2,1)S(1)} %pad_maximum_fusion.3), channel_id=1, source_target_pairs={{0,2},{1,3},{2,0},{3,1},{4,6},{5,7},{6,4},{7,5},{8,10},{9,11},{10,... | collective-permute-start | bytes 1400840 | tf_op jit(solution)/shard_map/ppermute | solution.py:599
  36.6 18.3 %collective-permute-start.3 = (bf16[4,24,2432]{2,1,0:T(8,128)(2,1)S(1)}, bf16[4,24,2432]{2,1,0:T(8,128)(2,1)S(1)}, u32[]{:S(2)}, u32[]{:S(2)}) collective-permute-start(bf16[4,24,2432]{2,1,0:T(8,128)(2,1)S(1)} %pad_maximum_fusion.3), channel_id=1, source_target_pairs={{0,4},{1,5},{2,6},{3,7},{4,0},{5,1},{6,2},{7,3},{8,12},{9,13},{10,... | collective-permute-start | bytes 1400840 | tf_op jit(solution)/shard_map/ppermute | solution.py:599
  38.2 24.6 %collective-permute-start.4 = (bf16[4,24,2432]{2,1,0:T(8,128)(2,1)S(1)}, bf16[4,24,2432]{2,1,0:T(8,128)(2,1)S(1)}, u32[]{:S(2)}, u32[]{:S(2)}) collective-permute-start(bf16[4,24,2432]{2,1,0:T(8,128)(2,1)S(1)} %pad_maximum_fusion.3), channel_id=1, source_target_pairs={{0,6},{1,7},{2,4},{3,5},{4,2},{5,3},{6,0},{7,1},{8,14},{9,15},{10,... | collective-permute-start | bytes 1400840 | tf_op jit(solution)/shard_map/ppermute | solution.py:599
  41.4 12.6 %collective-permute-start.6 = (bf16[2,96,768]{2,1,0:T(8,128)(2,1)S(1)}, bf16[2,96,768]{2,1,0:T(8,128)(2,1)S(1)}, u32[]{:S(2)}, u32[]{:S(2)}) collective-permute-start(bf16[2,96,768]{2,1,0:T(8,128)(2,1)S(1)} %pad_maximum_fusion.4), channel_id=1, source_target_pairs={{0,8},{1,9},{2,10},{3,11},{4,12},{5,13},{6,14},{7,15},{8,0},{9,1},... | collective-permute-start | bytes 884744 | tf_op jit(solution)/shard_map/ppermute | solution.py:599
  42.3 21.3 %copy-start.33 = (s32[16]{0:T(128)S(1)}, s32[16]{0:T(128)}, u32[]{:S(2)}) copy-start(s32[16]{0:T(128)} %constant.46.clone) | copy-start | bytes 196
  63.7 6.0 %collective-permute-start.7 = (bf16[16,24,2432]{2,1,0:T(8,128)(2,1)}, bf16[16,24,2432]{2,1,0:T(8,128)(2,1)}, u32[]{:S(2)}, u32[]{:S(2)}) collective-permute-start(bf16[16,24,2432]{2,1,0:T(8,128)(2,1)} %constant_dynamic-update-slice_fusion.held_ref), channel_id=1, source_target_pairs={{0,1},{1,0},{2,3},{3,2},{4,5},{5,4},{6,7},{7,6},{8,9},{9,8},{10,11... | collective-permute-start | bytes 5603336 | tf_op jit(solution)/shard_map/ppermute | solution.py:599
  64.2 31.5 %collective-permute-start.10 = (bf16[4,96,768]{2,1,0:T(8,128)(2,1)S(1)}, bf16[4,96,768]{2,1,0:T(8,128)(2,1)}, u32[]{:S(2)}, u32[]{:S(2)}) collective-permute-start(bf16[4,96,768]{2,1,0:T(8,128)(2,1)S(1)} %pad_maximum_fusion.2), channel_id=1, source_target_pairs={{0,6},{1,7},{2,4},{3,5},{4,2},{5,3},{6,0},{7,1},{8,14},{9,15},{10,... | collective-permute-start | bytes 1769480 | tf_op jit(solution)/shard_map/ppermute | solution.py:599
  65.5 37.2 %collective-permute-start.9 = (bf16[4,96,768]{2,1,0:T(8,128)(2,1)S(1)}, bf16[4,96,768]{2,1,0:T(8,128)(2,1)}, u32[]{:S(2)}, u32[]{:S(2)}) collective-permute-start(bf16[4,96,768]{2,1,0:T(8,128)(2,1)S(1)} %pad_maximum_fusion.2), channel_id=1, source_target_pairs={{0,4},{1,5},{2,6},{3,7},{4,0},{5,1},{6,2},{7,3},{8,12},{9,13},{10,... | collective-permute-start | bytes 1769480 | tf_op jit(solution)/shard_map/ppermute | solution.py:599
  67.4 35.3 %collective-permute-start.8 = (bf16[4,96,768]{2,1,0:T(8,128)(2,1)S(1)}, bf16[4,96,768]{2,1,0:T(8,128)(2,1)}, u32[]{:S(2)}, u32[]{:S(2)}) collective-permute-start(bf16[4,96,768]{2,1,0:T(8,128)(2,1)S(1)} %pad_maximum_fusion.2), channel_id=1, source_target_pairs={{0,2},{1,3},{2,0},{3,1},{4,6},{5,7},{6,4},{7,5},{8,10},{9,11},{10,... | collective-permute-start | bytes 1769480 | tf_op jit(solution)/shard_map/ppermute | solution.py:599
  95.7 10.5 %copy-start = (s32[32]{0:T(128)S(1)}, s32[32]{0:T(128)}, u32[]{:S(2)}) copy-start(s32[32]{0:T(128)} %constant.45.clone) | copy-start | bytes 388
  95.7 11.2 %copy-start.32 = (s32[32]{0:T(128)S(1)}, s32[32]{0:T(128)}, u32[]{:S(2)}) copy-start(s32[32]{0:T(128)} %constant.47.clone) | copy-start | bytes 388
  106.0 13.9 %copy-start.3 = (bf16[16,96,768]{2,1,0:T(8,128)(2,1)}, bf16[16,96,768]{2,1,0:T(8,128)(2,1)S(1)}, u32[]{:S(2)}) copy-start(bf16[16,96,768]{2,1,0:T(8,128)(2,1)S(1)} %constant_dynamic-update-slice_fusion.6.held_ref) | copy-start | bytes 7077892
  106.0 13.9 %collective-permute-start.11 = (bf16[16,96,768]{2,1,0:T(8,128)(2,1)S(1)}, bf16[16,96,768]{2,1,0:T(8,128)(2,1)}, u32[]{:S(2)}, u32[]{:S(2)}) collective-permute-start(bf16[16,96,768]{2,1,0:T(8,128)(2,1)S(1)} %constant_dynamic-update-slice_fusion.6.held_ref), channel_id=1, source_target_pairs={{0,1},{1,0},{2,3},{3,2},{4,5},{5,4},{6,7},{7,6},{8,9},{9,8},{10,11... | collective-permute-start | bytes 7077896 | tf_op jit(solution)/shard_map/ppermute | solution.py:599
  176.1 14.1 %collective-permute-start.13 = (bf16[16,96,768]{2,1,0:T(8,128)(2,1)}, bf16[16,96,768]{2,1,0:T(8,128)(2,1)S(1)}, u32[]{:S(2)}, u32[]{:S(2)}) collective-permute-start(bf16[16,96,768]{2,1,0:T(8,128)(2,1)} %get-tuple-element.104), channel_id=1, source_target_pairs={{0,1},{1,0},{2,3},{3,2},{4,5},{5,4},{6,7},{7,6},{8,9},{9,8},{10,11... | collective-permute-start | bytes 7077896 | tf_op jit(solution)/shard_map/ppermute | solution.py:599
  176.5 13.1 %copy-start.27 = (f32[12,768]{1,0:T(8,128)S(1)}, f32[12,768]{1,0:T(8,128)}, u32[]{:S(2)}) copy-start(f32[12,768]{1,0:T(8,128)} %get-tuple-element.135) | copy-start | bytes 110596
  176.5 13.7 %copy-start.6 = (bf16[16,96,768]{2,1,0:T(8,128)(2,1)S(1)}, bf16[16,96,768]{2,1,0:T(8,128)(2,1)}, u32[]{:S(2)}) copy-start(bf16[16,96,768]{2,1,0:T(8,128)(2,1)} %get-tuple-element.110) | copy-start | bytes 7077892
  189.5 13.4 %collective-permute-start.12 = (bf16[16,24,3840]{2,1,0:T(8,128)(2,1)}, bf16[16,24,3840]{2,1,0:T(8,128)(2,1)S(1)}, u32[]{:S(2)}, u32[]{:S(2)}) collective-permute-start(bf16[16,24,3840]{2,1,0:T(8,128)(2,1)} %get-tuple-element.108), channel_id=1, source_target_pairs={{0,1},{1,0},{2,3},{3,2},{4,5},{5,4},{6,7},{7,6},{8,9},{9,8},{10,11... | collective-permute-start | bytes 8847368 | tf_op jit(solution)/shard_map/ppermute | solution.py:599
  192.3 30.5 %collective-permute-start.15 = (bf16[8,96,768]{2,1,0:T(8,128)(2,1)}, bf16[8,96,768]{2,1,0:T(8,128)(2,1)}, u32[]{:S(2)}, u32[]{:S(2)}) collective-permute-start(bf16[8,96,768]{2,1,0:T(8,128)(2,1)} %get-tuple-element.176), channel_id=1, source_target_pairs={{0,2},{1,3},{2,0},{3,1},{4,6},{5,7},{6,4},{7,5},{8,10},{9,11},{10,... | collective-permute-start | bytes 3538952 | tf_op jit(solution)/shard_map/ppermute | solution.py:599
  193.7 9.1 %copy-start.4 = (bf16[16,24,3840]{2,1,0:T(8,128)(2,1)S(1)}, bf16[16,24,3840]{2,1,0:T(8,128)(2,1)}, u32[]{:S(2)}) copy-start(bf16[16,24,3840]{2,1,0:T(8,128)(2,1)} %get-tuple-element.114) | copy-start | bytes 8847364
  205.1 50.9 %collective-permute-start.14 = (bf16[8,24,3840]{2,1,0:T(8,128)(2,1)}, bf16[8,24,3840]{2,1,0:T(8,128)(2,1)}, u32[]{:S(2)}, u32[]{:S(2)}) collective-permute-start(bf16[8,24,3840]{2,1,0:T(8,128)(2,1)} %get-tuple-element.174), channel_id=1, source_target_pairs={{0,4},{1,5},{2,6},{3,7},{4,0},{5,1},{6,2},{7,3},{8,12},{9,13},{10,... | collective-permute-start | bytes 4423688 | tf_op jit(solution)/shard_map/ppermute | solution.py:599
  221.4 13.8 %collective-permute-start.16 = (bf16[16,24,1152]{2,1,0:T(8,128)(2,1)}, bf16[16,24,1152]{2,1,0:T(8,128)(2,1)S(1)}, u32[]{:S(2)}, u32[]{:S(2)}) collective-permute-start(bf16[16,24,1152]{2,1,0:T(8,128)(2,1)} %get-tuple-element.121), channel_id=1, source_target_pairs={{0,1},{1,0},{2,3},{3,2},{4,5},{5,4},{6,7},{7,6},{8,9},{9,8},{10,11... | collective-permute-start | bytes 2654216 | tf_op jit(solution)/shard_map/ppermute | solution.py:599
  224.3 28.1 %collective-permute-start.17 = (bf16[4,96,768]{2,1,0:T(8,128)(2,1)S(1)}, bf16[4,96,768]{2,1,0:T(8,128)(2,1)S(1)}, u32[]{:S(2)}, u32[]{:S(2)}) collective-permute-start(bf16[4,96,768]{2,1,0:T(8,128)(2,1)S(1)} %get-tuple-element.180), channel_id=1, source_target_pairs={{0,4},{1,5},{2,6},{3,7},{4,0},{5,1},{6,2},{7,3},{8,12},{9,13},{10,... | collective-permute-start | bytes 1769480 | tf_op jit(solution)/shard_map/ppermute | solution.py:599
  225.9 9.3 %copy-start.14 = (bf16[16,24,1152]{2,1,0:T(8,128)(2,1)S(1)}, bf16[16,24,1152]{2,1,0:T(8,128)(2,1)}, u32[]{:S(2)}) copy-start(bf16[16,24,1152]{2,1,0:T(8,128)(2,1)} %get-tuple-element.122) | copy-start | bytes 2654212
  235.4 19.4 %collective-permute-start.18 = (bf16[8,24,1152]{2,1,0:T(8,128)(2,1)S(1)}, bf16[8,24,1152]{2,1,0:T(8,128)(2,1)S(1)}, u32[]{:S(2)}, u32[]{:S(2)}) collective-permute-start(bf16[8,24,1152]{2,1,0:T(8,128)(2,1)S(1)} %get-tuple-element.186), channel_id=1, source_target_pairs={{0,2},{1,3},{2,0},{3,1},{4,6},{5,7},{6,4},{7,5},{8,10},{9,11},{10,... | collective-permute-start | bytes 1327112 | tf_op jit(solution)/shard_map/ppermute | solution.py:599
  245.0 11.0 %copy-start.1 = (bf16[8,24,3840]{2,1,0:T(8,128)(2,1)S(1)}, bf16[8,24,3840]{2,1,0:T(8,128)(2,1)}, u32[]{:S(2)}) copy-start(bf16[8,24,3840]{2,1,0:T(8,128)(2,1)} %get-tuple-element.125) | copy-start | bytes 4423684
  253.3 21.2 %collective-permute-start.20 = (bf16[2,96,768]{2,1,0:T(8,128)(2,1)}, bf16[2,96,768]{2,1,0:T(8,128)(2,1)}, u32[]{:S(2)}, u32[]{:S(2)}) collective-permute-start(bf16[2,96,768]{2,1,0:T(8,128)(2,1)} %get-tuple-element.190), channel_id=1, source_target_pairs={{0,8},{1,9},{2,10},{3,11},{4,12},{5,13},{6,14},{7,15},{8,0},{9,1},... | collective-permute-start | bytes 884744 | tf_op jit(solution)/shard_map/ppermute | solution.py:599
  255.7 22.5 %collective-permute-start.21 = (bf16[4,24,1152]{2,1,0:T(8,128)(2,1)}, bf16[4,24,1152]{2,1,0:T(8,128)(2,1)}, u32[]{:S(2)}, u32[]{:S(2)}) collective-permute-start(bf16[4,24,1152]{2,1,0:T(8,128)(2,1)} %get-tuple-element.194), channel_id=1, source_target_pairs={{0,4},{1,5},{2,6},{3,7},{4,0},{5,1},{6,2},{7,3},{8,12},{9,13},{10,... | collective-permute-start | bytes 663560 | tf_op jit(solution)/shard_map/ppermute | solution.py:599
  258.8 20.9 %collective-permute-start.19 = (bf16[4,24,3840]{2,1,0:T(8,128)(2,1)}, bf16[4,24,3840]{2,1,0:T(8,128)(2,1)}, u32[]{:S(2)}, u32[]{:S(2)}) collective-permute-start(bf16[4,24,3840]{2,1,0:T(8,128)(2,1)} %get-tuple-element.178), channel_id=1, source_target_pairs={{0,2},{1,3},{2,0},{3,1},{4,6},{5,7},{6,4},{7,5},{8,10},{9,11},{10,... | collective-permute-start | bytes 2211848 | tf_op jit(solution)/shard_map/ppermute | solution.py:599
  268.2 14.4 %collective-permute-start.22 = (bf16[16,24,1280]{2,1,0:T(8,128)(2,1)S(1)}, bf16[16,24,1280]{2,1,0:T(8,128)(2,1)S(1)}, u32[]{:S(2)}, u32[]{:S(2)}) collective-permute-start(bf16[16,24,1280]{2,1,0:T(8,128)(2,1)S(1)} %pad_maximum_fusion), channel_id=1, source_target_pairs={{0,1},{1,0},{2,3},{3,2},{4,5},{5,4},{6,7},{7,6},{8,9},{9,8},{10,11... | collective-permute-start | bytes 2949128 | tf_op jit(solution)/shard_map/ppermute | solution.py:599
  268.3 9.8 %copy-start.12 = (bf16[16,24,1152]{2,1,0:T(8,128)(2,1)S(1)}, bf16[16,24,1152]{2,1,0:T(8,128)(2,1)}, u32[]{:S(2)}) copy-start(bf16[16,24,1152]{2,1,0:T(8,128)(2,1)} %get-tuple-element.143) | copy-start | bytes 2654212
  275.7 16.5 %collective-permute-start.32 = (bf16[1,96,768]{2,1,0:T(8,128)(2,1)S(1)}, bf16[1,96,768]{2,1,0:T(8,128)(2,1)S(1)}, u32[]{:S(2)}, u32[]{:S(2)}) collective-permute-start(bf16[1,96,768]{2,1,0:T(8,128)(2,1)S(1)} %get-tuple-element.196), channel_id=1, source_target_pairs={{0,16},{1,17},{2,18},{3,19},{4,20},{5,21},{6,22},{7,23},{8,24},{9,... | collective-permute-start | bytes 442376 | tf_op jit(solution)/shard_map/ppermute | solution.py:599
  279.2 13.5 %collective-permute-start.23 = (bf16[2,24,1152]{2,1,0:T(8,128)(2,1)S(1)}, bf16[2,24,1152]{2,1,0:T(8,128)(2,1)S(1)}, u32[]{:S(2)}, u32[]{:S(2)}) collective-permute-start(bf16[2,24,1152]{2,1,0:T(8,128)(2,1)S(1)} %get-tuple-element.198), channel_id=1, source_target_pairs={{0,8},{1,9},{2,10},{3,11},{4,12},{5,13},{6,14},{7,15},{8,0},{9,1},... | collective-permute-start | bytes 331784 | tf_op jit(solution)/shard_map/ppermute | solution.py:599
  281.0 17.4 %collective-permute-start.30 = (bf16[2,24,3840]{2,1,0:T(8,128)(2,1)S(1)}, bf16[2,24,3840]{2,1,0:T(8,128)(2,1)S(1)}, u32[]{:S(2)}, u32[]{:S(2)}) collective-permute-start(bf16[2,24,3840]{2,1,0:T(8,128)(2,1)S(1)} %get-tuple-element.188), channel_id=1, source_target_pairs={{0,8},{1,9},{2,10},{3,11},{4,12},{5,13},{6,14},{7,15},{8,0},{9,1},... | collective-permute-start | bytes 1105928 | tf_op jit(solution)/shard_map/ppermute | solution.py:599
  282.9 15.8 %collective-permute-start.25 = (bf16[4,24,1280]{2,1,0:T(8,128)(2,1)S(1)}, bf16[4,24,1280]{2,1,0:T(8,128)(2,1)S(1)}, u32[]{:S(2)}, u32[]{:S(2)}) collective-permute-start(bf16[4,24,1280]{2,1,0:T(8,128)(2,1)S(1)} %get-tuple-element.184), channel_id=1, source_target_pairs={{0,2},{1,3},{2,0},{3,1},{4,6},{5,7},{6,4},{7,5},{8,10},{9,11},{10,... | collective-permute-start | bytes 737288 | tf_op jit(solution)/shard_map/ppermute | solution.py:599
  284.1 14.5 %collective-permute-start.26 = (bf16[4,24,1280]{2,1,0:T(8,128)(2,1)S(1)}, bf16[4,24,1280]{2,1,0:T(8,128)(2,1)S(1)}, u32[]{:S(2)}, u32[]{:S(2)}) collective-permute-start(bf16[4,24,1280]{2,1,0:T(8,128)(2,1)S(1)} %get-tuple-element.183), channel_id=1, source_target_pairs={{0,4},{1,5},{2,6},{3,7},{4,0},{5,1},{6,2},{7,3},{8,12},{9,13},{10,... | collective-permute-start | bytes 737288 | tf_op jit(solution)/shard_map/ppermute | solution.py:599
  292.1 7.8 %collective-permute-start.27 = (bf16[4,24,1280]{2,1,0:T(8,128)(2,1)S(1)}, bf16[4,24,1280]{2,1,0:T(8,128)(2,1)S(1)}, u32[]{:S(2)}, u32[]{:S(2)}) collective-permute-start(bf16[4,24,1280]{2,1,0:T(8,128)(2,1)S(1)} %get-tuple-element.182), channel_id=1, source_target_pairs={{0,6},{1,7},{2,4},{3,5},{4,2},{5,3},{6,0},{7,1},{8,14},{9,15},{10,... | collective-permute-start | bytes 737288 | tf_op jit(solution)/shard_map/ppermute | solution.py:599
  292.7 5.6 %collective-permute-start.24 = (bf16[1,24,1152]{2,1,0:T(8,128)(2,1)S(1)}, bf16[1,24,1152]{2,1,0:T(8,128)(2,1)S(1)}, u32[]{:S(2)}, u32[]{:S(2)}) collective-permute-start(bf16[1,24,1152]{2,1,0:T(8,128)(2,1)S(1)} %add_convert_fusion.30), channel_id=1, source_target_pairs={{0,16},{1,17},{2,18},{3,19},{4,20},{5,21},{6,22},{7,23},{8,24},{9,... | collective-permute-start | bytes 165896 | tf_op jit(solution)/shard_map/ppermute | solution.py:599
  294.5 12.8 %copy-start.10 = (f32[24,3072]{1,0:T(8,128)S(1)}, f32[24,3072]{1,0:T(8,128)}, u32[]{:S(2)}) copy-start(f32[24,3072]{1,0:T(8,128)} %param.30) | copy-start | bytes 884740
  294.5 12.8 %copy-start.19 = (f32[24,3072]{1,0:T(8,128)S(1)}, f32[24,3072]{1,0:T(8,128)}, u32[]{:S(2)}) copy-start(f32[24,3072]{1,0:T(8,128)} %param.40) | copy-start | bytes 884740
  294.5 12.8 %copy-start.20 = (f32[24,3072]{1,0:T(8,128)S(1)}, f32[24,3072]{1,0:T(8,128)}, u32[]{:S(2)}) copy-start(f32[24,3072]{1,0:T(8,128)} %param.35) | copy-start | bytes 884740
  298.4 8.8 %collective-permute-start.31 = (bf16[1,24,3840]{2,1,0:T(8,128)(2,1)S(1)}, bf16[1,24,3840]{2,1,0:T(8,128)(2,1)S(1)}, u32[]{:S(2)}, u32[]{:S(2)}) collective-permute-start(bf16[1,24,3840]{2,1,0:T(8,128)(2,1)S(1)} %add_convert_fusion.20), channel_id=1, source_target_pairs={{0,16},{1,17},{2,18},{3,19},{4,20},{5,21},{6,22},{7,23},{8,24},{9,... | collective-permute-start | bytes 552968 | tf_op jit(solution)/shard_map/ppermute | solution.py:599
  300.1 8.3 %collective-permute-start.28 = (bf16[2,24,1280]{2,1,0:T(8,128)(2,1)S(1)}, bf16[2,24,1280]{2,1,0:T(8,128)(2,1)S(1)}, u32[]{:S(2)}, u32[]{:S(2)}) collective-permute-start(bf16[2,24,1280]{2,1,0:T(8,128)(2,1)S(1)} %get-tuple-element.193), channel_id=1, source_target_pairs={{0,8},{1,9},{2,10},{3,11},{4,12},{5,13},{6,14},{7,15},{8,0},{9,1},... | collective-permute-start | bytes 368648 | tf_op jit(solution)/shard_map/ppermute | solution.py:599
  308.5 5.2 %collective-permute-start.29 = (bf16[1,24,1280]{2,1,0:T(8,128)(2,1)S(1)}, bf16[1,24,1280]{2,1,0:T(8,128)(2,1)S(1)}, u32[]{:S(2)}, u32[]{:S(2)}) collective-permute-start(bf16[1,24,1280]{2,1,0:T(8,128)(2,1)S(1)} %add_convert_fusion.28), channel_id=1, source_target_pairs={{0,16},{1,17},{2,18},{3,19},{4,20},{5,21},{6,22},{7,23},{8,24},{9,... | collective-permute-start | bytes 184328 | tf_op jit(solution)/shard_map/ppermute | solution.py:599
  (20 other events, 135.4 us)
Sparse Core Ops, SparseCore 0:
  11.5 100.3 all-gather.1

commit v4 on v3

--- a/solution.py
+++ b/solution.py
@@ -21,7 +21,6 @@
 
 LANES = 128
 ROWS = 256
-GROUPS = 2
 VMEM_BYTES = 56 * 1024 * 1024
 BF = jnp.bfloat16
 F32 = jnp.float32
@@ -166,13 +165,17 @@
     out_ref[2] = grad_v.astype(BF)
 
 
-def attend_backward(packed, lengths, lse, grad_mixed, group, which, filled):
+def pair_groups(pairs):
+    first = 2 * pairs // 3
+    return ((0, first), (first, pairs - first))
+
+
+def attend_backward(packed, lengths, lse, grad_mixed, span, which, filled):
     rows, width = grad_mixed.shape
     batch = lengths.shape[0]
     seq = rows // batch
     pairs = width // LANES
-    here = pairs // GROUPS
-    base = group * here
+    base, here = span
     grid_spec = pltpu.PrefetchScalarGridSpec(
         num_scalar_prefetch=1,
         grid=(here,),
@@ -238,12 +241,31 @@
     resid_ref,
     sum_ref,
     slope_ref,
-    *,
+    *down_refs,
     seq,
+    piece,
 ):
     step = pl.program_id(0)
     rows, width = x_ref.shape
     chunks = w_up.shape[1] // width
+    if down_refs:
+        columns_ref, w_down = w_down, down_refs[0]
+
+        @pl.when(step == 0)
+        def _():
+            def lay(pair, carry):
+                begin = pl.multiple_of(pair * 2 * piece, 16)
+                strips = [
+                    columns_ref[pl.ds(begin, 2 * piece), pl.ds(j * width, width)].astype(F32)
+                    for j in range(chunks)
+                ]
+                both = [strip[:piece] for strip in strips] + [strip[piece:] for strip in strips]
+                there = pl.multiple_of(pair * 2 * chunks * piece, 16)
+                w_down[pl.ds(there, 2 * chunks * piece), :] = jnp.concatenate(both, axis=0).astype(BF)
+                return carry
+
+            lax.fori_loop(0, width // (2 * piece), lay, 0)
+
     start = (step * rows) % seq
     length = len_ref[(step * rows) // seq]
 
@@ -309,9 +331,17 @@
         resid_ref[...] = jnp.zeros_like(resid_ref)
 
 
-def middle(x, mixed, cotangent, lengths, gathered, w_down, vec):
+def middle(x, mixed, cotangent, lengths, gathered, vec, piece):
     rows, width = x.shape
-    inner = w_down.shape[0]
+    inner = (gathered.shape[1] - width) // 2
+    ratio = inner // width
+    if piece % 8:
+        w_down = gathered[:, inner + width :].reshape(width // piece, piece, ratio, width)
+        w_down = w_down.transpose(0, 2, 1, 3).reshape(inner, width)
+        down_block = (inner, width), 0
+    else:
+        w_down = gathered
+        down_block = (width, inner), 1
     seq = rows // lengths.shape[0]
     once = pl.Buffered(1)
     thin = pl.BlockSpec((ROWS, width), lambda i, ln: (i, 0))
@@ -323,9 +353,9 @@
             thin,
             thin,
             thin,
-            pl.BlockSpec((width, width), lambda i, ln: (0, inner // width), pipeline_mode=once),
+            pl.BlockSpec((width, width), lambda i, ln: (0, 2 * ratio), pipeline_mode=once),
             pl.BlockSpec((width, inner), lambda i, ln: (0, 0), pipeline_mode=once),
-            pl.BlockSpec((inner, width), lambda i, ln: (0, 0), pipeline_mode=once),
+            pl.BlockSpec(down_block[0], lambda i, ln: (0, down_block[1]), pipeline_mode=once),
             pl.BlockSpec(vec.shape, lambda i, ln: (0, 0)),
         ],
         out_specs=[
@@ -339,12 +369,13 @@
             thin,
             pl.BlockSpec(vec.shape, lambda i, ln: (0, 0)),
         ],
-        scratch_shapes=[pltpu.VMEM((ROWS, inner), F32)],
+        scratch_shapes=[pltpu.VMEM((ROWS, inner), F32)]
+        + ([] if piece % 8 else [pltpu.VMEM((inner, width), BF)]),
     )
     low = jax.ShapeDtypeStruct((rows, width), BF)
     low_wide = jax.ShapeDtypeStruct((rows, inner), BF)
     return pl.pallas_call(
-        functools.partial(middle_kernel, seq=seq),
+        functools.partial(middle_kernel, seq=seq, piece=piece),
         grid_spec=grid_spec,
         out_shape=[
             low,
@@ -368,10 +399,15 @@
 
 
 def weight_kernel(src_ref, left_ref, right_ref, *refs, sums):
-    keep_ref, send_ref, acc_ref = refs[0], refs[1], refs[-1]
+    keep_ref, send_ref, acc_ref, turned_ref = refs[0], refs[1], refs[-2], refs[-1]
     half, piece, _ = keep_ref.shape
     right = right_ref[0] if len(right_ref.shape) == 3 else right_ref[...]
-    acc_ref[...] = dot(left_ref[...], right, TN)
+
+    @pl.when(pl.program_id(0) == 0)
+    def _():
+        turned_ref[...] = left_ref[...].T
+
+    acc_ref[...] = dot(turned_ref[...], right)
     if sums:
         refs[2][0] = jnp.broadcast_to(column_sum(right.astype(F32)), refs[2].shape[1:])
     for slot in range(half):
@@ -426,7 +462,7 @@
         grid=(steps,),
         in_specs=[left_block, right_block],
         out_specs=[block, block] + extra_specs,
-        scratch_shapes=[pltpu.VMEM((tall, tile), F32)],
+        scratch_shapes=[pltpu.VMEM((tall, tile), F32), pltpu.VMEM((tall, rows), BF)],
     )
     return pl.pallas_call(
         functools.partial(weight_kernel, sums=sums),
@@ -438,13 +474,27 @@
     )(source, left, right)
 
 
-def joint_kernel(src_ref, left_ref, last_left_ref, right_ref, last_right_ref, keep_ref, send_ref, acc_ref):
+def joint_kernel(
+    src_ref,
+    left_ref,
+    last_left_ref,
+    right_ref,
+    last_right_ref,
+    keep_ref,
+    send_ref,
+    acc_ref,
+    turned_ref,
+):
     half, piece, _ = keep_ref.shape
     last = pl.num_programs(0) - 1
 
+    @pl.when(pl.program_id(0) == 0)
+    def _():
+        turned_ref[...] = left_ref[...].T
+
     @pl.when(pl.program_id(0) < last)
     def _():
-        acc_ref[...] = dot(left_ref[...], right_ref[...], TN)
+        acc_ref[...] = dot(turned_ref[...], right_ref[...])
 
     @pl.when(pl.program_id(0) == last)
     def _():
@@ -479,7 +529,7 @@
             pl.BlockSpec((rows, tile), lambda j, s: (0, 0)),
         ],
         out_specs=[block, block],
-        scratch_shapes=[pltpu.VMEM((tall, tile), F32)],
+        scratch_shapes=[pltpu.VMEM((tall, tile), F32), pltpu.VMEM((tall, rows), BF)],
     )
     return pl.pallas_call(
         joint_kernel,
@@ -562,10 +612,12 @@
     out_ref = refs[-1]
     width = resid_ref.shape[1]
     total = resid_ref[...]
-    for group, grad_ref in enumerate(refs[:groups]):
+    base = 0
+    for grad_ref in refs[:groups]:
         here = grad_ref.shape[2]
         for part in range(3):
-            total = total + dot(grad_ref[part], w_ref[:, pl.ds(part * width + group * here, here)], NT)
+            total = total + dot(grad_ref[part], w_ref[:, pl.ds(part * width + base, here)], NT)
+        base += here
     out_ref[...] = total.astype(BF)
 
 
@@ -695,14 +747,6 @@
         out_ref[pl.ds(begin, 2 * piece), :] = both
 
 
-def lay_kernel(index_ref, odd_ref, held_ref, taken_ref, out_ref):
-    half, piece, _ = held_ref.shape
-    for slot in range(half):
-        for ref, flip in ((held_ref, 0), (taken_ref, 1)):
-            begin = pl.multiple_of((index_ref[slot] ^ flip) * piece, 16)
-            out_ref[pl.ds(begin, piece), :] = ref[slot]
-
-
 def lay_out(gather, me):
     held, taken = gather.held, gather.taken[0]
     half, piece, columns = held.shape
@@ -718,15 +762,16 @@
         natural = jnp.take(jnp.asarray(where, jnp.int32), jnp.arange(devices, dtype=jnp.int32) ^ me)
         both = jnp.concatenate([held, taken], axis=0)
         return jnp.take(both, natural, axis=0).reshape(devices * piece, columns)
-    whole = pl.BlockSpec(held.shape, lambda i, *s: (0, 0, 0))
+    tile = columns // 5 if columns % (5 * LANES) == 0 else columns
+    block = pl.BlockSpec((half, piece, tile), lambda i, *s: (0, 0, i))
     grid_spec = pltpu.PrefetchScalarGridSpec(
         num_scalar_prefetch=2,
-        grid=(1,),
-        in_specs=[whole, whole],
-        out_specs=pl.BlockSpec((devices * piece, columns), lambda i, *s: (0, 0)),
+        grid=(columns // tile,),
+        in_specs=[block, block],
+        out_specs=pl.BlockSpec((devices * piece, tile), lambda i, *s: (0, i)),
     )
     return pl.pallas_call(
-        lay_pairs_kernel if piece % 16 else lay_kernel,
+        lay_pairs_kernel,
         grid_spec=grid_spec,
         out_shape=jax.ShapeDtypeStruct((devices * piece, columns), BF),
         compiler_params=params(1),
@@ -782,28 +827,26 @@
     slot_of = jnp.take(jnp.asarray(slots, jnp.int32), jnp.arange(devices, dtype=jnp.int32) ^ me)
 
     entries = vectors.shape[0] // piece
+    ratio = inner // width
+    down_columns = proj_down.astype(BF).reshape(ratio, piece, width).transpose(1, 0, 2)
     wide = lax.all_gather(
-        jnp.concatenate([proj_up.astype(BF), proj_attn.astype(BF)], axis=1), "dp", axis=0, tiled=True
+        jnp.concatenate(
+            [proj_up.astype(BF), down_columns.reshape(piece, inner), proj_attn.astype(BF)], axis=1
+        ),
+        "dp",
+        axis=0,
+        tiled=True,
     )
     shard = jnp.concatenate(
         [
             proj_qkv.astype(BF),
-            jnp.pad(vectors.astype(BF).reshape(piece, entries), ((0, 0), (0, LANES - entries))),
+            jnp.pad(vectors.astype(BF).reshape(piece, entries), ((0, 0), (0, 2 * LANES - entries))),
         ],
         axis=1,
     )
     qkv = Gather(shard, outward, devices)
-    down = Gather(proj_down.astype(BF), outward, devices)
-    for _ in range(len(outward) - 2):
+    for _ in range(len(outward) - 1):
         qkv.send().join()
-    down.held = hold(down.held, qkv.held)
-    qkv.send()
-    for _ in range(len(outward) - 2):
-        down.send().join()
-    qkv.join()
-    down.held = hold(down.held, qkv.held)
-    qkv.held = hold(qkv.held, down.held)
-    down.send()
     qkv.send()
     gathered = lay_out(qkv, me)
     vec = gathered[:, 3 * width : 3 * width + entries].astype(F32).reshape(-1, width)
@@ -812,15 +855,9 @@
     filled = ()
     for which in range(batch):
         filled = attend_forward(packed, lengths, width, which, filled)
-        if which == 0:
-            down.taken = [hold(value, filled) for value in down.taken]
-            down.join()
-            packed = hold(packed, down.held)
-            down.send()
     mixed, lse = filled
-    w_down = lay_out(down, me)
     output, first_low, active, grad_upper, grad_branch, grad_attn, grad_mixed, grad_one, sums = middle(
-        hidden_in, mixed, cotangent, lengths, wide, w_down, vec
+        hidden_in, mixed, cotangent, lengths, wide, vec, piece
     )
 
     total = Reduce(*tall_gradient(active, grad_branch, source_of(by_x), slot_of), by_x, devices)
@@ -829,27 +866,31 @@
     joint = Reduce(
         *joint_gradient(first_low, grad_upper, mixed, grad_attn, source_of(by_y)), by_y, devices
     )
-    total.after(joint.parts).join()
+    total.after(joint.parts)
+    joint.parts = list(hold(tuple(joint.parts), *total.terms))
+    joint.send()
+    total.join()
+    joint.join()
     grad_mixed = hold(grad_mixed, total.parts, joint.parts)
     total.send()
     joint.send()
     parts, part_sums, queue = [], [], []
-    for group in range(GROUPS):
-        final = group == GROUPS - 1
+    spans = pair_groups(width // LANES)
+    for group, span in enumerate(spans):
+        final = group == len(spans) - 1
         part = ()
         for which in range(batch):
-            part = (attend_backward(packed, lengths, lse, grad_mixed, group, which, part),)
-            if which == 0 and group < 2:
-                chain = joint if group == 0 else queue[0]
-                chain.after(part).join()
-                grad_mixed = hold(grad_mixed, chain.parts)
-                chain.send()
+            part = (attend_backward(packed, lengths, lse, grad_mixed, span, which, part),)
+            if which == 0 and final:
+                queue[0].after(part).join()
+                grad_mixed = hold(grad_mixed, queue[0].parts)
+                queue[0].send()
         left = hidden_in
         if final:
-            for chain in (joint, total, *queue):
+            for chain in (joint, total):
                 chain.after(part).join()
-            left = hold(hidden_in, *(chain.parts for chain in (joint, total, *queue)))
-            for chain in (joint, total, *queue):
+            left = hold(hidden_in, joint.parts, total.parts)
+            for chain in (joint, total):
                 chain.send()
         order = both if final else by_x
         keep, send, part_sum = weight_gradient(left, part[0], source_of(order), sums=True)
@@ -857,9 +898,11 @@
         part_sums.append(part_sum)
         if group == 0:
             queue.append(Reduce(keep, send, order, devices).send())
-            total.after(keep).join()
-            grad_mixed = hold(grad_mixed, total.parts, keep)
-            total.send()
+            for chain in (joint, total):
+                chain.after(keep).join()
+            grad_mixed = hold(grad_mixed, joint.parts, total.parts, keep)
+            for chain in (joint, total):
+                chain.send()
     part_sums = jnp.concatenate(part_sums, axis=2)
     vector_sums = jnp.concatenate([part_sums[0, :1], part_sums[2, :1], sums[2:]], axis=0)
     ordered = jnp.take(vector_sums.reshape(devices, piece, entries), source_of(both), axis=0)
@@ -882,10 +925,15 @@
         chain.after(filled)
 
     total_qkv = [chain.finish() for chain in queue]
-    total_vectors = total_qkv[1][:, 3 * width // GROUPS : 3 * width // GROUPS + entries].reshape(-1)
-    here = width // GROUPS
+    here = spans[1][1] * LANES
+    total_vectors = total_qkv[1][:, 3 * here : 3 * here + entries].reshape(-1)
     total_qkv = jnp.concatenate(
-        [part[:, at * here : (at + 1) * here] for at in range(3) for part in total_qkv], axis=1
+        [
+            part[:, at * pairs * LANES : (at + 1) * pairs * LANES]
+            for at in range(3)
+            for part, (_, pairs) in zip(total_qkv, spans)
+        ],
+        axis=1,
     )
     total_wide = joint.finish()
     total_up, total_attn = total_wide[:, :inner], total_wide[:, inner:]

time: 327 us -> 305 us (0.933); the launches traced: 323 us -> 304 us
  local copies, waits for them, and re-layouts: 13.2 us -> 4.8 us
  Pallas kernels: 167 us -> 159 us
    all_gather x1, waiting for transfers between devices: 0.01 us -> 7.31 us  [on_device(): lax.all_gather(jnp.concatenate([proj_up.astype(BF), down_columns.reshape(...]
    pallas_call x3 -> x2, Pallas kernels: 50 us -> 42.7 us  [the longest x1 36 us: middle(): pl.pallas_call(functools.partial(middle_kernel, seq=seq, piece=piece), gr...]
    ppermute x33 -> x27, waiting for transfers between devices: 66.9 us -> 59.9 us  [swap(): lax.ppermute(value, 'dp', [(index, index ^ mask) for index in range(devic...]
    unnamed x81, local copies, waits for them, and re-layouts: 6.81 us -> 0.32 us
    ppermute x33 -> x27, starting transfers between devices: 32.9 us -> 31.2 us  [swap(): lax.ppermute(value, 'dp', [(index, index ^ mask) for index in range(devic...]
  transfers between devices with their start and end apart: 34 -> 28, of which waited for: 12 -> 14; matrix products, arithmetic and copies ran while one was open for 11% -> 9% of each run, Pallas kernels for 36% -> 37%
where the time goes in v4:
time: 305 us; the launch traced here: 304 us
  Pallas kernels  159 us (52%)
  waiting for transfers between devices  67.2 us (22%)
  starting transfers between devices  31.3 us (10%)
  other arithmetic  27.1 us (9%)
  between operations  14.7 us (5%)
  local copies, waits for them, and re-layouts  4.8 us (2%)
    ppermute x27, waiting for transfers between devices, swap(): lax.ppermute(value, 'dp', [(index, index ^ mask) for index in range(devic...  59.9 us
    pallas_call x4, Pallas kernels, attend_backward(): pl.pallas_call(functools.partial(attend_back_kernel, which=which), grid_s...  36 us
    pallas_call x1, Pallas kernels, middle(): pl.pallas_call(functools.partial(middle_kernel, seq=seq, piece=piece), gr...  36 us
    ppermute x27, starting transfers between devices, swap(): lax.ppermute(value, 'dp', [(index, index ^ mask) for index in range(devic...  31.2 us
    pallas_call x2, Pallas kernels, attend_forward(): pl.pallas_call(functools.partial(attend_kernel, which=which), grid_spec=g...  21.7 us
    convert_element_type x15, other arithmetic, join(): self.total(way * size, size).astype(BF)  15 us
    pallas_call x2, Pallas kernels, weight_gradient(): pl.pallas_call(functools.partial(weight_kernel, sums=sums), grid_spec=gri...  13.9 us
    pallas_call x1, Pallas kernels, joint_gradient(): pl.pallas_call(joint_kernel, grid_spec=grid_spec, out_shape=[shape, shape...  13.3 us
  transfers between devices with their start and end apart: 28, of which 14 were waited for; matrix products, arithmetic and copies ran while one was open for 9% of the time, Pallas kernels for 37%

profile of v4, /device:TPU:0, one launch (start us, length us, event | category | flops | bytes accessed | tf_op | source)
XLA Modules:
  0.0 304.1 jit_solution(1031262829528277307)
XLA Ops:
  11.2 4.1 %collective-permute-start = (bf16[1,24,2560]{2,1,0:T(8,128)(2,1)S(1)}, bf16[1,24,2560]{2,1,0:T(8,128)(2,1)S(1)}, u32[]{:S(2)}, u32[]{:S(2)}) collective-permute-start(bf16[1,24,2560]{2,1,0:T(8,128)(2,1)S(1)} %fusion.6), channel_id=1, source_target_pairs={{0,16},{1,17},{2,18},{3,19},{4,20},{5,21},{6,22},{7,23},{8,24},{9,... | collective-permute-start | bytes 368648 | tf_op jit(solution)/shard_map/ppermute | solution.py:651
  15.3 6.0 %collective-permute-done = bf16[1,24,2560]{2,1,0:T(8,128)(2,1)S(1)} collective-permute-done((bf16[1,24,2560]{2,1,0:T(8,128)(2,1)S(1)}, bf16[1,24,2560]{2,1,0:T(8,128)(2,1)S(1)}, u32[]{:S(2)}, u32[]{:S(2)}) %collective-permute-start) | collective-permute-done | bytes 122912 | tf_op jit(solution)/shard_map/ppermute | solution.py:651
  22.1 10.2 %collective-permute-done.1 = bf16[2,24,2560]{2,1,0:T(8,128)(2,1)S(1)} collective-permute-done((bf16[2,24,2560]{2,1,0:T(8,128)(2,1)S(1)}, bf16[2,24,2560]{2,1,0:T(8,128)(2,1)S(1)}, u32[]{:S(2)}, u32[]{:S(2)}) %collective-permute-start.1) | collective-permute-done | bytes 245792 | tf_op jit(solution)/shard_map/ppermute | solution.py:651
  32.3 1.4 collective-permute-start.2
  33.7 1.6 collective-permute-start.3
  36.0 10.9 %collective-permute-done.2 = bf16[4,24,2560]{2,1,0:T(8,128)(2,1)S(1)} collective-permute-done((bf16[4,24,2560]{2,1,0:T(8,128)(2,1)S(1)}, bf16[4,24,2560]{2,1,0:T(8,128)(2,1)S(1)}, u32[]{:S(2)}, u32[]{:S(2)}) %collective-permute-start.2) | collective-permute-done | bytes 491552 | tf_op jit(solution)/shard_map/ppermute | solution.py:651
  47.0 7.0 %collective-permute-done.3 = bf16[4,24,2560]{2,1,0:T(8,128)(2,1)S(1)} collective-permute-done((bf16[4,24,2560]{2,1,0:T(8,128)(2,1)S(1)}, bf16[4,24,2560]{2,1,0:T(8,128)(2,1)S(1)}, u32[]{:S(2)}, u32[]{:S(2)}) %collective-permute-start.3) | collective-permute-done | bytes 491552 | tf_op jit(solution)/shard_map/ppermute | solution.py:651
  54.0 9.7 %collective-permute-done.4 = bf16[4,24,2560]{2,1,0:T(8,128)(2,1)S(1)} collective-permute-done((bf16[4,24,2560]{2,1,0:T(8,128)(2,1)S(1)}, bf16[4,24,2560]{2,1,0:T(8,128)(2,1)S(1)}, u32[]{:S(2)}, u32[]{:S(2)}) %collective-permute-start.4) | collective-permute-done | bytes 491552 | tf_op jit(solution)/shard_map/ppermute | solution.py:651
  65.6 2.3 collective-permute-done.5.taken_ref
  67.9 6.7 %lay_out.1.w_ref = bf16[768,2560]{1,0:T(8,128)(2,1)} custom-call(s32[16]{0:T(128)} %broadcast_xor_fusion.2.index_ref, s32[1]{0:T(128)} %bitcast.odd_ref, bf16[16,24,2560]{2,1,0:T(8,128)(2,1)} %copy-done.6, bf16[16,24,2560]{2,1,0:T(8,128)(2,1)} %collective-permute-done.5.taken_ref), custom_call_target="tpu_custom_call" | custom-call | flops 1966080 | bytes 7864320 | tf_op jit(solution)/shard_map/lay_out/pallas_call | solution.py:773
  76.4 8.4 %project_qkv.1.q_ref.k_ref.v_ref = bf16[1024,2304]{1,0:T(8,128)(2,1)} custom-call(bf16[1024,768]{1,0:T(8,128)(2,1)} %left_ref.2, bf16[768,2560]{1,0:T(8,128)(2,1)} %lay_out.1.w_ref, f32[12,768]{1,0:T(8,128)} %reshape.92.vec_ref), custom_call_target="tpu_custom_call" | custom-call | flops 3623878656 | bytes 9830400 | tf_op jit(solution)/shard_map/project_qkv/pallas_call | solution.py:64
  84.8 10.9 %attend_forward.2 = (bf16[1024,768]{1,0:T(8,128)(2,1)}, f32[12,2,512]{2,1,0:T(2,128)}) custom-call(s32[2]{0:T(128)} %len_ref.13, bf16[1024,2304]{1,0:T(8,128)(2,1)} %project_qkv.1.q_ref.k_ref.v_ref, bf16[1024,2304]{1,0:T(8,128)(2,1)} %project_qkv.1.q_ref.k_ref.v_ref, bf16[1024,2304]{1,0:T(8,128)(2,1)} %project_qkv.1.q_ref.k_ref.v_ref), custom_call_target="tpu_custom_call" | custom-call | flops 3221225472 | bytes 3145728 | tf_op jit(solution)/shard_map/attend_forward/pallas_call | solution.py:122
  95.7 10.9 %attend_forward.3 = (bf16[1024,768]{1,0:T(8,128)(2,1)}, f32[12,2,512]{2,1,0:T(2,128)}) custom-call(s32[2]{0:T(128)} %len_ref.13, bf16[1024,2304]{1,0:T(8,128)(2,1)} %project_qkv.1.q_ref.k_ref.v_ref, bf16[1024,2304]{1,0:T(8,128)(2,1)} %project_qkv.1.q_ref.k_ref.v_ref, ...), custom_call_target="tpu_custom_call", output_to_operand_aliasing={{0}: (4, {}), {1}: (5, {})} | custom-call | flops 3221225472 | bytes 3145728 | tf_op jit(solution)/shard_map/attend_forward/pallas_call | solution.py:122
  106.6 7.3 %all-gather.2.cloned.1.call-done.w_attn.w_up.w_down = bf16[768,6912]{1,0:T(8,128)(2,1)} async-done(((bf16[24,6912]{1,0:T(8,128)(2,1)}), bf16[768,6912]{1,0:T(8,128)(2,1)}) %all-gather.2.cloned.1.call-update) | async-done | bytes 10616848 | tf_op jit(solution)/shard_map/all_gather | solution.py:832
  113.9 36.0 %middle.1 = (bf16[1024,768]{1,0:T(8,128)(2,1)}, bf16[1024,768]{1,0:T(8,128)(2,1)}, bf16[1024,3072]{1,0:T(8,128)(2,1)}, bf16[1024,3072]{1,0:T(8,128)(2,1)}, bf16[...) custom-call(s32[2]{0:T(128)} %len_ref.13, ...), custom_call_target="tpu_custom_call" | custom-call | flops 21743271936 | bytes 37748736 | tf_op jit(solution)/shard_map/middle/pallas_call | solution.py:377
  149.9 11.6 %tall_gradient.1 = (bf16[16,96,768]{2,1,0:T(8,128)(2,1)}, bf16[16,96,768]{2,1,0:T(8,128)(2,1)}) custom-call(s32[32]{0:T(128)} %get-tuple-element.190.slot_ref, bf16[1024,3072]{1,0:T(8,128)(2,1)} %get-tuple-element.86.left_ref, bf16[1024,768]{1,0:T(8,128)(2,1)} %get-tuple-element.87.right_ref), custom_call_target="tpu_custom_call" | custom-call | flops 4831838208 | bytes 12582912 | tf_op jit(solution)/shard_map/tall_gradient/pallas_call | solution.py:601
  161.4 3.7 %collective-permute-start.6 = (bf16[16,96,768]{2,1,0:T(8,128)(2,1)}, bf16[16,96,768]{2,1,0:T(8,128)(2,1)S(1)}, u32[]{:S(2)}, u32[]{:S(2)}) collective-permute-start(bf16[16,96,768]{2,1,0:T(8,128)(2,1)} %get-tuple-element.89), channel_id=1, source_target_pairs={{0,1},{1,0},{2,3},{3,2},{4,5},{5,4},{6,7},{7,6},{8,9},{9,8},{10,11... | collective-permute-start | bytes 7077896 | tf_op jit(solution)/shard_map/ppermute | solution.py:651
  165.1 13.3 %joint_gradient.1 = (bf16[16,24,3840]{2,1,0:T(8,128)(2,1)}, bf16[16,24,3840]{2,1,0:T(8,128)(2,1)}) custom-call(s32[32]{0:T(128)} %get-tuple-element.191.src_ref, bf16[1024,768]{1,0:T(8,128)(2,1)} %get-tuple-element.84.left_ref, bf16[1024,768]{1,0:T(8,128)(2,1)} %get-tuple-element.81.mixed_ref.last_left_ref, bf16[1024,3072]{1,0:T(8,128)(2,1)} %get-tuple-element.90.right_ref, ...), custom_call_target="tpu_custom_call" | custom-call | flops 48318382080 | bytes 16908288 | tf_op jit(solution)/shard_map/joint_gradient/pallas_call | solution.py:534
  180.7 2.2 add_convert_fusion.2
  182.9 1.1 collective-permute-done.7
  184.0 2.3 add_convert_fusion
  186.4 1.4 collective-permute-start.8
  187.8 11.0 %attend_backward.4.refs_0_ = bf16[3,1024,512]{2,1,0:T(8,128)(2,1)} custom-call(s32[2]{0:T(128)} %len_ref.13, bf16[1024,2304]{1,0:T(8,128)(2,1)} %project_qkv.1.q_ref.k_ref.v_ref, bf16[1024,2304]{1,0:T(8,128)(2,1)} %project_qkv.1.q_ref.k_ref.v_ref, bf16[1024,2304]{1,0:T(8,128)(2,1)} %project_qkv.1.q_ref.k_ref.v_ref, ...), custom_call_target="tpu_custom_call" | custom-call | flops 42949672960 | bytes 3670016 | tf_op jit(solution)/shard_map/attend_backward/pallas_call | solution.py:192
  198.8 11.1 %attend_backward.5.right_ref.refs_0_ = bf16[3,1024,512]{2,1,0:T(8,128)(2,1)} custom-call(s32[2]{0:T(128)} %len_ref.13, bf16[1024,2304]{1,0:T(8,128)(2,1)} %project_qkv.1.q_ref.k_ref.v_ref, bf16[1024,2304]{1,0:T(8,128)(2,1)} %project_qkv.1.q_ref.k_ref.v_ref, bf16[1024,2304]{1,0:T(8,128)(2,1)} %project_qkv.1.q_ref.k_ref.v_ref, ...), custom_call_target="tpu_custom_call", output_to_operand_aliasing={{}: (6, {})} | custom-call | flops 42949672960 | bytes 3670016 | tf_op jit(solution)/shard_map/attend_backward/pallas_call | solution.py:192
  209.8 7.7 %weight_gradient.2 = (bf16[16,24,1536]{2,1,0:T(8,128)(2,1)}, bf16[16,24,1536]{2,1,0:T(8,128)(2,1)}, f32[3,8,512]{2,1,0:T(8,128)}) custom-call(s32[32]{0:T(128)} %broadcast_xor_fusion.src_ref, bf16[1024,768]{1,0:T(8,128)(2,1)} %left_ref.2, bf16[3,1024,512]{2,1,0:T(8,128)(2,1)} %attend_backward.5.right_ref.refs_0_), custom_call_target="tpu_custom_call" | custom-call | flops 154618822656 | bytes 7077888 | tf_op jit(solution)/shard_map/weight_gradient/pallas_call | solution.py:467
  217.8 1.6 add_convert_fusion.8
  221.0 1.7 add_convert_fusion.4
  223.8 7.1 %attend_backward.6.refs_0_ = bf16[3,1024,256]{2,1,0:T(8,128)(2,1)} custom-call(s32[2]{0:T(128)} %len_ref.13, bf16[1024,2304]{1,0:T(8,128)(2,1)} %project_qkv.1.q_ref.k_ref.v_ref, bf16[1024,2304]{1,0:T(8,128)(2,1)} %project_qkv.1.q_ref.k_ref.v_ref, bf16[1024,2304]{1,0:T(8,128)(2,1)} %project_qkv.1.q_ref.k_ref.v_ref, ...), custom_call_target="tpu_custom_call" | custom-call | flops 21474836480 | bytes 1835008 | tf_op jit(solution)/shard_map/attend_backward/pallas_call | solution.py:192
  230.9 1.3 add_convert_fusion.6
  233.3 6.8 %attend_backward.7.right_ref.refs_1_ = bf16[3,1024,256]{2,1,0:T(8,128)(2,1)} custom-call(s32[2]{0:T(128)} %len_ref.13, bf16[1024,2304]{1,0:T(8,128)(2,1)} %project_qkv.1.q_ref.k_ref.v_ref, bf16[1024,2304]{1,0:T(8,128)(2,1)} %project_qkv.1.q_ref.k_ref.v_ref, bf16[1024,2304]{1,0:T(8,128)(2,1)} %project_qkv.1.q_ref.k_ref.v_ref, ...), custom_call_target="tpu_custom_call", output_to_operand_aliasing={{}: (6, {})} | custom-call | flops 21474836480 | bytes 1835008 | tf_op jit(solution)/shard_map/attend_backward/pallas_call | solution.py:192
  241.1 1.6 collective-permute-start.14
  242.7 1.1 add_convert_fusion.10
  243.8 1.2 collective-permute-start.13
  245.0 6.1 %weight_gradient.3 = (bf16[16,24,768]{2,1,0:T(8,128)(2,1)}, bf16[16,24,768]{2,1,0:T(8,128)(2,1)}, f32[3,8,256]{2,1,0:T(8,128)}) custom-call(s32[32]{0:T(128)} %get-tuple-element.191.src_ref, bf16[1024,768]{1,0:T(8,128)(2,1)} %left_ref.2, bf16[3,1024,256]{2,1,0:T(8,128)(2,1)} %attend_backward.7.right_ref.refs_1_), custom_call_target="tpu_custom_call" | custom-call | flops 77309411328 | bytes 4325376 | tf_op jit(solution)/shard_map/weight_gradient/pallas_call | solution.py:467
  253.5 5.7 %input_gradient.2.refs_2_ = bf16[1024,768]{1,0:T(8,128)(2,1)} custom-call(f32[1024,768]{1,0:T(8,128)} %get-tuple-element.130.resid_ref, bf16[768,2560]{1,0:T(8,128)(2,1)} %lay_out.1.w_ref, bf16[3,1024,512]{2,1,0:T(8,128)(2,1)} %attend_backward.5.right_ref.refs_0_, bf16[3,1024,256]{2,1,0:T(8,128)(2,1)} %attend_backward.7.right_ref.refs_1_), custom_call_target="tpu_custom_call" | custom-call | flops 115964116992 | bytes 6488064 | tf_op jit(solution)/shard_map/input_gradient/pallas_call | solution.py:628
  260.3 1.2 collective-permute-start.26
  261.6 1.2 add_convert_fusion.12
  262.8 1.4 collective-permute-start.17
  265.4 1.3 collective-permute-start.25
  267.9 1.4 collective-permute-start.21
  269.3 5.6 %input_gradient.3 = bf16[1024,768]{1,0:T(8,128)(2,1)} custom-call(f32[1024,768]{1,0:T(8,128)} %get-tuple-element.130.resid_ref, bf16[768,2560]{1,0:T(8,128)(2,1)} %lay_out.1.w_ref, bf16[3,1024,512]{2,1,0:T(8,128)(2,1)} %attend_backward.5.right_ref.refs_0_, bf16[3,1024,256]{2,1,0:T(8,128)(2,1)} %attend_backward.7.right_ref.refs_1_, ...), custom_call_target="tpu_custom_call", output_to_operand_aliasing={{}: (4, {})} | custom-call | flops 115964116992 | bytes 6488064 | tf_op jit(solution)/shard_map/input_gradient/pallas_call | solution.py:628
  275.0 1.2 collective-permute-start.22
  276.2 2.4 collective-permute-done.25
  281.7 2.5 collective-permute-done.18
  285.1 1.8 collective-permute-start.23
  286.9 3.4 %collective-permute-done.19 = bf16[1,24,1536]{2,1,0:T(8,128)(2,1)S(1)} collective-permute-done((bf16[1,24,1536]{2,1,0:T(8,128)(2,1)S(1)}, bf16[1,24,1536]{2,1,0:T(8,128)(2,1)S(1)}, u32[]{:S(2)}, u32[]{:S(2)}) %collective-permute-start.19) | collective-permute-done | bytes 73760 | tf_op jit(solution)/shard_map/ppermute | solution.py:651
  290.4 1.6 collective-permute-start.24
  292.1 3.4 %collective-permute-done.24 = bf16[1,24,896]{2,1,0:T(8,128)(2,1)S(1)} collective-permute-done((bf16[1,24,896]{2,1,0:T(8,128)(2,1)S(1)}, bf16[1,24,896]{2,1,0:T(8,128)(2,1)S(1)}, u32[]{:S(2)}, u32[]{:S(2)}) %collective-permute-start.24) | collective-permute-done | bytes 43040 | tf_op jit(solution)/shard_map/ppermute | solution.py:651
  (164 shorter events, 27.8 us)
Async XLA Ops:
  7.2 106.7 %all-gather.2.cloned.1.call-start = ((), (), s32[]{:S(2)}) async-start(), calls=%async_computation | async-start | bytes 10948608 | tf_op jit(solution)/shard_map/all_gather | solution.py:832
  11.2 10.1 %collective-permute-start = (bf16[1,24,2560]{2,1,0:T(8,128)(2,1)S(1)}, bf16[1,24,2560]{2,1,0:T(8,128)(2,1)S(1)}, u32[]{:S(2)}, u32[]{:S(2)}) collective-permute-start(bf16[1,24,2560]{2,1,0:T(8,128)(2,1)S(1)} %fusion.6), channel_id=1, source_target_pairs={{0,16},{1,17},{2,18},{3,19},{4,20},{5,21},{6,22},{7,23},{8,24},{9,... | collective-permute-start | bytes 368648 | tf_op jit(solution)/shard_map/ppermute | solution.py:651
  21.3 11.0 %collective-permute-start.1 = (bf16[2,24,2560]{2,1,0:T(8,128)(2,1)S(1)}, bf16[2,24,2560]{2,1,0:T(8,128)(2,1)S(1)}, u32[]{:S(2)}, u32[]{:S(2)}) collective-permute-start(bf16[2,24,2560]{2,1,0:T(8,128)(2,1)S(1)} %pad_maximum_fusion.4), channel_id=1, source_target_pairs={{0,8},{1,9},{2,10},{3,11},{4,12},{5,13},{6,14},{7,15},{8,0},{9,1},... | collective-permute-start | bytes 737288 | tf_op jit(solution)/shard_map/ppermute | solution.py:651
  32.3 14.6 %collective-permute-start.2 = (bf16[4,24,2560]{2,1,0:T(8,128)(2,1)S(1)}, bf16[4,24,2560]{2,1,0:T(8,128)(2,1)S(1)}, u32[]{:S(2)}, u32[]{:S(2)}) collective-permute-start(bf16[4,24,2560]{2,1,0:T(8,128)(2,1)S(1)} %pad_maximum_fusion.2), channel_id=1, source_target_pairs={{0,2},{1,3},{2,0},{3,1},{4,6},{5,7},{6,4},{7,5},{8,10},{9,11},{10,... | collective-permute-start | bytes 1474568 | tf_op jit(solution)/shard_map/ppermute | solution.py:651
  33.7 20.2 %collective-permute-start.3 = (bf16[4,24,2560]{2,1,0:T(8,128)(2,1)S(1)}, bf16[4,24,2560]{2,1,0:T(8,128)(2,1)S(1)}, u32[]{:S(2)}, u32[]{:S(2)}) collective-permute-start(bf16[4,24,2560]{2,1,0:T(8,128)(2,1)S(1)} %pad_maximum_fusion.2), channel_id=1, source_target_pairs={{0,4},{1,5},{2,6},{3,7},{4,0},{5,1},{6,2},{7,3},{8,12},{9,13},{10,... | collective-permute-start | bytes 1474568 | tf_op jit(solution)/shard_map/ppermute | solution.py:651
  35.4 28.3 %collective-permute-start.4 = (bf16[4,24,2560]{2,1,0:T(8,128)(2,1)S(1)}, bf16[4,24,2560]{2,1,0:T(8,128)(2,1)S(1)}, u32[]{:S(2)}, u32[]{:S(2)}) collective-permute-start(bf16[4,24,2560]{2,1,0:T(8,128)(2,1)S(1)} %pad_maximum_fusion.2), channel_id=1, source_target_pairs={{0,6},{1,7},{2,4},{3,5},{4,2},{5,3},{6,0},{7,1},{8,14},{9,15},{10,... | collective-permute-start | bytes 1474568 | tf_op jit(solution)/shard_map/ppermute | solution.py:651
  36.0 27.8 %copy-start = (s32[32]{0:T(128)S(1)}, s32[32]{0:T(128)}, u32[]{:S(2)}) copy-start(s32[32]{0:T(128)} %constant.45.clone) | copy-start | bytes 388
  36.0 28.5 %copy-start.34 = (s32[16]{0:T(128)S(1)}, s32[16]{0:T(128)}, u32[]{:S(2)}) copy-start(s32[16]{0:T(128)} %constant.46.clone) | copy-start | bytes 196
  36.0 29.0 %copy-start.33 = (s32[32]{0:T(128)S(1)}, s32[32]{0:T(128)}, u32[]{:S(2)}) copy-start(s32[32]{0:T(128)} %constant.47.clone) | copy-start | bytes 388
  63.7 4.2 %copy-start.6 = (bf16[16,24,2560]{2,1,0:T(8,128)(2,1)}, bf16[16,24,2560]{2,1,0:T(8,128)(2,1)S(1)}, u32[]{:S(2)}) copy-start(bf16[16,24,2560]{2,1,0:T(8,128)(2,1)S(1)} %constant_dynamic-update-slice_fusion.held_ref) | copy-start | bytes 5898244
  63.7 4.2 %collective-permute-start.5 = (bf16[16,24,2560]{2,1,0:T(8,128)(2,1)S(1)}, bf16[16,24,2560]{2,1,0:T(8,128)(2,1)}, u32[]{:S(2)}, u32[]{:S(2)}) collective-permute-start(bf16[16,24,2560]{2,1,0:T(8,128)(2,1)S(1)} %constant_dynamic-update-slice_fusion.held_ref), channel_id=1, source_target_pairs={{0,1},{1,0},{2,3},{3,2},{4,5},{5,4},{6,7},{7,6},{8,9},{9,8},{10,11... | collective-permute-start | bytes 5898248 | tf_op jit(solution)/shard_map/ppermute | solution.py:651
  161.4 17.0 %collective-permute-start.6 = (bf16[16,96,768]{2,1,0:T(8,128)(2,1)}, bf16[16,96,768]{2,1,0:T(8,128)(2,1)S(1)}, u32[]{:S(2)}, u32[]{:S(2)}) collective-permute-start(bf16[16,96,768]{2,1,0:T(8,128)(2,1)} %get-tuple-element.89), channel_id=1, source_target_pairs={{0,1},{1,0},{2,3},{3,2},{4,5},{5,4},{6,7},{7,6},{8,9},{9,8},{10,11... | collective-permute-start | bytes 7077896 | tf_op jit(solution)/shard_map/ppermute | solution.py:651
  165.1 14.9 %copy-start.27 = (f32[12,768]{1,0:T(8,128)S(1)}, f32[12,768]{1,0:T(8,128)}, u32[]{:S(2)}) copy-start(f32[12,768]{1,0:T(8,128)} %get-tuple-element.119) | copy-start | bytes 110596
  165.1 15.6 %copy-start.4 = (bf16[16,96,768]{2,1,0:T(8,128)(2,1)S(1)}, bf16[16,96,768]{2,1,0:T(8,128)(2,1)}, u32[]{:S(2)}) copy-start(bf16[16,96,768]{2,1,0:T(8,128)(2,1)} %get-tuple-element.94) | copy-start | bytes 7077892
  178.4 5.6 %collective-permute-start.7 = (bf16[16,24,3840]{2,1,0:T(8,128)(2,1)}, bf16[16,24,3840]{2,1,0:T(8,128)(2,1)S(1)}, u32[]{:S(2)}, u32[]{:S(2)}) collective-permute-start(bf16[16,24,3840]{2,1,0:T(8,128)(2,1)} %get-tuple-element.97), channel_id=1, source_target_pairs={{0,1},{1,0},{2,3},{3,2},{4,5},{5,4},{6,7},{7,6},{8,9},{9,8},{10,11... | collective-permute-start | bytes 8847368 | tf_op jit(solution)/shard_map/ppermute | solution.py:651
  182.9 34.7 %collective-permute-start.10 = (bf16[8,96,768]{2,1,0:T(8,128)(2,1)}, bf16[8,96,768]{2,1,0:T(8,128)(2,1)}, u32[]{:S(2)}, u32[]{:S(2)}) collective-permute-start(bf16[8,96,768]{2,1,0:T(8,128)(2,1)} %get-tuple-element.160), channel_id=1, source_target_pairs={{0,2},{1,3},{2,0},{3,1},{4,6},{5,7},{6,4},{7,5},{8,10},{9,11},{10,... | collective-permute-start | bytes 3538952 | tf_op jit(solution)/shard_map/ppermute | solution.py:651
  186.4 34.6 %collective-permute-start.8 = (bf16[8,24,3840]{2,1,0:T(8,128)(2,1)}, bf16[8,24,3840]{2,1,0:T(8,128)(2,1)}, u32[]{:S(2)}, u32[]{:S(2)}) collective-permute-start(bf16[8,24,3840]{2,1,0:T(8,128)(2,1)} %get-tuple-element.158), channel_id=1, source_target_pairs={{0,4},{1,5},{2,6},{3,7},{4,0},{5,1},{6,2},{7,3},{8,12},{9,13},{10,... | collective-permute-start | bytes 4423688 | tf_op jit(solution)/shard_map/ppermute | solution.py:651
  209.8 7.9 %copy-start.2 = (bf16[8,96,768]{2,1,0:T(8,128)(2,1)S(1)}, bf16[8,96,768]{2,1,0:T(8,128)(2,1)}, u32[]{:S(2)}) copy-start(bf16[8,96,768]{2,1,0:T(8,128)(2,1)} %get-tuple-element.104) | copy-start | bytes 3538948
  217.6 13.3 %collective-permute-start.11 = (bf16[16,24,1536]{2,1,0:T(8,128)(2,1)}, bf16[16,24,1536]{2,1,0:T(8,128)(2,1)S(1)}, u32[]{:S(2)}, u32[]{:S(2)}) collective-permute-start(bf16[16,24,1536]{2,1,0:T(8,128)(2,1)} %get-tuple-element.107), channel_id=1, source_target_pairs={{0,1},{1,0},{2,3},{3,2},{4,5},{5,4},{6,7},{7,6},{8,9},{9,8},{10,11... | collective-permute-start | bytes 3538952 | tf_op jit(solution)/shard_map/ppermute | solution.py:651
  219.4 20.7 %collective-permute-start.12 = (bf16[4,96,768]{2,1,0:T(8,128)(2,1)S(1)}, bf16[4,96,768]{2,1,0:T(8,128)(2,1)S(1)}, u32[]{:S(2)}, u32[]{:S(2)}) collective-permute-start(bf16[4,96,768]{2,1,0:T(8,128)(2,1)S(1)} %get-tuple-element.166), channel_id=1, source_target_pairs={{0,4},{1,5},{2,6},{3,7},{4,0},{5,1},{6,2},{7,3},{8,12},{9,13},{10,... | collective-permute-start | bytes 1769480 | tf_op jit(solution)/shard_map/ppermute | solution.py:651
  222.7 20.0 %collective-permute-start.9 = (bf16[4,24,3840]{2,1,0:T(8,128)(2,1)S(1)}, bf16[4,24,3840]{2,1,0:T(8,128)(2,1)S(1)}, u32[]{:S(2)}, u32[]{:S(2)}) collective-permute-start(bf16[4,24,3840]{2,1,0:T(8,128)(2,1)S(1)} %get-tuple-element.162), channel_id=1, source_target_pairs={{0,2},{1,3},{2,0},{3,1},{4,6},{5,7},{6,4},{7,5},{8,10},{9,11},{10,... | collective-permute-start | bytes 2211848 | tf_op jit(solution)/shard_map/ppermute | solution.py:651
  223.8 7.1 %copy-start.8 = (bf16[16,24,1536]{2,1,0:T(8,128)(2,1)S(1)}, bf16[16,24,1536]{2,1,0:T(8,128)(2,1)}, u32[]{:S(2)}) copy-start(bf16[16,24,1536]{2,1,0:T(8,128)(2,1)} %get-tuple-element.108) | copy-start | bytes 3538948
  232.2 27.0 %collective-permute-start.15 = (bf16[8,24,1536]{2,1,0:T(8,128)(2,1)}, bf16[8,24,1536]{2,1,0:T(8,128)(2,1)}, u32[]{:S(2)}, u32[]{:S(2)}) collective-permute-start(bf16[8,24,1536]{2,1,0:T(8,128)(2,1)} %get-tuple-element.164), channel_id=1, source_target_pairs={{0,2},{1,3},{2,0},{3,1},{4,6},{5,7},{6,4},{7,5},{8,10},{9,11},{10,... | collective-permute-start | bytes 1769480 | tf_op jit(solution)/shard_map/ppermute | solution.py:651
  241.1 18.1 %collective-permute-start.14 = (bf16[2,96,768]{2,1,0:T(8,128)(2,1)}, bf16[2,96,768]{2,1,0:T(8,128)(2,1)}, u32[]{:S(2)}, u32[]{:S(2)}) collective-permute-start(bf16[2,96,768]{2,1,0:T(8,128)(2,1)} %get-tuple-element.176), channel_id=1, source_target_pairs={{0,8},{1,9},{2,10},{3,11},{4,12},{5,13},{6,14},{7,15},{8,0},{9,1},... | collective-permute-start | bytes 884744 | tf_op jit(solution)/shard_map/ppermute | solution.py:651
  243.8 20.4 %collective-permute-start.13 = (bf16[2,24,3840]{2,1,0:T(8,128)(2,1)}, bf16[2,24,3840]{2,1,0:T(8,128)(2,1)}, u32[]{:S(2)}, u32[]{:S(2)}) collective-permute-start(bf16[2,24,3840]{2,1,0:T(8,128)(2,1)} %get-tuple-element.168), channel_id=1, source_target_pairs={{0,8},{1,9},{2,10},{3,11},{4,12},{5,13},{6,14},{7,15},{8,0},{9,1},... | collective-permute-start | bytes 1105928 | tf_op jit(solution)/shard_map/ppermute | solution.py:651
  245.0 6.9 %copy-start.23 = (bf16[10,768]{1,0:T(8,128)(2,1)S(1)}, bf16[10,768]{1,0:T(8,128)(2,1)}, u32[]{:S(2)}) copy-start(bf16[10,768]{1,0:T(8,128)(2,1)} %slice.280) | copy-start | bytes 46084
  245.0 8.2 %copy-start.30 = (pred[32]{0:T(512)(128)(4,1)S(1)}, pred[32]{0:T(512)(128)(4,1)}, u32[]{:S(2)}) copy-start(pred[32]{0:T(512)(128)(4,1)} %get-tuple-element.156) | copy-start | bytes 100
  253.4 13.3 %collective-permute-start.16 = (bf16[16,24,896]{2,1,0:T(8,128)(2,1)S(1)}, bf16[16,24,896]{2,1,0:T(8,128)(2,1)S(1)}, u32[]{:S(2)}, u32[]{:S(2)}) collective-permute-start(bf16[16,24,896]{2,1,0:T(8,128)(2,1)S(1)} %pad_maximum_fusion), channel_id=1, source_target_pairs={{0,1},{1,0},{2,3},{3,2},{4,5},{5,4},{6,7},{7,6},{8,9},{9,8},{10,11... | collective-permute-start | bytes 2064392 | tf_op jit(solution)/shard_map/ppermute | solution.py:651
  253.5 5.8 %copy-start.9 = (bf16[2,96,768]{2,1,0:T(8,128)(2,1)S(1)}, bf16[2,96,768]{2,1,0:T(8,128)(2,1)}, u32[]{:S(2)}) copy-start(bf16[2,96,768]{2,1,0:T(8,128)(2,1)} %get-tuple-element.123) | copy-start | bytes 884740
  253.5 8.1 %copy-start.5 = (bf16[8,24,1536]{2,1,0:T(8,128)(2,1)S(1)}, bf16[8,24,1536]{2,1,0:T(8,128)(2,1)}, u32[]{:S(2)}) copy-start(bf16[8,24,1536]{2,1,0:T(8,128)(2,1)} %get-tuple-element.125) | copy-start | bytes 1769476
  259.2 5.0 %copy-start.14 = (bf16[16,24,768]{2,1,0:T(8,128)(2,1)S(1)}, bf16[16,24,768]{2,1,0:T(8,128)(2,1)}, u32[]{:S(2)}) copy-start(bf16[16,24,768]{2,1,0:T(8,128)(2,1)} %get-tuple-element.127) | copy-start | bytes 1769476
  260.3 14.6 %collective-permute-start.26 = (bf16[1,96,768]{2,1,0:T(8,128)(2,1)S(1)}, bf16[1,96,768]{2,1,0:T(8,128)(2,1)S(1)}, u32[]{:S(2)}, u32[]{:S(2)}) collective-permute-start(bf16[1,96,768]{2,1,0:T(8,128)(2,1)S(1)} %get-tuple-element.184), channel_id=1, source_target_pairs={{0,16},{1,17},{2,18},{3,19},{4,20},{5,21},{6,22},{7,23},{8,24},{9,... | collective-permute-start | bytes 442376 | tf_op jit(solution)/shard_map/ppermute | solution.py:651
  262.8 15.8 %collective-permute-start.17 = (bf16[4,24,1536]{2,1,0:T(8,128)(2,1)S(1)}, bf16[4,24,1536]{2,1,0:T(8,128)(2,1)S(1)}, u32[]{:S(2)}, u32[]{:S(2)}) collective-permute-start(bf16[4,24,1536]{2,1,0:T(8,128)(2,1)S(1)} %get-tuple-element.174), channel_id=1, source_target_pairs={{0,4},{1,5},{2,6},{3,7},{4,0},{5,1},{6,2},{7,3},{8,12},{9,13},{10,... | collective-permute-start | bytes 884744 | tf_op jit(solution)/shard_map/ppermute | solution.py:651
  265.4 13.2 %collective-permute-start.25 = (bf16[1,24,3840]{2,1,0:T(8,128)(2,1)S(1)}, bf16[1,24,3840]{2,1,0:T(8,128)(2,1)S(1)}, u32[]{:S(2)}, u32[]{:S(2)}) collective-permute-start(bf16[1,24,3840]{2,1,0:T(8,128)(2,1)S(1)} %get-tuple-element.178), channel_id=1, source_target_pairs={{0,16},{1,17},{2,18},{3,19},{4,20},{5,21},{6,22},{7,23},{8,24},{9,... | collective-permute-start | bytes 552968 | tf_op jit(solution)/shard_map/ppermute | solution.py:651
  266.9 18.1 %collective-permute-start.20 = (bf16[4,24,896]{2,1,0:T(8,128)(2,1)S(1)}, bf16[4,24,896]{2,1,0:T(8,128)(2,1)S(1)}, u32[]{:S(2)}, u32[]{:S(2)}) collective-permute-start(bf16[4,24,896]{2,1,0:T(8,128)(2,1)S(1)} %get-tuple-element.172), channel_id=1, source_target_pairs={{0,2},{1,3},{2,0},{3,1},{4,6},{5,7},{6,4},{7,5},{8,10},{9,11},{10,... | collective-permute-start | bytes 516104 | tf_op jit(solution)/shard_map/ppermute | solution.py:651
  267.9 17.0 %collective-permute-start.21 = (bf16[4,24,896]{2,1,0:T(8,128)(2,1)S(1)}, bf16[4,24,896]{2,1,0:T(8,128)(2,1)S(1)}, u32[]{:S(2)}, u32[]{:S(2)}) collective-permute-start(bf16[4,24,896]{2,1,0:T(8,128)(2,1)S(1)} %get-tuple-element.171), channel_id=1, source_target_pairs={{0,4},{1,5},{2,6},{3,7},{4,0},{5,1},{6,2},{7,3},{8,12},{9,13},{10,... | collective-permute-start | bytes 516104 | tf_op jit(solution)/shard_map/ppermute | solution.py:651
  274.9 3.9 %copy-start.18 = (f32[24,3072]{1,0:T(8,128)S(1)}, f32[24,3072]{1,0:T(8,128)}, u32[]{:S(2)}) copy-start(f32[24,3072]{1,0:T(8,128)} %param.34) | copy-start | bytes 884740
  275.0 10.0 %collective-permute-start.22 = (bf16[4,24,896]{2,1,0:T(8,128)(2,1)S(1)}, bf16[4,24,896]{2,1,0:T(8,128)(2,1)S(1)}, u32[]{:S(2)}, u32[]{:S(2)}) collective-permute-start(bf16[4,24,896]{2,1,0:T(8,128)(2,1)S(1)} %get-tuple-element.170), channel_id=1, source_target_pairs={{0,6},{1,7},{2,4},{3,5},{4,2},{5,3},{6,0},{7,1},{8,14},{9,15},{10,... | collective-permute-start | bytes 516104 | tf_op jit(solution)/shard_map/ppermute | solution.py:651
  278.7 5.6 %collective-permute-start.18 = (bf16[2,24,1536]{2,1,0:T(8,128)(2,1)S(1)}, bf16[2,24,1536]{2,1,0:T(8,128)(2,1)S(1)}, u32[]{:S(2)}, u32[]{:S(2)}) collective-permute-start(bf16[2,24,1536]{2,1,0:T(8,128)(2,1)S(1)} %get-tuple-element.183), channel_id=1, source_target_pairs={{0,8},{1,9},{2,10},{3,11},{4,12},{5,13},{6,14},{7,15},{8,0},{9,1},... | collective-permute-start | bytes 442376 | tf_op jit(solution)/shard_map/ppermute | solution.py:651
  281.0 14.6 %copy-start.13 = (f32[24,2304]{1,0:T(8,128)S(1)}, f32[24,2304]{1,0:T(8,128)}, u32[]{:S(2)}) copy-start(f32[24,2304]{1,0:T(8,128)} %param.27) | copy-start | bytes 663556
  281.0 14.6 %copy-start.21 = (f32[24,2304]{1,0:T(8,128)S(1)}, f32[24,2304]{1,0:T(8,128)}, u32[]{:S(2)}) copy-start(f32[24,2304]{1,0:T(8,128)} %param.37) | copy-start | bytes 663556
  281.0 14.6 %copy-start.22 = (f32[24,2304]{1,0:T(8,128)S(1)}, f32[24,2304]{1,0:T(8,128)}, u32[]{:S(2)}) copy-start(f32[24,2304]{1,0:T(8,128)} %param.32) | copy-start | bytes 663556
  284.3 6.0 %collective-permute-start.19 = (bf16[1,24,1536]{2,1,0:T(8,128)(2,1)S(1)}, bf16[1,24,1536]{2,1,0:T(8,128)(2,1)S(1)}, u32[]{:S(2)}, u32[]{:S(2)}) collective-permute-start(bf16[1,24,1536]{2,1,0:T(8,128)(2,1)S(1)} %add_convert_fusion.28), channel_id=1, source_target_pairs={{0,16},{1,17},{2,18},{3,19},{4,20},{5,21},{6,22},{7,23},{8,24},{9,... | collective-permute-start | bytes 221192 | tf_op jit(solution)/shard_map/ppermute | solution.py:651
  285.0 11.6 %copy-start.29 = (f32[288]{0:T(512)S(1)}, f32[288]{0:T(512)}, u32[]{:S(2)}) copy-start(f32[288]{0:T(512)} %param.31) | copy-start | bytes 3460
  285.0 11.5 %copy-start.31 = (f32[288]{0:T(512)S(1)}, f32[288]{0:T(512)}, u32[]{:S(2)}) copy-start(f32[288]{0:T(512)} %param.41) | copy-start | bytes 3460
  285.1 11.5 %copy-start.32 = (f32[288]{0:T(512)S(1)}, f32[288]{0:T(512)}, u32[]{:S(2)}) copy-start(f32[288]{0:T(512)} %param.36) | copy-start | bytes 3460
  285.1 5.3 %collective-permute-start.23 = (bf16[2,24,896]{2,1,0:T(8,128)(2,1)S(1)}, bf16[2,24,896]{2,1,0:T(8,128)(2,1)S(1)}, u32[]{:S(2)}, u32[]{:S(2)}) collective-permute-start(bf16[2,24,896]{2,1,0:T(8,128)(2,1)S(1)} %get-tuple-element.181), channel_id=1, source_target_pairs={{0,8},{1,9},{2,10},{3,11},{4,12},{5,13},{6,14},{7,15},{8,0},{9,1},... | collective-permute-start | bytes 258056 | tf_op jit(solution)/shard_map/ppermute | solution.py:651
  290.4 5.0 %collective-permute-start.24 = (bf16[1,24,896]{2,1,0:T(8,128)(2,1)S(1)}, bf16[1,24,896]{2,1,0:T(8,128)(2,1)S(1)}, u32[]{:S(2)}, u32[]{:S(2)}) collective-permute-start(bf16[1,24,896]{2,1,0:T(8,128)(2,1)S(1)} %add_convert_fusion.30), channel_id=1, source_target_pairs={{0,16},{1,17},{2,18},{3,19},{4,20},{5,21},{6,22},{7,23},{8,24},{9,... | collective-permute-start | bytes 129032 | tf_op jit(solution)/shard_map/ppermute | solution.py:651
  (15 other events, 41.2 us)
Sparse Core Ops, SparseCore 0:
  11.5 102.2 all-gather.1

commit v5 on v4

--- a/solution.py
+++ b/solution.py
@@ -675,8 +675,11 @@
     low = [(bit,) for bit in range(min(3, bits))]
     by_x = low + rest
     by_y = low[:1] + low[1:][::-1] + rest
-    both = low[:1] + ([tuple(range(1, min(3, bits)))] if bits > 1 else []) + rest
-    return by_x, by_y, both
+    middle_bits = [tuple(range(1, min(3, bits)))] if bits > 1 else []
+    outward = (low[:1] + middle_bits + rest)[::-1]
+    high = range(3, bits)
+    pairs = [tuple(high[at : at + 2]) for at in range(0, len(high), 2)]
+    return by_x, by_y, low[:1] + middle_bits + pairs, outward
 
 
 class Reduce:
@@ -815,8 +818,7 @@
     piece = proj_qkv.shape[0]
     inner = proj_up.shape[1]
     batch = lengths.shape[0]
-    by_x, by_y, both = stage_orders(devices)
-    outward = both[::-1]
+    by_x, by_y, both, outward = stage_orders(devices)
 
     def source_of(order):
         return jnp.asarray(relative_order(order), jnp.int32) ^ me
@@ -860,20 +862,16 @@
         hidden_in, mixed, cotangent, lengths, wide, vec, piece
     )
 
-    total = Reduce(*tall_gradient(active, grad_branch, source_of(by_x), slot_of), by_x, devices)
-    total.send()
-    grad_upper = hold(grad_upper, total.parts)
     joint = Reduce(
         *joint_gradient(first_low, grad_upper, mixed, grad_attn, source_of(by_y)), by_y, devices
     )
-    total.after(joint.parts)
-    joint.parts = list(hold(tuple(joint.parts), *total.terms))
     joint.send()
-    total.join()
-    joint.join()
+    active = hold(active, joint.parts)
+    total = Reduce(*tall_gradient(active, grad_branch, source_of(by_x), slot_of), by_x, devices)
+    joint.after(total.parts).join()
     grad_mixed = hold(grad_mixed, total.parts, joint.parts)
+    joint.send()
     total.send()
-    joint.send()
     parts, part_sums, queue = [], [], []
     spans = pair_groups(width // LANES)
     for group, span in enumerate(spans):
@@ -881,10 +879,11 @@
         part = ()
         for which in range(batch):
             part = (attend_backward(packed, lengths, lse, grad_mixed, span, which, part),)
-            if which == 0 and final:
-                queue[0].after(part).join()
-                grad_mixed = hold(grad_mixed, queue[0].parts)
-                queue[0].send()
+            if which == 0:
+                chain = queue[0] if final else total
+                chain.after(part).join()
+                grad_mixed = hold(grad_mixed, chain.parts)
+                chain.send()
         left = hidden_in
         if final:
             for chain in (joint, total):
@@ -910,14 +909,20 @@
     keep = jnp.concatenate([keep, ordered[: devices // 2]], axis=2)
     send = jnp.concatenate([send, ordered[devices // 2 :]], axis=2)
     queue.append(Reduce(keep, send, both, devices).send())
-    grad_one = hold(grad_one, send)
+    for chain in (joint, total, queue[0]):
+        chain.after(keep).join()
+    grad_one = hold(grad_one, send, *(chain.parts for chain in (joint, total, queue[0])))
+    for chain in (queue[0], joint, total):
+        chain.send()
     filled = ()
     for which in range(batch):
         if which == batch - 1:
-            for chain in (queue[1], joint, total, queue[0]):
+            for chain in queue[::-1]:
                 chain.after(filled).join()
-            grad_one = hold(grad_one, *(chain.parts for chain in (joint, total, *queue)))
-            for chain in (queue[1], joint, total, queue[0]):
+            grad_one = hold(
+                grad_one, *(chain.parts for chain in queue), joint.terms, total.terms
+            )
+            for chain in queue[::-1]:
                 chain.send()
         filled = (input_gradient(grad_one, gathered, parts, which, batch, filled),)
     input_grad = filled[0]

time: 305 us -> 313 us (1.026)
  Pallas kernels: 159 us -> 163 us
  waiting for transfers between devices: 67.2 us -> 71 us
    ppermute x27 -> x28, waiting for transfers between devices: 59.9 us -> 63.7 us  [swap(): lax.ppermute(value, 'dp', [(index, index ^ mask) for index in range(devic...]
    pallas_call x1, Pallas kernels: 36 us -> 39.5 us  [middle(): pl.pallas_call(functools.partial(middle_kernel, seq=seq, piece=piece), gr...]
    ppermute x27 -> x28, starting transfers between devices: 31.2 us -> 29.7 us  [swap(): lax.ppermute(value, 'dp', [(index, index ^ mask) for index in range(devic...]
    convert_element_type x15 -> x14, other arithmetic: 15 us -> 16.2 us  [join(): self.total(way * size, size).astype(BF)]
  transfers between devices with their start and end apart: 28 -> 29, of which waited for: 14 -> 13; matrix products, arithmetic and copies ran while one was open for 9% -> 9% of each run, Pallas kernels for 37% -> 35%
where the time goes in v5:
time: 313 us; the launch traced here: 312 us
  Pallas kernels  163 us (52%)
  waiting for transfers between devices  71 us (23%)
  starting transfers between devices  29.7 us (9%)
  other arithmetic  28.4 us (9%)
  between operations  14.7 us (5%)
  local copies, waits for them, and re-layouts  5.62 us (2%)
    ppermute x28, waiting for transfers between devices, swap(): lax.ppermute(value, 'dp', [(index, index ^ mask) for index in range(devic...  63.7 us
    pallas_call x1, Pallas kernels, middle(): pl.pallas_call(functools.partial(middle_kernel, seq=seq, piece=piece), gr...  39.5 us
    pallas_call x4, Pallas kernels, attend_backward(): pl.pallas_call(functools.partial(attend_back_kernel, which=which), grid_s...  36.1 us
    ppermute x28, starting transfers between devices, swap(): lax.ppermute(value, 'dp', [(index, index ^ mask) for index in range(devic...  29.7 us
    pallas_call x2, Pallas kernels, attend_forward(): pl.pallas_call(functools.partial(attend_kernel, which=which), grid_spec=g...  21.7 us
    convert_element_type x14, other arithmetic, join(): self.total(way * size, size).astype(BF)  16.2 us
    pallas_call x2, Pallas kernels, weight_gradient(): pl.pallas_call(functools.partial(weight_kernel, sums=sums), grid_spec=gri...  13.8 us
    pallas_call x1, Pallas kernels, joint_gradient(): pl.pallas_call(joint_kernel, grid_spec=grid_spec, out_shape=[shape, shape...  13.5 us
  transfers between devices with their start and end apart: 29, of which 13 were waited for; matrix products, arithmetic and copies ran while one was open for 9% of the time, Pallas kernels for 35%

profile of v5, /device:TPU:0, one launch (start us, length us, event | category | flops | bytes accessed | tf_op | source)
XLA Modules:
  0.0 312.3 jit_solution(573237953365740579)
XLA Ops:
  11.2 4.1 %collective-permute-start = (bf16[1,24,2560]{2,1,0:T(8,128)(2,1)S(1)}, bf16[1,24,2560]{2,1,0:T(8,128)(2,1)S(1)}, u32[]{:S(2)}, u32[]{:S(2)}) collective-permute-start(bf16[1,24,2560]{2,1,0:T(8,128)(2,1)S(1)} %fusion.6), channel_id=1, source_target_pairs={{0,16},{1,17},{2,18},{3,19},{4,20},{5,21},{6,22},{7,23},{8,24},{9,... | collective-permute-start | bytes 368648 | tf_op jit(solution)/shard_map/ppermute | solution.py:651
  15.3 6.0 %collective-permute-done = bf16[1,24,2560]{2,1,0:T(8,128)(2,1)S(1)} collective-permute-done((bf16[1,24,2560]{2,1,0:T(8,128)(2,1)S(1)}, bf16[1,24,2560]{2,1,0:T(8,128)(2,1)S(1)}, u32[]{:S(2)}, u32[]{:S(2)}) %collective-permute-start) | collective-permute-done | bytes 122912 | tf_op jit(solution)/shard_map/ppermute | solution.py:651
  22.1 10.2 %collective-permute-done.1 = bf16[2,24,2560]{2,1,0:T(8,128)(2,1)S(1)} collective-permute-done((bf16[2,24,2560]{2,1,0:T(8,128)(2,1)S(1)}, bf16[2,24,2560]{2,1,0:T(8,128)(2,1)S(1)}, u32[]{:S(2)}, u32[]{:S(2)}) %collective-permute-start.1) | collective-permute-done | bytes 245792 | tf_op jit(solution)/shard_map/ppermute | solution.py:651
  32.3 1.4 collective-permute-start.2
  33.7 1.6 collective-permute-start.3
  36.0 10.9 %collective-permute-done.2 = bf16[4,24,2560]{2,1,0:T(8,128)(2,1)S(1)} collective-permute-done((bf16[4,24,2560]{2,1,0:T(8,128)(2,1)S(1)}, bf16[4,24,2560]{2,1,0:T(8,128)(2,1)S(1)}, u32[]{:S(2)}, u32[]{:S(2)}) %collective-permute-start.2) | collective-permute-done | bytes 491552 | tf_op jit(solution)/shard_map/ppermute | solution.py:651
  47.0 7.0 %collective-permute-done.3 = bf16[4,24,2560]{2,1,0:T(8,128)(2,1)S(1)} collective-permute-done((bf16[4,24,2560]{2,1,0:T(8,128)(2,1)S(1)}, bf16[4,24,2560]{2,1,0:T(8,128)(2,1)S(1)}, u32[]{:S(2)}, u32[]{:S(2)}) %collective-permute-start.3) | collective-permute-done | bytes 491552 | tf_op jit(solution)/shard_map/ppermute | solution.py:651
  54.0 9.7 %collective-permute-done.4 = bf16[4,24,2560]{2,1,0:T(8,128)(2,1)S(1)} collective-permute-done((bf16[4,24,2560]{2,1,0:T(8,128)(2,1)S(1)}, bf16[4,24,2560]{2,1,0:T(8,128)(2,1)S(1)}, u32[]{:S(2)}, u32[]{:S(2)}) %collective-permute-start.4) | collective-permute-done | bytes 491552 | tf_op jit(solution)/shard_map/ppermute | solution.py:651
  65.6 2.3 collective-permute-done.5.taken_ref
  67.9 6.7 %lay_out.1.w_ref = bf16[768,2560]{1,0:T(8,128)(2,1)} custom-call(s32[16]{0:T(128)} %broadcast_xor_fusion.3.index_ref, s32[1]{0:T(128)} %bitcast.odd_ref, bf16[16,24,2560]{2,1,0:T(8,128)(2,1)} %copy-done.5, bf16[16,24,2560]{2,1,0:T(8,128)(2,1)} %collective-permute-done.5.taken_ref), custom_call_target="tpu_custom_call" | custom-call | flops 1966080 | bytes 7864320 | tf_op jit(solution)/shard_map/lay_out/pallas_call | solution.py:776
  76.4 8.5 %project_qkv.1.q_ref.k_ref.v_ref = bf16[1024,2304]{1,0:T(8,128)(2,1)} custom-call(bf16[1024,768]{1,0:T(8,128)(2,1)} %left_ref.2, bf16[768,2560]{1,0:T(8,128)(2,1)} %lay_out.1.w_ref, f32[12,768]{1,0:T(8,128)} %reshape.92.vec_ref), custom_call_target="tpu_custom_call" | custom-call | flops 3623878656 | bytes 9830400 | tf_op jit(solution)/shard_map/project_qkv/pallas_call | solution.py:64
  84.9 10.8 %attend_forward.2 = (bf16[1024,768]{1,0:T(8,128)(2,1)}, f32[12,2,512]{2,1,0:T(2,128)}) custom-call(s32[2]{0:T(128)} %len_ref.13, bf16[1024,2304]{1,0:T(8,128)(2,1)} %project_qkv.1.q_ref.k_ref.v_ref, bf16[1024,2304]{1,0:T(8,128)(2,1)} %project_qkv.1.q_ref.k_ref.v_ref, bf16[1024,2304]{1,0:T(8,128)(2,1)} %project_qkv.1.q_ref.k_ref.v_ref), custom_call_target="tpu_custom_call" | custom-call | flops 3221225472 | bytes 3145728 | tf_op jit(solution)/shard_map/attend_forward/pallas_call | solution.py:122
  95.7 10.9 %attend_forward.3 = (bf16[1024,768]{1,0:T(8,128)(2,1)}, f32[12,2,512]{2,1,0:T(2,128)}) custom-call(s32[2]{0:T(128)} %len_ref.13, bf16[1024,2304]{1,0:T(8,128)(2,1)} %project_qkv.1.q_ref.k_ref.v_ref, bf16[1024,2304]{1,0:T(8,128)(2,1)} %project_qkv.1.q_ref.k_ref.v_ref, ...), custom_call_target="tpu_custom_call", output_to_operand_aliasing={{0}: (4, {}), {1}: (5, {})} | custom-call | flops 3221225472 | bytes 3145728 | tf_op jit(solution)/shard_map/attend_forward/pallas_call | solution.py:122
  106.6 7.3 %all-gather.2.cloned.1.call-done.w_attn.w_up.w_down = bf16[768,6912]{1,0:T(8,128)(2,1)} async-done(((bf16[24,6912]{1,0:T(8,128)(2,1)}), bf16[768,6912]{1,0:T(8,128)(2,1)}) %all-gather.2.cloned.1.call-update) | async-done | bytes 10616848 | tf_op jit(solution)/shard_map/all_gather | solution.py:834
  113.9 39.5 %middle.1 = (bf16[1024,768]{1,0:T(8,128)(2,1)}, bf16[1024,768]{1,0:T(8,128)(2,1)}, bf16[1024,3072]{1,0:T(8,128)(2,1)}, bf16[1024,3072]{1,0:T(8,128)(2,1)}, bf16[...) custom-call(s32[2]{0:T(128)} %len_ref.13, ...), custom_call_target="tpu_custom_call" | custom-call | flops 21743271936 | bytes 37748736 | tf_op jit(solution)/shard_map/middle/pallas_call | solution.py:377
  153.3 13.5 %joint_gradient.1 = (bf16[16,24,3840]{2,1,0:T(8,128)(2,1)}, bf16[16,24,3840]{2,1,0:T(8,128)(2,1)}) custom-call(s32[32]{0:T(128)} %get-tuple-element.198.src_ref, bf16[1024,768]{1,0:T(8,128)(2,1)} %get-tuple-element.87.left_ref, bf16[1024,768]{1,0:T(8,128)(2,1)} %get-tuple-element.84.mixed_ref.last_left_ref, bf16[1024,3072]{1,0:T(8,128)(2,1)} %get-tuple-element.88.right_ref, ...), custom_call_target="tpu_custom_call" | custom-call | flops 48318382080 | bytes 16908288 | tf_op jit(solution)/shard_map/joint_gradient/pallas_call | solution.py:534
  168.5 11.6 %tall_gradient.1 = (bf16[16,96,768]{2,1,0:T(8,128)(2,1)}, bf16[16,96,768]{2,1,0:T(8,128)(2,1)}) custom-call(s32[32]{0:T(128)} %get-tuple-element.197.slot_ref, bf16[1024,3072]{1,0:T(8,128)(2,1)} %get-tuple-element.93.left_ref, bf16[1024,768]{1,0:T(8,128)(2,1)} %get-tuple-element.94.right_ref), custom_call_target="tpu_custom_call" | custom-call | flops 4831838208 | bytes 12582912 | tf_op jit(solution)/shard_map/tall_gradient/pallas_call | solution.py:601
  181.3 2.3 add_convert_fusion
  183.6 1.5 collective-permute-start.7
  185.1 11.2 %attend_backward.4.refs_0_ = bf16[3,1024,512]{2,1,0:T(8,128)(2,1)} custom-call(s32[2]{0:T(128)} %len_ref.13, bf16[1024,2304]{1,0:T(8,128)(2,1)} %project_qkv.1.q_ref.k_ref.v_ref, bf16[1024,2304]{1,0:T(8,128)(2,1)} %project_qkv.1.q_ref.k_ref.v_ref, bf16[1024,2304]{1,0:T(8,128)(2,1)} %project_qkv.1.q_ref.k_ref.v_ref, ...), custom_call_target="tpu_custom_call" | custom-call | flops 42949672960 | bytes 3670016 | tf_op jit(solution)/shard_map/attend_backward/pallas_call | solution.py:192
  196.2 3.8 %add_convert_fusion.2 = (bf16[8,96,768]{2,1,0:T(8,128)(2,1)}, bf16[8,96,768]{2,1,0:T(8,128)(2,1)}) fusion(bf16[16,96,768]{2,1,0:T(8,128)(2,1)} %collective-permute-done.8, bf16[16,96,768]{2,1,0:T(8,128)(2,1)S(1)} %copy-done.4), kind=kLoop, calls=%fused_computation.4 | loop fusion | flops 4718592 | bytes 7077888 | tf_op jit(solution)/shard_map/convert_element_type | solution.py:708
  200.0 11.0 %attend_backward.5.right_ref.refs_0_ = bf16[3,1024,512]{2,1,0:T(8,128)(2,1)} custom-call(s32[2]{0:T(128)} %len_ref.13, bf16[1024,2304]{1,0:T(8,128)(2,1)} %project_qkv.1.q_ref.k_ref.v_ref, bf16[1024,2304]{1,0:T(8,128)(2,1)} %project_qkv.1.q_ref.k_ref.v_ref, bf16[1024,2304]{1,0:T(8,128)(2,1)} %project_qkv.1.q_ref.k_ref.v_ref, ...), custom_call_target="tpu_custom_call", output_to_operand_aliasing={{}: (6, {})} | custom-call | flops 42949672960 | bytes 3670016 | tf_op jit(solution)/shard_map/attend_backward/pallas_call | solution.py:192
  211.1 7.7 %weight_gradient.2 = (bf16[16,24,1536]{2,1,0:T(8,128)(2,1)}, bf16[16,24,1536]{2,1,0:T(8,128)(2,1)}, f32[3,8,512]{2,1,0:T(8,128)}) custom-call(s32[32]{0:T(128)} %get-tuple-element.199.src_ref, bf16[1024,768]{1,0:T(8,128)(2,1)} %left_ref.2, bf16[3,1024,512]{2,1,0:T(8,128)(2,1)} %attend_backward.5.right_ref.refs_0_), custom_call_target="tpu_custom_call" | custom-call | flops 154618822656 | bytes 7077888 | tf_op jit(solution)/shard_map/weight_gradient/pallas_call | solution.py:467
  219.6 8.4 %collective-permute-done.10 = bf16[8,96,768]{2,1,0:T(8,128)(2,1)} collective-permute-done((bf16[8,96,768]{2,1,0:T(8,128)(2,1)}, bf16[8,96,768]{2,1,0:T(8,128)(2,1)}, u32[]{:S(2)}, u32[]{:S(2)}) %collective-permute-start.10) | collective-permute-done | bytes 1179680 | tf_op jit(solution)/shard_map/ppermute | solution.py:651
  228.0 1.6 add_convert_fusion.8
  230.2 1.7 add_convert_fusion.4
  232.2 7.1 %attend_backward.6.refs_0_ = bf16[3,1024,256]{2,1,0:T(8,128)(2,1)} custom-call(s32[2]{0:T(128)} %len_ref.13, bf16[1024,2304]{1,0:T(8,128)(2,1)} %project_qkv.1.q_ref.k_ref.v_ref, bf16[1024,2304]{1,0:T(8,128)(2,1)} %project_qkv.1.q_ref.k_ref.v_ref, bf16[1024,2304]{1,0:T(8,128)(2,1)} %project_qkv.1.q_ref.k_ref.v_ref, ...), custom_call_target="tpu_custom_call" | custom-call | flops 21474836480 | bytes 1835008 | tf_op jit(solution)/shard_map/attend_backward/pallas_call | solution.py:192
  239.4 1.1 add_convert_fusion.6
  240.5 1.7 collective-permute-start.15
  242.2 6.8 %attend_backward.7.right_ref.refs_1_ = bf16[3,1024,256]{2,1,0:T(8,128)(2,1)} custom-call(s32[2]{0:T(128)} %len_ref.13, bf16[1024,2304]{1,0:T(8,128)(2,1)} %project_qkv.1.q_ref.k_ref.v_ref, bf16[1024,2304]{1,0:T(8,128)(2,1)} %project_qkv.1.q_ref.k_ref.v_ref, bf16[1024,2304]{1,0:T(8,128)(2,1)} %project_qkv.1.q_ref.k_ref.v_ref, ...), custom_call_target="tpu_custom_call", output_to_operand_aliasing={{}: (6, {})} | custom-call | flops 21474836480 | bytes 1835008 | tf_op jit(solution)/shard_map/attend_backward/pallas_call | solution.py:192
  249.9 1.5 collective-permute-start.14
  252.3 1.5 collective-permute-start.13
  253.8 6.2 %weight_gradient.3 = (bf16[16,24,768]{2,1,0:T(8,128)(2,1)}, bf16[16,24,768]{2,1,0:T(8,128)(2,1)}, f32[3,8,256]{2,1,0:T(8,128)}) custom-call(s32[32]{0:T(128)} %get-tuple-element.200.src_ref, bf16[1024,768]{1,0:T(8,128)(2,1)} %left_ref.2, bf16[3,1024,256]{2,1,0:T(8,128)(2,1)} %attend_backward.7.right_ref.refs_1_), custom_call_target="tpu_custom_call" | custom-call | flops 77309411328 | bytes 4325376 | tf_op jit(solution)/shard_map/weight_gradient/pallas_call | solution.py:467
  262.6 1.5 collective-permute-start.16
  264.2 1.7 add_convert_fusion.24
  265.9 1.8 collective-permute-start.19
  267.7 1.8 add_convert_fusion.16
  270.6 5.6 %input_gradient.2.refs_2_ = bf16[1024,768]{1,0:T(8,128)(2,1)} custom-call(f32[1024,768]{1,0:T(8,128)} %get-tuple-element.136.resid_ref, bf16[768,2560]{1,0:T(8,128)(2,1)} %lay_out.1.w_ref, bf16[3,1024,512]{2,1,0:T(8,128)(2,1)} %attend_backward.5.right_ref.refs_0_, bf16[3,1024,256]{2,1,0:T(8,128)(2,1)} %attend_backward.7.right_ref.refs_1_), custom_call_target="tpu_custom_call" | custom-call | flops 115964116992 | bytes 6488064 | tf_op jit(solution)/shard_map/input_gradient/pallas_call | solution.py:628
  276.3 1.4 collective-permute-start.20
  278.2 1.3 collective-permute-start.23
  279.6 1.1 collective-permute-done.19
  280.7 1.2 collective-permute-start.24
  281.9 2.0 collective-permute-done.18
  283.9 5.7 %input_gradient.3 = bf16[1024,768]{1,0:T(8,128)(2,1)} custom-call(f32[1024,768]{1,0:T(8,128)} %get-tuple-element.136.resid_ref, bf16[768,2560]{1,0:T(8,128)(2,1)} %lay_out.1.w_ref, bf16[3,1024,512]{2,1,0:T(8,128)(2,1)} %attend_backward.5.right_ref.refs_0_, bf16[3,1024,256]{2,1,0:T(8,128)(2,1)} %attend_backward.7.right_ref.refs_1_, ...), custom_call_target="tpu_custom_call", output_to_operand_aliasing={{}: (4, {})} | custom-call | flops 115964116992 | bytes 6488064 | tf_op jit(solution)/shard_map/input_gradient/pallas_call | solution.py:628
  292.8 2.3 collective-permute-done.21
  295.6 2.2 collective-permute-start.26
  297.8 1.9 collective-permute-start.27
  300.5 3.1 %collective-permute-done.27 = bf16[1,24,896]{2,1,0:T(8,128)(2,1)S(1)} collective-permute-done((bf16[1,24,896]{2,1,0:T(8,128)(2,1)S(1)}, bf16[1,24,896]{2,1,0:T(8,128)(2,1)S(1)}, u32[]{:S(2)}, u32[]{:S(2)}) %collective-permute-start.27) | collective-permute-done | bytes 43040 | tf_op jit(solution)/shard_map/ppermute | solution.py:651
  (163 shorter events, 25.7 us)
Async XLA Ops:
  7.2 106.7 %all-gather.2.cloned.1.call-start = ((), (), s32[]{:S(2)}) async-start(), calls=%async_computation | async-start | bytes 10948608 | tf_op jit(solution)/shard_map/all_gather | solution.py:834
  11.2 10.1 %collective-permute-start = (bf16[1,24,2560]{2,1,0:T(8,128)(2,1)S(1)}, bf16[1,24,2560]{2,1,0:T(8,128)(2,1)S(1)}, u32[]{:S(2)}, u32[]{:S(2)}) collective-permute-start(bf16[1,24,2560]{2,1,0:T(8,128)(2,1)S(1)} %fusion.6), channel_id=1, source_target_pairs={{0,16},{1,17},{2,18},{3,19},{4,20},{5,21},{6,22},{7,23},{8,24},{9,... | collective-permute-start | bytes 368648 | tf_op jit(solution)/shard_map/ppermute | solution.py:651
  21.3 11.0 %collective-permute-start.1 = (bf16[2,24,2560]{2,1,0:T(8,128)(2,1)S(1)}, bf16[2,24,2560]{2,1,0:T(8,128)(2,1)S(1)}, u32[]{:S(2)}, u32[]{:S(2)}) collective-permute-start(bf16[2,24,2560]{2,1,0:T(8,128)(2,1)S(1)} %pad_maximum_fusion.4), channel_id=1, source_target_pairs={{0,8},{1,9},{2,10},{3,11},{4,12},{5,13},{6,14},{7,15},{8,0},{9,1},... | collective-permute-start | bytes 737288 | tf_op jit(solution)/shard_map/ppermute | solution.py:651
  32.3 14.6 %collective-permute-start.2 = (bf16[4,24,2560]{2,1,0:T(8,128)(2,1)S(1)}, bf16[4,24,2560]{2,1,0:T(8,128)(2,1)S(1)}, u32[]{:S(2)}, u32[]{:S(2)}) collective-permute-start(bf16[4,24,2560]{2,1,0:T(8,128)(2,1)S(1)} %pad_maximum_fusion.2), channel_id=1, source_target_pairs={{0,2},{1,3},{2,0},{3,1},{4,6},{5,7},{6,4},{7,5},{8,10},{9,11},{10,... | collective-permute-start | bytes 1474568 | tf_op jit(solution)/shard_map/ppermute | solution.py:651
  33.7 20.2 %collective-permute-start.3 = (bf16[4,24,2560]{2,1,0:T(8,128)(2,1)S(1)}, bf16[4,24,2560]{2,1,0:T(8,128)(2,1)S(1)}, u32[]{:S(2)}, u32[]{:S(2)}) collective-permute-start(bf16[4,24,2560]{2,1,0:T(8,128)(2,1)S(1)} %pad_maximum_fusion.2), channel_id=1, source_target_pairs={{0,4},{1,5},{2,6},{3,7},{4,0},{5,1},{6,2},{7,3},{8,12},{9,13},{10,... | collective-permute-start | bytes 1474568 | tf_op jit(solution)/shard_map/ppermute | solution.py:651
  35.4 28.3 %collective-permute-start.4 = (bf16[4,24,2560]{2,1,0:T(8,128)(2,1)S(1)}, bf16[4,24,2560]{2,1,0:T(8,128)(2,1)S(1)}, u32[]{:S(2)}, u32[]{:S(2)}) collective-permute-start(bf16[4,24,2560]{2,1,0:T(8,128)(2,1)S(1)} %pad_maximum_fusion.2), channel_id=1, source_target_pairs={{0,6},{1,7},{2,4},{3,5},{4,2},{5,3},{6,0},{7,1},{8,14},{9,15},{10,... | collective-permute-start | bytes 1474568 | tf_op jit(solution)/shard_map/ppermute | solution.py:651
  36.0 27.8 %copy-start = (s32[32]{0:T(128)S(1)}, s32[32]{0:T(128)}, u32[]{:S(2)}) copy-start(s32[32]{0:T(128)} %constant.46.clone) | copy-start | bytes 388
  36.0 28.5 %copy-start.33 = (s32[16]{0:T(128)S(1)}, s32[16]{0:T(128)}, u32[]{:S(2)}) copy-start(s32[16]{0:T(128)} %constant.47.clone) | copy-start | bytes 196
  36.0 29.0 %copy-start.32 = (s32[32]{0:T(128)S(1)}, s32[32]{0:T(128)}, u32[]{:S(2)}) copy-start(s32[32]{0:T(128)} %constant.48.clone) | copy-start | bytes 388
  63.7 4.2 %collective-permute-start.5 = (bf16[16,24,2560]{2,1,0:T(8,128)(2,1)S(1)}, bf16[16,24,2560]{2,1,0:T(8,128)(2,1)}, u32[]{:S(2)}, u32[]{:S(2)}) collective-permute-start(bf16[16,24,2560]{2,1,0:T(8,128)(2,1)S(1)} %constant_dynamic-update-slice_fusion.held_ref), channel_id=1, source_target_pairs={{0,1},{1,0},{2,3},{3,2},{4,5},{5,4},{6,7},{7,6},{8,9},{9,8},{10,11... | collective-permute-start | bytes 5898248 | tf_op jit(solution)/shard_map/ppermute | solution.py:651
  153.3 13.6 %copy-start.31 = (s32[32]{0:T(128)S(1)}, s32[32]{0:T(128)}, u32[]{:S(2)}) copy-start(s32[32]{0:T(128)} %constant.49.clone) | copy-start | bytes 388
  166.9 14.4 %collective-permute-start.6 = (bf16[16,24,3840]{2,1,0:T(8,128)(2,1)}, bf16[16,24,3840]{2,1,0:T(8,128)(2,1)S(1)}, u32[]{:S(2)}, u32[]{:S(2)}) collective-permute-start(bf16[16,24,3840]{2,1,0:T(8,128)(2,1)} %get-tuple-element.91), channel_id=1, source_target_pairs={{0,1},{1,0},{2,3},{3,2},{4,5},{5,4},{6,7},{7,6},{8,9},{9,8},{10,11... | collective-permute-start | bytes 8847368 | tf_op jit(solution)/shard_map/ppermute | solution.py:651
  168.5 12.1 %copy-start.25 = (f32[12,768]{1,0:T(8,128)S(1)}, f32[12,768]{1,0:T(8,128)}, u32[]{:S(2)}) copy-start(f32[12,768]{1,0:T(8,128)} %get-tuple-element.123) | copy-start | bytes 110596
  168.5 12.7 %copy-start.3 = (bf16[16,24,3840]{2,1,0:T(8,128)(2,1)S(1)}, bf16[16,24,3840]{2,1,0:T(8,128)(2,1)}, u32[]{:S(2)}) copy-start(bf16[16,24,3840]{2,1,0:T(8,128)(2,1)} %get-tuple-element.97) | copy-start | bytes 8847364
  180.1 16.1 %collective-permute-start.8 = (bf16[16,96,768]{2,1,0:T(8,128)(2,1)}, bf16[16,96,768]{2,1,0:T(8,128)(2,1)}, u32[]{:S(2)}, u32[]{:S(2)}) collective-permute-start(bf16[16,96,768]{2,1,0:T(8,128)(2,1)} %get-tuple-element.96), channel_id=1, source_target_pairs={{0,1},{1,0},{2,3},{3,2},{4,5},{5,4},{6,7},{7,6},{8,9},{9,8},{10,11... | collective-permute-start | bytes 7077896 | tf_op jit(solution)/shard_map/ppermute | solution.py:651
  183.6 46.7 %collective-permute-start.7 = (bf16[8,24,3840]{2,1,0:T(8,128)(2,1)}, bf16[8,24,3840]{2,1,0:T(8,128)(2,1)}, u32[]{:S(2)}, u32[]{:S(2)}) collective-permute-start(bf16[8,24,3840]{2,1,0:T(8,128)(2,1)} %get-tuple-element.164), channel_id=1, source_target_pairs={{0,4},{1,5},{2,6},{3,7},{4,0},{5,1},{6,2},{7,3},{8,12},{9,13},{10,... | collective-permute-start | bytes 4423688 | tf_op jit(solution)/shard_map/ppermute | solution.py:651
  185.1 11.2 %copy-start.4 = (bf16[16,96,768]{2,1,0:T(8,128)(2,1)S(1)}, bf16[16,96,768]{2,1,0:T(8,128)(2,1)}, u32[]{:S(2)}) copy-start(bf16[16,96,768]{2,1,0:T(8,128)(2,1)} %get-tuple-element.102) | copy-start | bytes 7077892
  200.0 27.9 %collective-permute-start.10 = (bf16[8,96,768]{2,1,0:T(8,128)(2,1)}, bf16[8,96,768]{2,1,0:T(8,128)(2,1)}, u32[]{:S(2)}, u32[]{:S(2)}) collective-permute-start(bf16[8,96,768]{2,1,0:T(8,128)(2,1)} %get-tuple-element.166), channel_id=1, source_target_pairs={{0,2},{1,3},{2,0},{3,1},{4,6},{5,7},{6,4},{7,5},{8,10},{9,11},{10,... | collective-permute-start | bytes 3538952 | tf_op jit(solution)/shard_map/ppermute | solution.py:651
  211.1 16.9 %copy-start.2 = (bf16[8,96,768]{2,1,0:T(8,128)(2,1)S(1)}, bf16[8,96,768]{2,1,0:T(8,128)(2,1)}, u32[]{:S(2)}) copy-start(bf16[8,96,768]{2,1,0:T(8,128)(2,1)} %get-tuple-element.108) | copy-start | bytes 3538948
  218.8 20.6 %collective-permute-start.11 = (bf16[16,24,1536]{2,1,0:T(8,128)(2,1)}, bf16[16,24,1536]{2,1,0:T(8,128)(2,1)S(1)}, u32[]{:S(2)}, u32[]{:S(2)}) collective-permute-start(bf16[16,24,1536]{2,1,0:T(8,128)(2,1)} %get-tuple-element.111), channel_id=1, source_target_pairs={{0,1},{1,0},{2,3},{3,2},{4,5},{5,4},{6,7},{7,6},{8,9},{9,8},{10,11... | collective-permute-start | bytes 3538952 | tf_op jit(solution)/shard_map/ppermute | solution.py:651
  229.6 19.4 %collective-permute-start.12 = (bf16[4,96,768]{2,1,0:T(8,128)(2,1)S(1)}, bf16[4,96,768]{2,1,0:T(8,128)(2,1)S(1)}, u32[]{:S(2)}, u32[]{:S(2)}) collective-permute-start(bf16[4,96,768]{2,1,0:T(8,128)(2,1)S(1)} %get-tuple-element.172), channel_id=1, source_target_pairs={{0,4},{1,5},{2,6},{3,7},{4,0},{5,1},{6,2},{7,3},{8,12},{9,13},{10,... | collective-permute-start | bytes 1769480 | tf_op jit(solution)/shard_map/ppermute | solution.py:651
  231.9 19.5 %collective-permute-start.9 = (bf16[4,24,3840]{2,1,0:T(8,128)(2,1)S(1)}, bf16[4,24,3840]{2,1,0:T(8,128)(2,1)S(1)}, u32[]{:S(2)}, u32[]{:S(2)}) collective-permute-start(bf16[4,24,3840]{2,1,0:T(8,128)(2,1)S(1)} %get-tuple-element.168), channel_id=1, source_target_pairs={{0,2},{1,3},{2,0},{3,1},{4,6},{5,7},{6,4},{7,5},{8,10},{9,11},{10,... | collective-permute-start | bytes 2211848 | tf_op jit(solution)/shard_map/ppermute | solution.py:651
  232.2 7.1 %copy-start.6 = (bf16[16,24,1536]{2,1,0:T(8,128)(2,1)S(1)}, bf16[16,24,1536]{2,1,0:T(8,128)(2,1)}, u32[]{:S(2)}) copy-start(bf16[16,24,1536]{2,1,0:T(8,128)(2,1)} %get-tuple-element.112) | copy-start | bytes 3538948
  240.5 21.8 %collective-permute-start.15 = (bf16[8,24,1536]{2,1,0:T(8,128)(2,1)}, bf16[8,24,1536]{2,1,0:T(8,128)(2,1)S(1)}, u32[]{:S(2)}, u32[]{:S(2)}) collective-permute-start(bf16[8,24,1536]{2,1,0:T(8,128)(2,1)} %get-tuple-element.170), channel_id=1, source_target_pairs={{0,2},{1,3},{2,0},{3,1},{4,6},{5,7},{6,4},{7,5},{8,10},{9,11},{10,... | collective-permute-start | bytes 1769480 | tf_op jit(solution)/shard_map/ppermute | solution.py:651
  249.9 12.4 %collective-permute-start.14 = (bf16[2,96,768]{2,1,0:T(8,128)(2,1)}, bf16[2,96,768]{2,1,0:T(8,128)(2,1)}, u32[]{:S(2)}, u32[]{:S(2)}) collective-permute-start(bf16[2,96,768]{2,1,0:T(8,128)(2,1)} %get-tuple-element.182), channel_id=1, source_target_pairs={{0,8},{1,9},{2,10},{3,11},{4,12},{5,13},{6,14},{7,15},{8,0},{9,1},... | collective-permute-start | bytes 884744 | tf_op jit(solution)/shard_map/ppermute | solution.py:651
  252.3 15.4 %collective-permute-start.13 = (bf16[2,24,3840]{2,1,0:T(8,128)(2,1)}, bf16[2,24,3840]{2,1,0:T(8,128)(2,1)}, u32[]{:S(2)}, u32[]{:S(2)}) collective-permute-start(bf16[2,24,3840]{2,1,0:T(8,128)(2,1)} %get-tuple-element.174), channel_id=1, source_target_pairs={{0,8},{1,9},{2,10},{3,11},{4,12},{5,13},{6,14},{7,15},{8,0},{9,1},... | collective-permute-start | bytes 1105928 | tf_op jit(solution)/shard_map/ppermute | solution.py:651
  253.8 7.0 %copy-start.22 = (bf16[10,768]{1,0:T(8,128)(2,1)S(1)}, bf16[10,768]{1,0:T(8,128)(2,1)}, u32[]{:S(2)}) copy-start(bf16[10,768]{1,0:T(8,128)(2,1)} %slice.292) | copy-start | bytes 46084
  253.8 8.2 %copy-start.28 = (pred[32]{0:T(512)(128)(4,1)S(1)}, pred[32]{0:T(512)(128)(4,1)}, u32[]{:S(2)}) copy-start(pred[32]{0:T(512)(128)(4,1)} %get-tuple-element.162) | copy-start | bytes 100
  262.4 15.2 %collective-permute-start.17 = (bf16[16,24,896]{2,1,0:T(8,128)(2,1)S(1)}, bf16[16,24,896]{2,1,0:T(8,128)(2,1)S(1)}, u32[]{:S(2)}, u32[]{:S(2)}) collective-permute-start(bf16[16,24,896]{2,1,0:T(8,128)(2,1)S(1)} %pad_maximum_fusion), channel_id=1, source_target_pairs={{0,1},{1,0},{2,3},{3,2},{4,5},{5,4},{6,7},{7,6},{8,9},{9,8},{10,11... | collective-permute-start | bytes 2064392 | tf_op jit(solution)/shard_map/ppermute | solution.py:651
  262.6 13.6 %collective-permute-start.16 = (bf16[4,24,1536]{2,1,0:T(8,128)(2,1)S(1)}, bf16[4,24,1536]{2,1,0:T(8,128)(2,1)S(1)}, u32[]{:S(2)}, u32[]{:S(2)}) collective-permute-start(bf16[4,24,1536]{2,1,0:T(8,128)(2,1)S(1)} %get-tuple-element.180), channel_id=1, source_target_pairs={{0,4},{1,5},{2,6},{3,7},{4,0},{5,1},{6,2},{7,3},{8,12},{9,13},{10,... | collective-permute-start | bytes 884744 | tf_op jit(solution)/shard_map/ppermute | solution.py:651
  265.9 14.8 %collective-permute-start.19 = (bf16[1,96,768]{2,1,0:T(8,128)(2,1)S(1)}, bf16[1,96,768]{2,1,0:T(8,128)(2,1)S(1)}, u32[]{:S(2)}, u32[]{:S(2)}) collective-permute-start(bf16[1,96,768]{2,1,0:T(8,128)(2,1)S(1)} %get-tuple-element.191), channel_id=1, source_target_pairs={{0,16},{1,17},{2,18},{3,19},{4,20},{5,21},{6,22},{7,23},{8,24},{9,... | collective-permute-start | bytes 442376 | tf_op jit(solution)/shard_map/ppermute | solution.py:651
  269.5 14.4 %collective-permute-start.18 = (bf16[1,24,3840]{2,1,0:T(8,128)(2,1)S(1)}, bf16[1,24,3840]{2,1,0:T(8,128)(2,1)S(1)}, u32[]{:S(2)}, u32[]{:S(2)}) collective-permute-start(bf16[1,24,3840]{2,1,0:T(8,128)(2,1)S(1)} %get-tuple-element.184), channel_id=1, source_target_pairs={{0,16},{1,17},{2,18},{3,19},{4,20},{5,21},{6,22},{7,23},{8,24},{9,... | collective-permute-start | bytes 552968 | tf_op jit(solution)/shard_map/ppermute | solution.py:651
  276.3 13.4 %collective-permute-start.20 = (bf16[2,24,1536]{2,1,0:T(8,128)(2,1)S(1)}, bf16[2,24,1536]{2,1,0:T(8,128)(2,1)S(1)}, u32[]{:S(2)}, u32[]{:S(2)}) collective-permute-start(bf16[2,24,1536]{2,1,0:T(8,128)(2,1)S(1)} %get-tuple-element.189), channel_id=1, source_target_pairs={{0,8},{1,9},{2,10},{3,11},{4,12},{5,13},{6,14},{7,15},{8,0},{9,1},... | collective-permute-start | bytes 442376 | tf_op jit(solution)/shard_map/ppermute | solution.py:651
  277.8 17.3 %collective-permute-start.22 = (bf16[4,24,896]{2,1,0:T(8,128)(2,1)S(1)}, bf16[4,24,896]{2,1,0:T(8,128)(2,1)S(1)}, u32[]{:S(2)}, u32[]{:S(2)}) collective-permute-start(bf16[4,24,896]{2,1,0:T(8,128)(2,1)S(1)} %get-tuple-element.178), channel_id=1, source_target_pairs={{0,2},{1,3},{2,0},{3,1},{4,6},{5,7},{6,4},{7,5},{8,10},{9,11},{10,... | collective-permute-start | bytes 516104 | tf_op jit(solution)/shard_map/ppermute | solution.py:651
  278.2 16.9 %collective-permute-start.23 = (bf16[4,24,896]{2,1,0:T(8,128)(2,1)S(1)}, bf16[4,24,896]{2,1,0:T(8,128)(2,1)S(1)}, u32[]{:S(2)}, u32[]{:S(2)}) collective-permute-start(bf16[4,24,896]{2,1,0:T(8,128)(2,1)S(1)} %get-tuple-element.177), channel_id=1, source_target_pairs={{0,4},{1,5},{2,6},{3,7},{4,0},{5,1},{6,2},{7,3},{8,12},{9,13},{10,... | collective-permute-start | bytes 516104 | tf_op jit(solution)/shard_map/ppermute | solution.py:651
  280.7 14.5 %collective-permute-start.24 = (bf16[4,24,896]{2,1,0:T(8,128)(2,1)S(1)}, bf16[4,24,896]{2,1,0:T(8,128)(2,1)S(1)}, u32[]{:S(2)}, u32[]{:S(2)}) collective-permute-start(bf16[4,24,896]{2,1,0:T(8,128)(2,1)S(1)} %get-tuple-element.176), channel_id=1, source_target_pairs={{0,6},{1,7},{2,4},{3,5},{4,2},{5,3},{6,0},{7,1},{8,14},{9,15},{10,... | collective-permute-start | bytes 516104 | tf_op jit(solution)/shard_map/ppermute | solution.py:651
  283.9 5.9 %copy-start.16 = (f32[24,3072]{1,0:T(8,128)S(1)}, f32[24,3072]{1,0:T(8,128)}, u32[]{:S(2)}) copy-start(f32[24,3072]{1,0:T(8,128)} %param.39) | copy-start | bytes 884740
  283.9 5.9 %copy-start.17 = (f32[24,3072]{1,0:T(8,128)S(1)}, f32[24,3072]{1,0:T(8,128)}, u32[]{:S(2)}) copy-start(f32[24,3072]{1,0:T(8,128)} %param.34) | copy-start | bytes 884740
  289.7 5.4 %collective-permute-start.21 = (bf16[1,24,1536]{2,1,0:T(8,128)(2,1)S(1)}, bf16[1,24,1536]{2,1,0:T(8,128)(2,1)S(1)}, u32[]{:S(2)}, u32[]{:S(2)}) collective-permute-start(bf16[1,24,1536]{2,1,0:T(8,128)(2,1)S(1)} %add_convert_fusion.26), channel_id=1, source_target_pairs={{0,16},{1,17},{2,18},{3,19},{4,20},{5,21},{6,22},{7,23},{8,24},{9,... | collective-permute-start | bytes 221192 | tf_op jit(solution)/shard_map/ppermute | solution.py:651
  292.0 11.8 %copy-start.10 = (f32[24,2304]{1,0:T(8,128)S(1)}, f32[24,2304]{1,0:T(8,128)}, u32[]{:S(2)}) copy-start(f32[24,2304]{1,0:T(8,128)} %param.27) | copy-start | bytes 663556
  292.1 11.8 %copy-start.20 = (f32[24,2304]{1,0:T(8,128)S(1)}, f32[24,2304]{1,0:T(8,128)}, u32[]{:S(2)}) copy-start(f32[24,2304]{1,0:T(8,128)} %param.37) | copy-start | bytes 663556
  292.1 11.8 %copy-start.21 = (f32[24,2304]{1,0:T(8,128)S(1)}, f32[24,2304]{1,0:T(8,128)}, u32[]{:S(2)}) copy-start(f32[24,2304]{1,0:T(8,128)} %param.32) | copy-start | bytes 663556
  295.1 9.7 %copy-start.27 = (f32[288]{0:T(512)S(1)}, f32[288]{0:T(512)}, u32[]{:S(2)}) copy-start(f32[288]{0:T(512)} %param.31) | copy-start | bytes 3460
  295.1 9.7 %copy-start.29 = (f32[288]{0:T(512)S(1)}, f32[288]{0:T(512)}, u32[]{:S(2)}) copy-start(f32[288]{0:T(512)} %param.41) | copy-start | bytes 3460
  295.1 9.7 %copy-start.30 = (f32[288]{0:T(512)S(1)}, f32[288]{0:T(512)}, u32[]{:S(2)}) copy-start(f32[288]{0:T(512)} %param.36) | copy-start | bytes 3460
  295.3 4.5 %collective-permute-start.25 = (bf16[1,24,896]{2,1,0:T(8,128)(2,1)S(1)}, bf16[1,24,896]{2,1,0:T(8,128)(2,1)S(1)}, u32[]{:S(2)}, u32[]{:S(2)}) collective-permute-start(bf16[1,24,896]{2,1,0:T(8,128)(2,1)S(1)} %get-tuple-element.186), channel_id=1, source_target_pairs={{0,8},{1,9},{2,10},{3,11},{4,12},{5,13},{6,14},{7,15},{8,0},{9,1},... | collective-permute-start | bytes 129032 | tf_op jit(solution)/shard_map/ppermute | solution.py:651
  295.6 4.9 %collective-permute-start.26 = (bf16[1,24,896]{2,1,0:T(8,128)(2,1)S(1)}, bf16[1,24,896]{2,1,0:T(8,128)(2,1)S(1)}, u32[]{:S(2)}, u32[]{:S(2)}) collective-permute-start(bf16[1,24,896]{2,1,0:T(8,128)(2,1)S(1)} %get-tuple-element.188), channel_id=1, source_target_pairs={{0,16},{1,17},{2,18},{3,19},{4,20},{5,21},{6,22},{7,23},{8,24},{9,... | collective-permute-start | bytes 129032 | tf_op jit(solution)/shard_map/ppermute | solution.py:651
  297.8 5.8 %collective-permute-start.27 = (bf16[1,24,896]{2,1,0:T(8,128)(2,1)S(1)}, bf16[1,24,896]{2,1,0:T(8,128)(2,1)S(1)}, u32[]{:S(2)}, u32[]{:S(2)}) collective-permute-start(bf16[1,24,896]{2,1,0:T(8,128)(2,1)S(1)} %get-tuple-element.187), channel_id=1, source_target_pairs={{0,24},{1,25},{2,26},{3,27},{4,28},{5,29},{6,30},{7,31},{8,16},{9,... | collective-permute-start | bytes 129032 | tf_op jit(solution)/shard_map/ppermute | solution.py:651
  (15 other events, 42.4 us)
Sparse Core Ops, SparseCore 0:
  11.5 102.2 all-gather.1

commit v6 on v4

--- a/solution.py
+++ b/solution.py
@@ -77,6 +77,18 @@
     )(x, gathered, vec)
 
 
+def masked_scores(query, keyset, length, head):
+    lane = lax.broadcasted_iota(jnp.int32, query.shape, 1)
+    alive = lax.broadcasted_iota(jnp.int32, query.shape, 0) < length
+    mine = (lane < HEAD) if head == 0 else (lane >= HEAD)
+    spare = lane == (HEAD if head == 0 else 0)
+    zeros = jnp.zeros(query.shape, F32)
+    adding = jnp.where(alive, zeros, -1e30)
+    key_side = jnp.where(mine, keyset.astype(F32), jnp.where(spare, adding, zeros)).astype(BF)
+    query_side = jnp.where(mine, query.astype(F32), jnp.where(spare, 1.0, 0.0)).astype(BF)
+    return dot(key_side, query_side, NT)
+
+
 def attend_kernel(len_ref, q_ref, k_ref, v_ref, *refs, which):
     out_ref, lse_ref = refs[-2:]
     length = len_ref[which]
@@ -84,13 +96,9 @@
     query = q_ref[...] * jnp.asarray(1.0 / math.sqrt(HEAD), BF)
     keyset = k_ref[...]
     val_t = v_ref[...].T
-    lane = lax.broadcasted_iota(jnp.int32, (seq, LANES), 1)
-    alive = lax.broadcasted_iota(jnp.int32, (seq, seq), 0) < length
     mixed = []
     for head in range(2):
-        mine = (lane < HEAD) if head == 0 else (lane >= HEAD)
-        scores = dot(keyset, jnp.where(mine, query, jnp.zeros_like(query)), NT)
-        scores = jnp.where(alive, scores, -1e30)
+        scores = masked_scores(query, keyset, length, head)
         highest = jnp.max(scores, axis=0, keepdims=True)
         expo = jnp.exp(scores - highest)
         summed = jnp.sum(expo, axis=0, keepdims=True)
@@ -144,7 +152,6 @@
     grad = g_ref[...]
     key_t = keyset.T
     lane = lax.broadcasted_iota(jnp.int32, (seq, LANES), 1)
-    alive = lax.broadcasted_iota(jnp.int32, (seq, seq), 0) < length
     grad_q = []
     grad_k = 0.0
     grad_v = 0.0
@@ -152,7 +159,7 @@
         mine = (lane < HEAD) if head == 0 else (lane >= HEAD)
         query_h = jnp.where(mine, query, jnp.zeros_like(query))
         grad_h = jnp.where(mine, grad, jnp.zeros_like(grad))
-        scores = jnp.where(alive, dot(keyset, query_h, NT), -1e30)
+        scores = masked_scores(query, keyset, length, head)
         probs = jnp.exp(scores - lse_ref[0, head : head + 1, :])
         grad_probs = dot(valset, grad_h, NT)
         total = jnp.sum(probs * grad_probs, axis=0, keepdims=True)
@@ -165,17 +172,12 @@
     out_ref[2] = grad_v.astype(BF)
 
 
-def pair_groups(pairs):
-    first = 2 * pairs // 3
-    return ((0, first), (first, pairs - first))
-
-
-def attend_backward(packed, lengths, lse, grad_mixed, span, which, filled):
+def attend_backward(packed, lengths, lse, grad_mixed, which, filled):
     rows, width = grad_mixed.shape
     batch = lengths.shape[0]
     seq = rows // batch
     pairs = width // LANES
-    base, here = span
+    base, here = 0, pairs
     grid_spec = pltpu.PrefetchScalarGridSpec(
         num_scalar_prefetch=1,
         grid=(here,),
@@ -675,8 +677,11 @@
     low = [(bit,) for bit in range(min(3, bits))]
     by_x = low + rest
     by_y = low[:1] + low[1:][::-1] + rest
-    both = low[:1] + ([tuple(range(1, min(3, bits)))] if bits > 1 else []) + rest
-    return by_x, by_y, both
+    middle_bits = [tuple(range(1, min(3, bits)))] if bits > 1 else []
+    outward = (low[:1] + middle_bits + rest)[::-1]
+    high = range(3, bits)
+    pairs = [tuple(high[at : at + 2]) for at in range(0, len(high), 2)]
+    return by_x, by_y, low[:1] + middle_bits + pairs, outward
 
 
 class Reduce:
@@ -815,8 +820,7 @@
     piece = proj_qkv.shape[0]
     inner = proj_up.shape[1]
     batch = lengths.shape[0]
-    by_x, by_y, both = stage_orders(devices)
-    outward = both[::-1]
+    by_x, by_y, both, outward = stage_orders(devices)
 
     def source_of(order):
         return jnp.asarray(relative_order(order), jnp.int32) ^ me
@@ -874,67 +878,38 @@
     grad_mixed = hold(grad_mixed, total.parts, joint.parts)
     total.send()
     joint.send()
-    parts, part_sums, queue = [], [], []
-    spans = pair_groups(width // LANES)
-    for group, span in enumerate(spans):
-        final = group == len(spans) - 1
-        part = ()
-        for which in range(batch):
-            part = (attend_backward(packed, lengths, lse, grad_mixed, span, which, part),)
-            if which == 0 and final:
-                queue[0].after(part).join()
-                grad_mixed = hold(grad_mixed, queue[0].parts)
-                queue[0].send()
-        left = hidden_in
-        if final:
-            for chain in (joint, total):
-                chain.after(part).join()
-            left = hold(hidden_in, joint.parts, total.parts)
-            for chain in (joint, total):
-                chain.send()
-        order = both if final else by_x
-        keep, send, part_sum = weight_gradient(left, part[0], source_of(order), sums=True)
-        parts.append(part[0])
-        part_sums.append(part_sum)
-        if group == 0:
-            queue.append(Reduce(keep, send, order, devices).send())
-            for chain in (joint, total):
-                chain.after(keep).join()
-            grad_mixed = hold(grad_mixed, joint.parts, total.parts, keep)
-            for chain in (joint, total):
-                chain.send()
-    part_sums = jnp.concatenate(part_sums, axis=2)
+    part = ()
+    for which in range(batch):
+        part = (attend_backward(packed, lengths, lse, grad_mixed, which, part),)
+    for chain in (joint, total):
+        chain.after(part).join()
+    left = hold(hidden_in, joint.parts, total.parts)
+    for chain in (joint, total):
+        chain.send()
+    keep, send, part_sums = weight_gradient(left, part[0], source_of(both), sums=True)
     vector_sums = jnp.concatenate([part_sums[0, :1], part_sums[2, :1], sums[2:]], axis=0)
     ordered = jnp.take(vector_sums.reshape(devices, piece, entries), source_of(both), axis=0)
     ordered = jnp.pad(ordered.astype(BF), ((0, 0), (0, 0), (0, LANES - entries)))
     keep = jnp.concatenate([keep, ordered[: devices // 2]], axis=2)
     send = jnp.concatenate([send, ordered[devices // 2 :]], axis=2)
-    queue.append(Reduce(keep, send, both, devices).send())
+    narrow = Reduce(keep, send, both, devices).send()
     grad_one = hold(grad_one, send)
     filled = ()
     for which in range(batch):
         if which == batch - 1:
-            for chain in (queue[1], joint, total, queue[0]):
+            for chain in (narrow, joint, total):
                 chain.after(filled).join()
-            grad_one = hold(grad_one, *(chain.parts for chain in (joint, total, *queue)))
-            for chain in (queue[1], joint, total, queue[0]):
+            grad_one = hold(grad_one, *(chain.parts for chain in (narrow, joint, total)))
+            for chain in (narrow, joint, total):
                 chain.send()
-        filled = (input_gradient(grad_one, gathered, parts, which, batch, filled),)
+        filled = (input_gradient(grad_one, gathered, part, which, batch, filled),)
     input_grad = filled[0]
-    for chain in (joint, total, *queue):
+    for chain in (joint, total, narrow):
         chain.after(filled)
 
-    total_qkv = [chain.finish() for chain in queue]
-    here = spans[1][1] * LANES
-    total_vectors = total_qkv[1][:, 3 * here : 3 * here + entries].reshape(-1)
-    total_qkv = jnp.concatenate(
-        [
-            part[:, at * pairs * LANES : (at + 1) * pairs * LANES]
-            for at in range(3)
-            for part, (_, pairs) in zip(total_qkv, spans)
-        ],
-        axis=1,
-    )
+    total_narrow = narrow.finish()
+    total_qkv = total_narrow[:, : 3 * width]
+    total_vectors = total_narrow[:, 3 * width : 3 * width + entries].reshape(-1)
     total_wide = joint.finish()
     total_up, total_attn = total_wide[:, :inner], total_wide[:, inner:]
     total_down = total.finish()

time: 305 us -> 296 us (0.970)
  Pallas kernels: 159 us -> 152 us
  waiting for transfers between devices: 67.2 us -> 73.4 us
  other arithmetic: 27.1 us -> 22.4 us
  starting transfers between devices: 31.3 us -> 27 us
    convert_element_type x15 -> x10, other arithmetic: 15 us -> 8.58 us  [join(): self.total(way * size, size).astype(BF)]
    ppermute x27 -> x23, waiting for transfers between devices: 59.9 us -> 65.6 us  [swap(): lax.ppermute(value, 'dp', [(index, index ^ mask) for index in range(devic...]
    pallas_call x4 -> x2, Pallas kernels: 36 us -> 30.3 us  [attend_backward(): pl.pallas_call(functools.partial(attend_back_kernel, which=which), grid_s...]
    ppermute x27 -> x23, starting transfers between devices: 31.2 us -> 27 us  [swap(): lax.ppermute(value, 'dp', [(index, index ^ mask) for index in range(devic...]
    pallas_call x2 -> x1, Pallas kernels: 13.9 us -> 9.62 us  [weight_gradient(): pl.pallas_call(functools.partial(weight_kernel, sums=sums), grid_spec=gri...]
    pallas_call x1, Pallas kernels: 36 us -> 39.5 us  [middle(): pl.pallas_call(functools.partial(middle_kernel, seq=seq, piece=piece), gr...]
  transfers between devices with their start and end apart: 28 -> 24, of which waited for: 14 -> 12; matrix products, arithmetic and copies ran while one was open for 9% -> 7% of each run, Pallas kernels for 37% -> 34%
where the time goes in v6:
time: 296 us; the launch traced here: 295 us
  Pallas kernels  152 us (51%)
  waiting for transfers between devices  73.4 us (25%)
  starting transfers between devices  27 us (9%)
  other arithmetic  22.4 us (8%)
  between operations  14.6 us (5%)
  local copies, waits for them, and re-layouts  5.65 us (2%)
    ppermute x23, waiting for transfers between devices, swap(): lax.ppermute(value, 'dp', [(index, index ^ mask) for index in range(devic...  65.6 us
    pallas_call x1, Pallas kernels, middle(): pl.pallas_call(functools.partial(middle_kernel, seq=seq, piece=piece), gr...  39.5 us
    pallas_call x2, Pallas kernels, attend_backward(): pl.pallas_call(functools.partial(attend_back_kernel, which=which), grid_s...  30.3 us
    ppermute x23, starting transfers between devices, swap(): lax.ppermute(value, 'dp', [(index, index ^ mask) for index in range(devic...  27 us
    pallas_call x2, Pallas kernels, attend_forward(): pl.pallas_call(functools.partial(attend_kernel, which=which), grid_spec=g...  21.2 us
    pallas_call x1, Pallas kernels, joint_gradient(): pl.pallas_call(joint_kernel, grid_spec=grid_spec, out_shape=[shape, shape...  13.3 us
    pallas_call x1, Pallas kernels, tall_gradient(): pl.pallas_call(tall_kernel, grid_spec=grid_spec, out_shape=[shape, shape]...  11.6 us
    pallas_call x2, Pallas kernels, input_gradient(): pl.pallas_call(functools.partial(input_kernel, groups=len(grads)), grid=(...  11.4 us
  transfers between devices with their start and end apart: 24, of which 12 were waited for; matrix products, arithmetic and copies ran while one was open for 7% of the time, Pallas kernels for 34%

profile of v6, /device:TPU:0, one launch (start us, length us, event | category | flops | bytes accessed | tf_op | source)
XLA Modules:
  0.0 295.1 jit_solution(1661924807054865111)
XLA Ops:
  7.3 1.0 convert_element_type.290
  8.4 1.0 convert_element_type.289
  11.2 4.1 %collective-permute-start = (bf16[1,24,2560]{2,1,0:T(8,128)(2,1)S(1)}, bf16[1,24,2560]{2,1,0:T(8,128)(2,1)S(1)}, u32[]{:S(2)}, u32[]{:S(2)}) collective-permute-start(bf16[1,24,2560]{2,1,0:T(8,128)(2,1)S(1)} %fusion.6), channel_id=1, source_target_pairs={{0,16},{1,17},{2,18},{3,19},{4,20},{5,21},{6,22},{7,23},{8,24},{9,... | collective-permute-start | bytes 368648 | tf_op jit(solution)/shard_map/ppermute | solution.py:653
  15.3 6.0 %collective-permute-done = bf16[1,24,2560]{2,1,0:T(8,128)(2,1)S(1)} collective-permute-done((bf16[1,24,2560]{2,1,0:T(8,128)(2,1)S(1)}, bf16[1,24,2560]{2,1,0:T(8,128)(2,1)S(1)}, u32[]{:S(2)}, u32[]{:S(2)}) %collective-permute-start) | collective-permute-done | bytes 122912 | tf_op jit(solution)/shard_map/ppermute | solution.py:653
  22.1 10.2 %collective-permute-done.1 = bf16[2,24,2560]{2,1,0:T(8,128)(2,1)S(1)} collective-permute-done((bf16[2,24,2560]{2,1,0:T(8,128)(2,1)S(1)}, bf16[2,24,2560]{2,1,0:T(8,128)(2,1)S(1)}, u32[]{:S(2)}, u32[]{:S(2)}) %collective-permute-start.1) | collective-permute-done | bytes 245792 | tf_op jit(solution)/shard_map/ppermute | solution.py:653
  32.4 1.4 collective-permute-start.2
  33.8 1.6 collective-permute-start.3
  36.0 10.9 %collective-permute-done.2 = bf16[4,24,2560]{2,1,0:T(8,128)(2,1)S(1)} collective-permute-done((bf16[4,24,2560]{2,1,0:T(8,128)(2,1)S(1)}, bf16[4,24,2560]{2,1,0:T(8,128)(2,1)S(1)}, u32[]{:S(2)}, u32[]{:S(2)}) %collective-permute-start.2) | collective-permute-done | bytes 491552 | tf_op jit(solution)/shard_map/ppermute | solution.py:653
  47.0 7.0 %collective-permute-done.3 = bf16[4,24,2560]{2,1,0:T(8,128)(2,1)S(1)} collective-permute-done((bf16[4,24,2560]{2,1,0:T(8,128)(2,1)S(1)}, bf16[4,24,2560]{2,1,0:T(8,128)(2,1)S(1)}, u32[]{:S(2)}, u32[]{:S(2)}) %collective-permute-start.3) | collective-permute-done | bytes 491552 | tf_op jit(solution)/shard_map/ppermute | solution.py:653
  54.1 9.6 %collective-permute-done.4 = bf16[4,24,2560]{2,1,0:T(8,128)(2,1)S(1)} collective-permute-done((bf16[4,24,2560]{2,1,0:T(8,128)(2,1)S(1)}, bf16[4,24,2560]{2,1,0:T(8,128)(2,1)S(1)}, u32[]{:S(2)}, u32[]{:S(2)}) %collective-permute-start.4) | collective-permute-done | bytes 491552 | tf_op jit(solution)/shard_map/ppermute | solution.py:653
  65.6 2.3 collective-permute-done.5.taken_ref
  67.9 6.7 %lay_out.1.w_ref = bf16[768,2560]{1,0:T(8,128)(2,1)} custom-call(s32[16]{0:T(128)} %broadcast_xor_fusion.2.index_ref, s32[1]{0:T(128)} %bitcast.odd_ref, bf16[16,24,2560]{2,1,0:T(8,128)(2,1)} %copy-done.5, bf16[16,24,2560]{2,1,0:T(8,128)(2,1)} %collective-permute-done.5.taken_ref), custom_call_target="tpu_custom_call" | custom-call | flops 1966080 | bytes 7864320 | tf_op jit(solution)/shard_map/lay_out/pallas_call | solution.py:778
  74.6 1.0 slice_convert_fusion
  76.4 8.4 %project_qkv.1.q_ref.k_ref.v_ref = bf16[1024,2304]{1,0:T(8,128)(2,1)} custom-call(bf16[1024,768]{1,0:T(8,128)(2,1)} %left_ref, bf16[768,2560]{1,0:T(8,128)(2,1)} %lay_out.1.w_ref, f32[12,768]{1,0:T(8,128)} %reshape.92.vec_ref), custom_call_target="tpu_custom_call" | custom-call | flops 3623878656 | bytes 9830400 | tf_op jit(solution)/shard_map/project_qkv/pallas_call | solution.py:64
  84.8 10.6 %attend_forward.2 = (bf16[1024,768]{1,0:T(8,128)(2,1)}, f32[12,2,512]{2,1,0:T(2,128)}) custom-call(s32[2]{0:T(128)} %len_ref.9, bf16[1024,2304]{1,0:T(8,128)(2,1)} %project_qkv.1.q_ref.k_ref.v_ref, bf16[1024,2304]{1,0:T(8,128)(2,1)} %project_qkv.1.q_ref.k_ref.v_ref, bf16[1024,2304]{1,0:T(8,128)(2,1)} %project_qkv.1.q_ref.k_ref.v_ref), custom_call_target="tpu_custom_call" | custom-call | flops 3221225472 | bytes 3145728 | tf_op jit(solution)/shard_map/attend_forward/pallas_call | solution.py:130
  95.4 10.6 %attend_forward.3 = (bf16[1024,768]{1,0:T(8,128)(2,1)}, f32[12,2,512]{2,1,0:T(2,128)}) custom-call(s32[2]{0:T(128)} %len_ref.9, bf16[1024,2304]{1,0:T(8,128)(2,1)} %project_qkv.1.q_ref.k_ref.v_ref, bf16[1024,2304]{1,0:T(8,128)(2,1)} %project_qkv.1.q_ref.k_ref.v_ref, ...), custom_call_target="tpu_custom_call", output_to_operand_aliasing={{0}: (4, {}), {1}: (5, {})} | custom-call | flops 3221225472 | bytes 3145728 | tf_op jit(solution)/shard_map/attend_forward/pallas_call | solution.py:130
  106.0 7.8 %all-gather.2.cloned.1.call-done.w_attn.w_up.w_down = bf16[768,6912]{1,0:T(8,128)(2,1)} async-done(((bf16[24,6912]{1,0:T(8,128)(2,1)}), bf16[768,6912]{1,0:T(8,128)(2,1)}) %all-gather.2.cloned.1.call-update) | async-done | bytes 10616848 | tf_op jit(solution)/shard_map/all_gather | solution.py:836
  113.9 39.5 %middle.1 = (bf16[1024,768]{1,0:T(8,128)(2,1)}, bf16[1024,768]{1,0:T(8,128)(2,1)}, bf16[1024,3072]{1,0:T(8,128)(2,1)}, bf16[1024,3072]{1,0:T(8,128)(2,1)}, bf16[...) custom-call(s32[2]{0:T(128)} %len_ref.9, ...), custom_call_target="tpu_custom_call" | custom-call | flops 21743271936 | bytes 37748736 | tf_op jit(solution)/shard_map/middle/pallas_call | solution.py:379
  153.3 11.6 %tall_gradient.1 = (bf16[16,96,768]{2,1,0:T(8,128)(2,1)}, bf16[16,96,768]{2,1,0:T(8,128)(2,1)}) custom-call(s32[32]{0:T(128)} %get-tuple-element.151.slot_ref, bf16[1024,3072]{1,0:T(8,128)(2,1)} %get-tuple-element.71.left_ref, bf16[1024,768]{1,0:T(8,128)(2,1)} %get-tuple-element.72.right_ref), custom_call_target="tpu_custom_call" | custom-call | flops 4831838208 | bytes 12582912 | tf_op jit(solution)/shard_map/tall_gradient/pallas_call | solution.py:603
  165.2 13.3 %joint_gradient.1 = (bf16[16,24,3840]{2,1,0:T(8,128)(2,1)}, bf16[16,24,3840]{2,1,0:T(8,128)(2,1)}) custom-call(s32[32]{0:T(128)} %get-tuple-element.152.src_ref, bf16[1024,768]{1,0:T(8,128)(2,1)} %get-tuple-element.69.left_ref, bf16[1024,768]{1,0:T(8,128)(2,1)} %get-tuple-element.66.mixed_ref.last_left_ref, bf16[1024,3072]{1,0:T(8,128)(2,1)} %get-tuple-element.75.right_ref, ...), custom_call_target="tpu_custom_call" | custom-call | flops 48318382080 | bytes 16908288 | tf_op jit(solution)/shard_map/joint_gradient/pallas_call | solution.py:536
  181.0 1.7 add_convert_fusion.2
  182.7 1.4 collective-permute-start.9
  184.8 1.5 collective-permute-start.8
  186.3 15.2 %attend_backward.2.refs_0_ = bf16[3,1024,768]{2,1,0:T(8,128)(2,1)} custom-call(s32[2]{0:T(128)} %len_ref.9, bf16[1024,2304]{1,0:T(8,128)(2,1)} %project_qkv.1.q_ref.k_ref.v_ref, bf16[1024,2304]{1,0:T(8,128)(2,1)} %project_qkv.1.q_ref.k_ref.v_ref, bf16[1024,2304]{1,0:T(8,128)(2,1)} %project_qkv.1.q_ref.k_ref.v_ref, ...), custom_call_target="tpu_custom_call" | custom-call | flops 64424509440 | bytes 5505024 | tf_op jit(solution)/shard_map/attend_backward/pallas_call | solution.py:194
  201.5 15.2 %attend_backward.3.right_ref.refs_0_ = bf16[3,1024,768]{2,1,0:T(8,128)(2,1)} custom-call(s32[2]{0:T(128)} %len_ref.9, bf16[1024,2304]{1,0:T(8,128)(2,1)} %project_qkv.1.q_ref.k_ref.v_ref, bf16[1024,2304]{1,0:T(8,128)(2,1)} %project_qkv.1.q_ref.k_ref.v_ref, bf16[1024,2304]{1,0:T(8,128)(2,1)} %project_qkv.1.q_ref.k_ref.v_ref, ...), custom_call_target="tpu_custom_call", output_to_operand_aliasing={{}: (6, {})} | custom-call | flops 64424509440 | bytes 5505024 | tf_op jit(solution)/shard_map/attend_backward/pallas_call | solution.py:194
  216.7 1.3 add_convert_fusion.6
  219.3 1.5 add_convert_fusion.4
  220.8 1.4 collective-permute-start.11
  222.2 9.6 %weight_gradient.1 = (bf16[16,24,2304]{2,1,0:T(8,128)(2,1)}, bf16[16,24,2304]{2,1,0:T(8,128)(2,1)}, f32[3,8,768]{2,1,0:T(8,128)}) custom-call(s32[32]{0:T(128)} %broadcast_xor_fusion.1.src_ref, bf16[1024,768]{1,0:T(8,128)(2,1)} %left_ref, bf16[3,1024,768]{2,1,0:T(8,128)(2,1)} %attend_backward.3.right_ref.refs_0_), custom_call_target="tpu_custom_call" | custom-call | flops 231928233984 | bytes 9830400 | tf_op jit(solution)/shard_map/weight_gradient/pallas_call | solution.py:469
  233.9 1.6 pad_maximum_fusion
  235.6 5.7 %input_gradient.2.refs_1_ = bf16[1024,768]{1,0:T(8,128)(2,1)} custom-call(f32[1024,768]{1,0:T(8,128)} %get-tuple-element.102.resid_ref, bf16[768,2560]{1,0:T(8,128)(2,1)} %lay_out.1.w_ref, bf16[3,1024,768]{2,1,0:T(8,128)(2,1)} %attend_backward.3.right_ref.refs_0_), custom_call_target="tpu_custom_call" | custom-call | flops 115964116992 | bytes 6488064 | tf_op jit(solution)/shard_map/input_gradient/pallas_call | solution.py:630
  241.3 1.3 add_convert_fusion.14
  242.7 1.3 collective-permute-start.21
  244.1 1.0 copy-done.2
  245.1 1.3 add_convert_fusion.12
  248.4 1.4 collective-permute-start.14
  249.7 1.5 collective-permute-start.15
  251.3 5.7 %input_gradient.3 = bf16[1024,768]{1,0:T(8,128)(2,1)} custom-call(f32[1024,768]{1,0:T(8,128)} %get-tuple-element.102.resid_ref, bf16[768,2560]{1,0:T(8,128)(2,1)} %lay_out.1.w_ref, bf16[3,1024,768]{2,1,0:T(8,128)(2,1)} %attend_backward.3.right_ref.refs_0_, bf16[1024,768]{1,0:T(8,128)(2,1)} %input_gradient.2.refs_1_), custom_call_target="tpu_custom_call", output_to_operand_aliasing={{}: (3, {})} | custom-call | flops 115964116992 | bytes 6488064 | tf_op jit(solution)/shard_map/input_gradient/pallas_call | solution.py:630
  257.0 1.9 collective-permute-start.22
  258.9 2.5 collective-permute-done.19
  262.4 9.2 %collective-permute-done.22 = bf16[1,96,768]{2,1,0:T(8,128)(2,1)S(1)} collective-permute-done((bf16[1,96,768]{2,1,0:T(8,128)(2,1)S(1)}, bf16[1,96,768]{2,1,0:T(8,128)(2,1)S(1)}, u32[]{:S(2)}, u32[]{:S(2)}) %collective-permute-start.22) | collective-permute-done | bytes 147488 | tf_op jit(solution)/shard_map/ppermute | solution.py:653
  271.5 1.1 multiply_subtract_fusion
  272.6 1.3 collective-permute-done.20
  274.1 1.0 multiply_subtract_fusion.1
  275.5 2.3 collective-permute-start.17
  277.8 2.0 collective-permute-start.18
  280.5 5.8 %collective-permute-done.17 = bf16[1,24,2432]{2,1,0:T(8,128)(2,1)S(1)} collective-permute-done((bf16[1,24,2432]{2,1,0:T(8,128)(2,1)S(1)}, bf16[1,24,2432]{2,1,0:T(8,128)(2,1)S(1)}, u32[]{:S(2)}, u32[]{:S(2)}) %collective-permute-start.17) | collective-permute-done | bytes 116768 | tf_op jit(solution)/shard_map/ppermute | solution.py:653
  286.7 0.9 multiply_subtract_fusion.2
  (129 shorter events, 18.2 us)
Async XLA Ops:
  7.2 106.6 %all-gather.2.cloned.1.call-start = ((), (), s32[]{:S(2)}) async-start(), calls=%async_computation | async-start | bytes 10948608 | tf_op jit(solution)/shard_map/all_gather | solution.py:836
  11.2 10.1 %collective-permute-start = (bf16[1,24,2560]{2,1,0:T(8,128)(2,1)S(1)}, bf16[1,24,2560]{2,1,0:T(8,128)(2,1)S(1)}, u32[]{:S(2)}, u32[]{:S(2)}) collective-permute-start(bf16[1,24,2560]{2,1,0:T(8,128)(2,1)S(1)} %fusion.6), channel_id=1, source_target_pairs={{0,16},{1,17},{2,18},{3,19},{4,20},{5,21},{6,22},{7,23},{8,24},{9,... | collective-permute-start | bytes 368648 | tf_op jit(solution)/shard_map/ppermute | solution.py:653
  21.3 11.0 %collective-permute-start.1 = (bf16[2,24,2560]{2,1,0:T(8,128)(2,1)S(1)}, bf16[2,24,2560]{2,1,0:T(8,128)(2,1)S(1)}, u32[]{:S(2)}, u32[]{:S(2)}) collective-permute-start(bf16[2,24,2560]{2,1,0:T(8,128)(2,1)S(1)} %pad_maximum_fusion.4), channel_id=1, source_target_pairs={{0,8},{1,9},{2,10},{3,11},{4,12},{5,13},{6,14},{7,15},{8,0},{9,1},... | collective-permute-start | bytes 737288 | tf_op jit(solution)/shard_map/ppermute | solution.py:653
  32.3 31.5 %copy-start = (s32[32]{0:T(128)S(1)}, s32[32]{0:T(128)}, u32[]{:S(2)}) copy-start(s32[32]{0:T(128)} %constant.46.clone) | copy-start | bytes 388
  32.4 14.6 %collective-permute-start.2 = (bf16[4,24,2560]{2,1,0:T(8,128)(2,1)S(1)}, bf16[4,24,2560]{2,1,0:T(8,128)(2,1)S(1)}, u32[]{:S(2)}, u32[]{:S(2)}) collective-permute-start(bf16[4,24,2560]{2,1,0:T(8,128)(2,1)S(1)} %pad_maximum_fusion.2), channel_id=1, source_target_pairs={{0,2},{1,3},{2,0},{3,1},{4,6},{5,7},{6,4},{7,5},{8,10},{9,11},{10,... | collective-permute-start | bytes 1474568 | tf_op jit(solution)/shard_map/ppermute | solution.py:653
  33.8 30.8 %copy-start.29 = (s32[16]{0:T(128)S(1)}, s32[16]{0:T(128)}, u32[]{:S(2)}) copy-start(s32[16]{0:T(128)} %constant.47.clone) | copy-start | bytes 196
  33.8 20.3 %collective-permute-start.3 = (bf16[4,24,2560]{2,1,0:T(8,128)(2,1)S(1)}, bf16[4,24,2560]{2,1,0:T(8,128)(2,1)S(1)}, u32[]{:S(2)}, u32[]{:S(2)}) collective-permute-start(bf16[4,24,2560]{2,1,0:T(8,128)(2,1)S(1)} %pad_maximum_fusion.2), channel_id=1, source_target_pairs={{0,4},{1,5},{2,6},{3,7},{4,0},{5,1},{6,2},{7,3},{8,12},{9,13},{10,... | collective-permute-start | bytes 1474568 | tf_op jit(solution)/shard_map/ppermute | solution.py:653
  35.4 28.3 %collective-permute-start.4 = (bf16[4,24,2560]{2,1,0:T(8,128)(2,1)S(1)}, bf16[4,24,2560]{2,1,0:T(8,128)(2,1)S(1)}, u32[]{:S(2)}, u32[]{:S(2)}) collective-permute-start(bf16[4,24,2560]{2,1,0:T(8,128)(2,1)S(1)} %pad_maximum_fusion.2), channel_id=1, source_target_pairs={{0,6},{1,7},{2,4},{3,5},{4,2},{5,3},{6,0},{7,1},{8,14},{9,15},{10,... | collective-permute-start | bytes 1474568 | tf_op jit(solution)/shard_map/ppermute | solution.py:653
  36.0 29.0 %copy-start.27 = (s32[32]{0:T(128)S(1)}, s32[32]{0:T(128)}, u32[]{:S(2)}) copy-start(s32[32]{0:T(128)} %constant.48.clone) | copy-start | bytes 388
  63.7 4.2 %collective-permute-start.5 = (bf16[16,24,2560]{2,1,0:T(8,128)(2,1)S(1)}, bf16[16,24,2560]{2,1,0:T(8,128)(2,1)}, u32[]{:S(2)}, u32[]{:S(2)}) collective-permute-start(bf16[16,24,2560]{2,1,0:T(8,128)(2,1)S(1)} %constant_dynamic-update-slice_fusion.held_ref), channel_id=1, source_target_pairs={{0,1},{1,0},{2,3},{3,2},{4,5},{5,4},{6,7},{7,6},{8,9},{9,8},{10,11... | collective-permute-start | bytes 5898248 | tf_op jit(solution)/shard_map/ppermute | solution.py:653
  164.9 13.6 %collective-permute-start.6 = (bf16[16,96,768]{2,1,0:T(8,128)(2,1)}, bf16[16,96,768]{2,1,0:T(8,128)(2,1)S(1)}, u32[]{:S(2)}, u32[]{:S(2)}) collective-permute-start(bf16[16,96,768]{2,1,0:T(8,128)(2,1)} %get-tuple-element.74), channel_id=1, source_target_pairs={{0,1},{1,0},{2,3},{3,2},{4,5},{5,4},{6,7},{7,6},{8,9},{9,8},{10,11... | collective-permute-start | bytes 7077896 | tf_op jit(solution)/shard_map/ppermute | solution.py:653
  165.1 13.6 %copy-start.28 = (s32[32]{0:T(128)S(1)}, s32[32]{0:T(128)}, u32[]{:S(2)}) copy-start(s32[32]{0:T(128)} %constant.49.clone) | copy-start | bytes 388
  165.2 15.2 %copy-start.21 = (f32[12,768]{1,0:T(8,128)S(1)}, f32[12,768]{1,0:T(8,128)}, u32[]{:S(2)}) copy-start(f32[12,768]{1,0:T(8,128)} %get-tuple-element.93) | copy-start | bytes 110596
  165.2 15.8 %copy-start.3 = (bf16[16,96,768]{2,1,0:T(8,128)(2,1)S(1)}, bf16[16,96,768]{2,1,0:T(8,128)(2,1)}, u32[]{:S(2)}) copy-start(bf16[16,96,768]{2,1,0:T(8,128)(2,1)} %get-tuple-element.79) | copy-start | bytes 7077892
  178.5 5.6 %collective-permute-start.7 = (bf16[16,24,3840]{2,1,0:T(8,128)(2,1)}, bf16[16,24,3840]{2,1,0:T(8,128)(2,1)S(1)}, u32[]{:S(2)}, u32[]{:S(2)}) collective-permute-start(bf16[16,24,3840]{2,1,0:T(8,128)(2,1)} %get-tuple-element.82), channel_id=1, source_target_pairs={{0,1},{1,0},{2,3},{3,2},{4,5},{5,4},{6,7},{7,6},{8,9},{9,8},{10,11... | collective-permute-start | bytes 8847368 | tf_op jit(solution)/shard_map/ppermute | solution.py:653
  182.7 34.0 %collective-permute-start.9 = (bf16[8,96,768]{2,1,0:T(8,128)(2,1)}, bf16[8,96,768]{2,1,0:T(8,128)(2,1)S(1)}, u32[]{:S(2)}, u32[]{:S(2)}) collective-permute-start(bf16[8,96,768]{2,1,0:T(8,128)(2,1)} %get-tuple-element.130), channel_id=1, source_target_pairs={{0,2},{1,3},{2,0},{3,1},{4,6},{5,7},{6,4},{7,5},{8,10},{9,11},{10,... | collective-permute-start | bytes 3538952 | tf_op jit(solution)/shard_map/ppermute | solution.py:653
  184.8 34.5 %collective-permute-start.8 = (bf16[8,24,3840]{2,1,0:T(8,128)(2,1)S(1)}, bf16[8,24,3840]{2,1,0:T(8,128)(2,1)S(1)}, u32[]{:S(2)}, u32[]{:S(2)}) collective-permute-start(bf16[8,24,3840]{2,1,0:T(8,128)(2,1)S(1)} %get-tuple-element.128), channel_id=1, source_target_pairs={{0,4},{1,5},{2,6},{3,7},{4,0},{5,1},{6,2},{7,3},{8,12},{9,13},{10,... | collective-permute-start | bytes 4423688 | tf_op jit(solution)/shard_map/ppermute | solution.py:653
  218.0 23.3 %collective-permute-start.12 = (bf16[4,96,768]{2,1,0:T(8,128)(2,1)}, bf16[4,96,768]{2,1,0:T(8,128)(2,1)}, u32[]{:S(2)}, u32[]{:S(2)}) collective-permute-start(bf16[4,96,768]{2,1,0:T(8,128)(2,1)} %get-tuple-element.138), channel_id=1, source_target_pairs={{0,4},{1,5},{2,6},{3,7},{4,0},{5,1},{6,2},{7,3},{8,12},{9,13},{10,... | collective-permute-start | bytes 1769480 | tf_op jit(solution)/shard_map/ppermute | solution.py:653
  220.8 23.4 %collective-permute-start.11 = (bf16[4,24,3840]{2,1,0:T(8,128)(2,1)}, bf16[4,24,3840]{2,1,0:T(8,128)(2,1)}, u32[]{:S(2)}, u32[]{:S(2)}) collective-permute-start(bf16[4,24,3840]{2,1,0:T(8,128)(2,1)} %get-tuple-element.136), channel_id=1, source_target_pairs={{0,2},{1,3},{2,0},{3,1},{4,6},{5,7},{6,4},{7,5},{8,10},{9,11},{10,... | collective-permute-start | bytes 2211848 | tf_op jit(solution)/shard_map/ppermute | solution.py:653
  222.2 10.4 %copy-start.18 = (bf16[10,768]{1,0:T(8,128)(2,1)S(1)}, bf16[10,768]{1,0:T(8,128)(2,1)}, u32[]{:S(2)}) copy-start(bf16[10,768]{1,0:T(8,128)(2,1)} %slice.217) | copy-start | bytes 46084
  222.2 11.6 %copy-start.24 = (pred[32]{0:T(512)(128)(4,1)S(1)}, pred[32]{0:T(512)(128)(4,1)}, u32[]{:S(2)}) copy-start(pred[32]{0:T(512)(128)(4,1)} %get-tuple-element.126) | copy-start | bytes 100
  235.6 11.7 %collective-permute-start.10 = (bf16[16,24,2432]{2,1,0:T(8,128)(2,1)S(1)}, bf16[16,24,2432]{2,1,0:T(8,128)(2,1)S(1)}, u32[]{:S(2)}, u32[]{:S(2)}) collective-permute-start(bf16[16,24,2432]{2,1,0:T(8,128)(2,1)S(1)} %pad_maximum_fusion), channel_id=1, source_target_pairs={{0,1},{1,0},{2,3},{3,2},{4,5},{5,4},{6,7},{7,6},{8,9},{9,8},{10,11... | collective-permute-start | bytes 5603336 | tf_op jit(solution)/shard_map/ppermute | solution.py:653
  235.6 5.7 %copy-start.4 = (bf16[4,96,768]{2,1,0:T(8,128)(2,1)S(1)}, bf16[4,96,768]{2,1,0:T(8,128)(2,1)}, u32[]{:S(2)}) copy-start(bf16[4,96,768]{2,1,0:T(8,128)(2,1)} %get-tuple-element.100) | copy-start | bytes 1769476
  242.7 14.3 %collective-permute-start.21 = (bf16[2,96,768]{2,1,0:T(8,128)(2,1)S(1)}, bf16[2,96,768]{2,1,0:T(8,128)(2,1)S(1)}, u32[]{:S(2)}, u32[]{:S(2)}) collective-permute-start(bf16[2,96,768]{2,1,0:T(8,128)(2,1)S(1)} %get-tuple-element.145), channel_id=1, source_target_pairs={{0,8},{1,9},{2,10},{3,11},{4,12},{5,13},{6,14},{7,15},{8,0},{9,1},... | collective-permute-start | bytes 884744 | tf_op jit(solution)/shard_map/ppermute | solution.py:653
  246.4 15.0 %collective-permute-start.19 = (bf16[2,24,3840]{2,1,0:T(8,128)(2,1)S(1)}, bf16[2,24,3840]{2,1,0:T(8,128)(2,1)S(1)}, u32[]{:S(2)}, u32[]{:S(2)}) collective-permute-start(bf16[2,24,3840]{2,1,0:T(8,128)(2,1)S(1)} %get-tuple-element.143), channel_id=1, source_target_pairs={{0,8},{1,9},{2,10},{3,11},{4,12},{5,13},{6,14},{7,15},{8,0},{9,1},... | collective-permute-start | bytes 1105928 | tf_op jit(solution)/shard_map/ppermute | solution.py:653
  247.7 27.4 %collective-permute-start.13 = (bf16[4,24,2432]{2,1,0:T(8,128)(2,1)S(1)}, bf16[4,24,2432]{2,1,0:T(8,128)(2,1)S(1)}, u32[]{:S(2)}, u32[]{:S(2)}) collective-permute-start(bf16[4,24,2432]{2,1,0:T(8,128)(2,1)S(1)} %get-tuple-element.134), channel_id=1, source_target_pairs={{0,2},{1,3},{2,0},{3,1},{4,6},{5,7},{6,4},{7,5},{8,10},{9,11},{10,... | collective-permute-start | bytes 1400840 | tf_op jit(solution)/shard_map/ppermute | solution.py:653
  248.4 26.7 %collective-permute-start.14 = (bf16[4,24,2432]{2,1,0:T(8,128)(2,1)S(1)}, bf16[4,24,2432]{2,1,0:T(8,128)(2,1)S(1)}, u32[]{:S(2)}, u32[]{:S(2)}) collective-permute-start(bf16[4,24,2432]{2,1,0:T(8,128)(2,1)S(1)} %get-tuple-element.133), channel_id=1, source_target_pairs={{0,4},{1,5},{2,6},{3,7},{4,0},{5,1},{6,2},{7,3},{8,12},{9,13},{10,... | collective-permute-start | bytes 1400840 | tf_op jit(solution)/shard_map/ppermute | solution.py:653
  249.7 25.4 %collective-permute-start.15 = (bf16[4,24,2432]{2,1,0:T(8,128)(2,1)S(1)}, bf16[4,24,2432]{2,1,0:T(8,128)(2,1)S(1)}, u32[]{:S(2)}, u32[]{:S(2)}) collective-permute-start(bf16[4,24,2432]{2,1,0:T(8,128)(2,1)S(1)} %get-tuple-element.132), channel_id=1, source_target_pairs={{0,6},{1,7},{2,4},{3,5},{4,2},{5,3},{6,0},{7,1},{8,14},{9,15},{10,... | collective-permute-start | bytes 1400840 | tf_op jit(solution)/shard_map/ppermute | solution.py:653
  251.3 20.2 %copy-start.7 = (f32[96,768]{1,0:T(8,128)S(1)}, f32[96,768]{1,0:T(8,128)}, u32[]{:S(2)}) copy-start(f32[96,768]{1,0:T(8,128)} %param.29) | copy-start | bytes 884740
  251.3 20.2 %copy-start.11 = (f32[96,768]{1,0:T(8,128)S(1)}, f32[96,768]{1,0:T(8,128)}, u32[]{:S(2)}) copy-start(f32[96,768]{1,0:T(8,128)} %param.39) | copy-start | bytes 884740
  251.3 20.2 %copy-start.12 = (f32[96,768]{1,0:T(8,128)S(1)}, f32[96,768]{1,0:T(8,128)}, u32[]{:S(2)}) copy-start(f32[96,768]{1,0:T(8,128)} %param.34) | copy-start | bytes 884740
  257.0 17.0 %copy-start.8 = (f32[24,3072]{1,0:T(8,128)S(1)}, f32[24,3072]{1,0:T(8,128)}, u32[]{:S(2)}) copy-start(f32[24,3072]{1,0:T(8,128)} %param.28) | copy-start | bytes 884740
  257.0 17.0 %copy-start.14 = (f32[24,3072]{1,0:T(8,128)S(1)}, f32[24,3072]{1,0:T(8,128)}, u32[]{:S(2)}) copy-start(f32[24,3072]{1,0:T(8,128)} %param.38) | copy-start | bytes 884740
  257.0 17.0 %copy-start.15 = (f32[24,3072]{1,0:T(8,128)S(1)}, f32[24,3072]{1,0:T(8,128)}, u32[]{:S(2)}) copy-start(f32[24,3072]{1,0:T(8,128)} %param.33) | copy-start | bytes 884740
  257.0 14.5 %collective-permute-start.22 = (bf16[1,96,768]{2,1,0:T(8,128)(2,1)S(1)}, bf16[1,96,768]{2,1,0:T(8,128)(2,1)S(1)}, u32[]{:S(2)}, u32[]{:S(2)}) collective-permute-start(bf16[1,96,768]{2,1,0:T(8,128)(2,1)S(1)} %add_convert_fusion.18), channel_id=1, source_target_pairs={{0,16},{1,17},{2,18},{3,19},{4,20},{5,21},{6,22},{7,23},{8,24},{9,... | collective-permute-start | bytes 442376 | tf_op jit(solution)/shard_map/ppermute | solution.py:653
  261.5 12.5 %collective-permute-start.20 = (bf16[1,24,3840]{2,1,0:T(8,128)(2,1)S(1)}, bf16[1,24,3840]{2,1,0:T(8,128)(2,1)S(1)}, u32[]{:S(2)}, u32[]{:S(2)}) collective-permute-start(bf16[1,24,3840]{2,1,0:T(8,128)(2,1)S(1)} %add_convert_fusion.16), channel_id=1, source_target_pairs={{0,16},{1,17},{2,18},{3,19},{4,20},{5,21},{6,22},{7,23},{8,24},{9,... | collective-permute-start | bytes 552968 | tf_op jit(solution)/shard_map/ppermute | solution.py:653
  274.0 5.8 %copy-start.13 = (f32[24,768]{1,0:T(8,128)S(1)}, f32[24,768]{1,0:T(8,128)}, u32[]{:S(2)}) copy-start(f32[24,768]{1,0:T(8,128)} %param.27) | copy-start | bytes 221188
  274.0 5.8 %copy-start.19 = (f32[24,768]{1,0:T(8,128)S(1)}, f32[24,768]{1,0:T(8,128)}, u32[]{:S(2)}) copy-start(f32[24,768]{1,0:T(8,128)} %param.37) | copy-start | bytes 221188
  274.1 5.8 %copy-start.20 = (f32[24,768]{1,0:T(8,128)S(1)}, f32[24,768]{1,0:T(8,128)}, u32[]{:S(2)}) copy-start(f32[24,768]{1,0:T(8,128)} %param.32) | copy-start | bytes 221188
  275.1 11.5 %copy-start.10 = (f32[24,2304]{1,0:T(8,128)S(1)}, f32[24,2304]{1,0:T(8,128)}, u32[]{:S(2)}) copy-start(f32[24,2304]{1,0:T(8,128)} %param.26) | copy-start | bytes 663556
  275.1 11.5 %copy-start.16 = (f32[24,2304]{1,0:T(8,128)S(1)}, f32[24,2304]{1,0:T(8,128)}, u32[]{:S(2)}) copy-start(f32[24,2304]{1,0:T(8,128)} %param.36) | copy-start | bytes 663556
  275.1 11.5 %copy-start.17 = (f32[24,2304]{1,0:T(8,128)S(1)}, f32[24,2304]{1,0:T(8,128)}, u32[]{:S(2)}) copy-start(f32[24,2304]{1,0:T(8,128)} %param.31) | copy-start | bytes 663556
  275.3 12.3 %copy-start.23 = (f32[288]{0:T(512)S(1)}, f32[288]{0:T(512)}, u32[]{:S(2)}) copy-start(f32[288]{0:T(512)} %param.30) | copy-start | bytes 3460
  275.4 12.3 %copy-start.25 = (f32[288]{0:T(512)S(1)}, f32[288]{0:T(512)}, u32[]{:S(2)}) copy-start(f32[288]{0:T(512)} %param.40) | copy-start | bytes 3460
  275.4 12.2 %copy-start.26 = (f32[288]{0:T(512)S(1)}, f32[288]{0:T(512)}, u32[]{:S(2)}) copy-start(f32[288]{0:T(512)} %param.35) | copy-start | bytes 3460
  275.4 5.2 %collective-permute-start.16 = (bf16[1,24,2432]{2,1,0:T(8,128)(2,1)S(1)}, bf16[1,24,2432]{2,1,0:T(8,128)(2,1)S(1)}, u32[]{:S(2)}, u32[]{:S(2)}) collective-permute-start(bf16[1,24,2432]{2,1,0:T(8,128)(2,1)S(1)} %get-tuple-element.140), channel_id=1, source_target_pairs={{0,8},{1,9},{2,10},{3,11},{4,12},{5,13},{6,14},{7,15},{8,0},{9,1},... | collective-permute-start | bytes 350216 | tf_op jit(solution)/shard_map/ppermute | solution.py:653
  275.5 10.9 %collective-permute-start.17 = (bf16[1,24,2432]{2,1,0:T(8,128)(2,1)S(1)}, bf16[1,24,2432]{2,1,0:T(8,128)(2,1)S(1)}, u32[]{:S(2)}, u32[]{:S(2)}) collective-permute-start(bf16[1,24,2432]{2,1,0:T(8,128)(2,1)S(1)} %get-tuple-element.142), channel_id=1, source_target_pairs={{0,16},{1,17},{2,18},{3,19},{4,20},{5,21},{6,22},{7,23},{8,24},{9,... | collective-permute-start | bytes 350216 | tf_op jit(solution)/shard_map/ppermute | solution.py:653
  277.8 8.6 %collective-permute-start.18 = (bf16[1,24,2432]{2,1,0:T(8,128)(2,1)S(1)}, bf16[1,24,2432]{2,1,0:T(8,128)(2,1)S(1)}, u32[]{:S(2)}, u32[]{:S(2)}) collective-permute-start(bf16[1,24,2432]{2,1,0:T(8,128)(2,1)S(1)} %get-tuple-element.141), channel_id=1, source_target_pairs={{0,24},{1,25},{2,26},{3,27},{4,28},{5,29},{6,30},{7,31},{8,16},{9,... | collective-permute-start | bytes 350216 | tf_op jit(solution)/shard_map/ppermute | solution.py:653
  (6 other events, 18.8 us)
Sparse Core Ops, SparseCore 0:
  11.5 102.2 all-gather.1

commit v7 on v6

--- a/solution.py
+++ b/solution.py
@@ -892,15 +892,17 @@
     ordered = jnp.pad(ordered.astype(BF), ((0, 0), (0, 0), (0, LANES - entries)))
     keep = jnp.concatenate([keep, ordered[: devices // 2]], axis=2)
     send = jnp.concatenate([send, ordered[devices // 2 :]], axis=2)
-    narrow = Reduce(keep, send, both, devices).send()
-    grad_one = hold(grad_one, send)
+    send = hold(send, joint.terms, total.terms)
+    narrow = Reduce(keep, send, both, devices).send().join()
+    grad_one = hold(grad_one, narrow.parts)
+    narrow.send()
     filled = ()
     for which in range(batch):
         if which == batch - 1:
-            for chain in (narrow, joint, total):
+            for chain in (joint, total):
                 chain.after(filled).join()
-            grad_one = hold(grad_one, *(chain.parts for chain in (narrow, joint, total)))
-            for chain in (narrow, joint, total):
+            grad_one = hold(grad_one, joint.parts, total.parts)
+            for chain in (joint, total):
                 chain.send()
         filled = (input_gradient(grad_one, gathered, part, which, batch, filled),)
     input_grad = filled[0]

time: 296 us -> 302 us (1.020)
  waiting for transfers between devices: 73.4 us -> 77.2 us
  starting transfers between devices: 27 us -> 30.4 us
  other arithmetic: 22.4 us -> 25.7 us
    ppermute x23, waiting for transfers between devices: 65.6 us -> 69.3 us  [swap(): lax.ppermute(value, 'dp', [(index, index ^ mask) for index in range(devic...]
    pallas_call x1, Pallas kernels: 39.5 us -> 36 us  [middle(): pl.pallas_call(functools.partial(middle_kernel, seq=seq, piece=piece), gr...]
    ppermute x23, starting transfers between devices: 27 us -> 30.4 us  [swap(): lax.ppermute(value, 'dp', [(index, index ^ mask) for index in range(devic...]
  transfers between devices with their start and end apart: 24 -> 24, of which waited for: 12 -> 14; matrix products, arithmetic and copies ran while one was open for 7% -> 7% of each run, Pallas kernels for 34% -> 34%
where the time goes in v7:
time: 302 us; the launch traced here: 301 us
  Pallas kernels  149 us (49%)
  waiting for transfers between devices  77.2 us (26%)
  starting transfers between devices  30.4 us (10%)
  other arithmetic  25.7 us (9%)
  between operations  14.5 us (5%)
  local copies, waits for them, and re-layouts  4.68 us (2%)
    ppermute x23, waiting for transfers between devices, swap(): lax.ppermute(value, 'dp', [(index, index ^ mask) for index in range(devic...  69.3 us
    pallas_call x1, Pallas kernels, middle(): pl.pallas_call(functools.partial(middle_kernel, seq=seq, piece=piece), gr...  36 us
    ppermute x23, starting transfers between devices, swap(): lax.ppermute(value, 'dp', [(index, index ^ mask) for index in range(devic...  30.4 us
    pallas_call x2, Pallas kernels, attend_backward(): pl.pallas_call(functools.partial(attend_back_kernel, which=which), grid_s...  30.4 us
    pallas_call x2, Pallas kernels, attend_forward(): pl.pallas_call(functools.partial(attend_kernel, which=which), grid_spec=g...  21.2 us
    pallas_call x1, Pallas kernels, joint_gradient(): pl.pallas_call(joint_kernel, grid_spec=grid_spec, out_shape=[shape, shape...  13.4 us
    pallas_call x1, Pallas kernels, tall_gradient(): pl.pallas_call(tall_kernel, grid_spec=grid_spec, out_shape=[shape, shape]...  11.6 us
    pallas_call x2, Pallas kernels, input_gradient(): pl.pallas_call(functools.partial(input_kernel, groups=len(grads)), grid=(...  11.3 us
  transfers between devices with their start and end apart: 24, of which 14 were waited for; matrix products, arithmetic and copies ran while one was open for 7% of the time, Pallas kernels for 34%

profile of v7, /device:TPU:0, one launch (start us, length us, event | category | flops | bytes accessed | tf_op | source)
XLA Modules:
  0.0 301.1 jit_solution(16258082863660295222)
XLA Ops:
  7.3 1.0 convert_element_type.290
  11.2 4.1 %collective-permute-start = (bf16[1,24,2560]{2,1,0:T(8,128)(2,1)S(1)}, bf16[1,24,2560]{2,1,0:T(8,128)(2,1)S(1)}, u32[]{:S(2)}, u32[]{:S(2)}) collective-permute-start(bf16[1,24,2560]{2,1,0:T(8,128)(2,1)S(1)} %fusion.9), channel_id=1, source_target_pairs={{0,16},{1,17},{2,18},{3,19},{4,20},{5,21},{6,22},{7,23},{8,24},{9,... | collective-permute-start | bytes 368648 | tf_op jit(solution)/shard_map/ppermute | solution.py:653
  15.3 6.0 %collective-permute-done = bf16[1,24,2560]{2,1,0:T(8,128)(2,1)S(1)} collective-permute-done((bf16[1,24,2560]{2,1,0:T(8,128)(2,1)S(1)}, bf16[1,24,2560]{2,1,0:T(8,128)(2,1)S(1)}, u32[]{:S(2)}, u32[]{:S(2)}) %collective-permute-start) | collective-permute-done | bytes 122912 | tf_op jit(solution)/shard_map/ppermute | solution.py:653
  22.1 10.2 %collective-permute-done.1 = bf16[2,24,2560]{2,1,0:T(8,128)(2,1)S(1)} collective-permute-done((bf16[2,24,2560]{2,1,0:T(8,128)(2,1)S(1)}, bf16[2,24,2560]{2,1,0:T(8,128)(2,1)S(1)}, u32[]{:S(2)}, u32[]{:S(2)}) %collective-permute-start.1) | collective-permute-done | bytes 245792 | tf_op jit(solution)/shard_map/ppermute | solution.py:653
  32.4 1.4 collective-permute-start.2
  33.8 1.6 collective-permute-start.3
  36.0 10.9 %collective-permute-done.2 = bf16[4,24,2560]{2,1,0:T(8,128)(2,1)S(1)} collective-permute-done((bf16[4,24,2560]{2,1,0:T(8,128)(2,1)S(1)}, bf16[4,24,2560]{2,1,0:T(8,128)(2,1)S(1)}, u32[]{:S(2)}, u32[]{:S(2)}) %collective-permute-start.2) | collective-permute-done | bytes 491552 | tf_op jit(solution)/shard_map/ppermute | solution.py:653
  47.0 7.0 %collective-permute-done.3 = bf16[4,24,2560]{2,1,0:T(8,128)(2,1)S(1)} collective-permute-done((bf16[4,24,2560]{2,1,0:T(8,128)(2,1)S(1)}, bf16[4,24,2560]{2,1,0:T(8,128)(2,1)S(1)}, u32[]{:S(2)}, u32[]{:S(2)}) %collective-permute-start.3) | collective-permute-done | bytes 491552 | tf_op jit(solution)/shard_map/ppermute | solution.py:653
  54.1 9.6 %collective-permute-done.4 = bf16[4,24,2560]{2,1,0:T(8,128)(2,1)S(1)} collective-permute-done((bf16[4,24,2560]{2,1,0:T(8,128)(2,1)S(1)}, bf16[4,24,2560]{2,1,0:T(8,128)(2,1)S(1)}, u32[]{:S(2)}, u32[]{:S(2)}) %collective-permute-start.4) | collective-permute-done | bytes 491552 | tf_op jit(solution)/shard_map/ppermute | solution.py:653
  65.6 2.3 collective-permute-done.5.taken_ref
  67.9 6.7 %lay_out.1.w_ref = bf16[768,2560]{1,0:T(8,128)(2,1)} custom-call(s32[16]{0:T(128)} %broadcast_xor_fusion.2.index_ref, s32[1]{0:T(128)} %bitcast.odd_ref, bf16[16,24,2560]{2,1,0:T(8,128)(2,1)} %copy-done.5, bf16[16,24,2560]{2,1,0:T(8,128)(2,1)} %collective-permute-done.5.taken_ref), custom_call_target="tpu_custom_call" | custom-call | flops 1966080 | bytes 7864320 | tf_op jit(solution)/shard_map/lay_out/pallas_call | solution.py:778
  76.4 8.4 %project_qkv.1.q_ref.k_ref.v_ref = bf16[1024,2304]{1,0:T(8,128)(2,1)} custom-call(bf16[1024,768]{1,0:T(8,128)(2,1)} %left_ref, bf16[768,2560]{1,0:T(8,128)(2,1)} %lay_out.1.w_ref, f32[12,768]{1,0:T(8,128)} %reshape.92.vec_ref), custom_call_target="tpu_custom_call" | custom-call | flops 3623878656 | bytes 9830400 | tf_op jit(solution)/shard_map/project_qkv/pallas_call | solution.py:64
  84.8 10.6 %attend_forward.2 = (bf16[1024,768]{1,0:T(8,128)(2,1)}, f32[12,2,512]{2,1,0:T(2,128)}) custom-call(s32[2]{0:T(128)} %len_ref.9, bf16[1024,2304]{1,0:T(8,128)(2,1)} %project_qkv.1.q_ref.k_ref.v_ref, bf16[1024,2304]{1,0:T(8,128)(2,1)} %project_qkv.1.q_ref.k_ref.v_ref, bf16[1024,2304]{1,0:T(8,128)(2,1)} %project_qkv.1.q_ref.k_ref.v_ref), custom_call_target="tpu_custom_call" | custom-call | flops 3221225472 | bytes 3145728 | tf_op jit(solution)/shard_map/attend_forward/pallas_call | solution.py:130
  95.4 10.6 %attend_forward.3 = (bf16[1024,768]{1,0:T(8,128)(2,1)}, f32[12,2,512]{2,1,0:T(2,128)}) custom-call(s32[2]{0:T(128)} %len_ref.9, bf16[1024,2304]{1,0:T(8,128)(2,1)} %project_qkv.1.q_ref.k_ref.v_ref, bf16[1024,2304]{1,0:T(8,128)(2,1)} %project_qkv.1.q_ref.k_ref.v_ref, ...), custom_call_target="tpu_custom_call", output_to_operand_aliasing={{0}: (4, {}), {1}: (5, {})} | custom-call | flops 3221225472 | bytes 3145728 | tf_op jit(solution)/shard_map/attend_forward/pallas_call | solution.py:130
  106.0 7.9 %all-gather.2.cloned.1.call-done.w_attn.w_up.w_down = bf16[768,6912]{1,0:T(8,128)(2,1)} async-done(((bf16[24,6912]{1,0:T(8,128)(2,1)}), bf16[768,6912]{1,0:T(8,128)(2,1)}) %all-gather.2.cloned.1.call-update) | async-done | bytes 10616848 | tf_op jit(solution)/shard_map/all_gather | solution.py:836
  113.9 36.0 %middle.1 = (bf16[1024,768]{1,0:T(8,128)(2,1)}, bf16[1024,768]{1,0:T(8,128)(2,1)}, bf16[1024,3072]{1,0:T(8,128)(2,1)}, bf16[1024,3072]{1,0:T(8,128)(2,1)}, bf16[...) custom-call(s32[2]{0:T(128)} %len_ref.9, ...), custom_call_target="tpu_custom_call" | custom-call | flops 21743271936 | bytes 37748736 | tf_op jit(solution)/shard_map/middle/pallas_call | solution.py:379
  149.9 11.6 %tall_gradient.1 = (bf16[16,96,768]{2,1,0:T(8,128)(2,1)}, bf16[16,96,768]{2,1,0:T(8,128)(2,1)}) custom-call(s32[32]{0:T(128)} %get-tuple-element.149.slot_ref, bf16[1024,3072]{1,0:T(8,128)(2,1)} %get-tuple-element.70.left_ref, bf16[1024,768]{1,0:T(8,128)(2,1)} %get-tuple-element.71.right_ref), custom_call_target="tpu_custom_call" | custom-call | flops 4831838208 | bytes 12582912 | tf_op jit(solution)/shard_map/tall_gradient/pallas_call | solution.py:603
  161.4 3.7 %collective-permute-start.6 = (bf16[16,96,768]{2,1,0:T(8,128)(2,1)}, bf16[16,96,768]{2,1,0:T(8,128)(2,1)S(1)}, u32[]{:S(2)}, u32[]{:S(2)}) collective-permute-start(bf16[16,96,768]{2,1,0:T(8,128)(2,1)} %get-tuple-element.73), channel_id=1, source_target_pairs={{0,1},{1,0},{2,3},{3,2},{4,5},{5,4},{6,7},{7,6},{8,9},{9,8},{10,11... | collective-permute-start | bytes 7077896 | tf_op jit(solution)/shard_map/ppermute | solution.py:653
  165.2 13.4 %joint_gradient.1 = (bf16[16,24,3840]{2,1,0:T(8,128)(2,1)}, bf16[16,24,3840]{2,1,0:T(8,128)(2,1)}) custom-call(s32[32]{0:T(128)} %get-tuple-element.150.src_ref, bf16[1024,768]{1,0:T(8,128)(2,1)} %get-tuple-element.68.left_ref, bf16[1024,768]{1,0:T(8,128)(2,1)} %get-tuple-element.65.mixed_ref.last_left_ref, bf16[1024,3072]{1,0:T(8,128)(2,1)} %get-tuple-element.74.right_ref, ...), custom_call_target="tpu_custom_call" | custom-call | flops 48318382080 | bytes 16908288 | tf_op jit(solution)/shard_map/joint_gradient/pallas_call | solution.py:536
  180.8 1.7 add_convert_fusion.2
  182.5 1.6 collective-permute-start.9
  185.0 15.2 %attend_backward.2.refs_0_ = bf16[3,1024,768]{2,1,0:T(8,128)(2,1)} custom-call(s32[2]{0:T(128)} %len_ref.9, bf16[1024,2304]{1,0:T(8,128)(2,1)} %project_qkv.1.q_ref.k_ref.v_ref, bf16[1024,2304]{1,0:T(8,128)(2,1)} %project_qkv.1.q_ref.k_ref.v_ref, bf16[1024,2304]{1,0:T(8,128)(2,1)} %project_qkv.1.q_ref.k_ref.v_ref, ...), custom_call_target="tpu_custom_call" | custom-call | flops 64424509440 | bytes 5505024 | tf_op jit(solution)/shard_map/attend_backward/pallas_call | solution.py:194
  200.1 15.2 %attend_backward.3.right_ref.refs_0_ = bf16[3,1024,768]{2,1,0:T(8,128)(2,1)} custom-call(s32[2]{0:T(128)} %len_ref.9, bf16[1024,2304]{1,0:T(8,128)(2,1)} %project_qkv.1.q_ref.k_ref.v_ref, bf16[1024,2304]{1,0:T(8,128)(2,1)} %project_qkv.1.q_ref.k_ref.v_ref, bf16[1024,2304]{1,0:T(8,128)(2,1)} %project_qkv.1.q_ref.k_ref.v_ref, ...), custom_call_target="tpu_custom_call", output_to_operand_aliasing={{}: (6, {})} | custom-call | flops 64424509440 | bytes 5505024 | tf_op jit(solution)/shard_map/attend_backward/pallas_call | solution.py:194
  215.4 1.3 add_convert_fusion.6
  216.7 2.0 collective-permute-start.11
  219.2 1.4 add_convert_fusion.4
  220.7 1.5 collective-permute-start.10
  222.2 9.6 %weight_gradient.1 = (bf16[16,24,2304]{2,1,0:T(8,128)(2,1)}, bf16[16,24,2304]{2,1,0:T(8,128)(2,1)}, f32[3,8,768]{2,1,0:T(8,128)}) custom-call(s32[32]{0:T(128)} %broadcast_xor_fusion.1.src_ref, bf16[1024,768]{1,0:T(8,128)(2,1)} %left_ref, bf16[3,1024,768]{2,1,0:T(8,128)(2,1)} %attend_backward.3.right_ref.refs_0_), custom_call_target="tpu_custom_call" | custom-call | flops 231928233984 | bytes 9830400 | tf_op jit(solution)/shard_map/weight_gradient/pallas_call | solution.py:469
  234.0 1.7 pad_maximum_fusion
  235.7 2.9 collective-permute-done.10
  238.6 3.8 %collective-permute-done.12 = bf16[16,24,2432]{2,1,0:T(8,128)(2,1)S(1)} collective-permute-done((bf16[16,24,2432]{2,1,0:T(8,128)(2,1)S(1)}, bf16[16,24,2432]{2,1,0:T(8,128)(2,1)S(1)}, u32[]{:S(2)}, u32[]{:S(2)}) %collective-permute-start.12) | collective-permute-done | bytes 1867808 | tf_op jit(solution)/shard_map/ppermute | solution.py:653
  242.5 1.5 add_convert_fusion.8
  244.0 1.7 collective-permute-start.13
  246.3 1.2 collective-permute-start.15
  247.5 5.7 %input_gradient.2.refs_1_ = bf16[1024,768]{1,0:T(8,128)(2,1)} custom-call(f32[1024,768]{1,0:T(8,128)} %get-tuple-element.100.resid_ref, bf16[768,2560]{1,0:T(8,128)(2,1)} %lay_out.1.w_ref, bf16[3,1024,768]{2,1,0:T(8,128)(2,1)} %attend_backward.3.right_ref.refs_0_), custom_call_target="tpu_custom_call" | custom-call | flops 115964116992 | bytes 6488064 | tf_op jit(solution)/shard_map/input_gradient/pallas_call | solution.py:630
  253.2 1.3 add_convert_fusion.14
  254.4 1.7 collective-permute-start.21
  256.2 1.3 add_convert_fusion.12
  257.9 5.7 %input_gradient.3 = bf16[1024,768]{1,0:T(8,128)(2,1)} custom-call(f32[1024,768]{1,0:T(8,128)} %get-tuple-element.100.resid_ref, bf16[768,2560]{1,0:T(8,128)(2,1)} %lay_out.1.w_ref, bf16[3,1024,768]{2,1,0:T(8,128)(2,1)} %attend_backward.3.right_ref.refs_0_, bf16[1024,768]{1,0:T(8,128)(2,1)} %input_gradient.2.refs_1_), custom_call_target="tpu_custom_call", output_to_operand_aliasing={{}: (3, {})} | custom-call | flops 115964116992 | bytes 6488064 | tf_op jit(solution)/shard_map/input_gradient/pallas_call | solution.py:630
  264.5 2.0 collective-permute-start.22
  266.5 7.2 %collective-permute-done.19 = bf16[2,24,3840]{2,1,0:T(8,128)(2,1)S(1)} collective-permute-done((bf16[2,24,3840]{2,1,0:T(8,128)(2,1)S(1)}, bf16[2,24,3840]{2,1,0:T(8,128)(2,1)S(1)}, u32[]{:S(2)}, u32[]{:S(2)}) %collective-permute-start.19) | collective-permute-done | bytes 368672 | tf_op jit(solution)/shard_map/ppermute | solution.py:653
  274.3 1.1 multiply_subtract_fusion
  275.4 1.5 add_convert_fusion.22
  277.0 2.2 collective-permute-start.16
  279.7 2.0 collective-permute-start.18
  281.7 7.3 %collective-permute-done.20 = bf16[1,24,3840]{2,1,0:T(8,128)(2,1)S(1)} collective-permute-done((bf16[1,24,3840]{2,1,0:T(8,128)(2,1)S(1)}, bf16[1,24,3840]{2,1,0:T(8,128)(2,1)S(1)}, u32[]{:S(2)}, u32[]{:S(2)}) %collective-permute-start.20) | collective-permute-done | bytes 184352 | tf_op jit(solution)/shard_map/ppermute | solution.py:653
  289.1 1.0 multiply_subtract_fusion.1
  291.5 1.1 add_bitcast_fusion.1
  (130 shorter events, 19.8 us)
Async XLA Ops:
  7.2 3.8 %copy-start.10 = (f32[24,2304]{1,0:T(8,128)S(1)}, f32[24,2304]{1,0:T(8,128)}, u32[]{:S(2)}) copy-start(f32[24,2304]{1,0:T(8,128)} %param.26) | copy-start | bytes 663556
  7.2 3.9 %copy-start.23 = (f32[288]{0:T(512)S(1)}, f32[288]{0:T(512)}, u32[]{:S(2)}) copy-start(f32[288]{0:T(512)} %param.30) | copy-start | bytes 3460
  7.2 106.7 %all-gather.2.cloned.1.call-start = ((), (), s32[]{:S(2)}) async-start(), calls=%async_computation | async-start | bytes 10948608 | tf_op jit(solution)/shard_map/all_gather | solution.py:836
  11.2 10.1 %collective-permute-start = (bf16[1,24,2560]{2,1,0:T(8,128)(2,1)S(1)}, bf16[1,24,2560]{2,1,0:T(8,128)(2,1)S(1)}, u32[]{:S(2)}, u32[]{:S(2)}) collective-permute-start(bf16[1,24,2560]{2,1,0:T(8,128)(2,1)S(1)} %fusion.9), channel_id=1, source_target_pairs={{0,16},{1,17},{2,18},{3,19},{4,20},{5,21},{6,22},{7,23},{8,24},{9,... | collective-permute-start | bytes 368648 | tf_op jit(solution)/shard_map/ppermute | solution.py:653
  21.3 11.0 %collective-permute-start.1 = (bf16[2,24,2560]{2,1,0:T(8,128)(2,1)S(1)}, bf16[2,24,2560]{2,1,0:T(8,128)(2,1)S(1)}, u32[]{:S(2)}, u32[]{:S(2)}) collective-permute-start(bf16[2,24,2560]{2,1,0:T(8,128)(2,1)S(1)} %pad_maximum_fusion.4), channel_id=1, source_target_pairs={{0,8},{1,9},{2,10},{3,11},{4,12},{5,13},{6,14},{7,15},{8,0},{9,1},... | collective-permute-start | bytes 737288 | tf_op jit(solution)/shard_map/ppermute | solution.py:653
  32.3 31.5 %copy-start = (s32[32]{0:T(128)S(1)}, s32[32]{0:T(128)}, u32[]{:S(2)}) copy-start(s32[32]{0:T(128)} %constant.46.clone) | copy-start | bytes 388
  32.4 14.6 %collective-permute-start.2 = (bf16[4,24,2560]{2,1,0:T(8,128)(2,1)S(1)}, bf16[4,24,2560]{2,1,0:T(8,128)(2,1)S(1)}, u32[]{:S(2)}, u32[]{:S(2)}) collective-permute-start(bf16[4,24,2560]{2,1,0:T(8,128)(2,1)S(1)} %pad_maximum_fusion.1), channel_id=1, source_target_pairs={{0,2},{1,3},{2,0},{3,1},{4,6},{5,7},{6,4},{7,5},{8,10},{9,11},{10,... | collective-permute-start | bytes 1474568 | tf_op jit(solution)/shard_map/ppermute | solution.py:653
  33.8 30.8 %copy-start.30 = (s32[16]{0:T(128)S(1)}, s32[16]{0:T(128)}, u32[]{:S(2)}) copy-start(s32[16]{0:T(128)} %constant.47.clone) | copy-start | bytes 196
  33.8 20.3 %collective-permute-start.3 = (bf16[4,24,2560]{2,1,0:T(8,128)(2,1)S(1)}, bf16[4,24,2560]{2,1,0:T(8,128)(2,1)S(1)}, u32[]{:S(2)}, u32[]{:S(2)}) collective-permute-start(bf16[4,24,2560]{2,1,0:T(8,128)(2,1)S(1)} %pad_maximum_fusion.1), channel_id=1, source_target_pairs={{0,4},{1,5},{2,6},{3,7},{4,0},{5,1},{6,2},{7,3},{8,12},{9,13},{10,... | collective-permute-start | bytes 1474568 | tf_op jit(solution)/shard_map/ppermute | solution.py:653
  35.4 28.3 %collective-permute-start.4 = (bf16[4,24,2560]{2,1,0:T(8,128)(2,1)S(1)}, bf16[4,24,2560]{2,1,0:T(8,128)(2,1)S(1)}, u32[]{:S(2)}, u32[]{:S(2)}) collective-permute-start(bf16[4,24,2560]{2,1,0:T(8,128)(2,1)S(1)} %pad_maximum_fusion.1), channel_id=1, source_target_pairs={{0,6},{1,7},{2,4},{3,5},{4,2},{5,3},{6,0},{7,1},{8,14},{9,15},{10,... | collective-permute-start | bytes 1474568 | tf_op jit(solution)/shard_map/ppermute | solution.py:653
  36.0 29.0 %copy-start.28 = (s32[32]{0:T(128)S(1)}, s32[32]{0:T(128)}, u32[]{:S(2)}) copy-start(s32[32]{0:T(128)} %constant.48.clone) | copy-start | bytes 388
  63.7 4.2 %copy-start.5 = (bf16[16,24,2560]{2,1,0:T(8,128)(2,1)}, bf16[16,24,2560]{2,1,0:T(8,128)(2,1)S(1)}, u32[]{:S(2)}) copy-start(bf16[16,24,2560]{2,1,0:T(8,128)(2,1)S(1)} %constant_dynamic-update-slice_fusion.held_ref) | copy-start | bytes 5898244
  63.7 4.2 %collective-permute-start.5 = (bf16[16,24,2560]{2,1,0:T(8,128)(2,1)S(1)}, bf16[16,24,2560]{2,1,0:T(8,128)(2,1)}, u32[]{:S(2)}, u32[]{:S(2)}) collective-permute-start(bf16[16,24,2560]{2,1,0:T(8,128)(2,1)S(1)} %constant_dynamic-update-slice_fusion.held_ref), channel_id=1, source_target_pairs={{0,1},{1,0},{2,3},{3,2},{4,5},{5,4},{6,7},{7,6},{8,9},{9,8},{10,11... | collective-permute-start | bytes 5898248 | tf_op jit(solution)/shard_map/ppermute | solution.py:653
  161.4 17.1 %collective-permute-start.6 = (bf16[16,96,768]{2,1,0:T(8,128)(2,1)}, bf16[16,96,768]{2,1,0:T(8,128)(2,1)S(1)}, u32[]{:S(2)}, u32[]{:S(2)}) collective-permute-start(bf16[16,96,768]{2,1,0:T(8,128)(2,1)} %get-tuple-element.73), channel_id=1, source_target_pairs={{0,1},{1,0},{2,3},{3,2},{4,5},{5,4},{6,7},{7,6},{8,9},{9,8},{10,11... | collective-permute-start | bytes 7077896 | tf_op jit(solution)/shard_map/ppermute | solution.py:653
  165.1 13.4 %copy-start.29 = (s32[32]{0:T(128)S(1)}, s32[32]{0:T(128)}, u32[]{:S(2)}) copy-start(s32[32]{0:T(128)} %constant.49.clone) | copy-start | bytes 388
  165.1 15.0 %copy-start.22 = (f32[12,768]{1,0:T(8,128)S(1)}, f32[12,768]{1,0:T(8,128)}, u32[]{:S(2)}) copy-start(f32[12,768]{1,0:T(8,128)} %get-tuple-element.92) | copy-start | bytes 110596
  165.2 15.7 %copy-start.3 = (bf16[16,96,768]{2,1,0:T(8,128)(2,1)S(1)}, bf16[16,96,768]{2,1,0:T(8,128)(2,1)}, u32[]{:S(2)}) copy-start(bf16[16,96,768]{2,1,0:T(8,128)(2,1)} %get-tuple-element.78) | copy-start | bytes 7077892
  178.5 5.6 %collective-permute-start.7 = (bf16[16,24,3840]{2,1,0:T(8,128)(2,1)}, bf16[16,24,3840]{2,1,0:T(8,128)(2,1)S(1)}, u32[]{:S(2)}, u32[]{:S(2)}) collective-permute-start(bf16[16,24,3840]{2,1,0:T(8,128)(2,1)} %get-tuple-element.81), channel_id=1, source_target_pairs={{0,1},{1,0},{2,3},{3,2},{4,5},{5,4},{6,7},{7,6},{8,9},{9,8},{10,11... | collective-permute-start | bytes 8847368 | tf_op jit(solution)/shard_map/ppermute | solution.py:653
  182.5 32.8 %collective-permute-start.9 = (bf16[8,96,768]{2,1,0:T(8,128)(2,1)}, bf16[8,96,768]{2,1,0:T(8,128)(2,1)S(1)}, u32[]{:S(2)}, u32[]{:S(2)}) collective-permute-start(bf16[8,96,768]{2,1,0:T(8,128)(2,1)} %get-tuple-element.128), channel_id=1, source_target_pairs={{0,2},{1,3},{2,0},{3,1},{4,6},{5,7},{6,4},{7,5},{8,10},{9,11},{10,... | collective-permute-start | bytes 3538952 | tf_op jit(solution)/shard_map/ppermute | solution.py:653
  184.9 34.4 %collective-permute-start.8 = (bf16[8,24,3840]{2,1,0:T(8,128)(2,1)S(1)}, bf16[8,24,3840]{2,1,0:T(8,128)(2,1)S(1)}, u32[]{:S(2)}, u32[]{:S(2)}) collective-permute-start(bf16[8,24,3840]{2,1,0:T(8,128)(2,1)S(1)} %get-tuple-element.126), channel_id=1, source_target_pairs={{0,4},{1,5},{2,6},{3,7},{4,0},{5,1},{6,2},{7,3},{8,12},{9,13},{10,... | collective-permute-start | bytes 4423688 | tf_op jit(solution)/shard_map/ppermute | solution.py:653
  216.7 19.0 %collective-permute-start.11 = (bf16[4,96,768]{2,1,0:T(8,128)(2,1)}, bf16[4,96,768]{2,1,0:T(8,128)(2,1)}, u32[]{:S(2)}, u32[]{:S(2)}) collective-permute-start(bf16[4,96,768]{2,1,0:T(8,128)(2,1)} %get-tuple-element.136), channel_id=1, source_target_pairs={{0,4},{1,5},{2,6},{3,7},{4,0},{5,1},{6,2},{7,3},{8,12},{9,13},{10,... | collective-permute-start | bytes 1769480 | tf_op jit(solution)/shard_map/ppermute | solution.py:653
  220.7 18.0 %collective-permute-start.10 = (bf16[4,24,3840]{2,1,0:T(8,128)(2,1)}, bf16[4,24,3840]{2,1,0:T(8,128)(2,1)}, u32[]{:S(2)}, u32[]{:S(2)}) collective-permute-start(bf16[4,24,3840]{2,1,0:T(8,128)(2,1)} %get-tuple-element.134), channel_id=1, source_target_pairs={{0,2},{1,3},{2,0},{3,1},{4,6},{5,7},{6,4},{7,5},{8,10},{9,11},{10,... | collective-permute-start | bytes 2211848 | tf_op jit(solution)/shard_map/ppermute | solution.py:653
  222.2 10.4 %copy-start.19 = (bf16[10,768]{1,0:T(8,128)(2,1)S(1)}, bf16[10,768]{1,0:T(8,128)(2,1)}, u32[]{:S(2)}) copy-start(bf16[10,768]{1,0:T(8,128)(2,1)} %slice.217) | copy-start | bytes 46084
  222.2 11.6 %copy-start.25 = (pred[32]{0:T(512)(128)(4,1)S(1)}, pred[32]{0:T(512)(128)(4,1)}, u32[]{:S(2)}) copy-start(pred[32]{0:T(512)(128)(4,1)} %get-tuple-element.124) | copy-start | bytes 100
  233.9 8.5 %copy-start.7 = (bf16[16,24,2304]{2,1,0:T(8,128)(2,1)S(1)}, bf16[16,24,2304]{2,1,0:T(8,128)(2,1)}, u32[]{:S(2)}) copy-start(bf16[16,24,2304]{2,1,0:T(8,128)(2,1)} %get-tuple-element.90) | copy-start | bytes 5308420
  238.6 3.8 %collective-permute-start.12 = (bf16[16,24,2432]{2,1,0:T(8,128)(2,1)S(1)}, bf16[16,24,2432]{2,1,0:T(8,128)(2,1)S(1)}, u32[]{:S(2)}, u32[]{:S(2)}) collective-permute-start(bf16[16,24,2432]{2,1,0:T(8,128)(2,1)S(1)} %pad_maximum_fusion), channel_id=1, source_target_pairs={{0,1},{1,0},{2,3},{3,2},{4,5},{5,4},{6,7},{7,6},{8,9},{9,8},{10,11... | collective-permute-start | bytes 5603336 | tf_op jit(solution)/shard_map/ppermute | solution.py:653
  244.0 31.4 %collective-permute-start.13 = (bf16[4,24,2432]{2,1,0:T(8,128)(2,1)}, bf16[4,24,2432]{2,1,0:T(8,128)(2,1)}, u32[]{:S(2)}, u32[]{:S(2)}) collective-permute-start(bf16[4,24,2432]{2,1,0:T(8,128)(2,1)} %get-tuple-element.132), channel_id=1, source_target_pairs={{0,2},{1,3},{2,0},{3,1},{4,6},{5,7},{6,4},{7,5},{8,10},{9,11},{10,... | collective-permute-start | bytes 1400840 | tf_op jit(solution)/shard_map/ppermute | solution.py:653
  245.7 29.7 %collective-permute-start.14 = (bf16[4,24,2432]{2,1,0:T(8,128)(2,1)}, bf16[4,24,2432]{2,1,0:T(8,128)(2,1)}, u32[]{:S(2)}, u32[]{:S(2)}) collective-permute-start(bf16[4,24,2432]{2,1,0:T(8,128)(2,1)} %get-tuple-element.131), channel_id=1, source_target_pairs={{0,4},{1,5},{2,6},{3,7},{4,0},{5,1},{6,2},{7,3},{8,12},{9,13},{10,... | collective-permute-start | bytes 1400840 | tf_op jit(solution)/shard_map/ppermute | solution.py:653
  246.3 29.1 %collective-permute-start.15 = (bf16[4,24,2432]{2,1,0:T(8,128)(2,1)}, bf16[4,24,2432]{2,1,0:T(8,128)(2,1)}, u32[]{:S(2)}, u32[]{:S(2)}) collective-permute-start(bf16[4,24,2432]{2,1,0:T(8,128)(2,1)} %get-tuple-element.130), channel_id=1, source_target_pairs={{0,6},{1,7},{2,4},{3,5},{4,2},{5,3},{6,0},{7,1},{8,14},{9,15},{10,... | collective-permute-start | bytes 1400840 | tf_op jit(solution)/shard_map/ppermute | solution.py:653
  247.5 5.7 %copy-start.4 = (bf16[4,96,768]{2,1,0:T(8,128)(2,1)S(1)}, bf16[4,96,768]{2,1,0:T(8,128)(2,1)}, u32[]{:S(2)}) copy-start(bf16[4,96,768]{2,1,0:T(8,128)(2,1)} %get-tuple-element.98) | copy-start | bytes 1769476
  254.4 10.0 %collective-permute-start.21 = (bf16[2,96,768]{2,1,0:T(8,128)(2,1)S(1)}, bf16[2,96,768]{2,1,0:T(8,128)(2,1)S(1)}, u32[]{:S(2)}, u32[]{:S(2)}) collective-permute-start(bf16[2,96,768]{2,1,0:T(8,128)(2,1)S(1)} %get-tuple-element.143), channel_id=1, source_target_pairs={{0,8},{1,9},{2,10},{3,11},{4,12},{5,13},{6,14},{7,15},{8,0},{9,1},... | collective-permute-start | bytes 884744 | tf_op jit(solution)/shard_map/ppermute | solution.py:653
  257.4 16.3 %collective-permute-start.19 = (bf16[2,24,3840]{2,1,0:T(8,128)(2,1)S(1)}, bf16[2,24,3840]{2,1,0:T(8,128)(2,1)S(1)}, u32[]{:S(2)}, u32[]{:S(2)}) collective-permute-start(bf16[2,24,3840]{2,1,0:T(8,128)(2,1)S(1)} %get-tuple-element.141), channel_id=1, source_target_pairs={{0,8},{1,9},{2,10},{3,11},{4,12},{5,13},{6,14},{7,15},{8,0},{9,1},... | collective-permute-start | bytes 1105928 | tf_op jit(solution)/shard_map/ppermute | solution.py:653
  257.8 16.4 %copy-start.8 = (f32[96,768]{1,0:T(8,128)S(1)}, f32[96,768]{1,0:T(8,128)}, u32[]{:S(2)}) copy-start(f32[96,768]{1,0:T(8,128)} %param.29) | copy-start | bytes 884740
  257.9 16.4 %copy-start.12 = (f32[96,768]{1,0:T(8,128)S(1)}, f32[96,768]{1,0:T(8,128)}, u32[]{:S(2)}) copy-start(f32[96,768]{1,0:T(8,128)} %param.39) | copy-start | bytes 884740
  257.9 16.4 %copy-start.13 = (f32[96,768]{1,0:T(8,128)S(1)}, f32[96,768]{1,0:T(8,128)}, u32[]{:S(2)}) copy-start(f32[96,768]{1,0:T(8,128)} %param.34) | copy-start | bytes 884740
  263.5 11.9 %copy-start.6 = (bf16[4,24,2432]{2,1,0:T(8,128)(2,1)S(1)}, bf16[4,24,2432]{2,1,0:T(8,128)(2,1)}, u32[]{:S(2)}) copy-start(bf16[4,24,2432]{2,1,0:T(8,128)(2,1)} %get-tuple-element.101) | copy-start | bytes 1400836
  264.5 9.8 %collective-permute-start.22 = (bf16[1,96,768]{2,1,0:T(8,128)(2,1)S(1)}, bf16[1,96,768]{2,1,0:T(8,128)(2,1)S(1)}, u32[]{:S(2)}, u32[]{:S(2)}) collective-permute-start(bf16[1,96,768]{2,1,0:T(8,128)(2,1)S(1)} %add_convert_fusion.18), channel_id=1, source_target_pairs={{0,16},{1,17},{2,18},{3,19},{4,20},{5,21},{6,22},{7,23},{8,24},{9,... | collective-permute-start | bytes 442376 | tf_op jit(solution)/shard_map/ppermute | solution.py:653
  273.8 15.2 %collective-permute-start.20 = (bf16[1,24,3840]{2,1,0:T(8,128)(2,1)S(1)}, bf16[1,24,3840]{2,1,0:T(8,128)(2,1)S(1)}, u32[]{:S(2)}, u32[]{:S(2)}) collective-permute-start(bf16[1,24,3840]{2,1,0:T(8,128)(2,1)S(1)} %add_convert_fusion.16), channel_id=1, source_target_pairs={{0,16},{1,17},{2,18},{3,19},{4,20},{5,21},{6,22},{7,23},{8,24},{9,... | collective-permute-start | bytes 552968 | tf_op jit(solution)/shard_map/ppermute | solution.py:653
  275.4 13.6 %copy-start.9 = (f32[24,3072]{1,0:T(8,128)S(1)}, f32[24,3072]{1,0:T(8,128)}, u32[]{:S(2)}) copy-start(f32[24,3072]{1,0:T(8,128)} %param.28) | copy-start | bytes 884740
  275.4 13.6 %copy-start.15 = (f32[24,3072]{1,0:T(8,128)S(1)}, f32[24,3072]{1,0:T(8,128)}, u32[]{:S(2)}) copy-start(f32[24,3072]{1,0:T(8,128)} %param.38) | copy-start | bytes 884740
  275.4 13.7 %copy-start.16 = (f32[24,3072]{1,0:T(8,128)S(1)}, f32[24,3072]{1,0:T(8,128)}, u32[]{:S(2)}) copy-start(f32[24,3072]{1,0:T(8,128)} %param.33) | copy-start | bytes 884740
  277.0 13.2 %copy-start.14 = (f32[24,768]{1,0:T(8,128)S(1)}, f32[24,768]{1,0:T(8,128)}, u32[]{:S(2)}) copy-start(f32[24,768]{1,0:T(8,128)} %param.27) | copy-start | bytes 221188
  277.0 13.2 %copy-start.20 = (f32[24,768]{1,0:T(8,128)S(1)}, f32[24,768]{1,0:T(8,128)}, u32[]{:S(2)}) copy-start(f32[24,768]{1,0:T(8,128)} %param.37) | copy-start | bytes 221188
  277.0 13.2 %copy-start.21 = (f32[24,768]{1,0:T(8,128)S(1)}, f32[24,768]{1,0:T(8,128)}, u32[]{:S(2)}) copy-start(f32[24,768]{1,0:T(8,128)} %param.32) | copy-start | bytes 221188
  277.0 13.9 %collective-permute-start.16 = (bf16[1,24,2432]{2,1,0:T(8,128)(2,1)S(1)}, bf16[1,24,2432]{2,1,0:T(8,128)(2,1)S(1)}, u32[]{:S(2)}, u32[]{:S(2)}) collective-permute-start(bf16[1,24,2432]{2,1,0:T(8,128)(2,1)S(1)} %get-tuple-element.138), channel_id=1, source_target_pairs={{0,8},{1,9},{2,10},{3,11},{4,12},{5,13},{6,14},{7,15},{8,0},{9,1},... | collective-permute-start | bytes 350216 | tf_op jit(solution)/shard_map/ppermute | solution.py:653
  279.3 12.2 %collective-permute-start.17 = (bf16[1,24,2432]{2,1,0:T(8,128)(2,1)S(1)}, bf16[1,24,2432]{2,1,0:T(8,128)(2,1)S(1)}, u32[]{:S(2)}, u32[]{:S(2)}) collective-permute-start(bf16[1,24,2432]{2,1,0:T(8,128)(2,1)S(1)} %get-tuple-element.140), channel_id=1, source_target_pairs={{0,16},{1,17},{2,18},{3,19},{4,20},{5,21},{6,22},{7,23},{8,24},{9,... | collective-permute-start | bytes 350216 | tf_op jit(solution)/shard_map/ppermute | solution.py:653
  279.7 11.8 %collective-permute-start.18 = (bf16[1,24,2432]{2,1,0:T(8,128)(2,1)S(1)}, bf16[1,24,2432]{2,1,0:T(8,128)(2,1)S(1)}, u32[]{:S(2)}, u32[]{:S(2)}) collective-permute-start(bf16[1,24,2432]{2,1,0:T(8,128)(2,1)S(1)} %get-tuple-element.139), channel_id=1, source_target_pairs={{0,24},{1,25},{2,26},{3,27},{4,28},{5,29},{6,30},{7,31},{8,16},{9,... | collective-permute-start | bytes 350216 | tf_op jit(solution)/shard_map/ppermute | solution.py:653
  289.1 3.6 %copy-start.11 = (f32[24,2304]{1,0:T(8,128)S(1)}, f32[24,2304]{1,0:T(8,128)}, u32[]{:S(2)}) copy-start(f32[24,2304]{1,0:T(8,128)} %param.26) | copy-start | bytes 663556
  (7 other events, 24.1 us)
Sparse Core Ops, SparseCore 0:
  11.5 102.3 all-gather.1
